TPU v7x, 32 devices: a whole 2x2x4 slice. The times are simulated.
32 devices in a mesh: seq: 8 (over y, x, core), head: 4 (over z).
Axes of the slice: x: 2, y: 2, z: 4, core: 2. Of those that a mesh axis runs over, the one named last changes fastest.
Arguments:
- x_input: bfloat16 [8192, 1024], P('seq'), may hold values from -6 to 6
- seg_ids: int32 [8192], P('seq'), may hold values from 0 to 1, as said below
- cotangent: bfloat16 [8192, 1024], P('seq'), may hold values from -6 to 6
- norm_gain: float32 [2, 1024], replicated, may hold values from 0.5 to 1.5
- w_z: bfloat16 [2, 1024, 2048], P(None, None, 'head'), may hold values from -0.1875 to 0.1875
- w_x: bfloat16 [2, 1024, 2048], P(None, None, 'head'), may hold values from -0.1875 to 0.1875
- w_bc: bfloat16 [2, 1024, 256], replicated, may hold values from -0.1875 to 0.1875
- w_dt: bfloat16 [2, 1024, 32], P(None, None, 'head'), may hold values from -0.1875 to 0.1875
- conv_x: float32 [2, 4, 2048], P(None, None, 'head'), may hold values from -3 to 3
- conv_bc: float32 [2, 4, 256], replicated, may hold values from -3 to 3
- bias_x: float32 [2, 2048], P(None, 'head'), may hold values from -2 to 2
- bias_bc: float32 [2, 256], replicated, may hold values from -2 to 2
- dt_bias: float32 [2, 32], P(None, 'head'), may hold values from -30 to -3
- a_log: float32 [2, 32], P(None, 'head'), may hold values from 0 to 1
- d_skip: float32 [2, 32], P(None, 'head'), may hold values from 0.5 to 1.5
- gate_gain: float32 [2, 2048], P(None, 'head'), may hold values from 0.5 to 1.5
- w_out: bfloat16 [2, 1024, 2048], P(None, None, 'head'), may hold values from -0.125 to 0.125
Outputs:
- block_out: bfloat16 [8192, 1024], P('seq')
- input_grad: float32 [8192, 1024], P('seq')
- grad_norm_gain: float32 [2, 1024], replicated
- grad_w_z: float32 [2, 1024, 2048], P(None, 'seq', 'head')
- grad_w_x: float32 [2, 1024, 2048], P(None, 'seq', 'head')
- grad_w_bc: float32 [2, 1024, 256], P(None, 'seq')
- grad_w_dt: float32 [2, 1024, 32], P(None, 'seq', 'head')
- grad_conv_x: float32 [2, 4, 2048], P(None, None, 'head')
- grad_conv_bc: float32 [2, 4, 256], replicated
- grad_bias_x: float32 [2, 2048], P(None, 'head')
- grad_bias_bc: float32 [2, 256], replicated
- grad_dt_bias: float32 [2, 32], P(None, 'head')
- grad_a_log: float32 [2, 32], P(None, 'head')
- grad_d_skip: float32 [2, 32], P(None, 'head')
- grad_gate_gain: float32 [2, 2048], P(None, 'head')
- grad_w_out: float32 [2, 1024, 2048], P(None, 'seq', 'head')
Inputs may be any that keep to these rules, and one draw needn't show every extreme that they name: `seg_ids`: ids start at 0 and each token's id equals the previous token's or is one more. There are exactly 2 documents, each of more than 1280 tokens; no document but the first starts at the first token of a block of 1024 tokens.
All inputs are finite; a program needn't handle non-finite values.
Results may differ from a plain program's by a relative error of at most 0.012.
Values sent between devices are 32-bit elements; how exact they have to be, the bound alone decides.
No kernel may reach another device: no remote copies, remote signals or barrier semaphores. Data moves between devices by JAX's collectives and lax.ppermute only.
A program may use at most 192 MiB of HBM per device.

v0:
```python
import jax
import jax.numpy as jnp
from jax import lax
from jax.sharding import PartitionSpec as P

HEADDIM = 64
STATE = 128
CONV = 4
GROUP = 256
LAYERS = 2
INNER = 2048


epsilon = 1e-05
highest = lax.Precision.HIGHEST


def shifted(value, axis, steps):
    count = lax.axis_size(axis)
    leading, last = (max(0, -steps), min(count, count - steps))
    return lax.ppermute(value, axis, [(source, source + steps) for source in range(leading, last)])


def prefix(part, axis, combine, identity, reverse):
    count = lax.axis_size(axis)
    place = lax.axis_index(axis)
    ahead = count - 1 - place if reverse else place
    gathered = jax.tree.map(lambda a: lax.all_gather(a, axis), part)
    state = jax.tree.map(lambda a, e: jnp.zeros_like(a) + jnp.asarray(e, a.dtype), part, identity)

    def one(lap, state):
        source = count - 1 - lap if reverse else lap
        return combine(
            state, jax.tree.map(lambda a: lax.dynamic_index_in_dim(a, source, 0, False), gathered)
        )

    return lax.fori_loop(0, ahead, one, state)


def silu_slope(value):
    sigma = jax.nn.sigmoid(value)
    return sigma * (1.0 + value * (1.0 - sigma))


def contract_rows(left, right):
    return lax.dot_general(
        left, right, (((1,), (1,)), ((), ())), preferred_element_type=jnp.float32
    )


def contract_tokens(left, right):
    return lax.dot_general(
        left, right, (((0,), (0,)), ((), ())), preferred_element_type=jnp.float32
    )


def run_labels(parity_ext):
    change = (parity_ext[1:] != parity_ext[:-1]).astype(jnp.int32)
    return jnp.concatenate([jnp.zeros((1,), jnp.int32), jnp.cumsum(change)])


def conv_apply(rows_ext, labels_ext, kernel, offset):
    row_count = rows_ext.shape[0] - CONV + 1
    conv_total = jnp.zeros((row_count, rows_ext.shape[1]), jnp.float32) + offset[None, :]
    for tap_idx in range(CONV):
        same_run = (labels_ext[tap_idx : tap_idx + row_count] == labels_ext[CONV - 1 :]).astype(
            jnp.float32
        )
        conv_total = (
            conv_total
            + kernel[tap_idx][None, :] * rows_ext[tap_idx : tap_idx + row_count] * same_run[:, None]
        )
    return conv_total


def conv_grads(rows_ext, labels_ext, kernel, grad_pre):
    row_count = grad_pre.shape[0]
    grad_rows = jnp.zeros(rows_ext.shape, jnp.float32)
    tap_grads = []
    for tap_idx in range(CONV):
        same_run = (labels_ext[tap_idx : tap_idx + row_count] == labels_ext[CONV - 1 :]).astype(
            jnp.float32
        )
        masked = grad_pre * same_run[:, None]
        grad_rows = grad_rows + jnp.pad(
            kernel[tap_idx][None, :] * masked, ((tap_idx, CONV - 1 - tap_idx), (0, 0))
        )
        tap_grads.append(jnp.sum(rows_ext[tap_idx : tap_idx + row_count] * masked, axis=0))
    return (grad_rows, jnp.stack(tap_grads), jnp.sum(grad_pre, axis=0))


def group_tables(x_heads, bvalue, cvalue, dt_value, da_value, labels, starts):
    nchunk = x_heads.shape[0] // GROUP
    heads_dev = x_heads.shape[1]
    x_groups = x_heads.reshape(nchunk, GROUP, heads_dev, HEADDIM)
    b_groups = bvalue.reshape(nchunk, GROUP, STATE)
    c_groups = cvalue.reshape(nchunk, GROUP, STATE)
    dt_groups = dt_value.reshape(nchunk, GROUP, heads_dev)
    cumulative = jnp.cumsum(da_value.reshape(nchunk, GROUP, heads_dev), axis=1)
    totals = cumulative[:, -1]
    run_groups = labels.reshape(nchunk, GROUP)
    alive_mask = (jnp.cumsum(starts.reshape(nchunk, GROUP), axis=1) == 0).astype(jnp.float32)
    position = jnp.arange(GROUP)
    same_run = (run_groups[:, :, None] == run_groups[:, None, :]) & (
        position[:, None] >= position[None, :]
    )[None]
    mask_four = same_run[:, None]
    cum_heads = jnp.swapaxes(cumulative, 1, 2)
    log_gap = cum_heads[:, :, :, None] - cum_heads[:, :, None, :]
    decay_mat = jnp.where(mask_four, jnp.exp(jnp.where(mask_four, log_gap, 0.0)), 0.0)
    inner_prod = jnp.einsum("ctn,csn->cts", c_groups, b_groups, precision=highest)
    dt_cols = jnp.swapaxes(dt_groups, 1, 2)
    weights = decay_mat * inner_prod[:, None] * dt_cols[:, :, None, :]
    end_mask = (run_groups == run_groups[:, -1:]).astype(jnp.float32)
    tail_base = jnp.exp(totals[:, None, :] - cumulative) * end_mask[:, :, None]
    tail_weight = tail_base * dt_groups
    entry_decay = jnp.exp(cumulative) * alive_mask[:, :, None]
    through = alive_mask[:, -1][:, None] * jnp.exp(totals)
    contrib = jnp.einsum("csh,cshp,csn->chpn", tail_weight, x_groups, b_groups, precision=highest)
    return {
        "x_groups": x_groups,
        "b_groups": b_groups,
        "c_groups": c_groups,
        "dt_cols": dt_cols,
        "inner_prod": inner_prod,
        "decay_mat": decay_mat,
        "weights": weights,
        "tail_base": tail_base,
        "tail_weight": tail_weight,
        "entry_decay": entry_decay,
        "through": through,
        "contrib": contrib,
    }


def local_chain(tables):
    through = tables["through"]
    contrib = tables["contrib"]
    carry = jnp.zeros_like(contrib[0])
    decay_acc = jnp.ones_like(through[0])
    states = []
    prefixes = []
    for group_idx in range(through.shape[0]):
        states.append(carry)
        prefixes.append(decay_acc)
        carry = through[group_idx][:, None, None] * carry + contrib[group_idx]
        decay_acc = decay_acc * through[group_idx]
    return (decay_acc, carry, jnp.stack(states), jnp.stack(prefixes))


def chain_combine(earlier, later):
    return (earlier[0] * later[0], later[0][:, None, None] * earlier[1] + later[1])


def inter_grads(tables, states_full, grad_y):
    weighted = tables["entry_decay"][..., None] * grad_y
    grad_cvalue = jnp.einsum("cthp,chpn->ctn", weighted, states_full, precision=highest)
    grad_states = jnp.einsum("cthp,ctn->chpn", weighted, tables["c_groups"], precision=highest)
    proj_state = jnp.einsum("ctn,chpn->cthp", tables["c_groups"], states_full, precision=highest)
    grad_cum = jnp.sum(weighted * proj_state, axis=3)
    through = tables["through"]
    carry = jnp.zeros_like(grad_states[0])
    decay_acc = jnp.ones_like(through[0])
    backs = []
    suffixes = []
    for group_idx in reversed(range(through.shape[0])):
        carry = grad_states[group_idx] + through[group_idx][:, None, None] * carry
        decay_acc = decay_acc * through[group_idx]
        backs.insert(0, carry)
        suffixes.insert(0, decay_acc)
    return (grad_cvalue, grad_cum, jnp.stack(backs), jnp.stack(suffixes), decay_acc, carry)


def group_grads(tables, states_full, grad_y, grad_cvalue, grad_cum, next_stack):
    x_groups = tables["x_groups"]
    b_groups = tables["b_groups"]
    c_groups = tables["c_groups"]
    through = tables["through"]
    grad_tot = through * jnp.sum(next_stack * states_full, axis=(2, 3))
    state_b = jnp.einsum("chpn,csn->cshp", next_stack, b_groups, precision=highest)
    grad_xs = tables["tail_weight"][..., None] * state_b
    tail_dot = jnp.sum(x_groups * state_b, axis=3)
    grad_bvalue = jnp.einsum(
        "csh,cshp,chpn->csn", tables["tail_weight"], x_groups, next_stack, precision=highest
    )
    grad_dt = tables["tail_base"] * tail_dot
    tail_term = tables["tail_weight"] * tail_dot
    grad_tot = grad_tot + jnp.sum(tail_term, axis=1)
    grad_cum = grad_cum - tail_term
    grad_w = jnp.einsum("cthp,cshp->chts", grad_y, x_groups, precision=highest)
    grad_xs = grad_xs + jnp.einsum("chts,cthp->cshp", tables["weights"], grad_y, precision=highest)
    kernel_term = grad_w * tables["weights"]
    grad_cum = (
        grad_cum
        + jnp.swapaxes(jnp.sum(kernel_term, axis=3), 1, 2)
        - jnp.swapaxes(jnp.sum(kernel_term, axis=2), 1, 2)
    )
    grad_decay = grad_w * tables["decay_mat"]
    grad_inner = jnp.einsum("chts,chs->cts", grad_decay, tables["dt_cols"], precision=highest)
    grad_dt = grad_dt + jnp.swapaxes(
        jnp.einsum("chts,cts->chs", grad_decay, tables["inner_prod"], precision=highest), 1, 2
    )
    grad_cvalue = grad_cvalue + jnp.einsum("cts,csn->ctn", grad_inner, b_groups, precision=highest)
    grad_bvalue = grad_bvalue + jnp.einsum("cts,ctn->csn", grad_inner, c_groups, precision=highest)
    last_row = (jnp.arange(GROUP) == GROUP - 1).astype(jnp.float32)
    grad_cum = grad_cum + last_row[None, :, None] * grad_tot[:, None, :]
    grad_da = jnp.flip(jnp.cumsum(jnp.flip(grad_cum, 1), axis=1), 1)
    return (grad_xs, grad_bvalue, grad_cvalue, grad_dt, grad_da)


def shards(
    x_input,
    seg_ids,
    cotangent,
    norm_gain,
    w_z,
    w_x,
    w_bc,
    w_dt,
    conv_x,
    conv_bc,
    bias_x,
    bias_bc,
    dt_bias,
    a_log,
    d_skip,
    gate_gain,
    w_out,
):
    tok_rows = x_input.shape[0]
    inner_dev = w_z.shape[2]
    heads_dev = w_dt.shape[2]
    rim_rows = CONV - 1
    parity = (seg_ids % 2).astype(jnp.float32)
    hidden = x_input.astype(jnp.float32)
    stored = []
    for layer_idx in range(LAYERS):
        inv_rms = lax.rsqrt(jnp.mean(hidden * hidden, axis=1, keepdims=True) + epsilon)
        normed = (hidden * inv_rms * norm_gain[layer_idx][None, :]).astype(jnp.bfloat16)
        zvalue = jnp.dot(normed, w_z[layer_idx], preferred_element_type=jnp.float32)
        conv_in = jnp.concatenate(
            [
                jnp.dot(normed, w_x[layer_idx], preferred_element_type=jnp.float32),
                jnp.dot(normed, w_bc[layer_idx], preferred_element_type=jnp.float32),
            ],
            axis=1,
        )
        dt_pre = jnp.dot(normed, w_dt[layer_idx], preferred_element_type=jnp.float32)
        edge_rows, edge_parity = shifted(
            (conv_in[tok_rows - rim_rows :], parity[tok_rows - rim_rows :]), "seq", 1
        )
        rows_ext = jnp.concatenate([edge_rows, conv_in], axis=0)
        labels_ext = run_labels(jnp.concatenate([edge_parity, parity]))
        labels = labels_ext[rim_rows:]
        starts = (labels_ext[rim_rows:] != labels_ext[rim_rows - 1 : -1]).astype(jnp.int32)
        kernel = jnp.concatenate([conv_x[layer_idx], conv_bc[layer_idx]], axis=1)
        offset = jnp.concatenate([bias_x[layer_idx], bias_bc[layer_idx]])
        conv_pre = conv_apply(rows_ext, labels_ext, kernel, offset)
        active = jax.nn.silu(conv_pre)
        x_heads = active[:, :inner_dev].reshape(tok_rows, heads_dev, HEADDIM)
        bvalue = active[:, inner_dev : inner_dev + STATE]
        cvalue = active[:, inner_dev + STATE :]
        dt_value = jax.nn.softplus(dt_pre + dt_bias[layer_idx][None, :])
        a_value = -jnp.exp(a_log[layer_idx])
        tables = group_tables(
            x_heads, bvalue, cvalue, dt_value, dt_value * a_value[None, :], labels, starts
        )
        dev_decay, dev_state, local_states, prefixes = local_chain(tables)
        state_in = prefix(
            (dev_decay, dev_state),
            "seq",
            chain_combine,
            (jnp.ones_like(dev_decay), jnp.zeros_like(dev_state)),
            False,
        )[1]
        states_full = local_states + prefixes[:, :, None, None] * state_in[None]
        y_intra = jnp.einsum(
            "chts,cshp->cthp", tables["weights"], tables["x_groups"], precision=highest
        )
        y_inter = tables["entry_decay"][..., None] * jnp.einsum(
            "ctn,chpn->cthp", tables["c_groups"], states_full, precision=highest
        )
        yvalue = (y_intra + y_inter).reshape(tok_rows, heads_dev, HEADDIM) + d_skip[layer_idx][
            None, :, None
        ] * x_heads
        y_flat = yvalue.reshape(tok_rows, inner_dev)
        gated_out = y_flat * jax.nn.silu(zvalue)
        gate_in = (gated_out * gate_gain[layer_idx][None, :]).astype(jnp.bfloat16)
        proj_part = contract_rows(gate_in, w_out[layer_idx])
        proj_sum, square_sum = lax.psum((proj_part, jnp.sum(gated_out * gated_out, axis=1)), "head")
        gate_scale = lax.rsqrt(square_sum / INNER + epsilon)
        stored.append(
            {
                "hidden": hidden,
                "inv_rms": inv_rms,
                "normed": normed,
                "zvalue": zvalue,
                "rows_ext": rows_ext,
                "labels_ext": labels_ext,
                "kernel": kernel,
                "conv_pre": conv_pre,
                "dt_pre": dt_pre,
                "dt_value": dt_value,
                "a_value": a_value,
                "tables": tables,
                "states_full": states_full,
                "x_heads": x_heads,
                "y_flat": y_flat,
                "gated_out": gated_out,
                "gate_in": gate_in,
                "proj_sum": proj_sum,
                "gate_scale": gate_scale,
            }
        )
        hidden = hidden + gate_scale[:, None] * proj_sum
    final_out = hidden.astype(jnp.bfloat16)
    grad_h = cotangent.astype(jnp.float32)
    matrix_list = [None] * LAYERS
    vector_list = [None] * LAYERS
    for layer_idx in reversed(range(LAYERS)):
        saved_layer = stored[layer_idx]
        gate_scale = saved_layer["gate_scale"]
        gated_out = saved_layer["gated_out"]
        zvalue = saved_layer["zvalue"]
        tables = saved_layer["tables"]
        states_full = saved_layer["states_full"]
        grad_proj = (gate_scale[:, None] * grad_h).astype(jnp.bfloat16)
        grad_scale = jnp.sum(grad_h * saved_layer["proj_sum"], axis=1)
        grad_wout = contract_tokens(grad_proj, saved_layer["gate_in"])
        grad_gate_in = jnp.dot(grad_proj, w_out[layer_idx], preferred_element_type=jnp.float32)
        grad_square = grad_scale * -0.5 * gate_scale**3 / INNER
        grad_gated = (
            grad_gate_in * gate_gain[layer_idx][None, :] + 2.0 * gated_out * grad_square[:, None]
        )
        grad_ggain = jnp.sum(grad_gate_in * gated_out, axis=0)
        grad_y = grad_gated * jax.nn.silu(zvalue)
        grad_z = grad_gated * saved_layer["y_flat"] * silu_slope(zvalue)
        grad_y3 = grad_y.reshape(tok_rows, heads_dev, HEADDIM)
        grad_y4 = grad_y3.reshape(tok_rows // GROUP, GROUP, heads_dev, HEADDIM)
        grad_dskip = jnp.sum(grad_y3 * saved_layer["x_heads"], axis=(0, 2))
        grad_cvalue, grad_cum, backs, suffixes, dev_decay, dev_grad = inter_grads(
            tables, states_full, grad_y4
        )
        grad_out = prefix(
            (dev_decay, dev_grad),
            "seq",
            chain_combine,
            (jnp.ones_like(dev_decay), jnp.zeros_like(dev_grad)),
            True,
        )[1]
        full_grads = backs + suffixes[:, :, None, None] * grad_out[None]
        next_stack = jnp.concatenate([full_grads[1:], grad_out[None]], axis=0)
        grad_xs, grad_bvalue, grad_cvalue, grad_dt, grad_da = group_grads(
            tables, states_full, grad_y4, grad_cvalue, grad_cum, next_stack
        )
        grad_xflat = (
            grad_xs.reshape(tok_rows, heads_dev, HEADDIM)
            + d_skip[layer_idx][None, :, None] * grad_y3
        ).reshape(tok_rows, inner_dev)
        grad_da = grad_da.reshape(tok_rows, heads_dev)
        dt_value = saved_layer["dt_value"]
        a_value = saved_layer["a_value"]
        grad_dtv = grad_dt.reshape(tok_rows, heads_dev) + grad_da * a_value[None, :]
        grad_alog = jnp.sum(grad_da * dt_value, axis=0) * a_value
        grad_dtpre = grad_dtv * jax.nn.sigmoid(saved_layer["dt_pre"] + dt_bias[layer_idx][None, :])
        grad_dtbias = jnp.sum(grad_dtpre, axis=0)
        shared_part = jnp.concatenate(
            [grad_bvalue.reshape(tok_rows, STATE), grad_cvalue.reshape(tok_rows, STATE)], axis=1
        )
        shared_sum = lax.psum(shared_part, "head")
        grad_active = jnp.concatenate([grad_xflat, shared_sum], axis=1)
        grad_pre = grad_active * silu_slope(saved_layer["conv_pre"])
        grad_rows, grad_kernel, grad_offset = conv_grads(
            saved_layer["rows_ext"], saved_layer["labels_ext"], saved_layer["kernel"], grad_pre
        )
        rim_back = shifted(grad_rows[:rim_rows], "seq", -1)
        grad_conv_in = grad_rows[rim_rows:] + jnp.pad(rim_back, ((tok_rows - rim_rows, 0), (0, 0)))
        grad_xpre = grad_conv_in[:, :inner_dev].astype(jnp.bfloat16)
        grad_bcpre = grad_conv_in[:, inner_dev:].astype(jnp.bfloat16)
        grad_zlow = grad_z.astype(jnp.bfloat16)
        grad_dtlow = grad_dtpre.astype(jnp.bfloat16)
        partial_in = (
            contract_rows(grad_zlow, w_z[layer_idx])
            + contract_rows(grad_xpre, w_x[layer_idx])
            + contract_rows(grad_dtlow, w_dt[layer_idx])
        )
        grad_normed = lax.psum(partial_in, "head") + contract_rows(grad_bcpre, w_bc[layer_idx])
        normed = saved_layer["normed"]
        grad_wz = contract_tokens(normed, grad_zlow)
        grad_wx = contract_tokens(normed, grad_xpre)
        grad_wbc = contract_tokens(normed, grad_bcpre)
        grad_wdt = contract_tokens(normed, grad_dtlow)
        hidden_in = saved_layer["hidden"]
        inv_rms = saved_layer["inv_rms"]
        grad_ngain = jnp.sum(grad_normed * hidden_in * inv_rms, axis=0)
        back_scaled = grad_normed * norm_gain[layer_idx][None, :]
        grad_h = grad_h + inv_rms * (
            back_scaled
            - hidden_in
            * inv_rms
            * inv_rms
            * jnp.mean(back_scaled * hidden_in, axis=1, keepdims=True)
        )
        matrices = (grad_wz, grad_wx, grad_wbc, grad_wdt, grad_wout)
        vectors = (
            grad_ngain,
            grad_kernel[:, :inner_dev],
            grad_kernel[:, inner_dev:],
            grad_offset[:inner_dev],
            grad_offset[inner_dev:],
            grad_dtbias,
            grad_alog,
            grad_dskip,
            grad_ggain,
        )
        matrix_list[layer_idx] = matrices
        vector_list[layer_idx] = vectors
    matrix_stack = tuple(
        (
            jnp.stack([matrix_list[layer_idx][member] for layer_idx in range(LAYERS)])
            for member in range(5)
        )
    )
    vector_stack = tuple(
        (
            jnp.stack([vector_list[layer_idx][member] for layer_idx in range(LAYERS)])
            for member in range(9)
        )
    )
    matrix_stack = lax.psum_scatter(matrix_stack, "seq", scatter_dimension=1, tiled=True)
    vector_stack = lax.psum(vector_stack, "seq")
    return (
        final_out,
        grad_h,
        vector_stack[0],
        matrix_stack[0],
        matrix_stack[1],
        matrix_stack[2],
        matrix_stack[3],
        vector_stack[1],
        vector_stack[2],
        vector_stack[3],
        vector_stack[4],
        vector_stack[5],
        vector_stack[6],
        vector_stack[7],
        vector_stack[8],
        matrix_stack[4],
    )


def solution(mesh):
    placed = (
        P("seq", None),
        P("seq"),
        P("seq", None),
        P(),
        P(None, None, "head"),
        P(None, None, "head"),
        P(),
        P(None, None, "head"),
        P(None, None, "head"),
        P(),
        P(None, "head"),
        P(),
        P(None, "head"),
        P(None, "head"),
        P(None, "head"),
        P(None, "head"),
        P(None, None, "head"),
    )
    return jax.shard_map(
        shards,
        mesh=mesh,
        in_specs=placed,
        out_specs=(
            P("seq", None),
            P("seq", None),
            P(),
            P(None, "seq", "head"),
            P(None, "seq", "head"),
            P(None, "seq", None),
            P(None, "seq", "head"),
            P(None, None, "head"),
            P(),
            P(None, "head"),
            P(),
            P(None, "head"),
            P(None, "head"),
            P(None, "head"),
            P(None, "head"),
            P(None, "seq", "head"),
        ),
        check_vma=False,
    )
```

profile of v0, /device:TPU:0, one launch (start us, length us, event | category | flops | bytes accessed | tf_op | source)
XLA Modules:
  0.0 1508.9 jit_solution(14254054669846838797)
XLA Ops:
  65.9 9.2 all-gather
  94.6 10.4 bitcast_add_fusion.7
  119.2 12.5 psum.119
  131.7 152.5 %all-reduce.19.cloned.1.call-done = f32[1024,1024]{1,0:T(8,128)} async-done(((f32[1024,1024]{1,0:T(8,128)}), f32[1024,1024]{1,0:T(8,128)}) %all-reduce.19.cloned.1.call-update) | async-done | bytes 4194320 | tf_op jit(solution)/shard_map/psum | solution.py:290
  331.5 12.8 all-gather.1
  362.7 10.4 bitcast_add_fusion.6
  387.8 20.6 %all-gather.2 = f32[8,1,8]{2,1,0:T(1,128)} all-gather(f32[1,1,8]{2,1,0:T(1,128)} %bitcast.522), channel_id=1, replica_groups=mesh['seq'=8,'head'=4] {'seq'}, dimensions={0}, use_global_device_ids=true | all-gather | bytes 288 | tf_op jit(solution)/shard_map/all_gather | solution.py:28
  408.4 12.6 psum.121
  420.9 132.2 %all-reduce.21.cloned.1.call-done = f32[1024,1024]{1,0:T(8,128)} async-done(((f32[1024,1024]{1,0:T(8,128)}), f32[1024,1024]{1,0:T(8,128)}) %all-reduce.21.cloned.1.call-update) | async-done | bytes 4194320 | tf_op jit(solution)/shard_map/psum | solution.py:290
  557.6 7.6 multiply_reduce_fusion.18
  577.2 15.6 %fusion.13 = (f32[4,8,256]{2,1,0:T(8,128)S(1)}, f32[4,8,256]{2,1,0:T(8,128)}, f32[4,8,256,256]{3,2,1,0:T(8,128)}) fusion(f32[4,8,256]{2,1,0:T(8,128)S(1)} %bitcast.492, f32[4,256,256]{2,1,0:T(8,128)} %fusion.247, f32[4,8,256]{2,1,0:T(8,128)S(1)} %copy-done.112, pred[4,256,256]{2,1,0:T(8,128)(4,1)S(1)} %compare_and_fusion, ...), kind=kOutput, calls=%fused_computation.37 | convolution fusion | flops 1627373568 | bytes 14024704 | tf_op jit(solution)/shard_map/cthp,cshp->chts/dot_general | solution.py:190
  593.8 6.7 multiply_reduce_fusion.2
  624.2 12.4 while.54
  647.9 11.1 bitcast_add_fusion.5
  681.5 36.8 %all-reduce.23.cloned.1.call-done = f32[1024,256]{0,1:T(8,128)} async-done(((f32[1024,256]{0,1:T(8,128)}), f32[1024,256]{0,1:T(8,128)}) %all-reduce.23.cloned.1.call-update) | async-done | bytes 1048592 | tf_op jit(solution)/shard_map/psum | solution.py:370
  736.6 13.7 all-gather.3
  750.3 144.1 %all-reduce.25.cloned.1.call-done = f32[1024,1024]{1,0:T(8,128)} async-done(((f32[1024,1024]{1,0:T(8,128)}), f32[1024,1024]{1,0:T(8,128)}) %all-reduce.25.cloned.1.call-update) | async-done | bytes 4194320 | tf_op jit(solution)/shard_map/psum | solution.py:387
  894.5 6.0 multiply_reduce_fusion.4
  907.5 9.4 multiply_reduce_fusion.19
  928.1 14.7 fusion.11
  944.6 6.9 multiply_reduce_fusion
  975.2 12.4 while.55
  999.0 11.4 bitcast_add_fusion.4
  1032.7 36.8 %all-reduce.27.cloned.1.call-done = f32[1024,256]{0,1:T(8,128)} async-done(((f32[1024,256]{0,1:T(8,128)}), f32[1024,256]{0,1:T(8,128)}) %all-reduce.27.cloned.1.call-update) | async-done | bytes 1048592 | tf_op jit(solution)/shard_map/psum | solution.py:370
  1069.5 13.4 multiply_reduce_fusion.11
  1136.5 120.1 %all-reduce.29.cloned.1.call-done = f32[1024,1024]{1,0:T(8,128)} async-done(((f32[1024,1024]{1,0:T(8,128)}), f32[1024,1024]{1,0:T(8,128)}) %all-reduce.29.cloned.1.call-update) | async-done | bytes 4194320 | tf_op jit(solution)/shard_map/psum | solution.py:387
  1262.5 25.1 %all-reduce.11 = (f32[2,1024]{1,0:T(2,128)}, f32[2,4,512]{2,1,0:T(4,128)}, f32[2,4,256]{2,1,0:T(4,128)}, f32[2,512]{1,0:T(2,128)}, f32[2,256]{1,0:T(2,128)}, /*i...) all-reduce(f32[2,1024]{1,0:T(2,128)S(1)} %pad_maximum_fusion.25, ...), channel_id=1, replica_groups=mesh['seq'=8,'head'=4] {'seq'}, use_global_device_ids=true, to_apply=%region_50.51 | all-reduce | flops 10800 | bytes 86400 | tf_op jit(solution)/shard_map/psum | solution.py:431
  1287.6 6.9 fusion.18
  1294.5 51.8 %reduce-scatter.14.cloned.1.call-done = f32[2,128,512]{2,1,0:T(8,128)} async-done(((f32[2,1024,512]{2,1,0:T(8,128)}), f32[2,128,512]{2,1,0:T(8,128)}) %reduce-scatter.14.cloned.1.call-update) | async-done | bytes 524304 | tf_op jit(solution)/shard_map/reduce_scatter | solution.py:430
  1346.2 55.3 %reduce-scatter.6.cloned.1.call-done = f32[2,128,512]{2,1,0:T(8,128)} async-done(((f32[2,1024,512]{2,1,0:T(8,128)}), f32[2,128,512]{2,1,0:T(8,128)}) %reduce-scatter.6.cloned.1.call-update) | async-done | bytes 524304 | tf_op jit(solution)/shard_map/reduce_scatter | solution.py:430
  1401.5 45.3 %reduce-scatter.10.cloned.1.call-done = f32[2,128,256]{2,1,0:T(8,128)} async-done(((f32[2,1024,256]{2,1,0:T(8,128)}), f32[2,128,256]{2,1,0:T(8,128)}) %reduce-scatter.10.cloned.1.call-update) | async-done | bytes 262160 | tf_op jit(solution)/shard_map/reduce_scatter | solution.py:430
  1446.8 55.1 %reduce-scatter.8.cloned.1.call-done = f32[2,128,512]{2,1,0:T(8,128)} async-done(((f32[2,1024,512]{2,1,0:T(8,128)}), f32[2,128,512]{2,1,0:T(8,128)}) %reduce-scatter.8.cloned.1.call-update) | async-done | bytes 524304 | tf_op jit(solution)/shard_map/reduce_scatter | solution.py:430
  (891 shorter events, 424.1 us)
Async XLA Ops:
  7.2 82.9 %all-gather.9.cloned.1.call-start = ((), (), s32[]{:S(2)}) async-start(), calls=%async_computation.5 | async-start | bytes 2359296 | tf_op jit(solution)/shard_map/all_gather | solution.py:28
  8.2 24.7 %collective-permute-start.1 = (f32[3]{0:T(128)S(1)}, f32[3]{0:T(128)S(1)}, u32[]{:S(2)}, u32[]{:S(2)}) collective-permute-start(f32[3]{0:T(128)S(1)} %slice.466), channel_id=1, source_target_pairs={{0,4},{4,8},{8,12},{12,16},{16,20},{20,24},{24,28},{1,5},{5,9},{9,... | collective-permute-start | bytes 44 | tf_op jit(solution)/shard_map/ppermute | solution.py:21
  18.1 23.5 %collective-permute-start = (f32[3,768]{0,1:T(8,128)}, f32[3,768]{0,1:T(8,128)}, u32[]{:S(2)}, u32[]{:S(2)}) collective-permute-start(f32[3,768]{0,1:T(8,128)} %fusion.164), channel_id=1, source_target_pairs={{0,4},{4,8},{8,12},{12,16},{16,20},{20,24},{24,28},{1,5},{5,9},{9,... | collective-permute-start | bytes 27656 | tf_op jit(solution)/shard_map/ppermute | solution.py:21
  33.8 279.3 %copy-start.134 = (f32[1024]{0:T(1024)}, f32[1024]{0:T(1024)S(1)}, u32[]{:S(2)}) copy-start(f32[1024]{0:T(1024)S(1)} %get-tuple-element.442) | copy-start | bytes 12292
  33.8 279.3 %copy-start.136 = (f32[1024]{0:T(1024)}, f32[1024]{0:T(1024)S(1)}, u32[]{:S(2)}) copy-start(f32[1024]{0:T(1024)S(1)} %get-tuple-element.443) | copy-start | bytes 12292
  33.8 279.3 %copy-start.139 = (f32[1024]{0:T(1024)}, f32[1024]{0:T(1024)S(1)}, u32[]{:S(2)}) copy-start(f32[1024]{0:T(1024)S(1)} %get-tuple-element.444) | copy-start | bytes 12292
  61.0 223.1 %all-reduce.19.cloned.1.call-start = ((), (), s32[]{:S(2)}) async-start(), calls=%async_computation.6 | async-start | bytes 8388608 | tf_op jit(solution)/shard_map/psum | solution.py:290
  117.3 240.9 %all-gather.11.cloned.1.call-start = ((), (), s32[]{:S(2)}) async-start(), calls=%async_computation.7 | async-start | bytes 2359296 | tf_op jit(solution)/shard_map/all_gather | solution.py:28
  118.6 194.5 %copy-start.164 = (f32[768]{0:T(1024)}, f32[768]{0:T(1024)S(1)}, u32[]{:S(2)}) copy-start(f32[768]{0:T(1024)S(1)} %get-tuple-element.300) | copy-start | bytes 9220
  131.7 155.5 %copy-start.174 = (f32[1024]{0:T(1024)}, f32[1024]{0:T(1024)S(1)}, u32[]{:S(2)}) copy-start(f32[1024]{0:T(1024)S(1)} %psum.119) | copy-start | bytes 12292
  131.7 155.5 %copy-start.171 = (f32[1024]{0:T(1024)}, f32[1024]{0:T(1024)S(1)}, u32[]{:S(2)}) copy-start(f32[1024]{0:T(1024)S(1)} %add_rsqrt_fusion.2) | copy-start | bytes 12292
  131.7 155.6 %copy-start.150 = (f32[1,1024]{1,0:T(1,128)S(1)}, f32[1,1024]{1,0:T(1,128)}, u32[]{:S(2)}) copy-start(f32[1,1024]{1,0:T(1,128)} %get-tuple-element.439) | copy-start | bytes 12292
  303.6 7.4 collective-permute-start.2
  328.9 224.3 %all-reduce.21.cloned.1.call-start = ((), (), s32[]{:S(2)}) async-start(), calls=%async_computation.8 | async-start | bytes 8388608 | tf_op jit(solution)/shard_map/psum | solution.py:290
  385.9 238.3 %all-gather.13.cloned.1.call-start = ((), (), s32[]{:S(2)}) async-start(), calls=%async_computation.9 | async-start | bytes 2359296 | tf_op jit(solution)/shard_map/all_gather | solution.py:28
  573.2 145.0 %all-reduce.23.cloned.1.call-start = ((), (), s32[]{:S(2)}) async-start(), calls=%async_computation.10 | async-start | bytes 2097152 | tf_op jit(solution)/shard_map/psum | solution.py:370
  669.1 225.3 %all-reduce.25.cloned.1.call-start = ((), (), s32[]{:S(2)}) async-start(), calls=%async_computation.11 | async-start | bytes 8388608 | tf_op jit(solution)/shard_map/psum | solution.py:387
  723.4 4.1 collective-permute-start.3
  735.3 159.1 %copy-start.149 = (f32[1024]{0:T(1024)S(1)}, f32[1024]{0:T(1024)}, u32[]{:S(2)}) copy-start(f32[1024]{0:T(1024)} %copy-done.148) | copy-start | bytes 12292
  735.4 159.1 %copy-start.151 = (f32[1,1024]{1,0:T(1,128)S(1)}, f32[1,1024]{1,0:T(1,128)}, u32[]{:S(2)}) copy-start(f32[1,1024]{1,0:T(1,128)} %get-tuple-element.439) | copy-start | bytes 12292
  735.4 165.1 %copy-start.46 = (bf16[1024,1024]{1,0:T(8,128)(2,1)S(1)}, bf16[1024,1024]{1,0:T(8,128)(2,1)}, u32[]{:S(2)}) copy-start(bf16[1024,1024]{1,0:T(8,128)(2,1)} %param.27) | copy-start | bytes 6291460
  735.4 239.8 %all-gather.15.cloned.1.call-start = ((), (), s32[]{:S(2)}) async-start(), calls=%async_computation.12 | async-start | bytes 2359296 | tf_op jit(solution)/shard_map/all_gather | solution.py:28
  750.3 150.2 %copy-start.188 = (f32[1024]{0:T(1024)S(1)}, f32[1024]{0:T(1024)}, u32[]{:S(2)}) copy-start(f32[1024]{0:T(1024)} %copy-done.187) | copy-start | bytes 12292
  922.6 146.9 %all-reduce.27.cloned.1.call-start = ((), (), s32[]{:S(2)}) async-start(), calls=%async_computation.13 | async-start | bytes 2097152 | tf_op jit(solution)/shard_map/psum | solution.py:370
  1020.3 236.3 %all-reduce.29.cloned.1.call-start = ((), (), s32[]{:S(2)}) async-start(), calls=%async_computation.14 | async-start | bytes 8388608 | tf_op jit(solution)/shard_map/psum | solution.py:387
  1086.7 4.1 collective-permute-start.4
  1097.4 197.1 %reduce-scatter.12.cloned.1.call-start = ((), (), s32[]{:S(2)}) async-start(), calls=%async_computation.18 | async-start | bytes 73728 | tf_op jit(solution)/shard_map/reduce_scatter | solution.py:430
  1108.9 237.3 %reduce-scatter.14.cloned.1.call-start = ((), (), s32[]{:S(2)}) async-start(), calls=%async_computation.19 | async-start | bytes 4718592 | tf_op jit(solution)/shard_map/reduce_scatter | solution.py:430
  1113.7 287.8 %reduce-scatter.6.cloned.1.call-start = ((), (), s32[]{:S(2)}) async-start(), calls=%async_computation.15 | async-start | bytes 4718592 | tf_op jit(solution)/shard_map/reduce_scatter | solution.py:430
  1121.6 325.2 %reduce-scatter.10.cloned.1.call-start = ((), (), s32[]{:S(2)}) async-start(), calls=%async_computation.17 | async-start | bytes 2359296 | tf_op jit(solution)/shard_map/reduce_scatter | solution.py:430
  1127.5 374.5 %reduce-scatter.8.cloned.1.call-start = ((), (), s32[]{:S(2)}) async-start(), calls=%async_computation.16 | async-start | bytes 4718592 | tf_op jit(solution)/shard_map/reduce_scatter | solution.py:430
  1136.5 126.0 %copy-start.190 = (f32[1024]{0:T(1024)S(1)}, f32[1024]{0:T(1024)}, u32[]{:S(2)}) copy-start(f32[1024]{0:T(1024)} %get-tuple-element.276) | copy-start | bytes 12292
  (252 other events, 1965.1 us)
Sparse Core Ops, SparseCore 0:
  61.2 27.4 all-gather.8
  117.4 166.7 all-reduce.18
  329.0 28.8 all-gather.10
  386.0 167.0 all-reduce.20
  573.4 26.8 all-gather.12
  669.2 48.9 all-reduce.22
  735.5 158.8 all-reduce.24
  922.8 26.9 all-gather.14
  1020.5 48.9 all-reduce.26
  1097.5 159.0 all-reduce.28
  1260.2 30.4 reduce-scatter.11
  1294.9 51.3 reduce-scatter.13
  1350.2 51.2 reduce-scatter.5
  1405.6 41.2 reduce-scatter.9
  1450.6 51.3 reduce-scatter.7
where the time goes:
time: 1520 us; the launch traced here: 1510 us
  waiting for transfers between devices  830 us (55%)
  matrix products  232 us (15%)
  other arithmetic  181 us (12%)
  local copies, waits for them, and re-layouts  128 us (8%)
  blocking collectives  106 us (7%)
  between operations  17.5 us (1%)
    psum x2, waiting for transfers between devices, shards(): lax.psum((proj_part, jnp.sum(gated_out * gated_out, axis=1)), 'head')  285 us
    psum x2, waiting for transfers between devices, shards(): lax.psum(partial_in, 'head') + contract_rows(grad_bcpre, w_bc[layer_idx])  264 us
    reduce_scatter x5, waiting for transfers between devices, shards(): lax.psum_scatter(matrix_stack, 'seq', scatter_dimension=1, tiled=True)  207 us
    psum x2, waiting for transfers between devices, shards(): shared_sum = lax.psum(shared_part, 'head')  73.5 us
    all_gather x4, blocking collectives, prefix(): gathered = jax.tree.map(lambda a: lax.all_gather(a, axis), part)  56.2 us
    dot_general x10, matrix products, contract_rows(): lax.dot_general(left, right, (((1,), (1,)), ((), ())), preferred_element_...  42.2 us
    unnamed x532, local copies, waits for them, and re-layouts  31 us
  transfers between devices with their start and end apart: 20, of which 10 were waited for; matrix products, arithmetic and copies ran while one was open for 16% of the time, Pallas kernels for 0%

commit v1 on v0

v1 whole, which is shorter than its diff:
```python
import functools

import jax
import jax.numpy as jnp
from jax import lax
from jax.experimental import pallas as pl
from jax.experimental.pallas import tpu as pltpu
from jax.sharding import PartitionSpec as P

HEADDIM = 64
STATE = 128
CONV = 4
GROUP = 256
LAYERS = 2
INNER = 2048
LANES = 128
ROWS = 8
BC = 2 * STATE

epsilon = 1e-05
highest = lax.Precision.HIGHEST
f32 = jnp.float32
bf16 = jnp.bfloat16


def mm(left, right, dims=((1,), (0,)), precision=None):
    return lax.dot_general(
        left, right, (dims, ((), ())), preferred_element_type=f32, precision=precision
    )


def softplus(value):
    small = jnp.exp(-jnp.abs(value))
    series = small * (1.0 - small * (0.5 - small * (1.0 / 3.0 - small * (0.25 - small * 0.2))))
    return jnp.maximum(value, 0.0) + jnp.where(small < 0.03, series, jnp.log(1.0 + small))


def silu_slope(value, sigma):
    return sigma * (1.0 + value * (1.0 - sigma))


def spread(heads, expand):
    return mm(heads, expand, precision=highest)


def gather_heads(lanes, expand):
    return mm(lanes, expand, ((1,), (1,)), precision=highest)


def in_kernel(
    hid, wall, ngain, taps, bias, dtb, avec, mask, halo, expand, tri,
    normed, zval, cin, cpre, dtp, cum, dtv, xdt, bc, sloc, pref, send,
    state, thru, prev,
):
    step = pl.program_id(0)
    inner = expand.shape[1]

    @pl.when(step == 0)
    def _():
        state[...] = jnp.zeros_like(state)
        thru[...] = jnp.ones_like(thru)
        prev[...] = halo[...]

    h = hid[...].astype(f32)
    inv = lax.rsqrt(jnp.mean(h * h, axis=1, keepdims=True) + epsilon)
    low = (h * inv * ngain[...]).astype(bf16)
    normed[...] = low
    zval[...] = mm(low, wall[:, :inner])
    rows = mm(low, wall[:, inner : 2 * inner + BC])
    pre_dt = mm(low, wall[:, 2 * inner + BC :])
    dtp[...] = pre_dt
    cin[...] = rows
    ext = jnp.concatenate([prev[...], rows], axis=0)
    prev[...] = rows[GROUP - ROWS :]
    total = taps[CONV - 1 : CONV, :] * rows + bias[0:1, :]
    for k in range(CONV - 1):
        first = ROWS - CONV + 1 + k
        total = total + taps[k : k + 1, :] * ext[first : first + GROUP] * mask[:, k : k + 1]
    cpre[...] = total
    act = total * jax.nn.sigmoid(total)
    x = act[:, :inner]
    low_bc = act[:, inner:].astype(bf16)
    bc[...] = low_bc
    dt = softplus(pre_dt + dtb[0:1, :])
    dtv[...] = dt
    run = mm(tri[...], dt * avec[0:1, :], precision=highest)
    cum[...] = run
    last = run[GROUP - 1 : GROUP]
    xdt[...] = (x * spread(dt, expand[...])).astype(bf16)
    tail = jnp.exp(last - run) * mask[:, 4:5] * dt
    contrib = mm(low_bc[:, :STATE], (x * spread(tail, expand[...])).astype(bf16), ((0,), (0,)))
    through = jnp.broadcast_to(jnp.exp(last) * mask[GROUP - 1 : GROUP, 3:4], (ROWS, LANES))
    through = spread(through, expand[...])
    sloc[0] = state[...]
    pref[0] = thru[...]
    state[...] = through[0:1] * state[...] + contrib
    thru[...] = thru[...] * through

    @pl.when(step == pl.num_programs(0) - 1)
    def _():
        send[:STATE] = state[...]
        send[STATE:] = thru[...]


def pair_lanes(value, which):
    lane = lax.broadcasted_iota(jnp.int32, value.shape, 1)
    keep = lane < HEADDIM if which == 0 else lane >= HEADDIM
    return jnp.where(keep, value, jnp.zeros_like(value))


def intra_kernel(cum, xdt, bc, seg, segrow, y):
    inner = xdt.shape[1]
    run = cum[...]
    run_t = run.T
    base = mm(bc[:, STATE:], bc[:, :STATE], ((1,), (1,)))
    t_at = lax.broadcasted_iota(jnp.int32, (GROUP, GROUP), 0)
    s_at = lax.broadcasted_iota(jnp.int32, (GROUP, GROUP), 1)
    same = (seg[:, 0:1] == segrow[0:1, :]) & (t_at >= s_at)
    closed = jnp.where(same, 0.0, -1e30)
    for pair in range(inner // LANES):
        cols = slice(pair * LANES, (pair + 1) * LANES)
        xs = xdt[:, cols]
        parts = []
        for which in range(2):
            head = 2 * pair + which
            decay = jnp.exp(run[:, head : head + 1] - run_t[head : head + 1, :] + closed)
            parts.append(mm((decay * base).astype(bf16), xs))
        lane = lax.broadcasted_iota(jnp.int32, (GROUP, LANES), 1)
        y[:, cols] = jnp.where(lane < HEADDIM, parts[0], parts[1])


def out_kernel(
    yin, cpre, cum, bc, mask, zval, sloc, pref, entry, dskip, ggain, wout, expand, cot,
    y, gate_in, proj, sums,
):
    inner = expand.shape[1]
    pre = cpre[...]
    x = pre * jax.nn.sigmoid(pre)
    full = sloc[0] + pref[0][0:1] * entry[...]
    reach = spread(jnp.exp(cum[...]) * mask[:, 3:4], expand[...])
    value = yin[...] + reach * mm(bc[:, STATE:], full.astype(bf16)) + dskip[0:1, :] * x
    y[...] = value
    z = zval[...]
    gated = value * (z * jax.nn.sigmoid(z))
    low = (gated * ggain[0:1, :]).astype(bf16)
    gate_in[...] = low
    proj[...] = mm(low, wout[...], ((1,), (1,)))
    ones = jnp.ones((ROWS, inner), f32)
    squares = mm(ones, gated * gated, ((1,), (1,)), precision=highest)
    back = mm(cot[...], wout[...])
    dots = mm(ones, low.astype(f32) * back, ((1,), (1,)), precision=highest)
    row = lax.broadcasted_iota(jnp.int32, squares.shape, 0)
    sums[...] = jnp.where(row == 0, squares, dots)


def gate_kernel(
    gh, scale, gsq, y, zval, ggain, wout, cum, bc, mask, expand,
    gproj, dy, dz, gloc, suf, send, acc,
    carry, thru,
):
    step = pl.program_id(0)

    @pl.when(step == 0)
    def _():
        carry[...] = jnp.zeros_like(carry)
        thru[...] = jnp.ones_like(thru)
        acc[...] = jnp.zeros_like(acc)

    gp = (scale[...] * gh[...].astype(f32)).astype(bf16)
    gproj[...] = gp
    ggi = mm(gp, wout[...])
    z = zval[...]
    sigma = jax.nn.sigmoid(z)
    silu = z * sigma
    value = y[...]
    gated = value * silu
    ggated = ggi * ggain[0:1, :] + gated * gsq[...]
    acc[0:1, :] += jnp.sum(ggi * gated, axis=0, keepdims=True)
    low = (ggated * silu).astype(bf16)
    dy[...] = low
    dz[...] = (ggated * value * silu_slope(z, sigma)).astype(bf16)
    run = cum[...]
    last = run[GROUP - 1 : GROUP]
    reach = spread(jnp.exp(run) * mask[:, 3:4], expand[...])
    back = mm(bc[:, STATE:], (reach * low.astype(f32)).astype(bf16), ((0,), (0,)))
    through = jnp.broadcast_to(jnp.exp(last) * mask[GROUP - 1 : GROUP, 3:4], (ROWS, LANES))
    through = spread(through, expand[...])
    gloc[0] = carry[...]
    suf[0] = thru[...]
    carry[...] = back + through[0:1] * carry[...]
    thru[...] = thru[...] * through

    @pl.when(step == pl.num_programs(0) - 1)
    def _():
        send[:STATE] = carry[...]
        send[STATE:] = thru[...]


def intra_back_kernel(cum, xdt, bc, seg, segrow, dy, u, dbc):
    inner = xdt.shape[1]
    run = cum[...]
    run_t = run.T
    base = mm(bc[:, :STATE], bc[:, STATE:], ((1,), (1,)))
    s_at = lax.broadcasted_iota(jnp.int32, (GROUP, GROUP), 0)
    t_at = lax.broadcasted_iota(jnp.int32, (GROUP, GROUP), 1)
    same = (seg[:, 0:1] == segrow[0:1, :]) & (t_at >= s_at)
    closed = jnp.where(same, 0.0, -1e30)
    grad_base = jnp.zeros((GROUP, GROUP), f32)
    for pair in range(inner // LANES):
        cols = slice(pair * LANES, (pair + 1) * LANES)
        xs = xdt[:, cols]
        ds = dy[:, cols]
        parts = []
        for which in range(2):
            head = 2 * pair + which
            decay = jnp.exp(run_t[head : head + 1, :] - run[:, head : head + 1] + closed)
            parts.append(mm((decay * base).astype(bf16), ds))
            grad_base = grad_base + decay * mm(xs, pair_lanes(ds, which), ((1,), (1,)))
        lane = lax.broadcasted_iota(jnp.int32, (GROUP, LANES), 1)
        u[:, cols] = jnp.where(lane < HEADDIM, parts[0], parts[1])
    low = grad_base.astype(bf16)
    dbc[:, :STATE] = mm(low, bc[:, STATE:])
    dbc[:, STATE:] = mm(low, bc[:, :STATE], ((0,), (0,)))


def in_back_kernel(
    uin, dbc, dy, dz, y, cpre, cin, dtp, dtv, cum, xdt, bc, mask, sloc, pref, entry, gloc, suf,
    gout, halo, taps, dtb, avec, dskip, expand, triback,
    gall, last8, rim, gtaps, vecs, dsk,
    nexts,
):
    step = pl.program_id(0)
    inner = expand.shape[1]

    @pl.when(step == 0)
    def _():
        nexts[...] = jnp.zeros_like(nexts)
        gtaps[...] = jnp.zeros_like(gtaps)
        vecs[...] = jnp.zeros_like(vecs)
        dsk[...] = jnp.zeros_like(dsk)

    e = expand[...]
    pre = cpre[...]
    sigma = jax.nn.sigmoid(pre)
    x = (pre * sigma)[:, :inner]
    full = sloc[0] + pref[0][0:1] * entry[...]
    nxt = gloc[0] + suf[0][0:1] * gout[...]
    nxt_low = nxt.astype(bf16)
    run = cum[...]
    last = run[GROUP - 1 : GROUP]
    dt = dtv[...]
    low_dy = dy[...].astype(f32)
    xw = xdt[...].astype(f32)
    tail = spread(jnp.exp(last - run) * mask[:, 4:5], e)
    reach = spread(jnp.exp(run) * mask[:, 3:4], e)
    u_inter = tail * mm(bc[:, :STATE], nxt_low)
    u = uin[...] + u_inter
    dx = spread(dt, e) * u + dskip[0:1, :] * low_dy
    dsk[0:1, :] += jnp.sum(low_dy * x, axis=0, keepdims=True)
    db = dbc[:, :STATE] + mm((tail * xw).astype(bf16), nxt_low, ((1,), (1,)))
    dc = dbc[:, STATE:] + mm((reach * low_dy).astype(bf16), full.astype(bf16), ((1,), (1,)))
    grad_dt = gather_heads(x * u, e)
    y_plain = y[...] - dskip[0:1, :] * x
    grad_cum = gather_heads(low_dy * y_plain - xw * u, e)
    flow = jnp.sum(nxt * full, axis=0, keepdims=True)
    flow = gather_heads(jnp.broadcast_to(flow, (ROWS, inner)), e)[0:1]
    ends = jnp.sum(xw * u_inter, axis=0, keepdims=True)
    ends = gather_heads(jnp.broadcast_to(ends, (ROWS, inner)), e)[0:1]
    grad_tot = mask[GROUP - 1 : GROUP, 3:4] * jnp.exp(last) * flow + ends
    grad_da = mm(triback[...], grad_cum, precision=highest) + grad_tot
    a = avec[0:1, :]
    grad_dtv = grad_dt + grad_da * a
    grad_dtpre = grad_dtv * jax.nn.sigmoid(dtp[...] + dtb[0:1, :])
    vecs[0:1, :] += jnp.sum(grad_da * dt, axis=0, keepdims=True) * a
    vecs[1:2, :] += jnp.sum(grad_dtpre, axis=0, keepdims=True)
    slope = silu_slope(pre, sigma)
    grad_pre = jnp.concatenate([dx, db, dc], axis=1) * slope
    gtaps[4:5, :] += jnp.sum(grad_pre, axis=0, keepdims=True)
    rows = cin[...]
    grad_rows = taps[CONV - 1 : CONV, :] * grad_pre
    gtaps[3:4, :] += jnp.sum(rows * grad_pre, axis=0, keepdims=True)
    masked = []
    for k in range(CONV - 1):
        m = grad_pre * mask[:, k : k + 1]
        masked.append(m[:ROWS])
        ahead = CONV - 1 - k
        shifted = jnp.concatenate([m, nexts[k]], axis=0)[ahead : ahead + GROUP]
        grad_rows = grad_rows + taps[k : k + 1, :] * shifted
        gtaps[k : k + 1, :] += jnp.sum(rows * shifted, axis=0, keepdims=True)
    for k in range(CONV - 1):
        nexts[k] = masked[k]
    gall[:, :inner] = dz[...]
    gall[:, inner : 2 * inner + BC] = grad_rows.astype(bf16)
    gall[:, 2 * inner + BC :] = grad_dtpre.astype(bf16)

    @pl.when(step == 0)
    def _():
        last8[...] = grad_rows[GROUP - ROWS :]

    @pl.when(step == pl.num_programs(0) - 1)
    def _():
        spill = jnp.zeros((ROWS, inner + BC), f32)
        edge = halo[...]
        for k in range(CONV - 1):
            down = ROWS - CONV + 1 + k
            moved = jnp.concatenate([jnp.zeros((ROWS, inner + BC), f32), masked[k]], axis=0)
            moved = moved[ROWS - down : 2 * ROWS - down]
            spill = spill + taps[k : k + 1, :] * moved
            gtaps[k : k + 1, :] += jnp.sum(edge * moved, axis=0, keepdims=True)
        rim[...] = spill


def whole(shape):
    return pl.BlockSpec(shape, lambda c: (0,) * len(shape))


def by_rows(cols, count, reverse=False):
    if reverse:
        return pl.BlockSpec((GROUP, cols), lambda c: (count - 1 - c, 0))
    return pl.BlockSpec((GROUP, cols), lambda c: (c, 0))


def by_group(shape, count, reverse=False):
    if reverse:
        return pl.BlockSpec((1,) + shape, lambda c: (count - 1 - c, 0, 0))
    return pl.BlockSpec((1,) + shape, lambda c: (c, 0, 0))


def by_cols(count):
    return pl.BlockSpec((ROWS, GROUP), lambda c: (0, c))


def call(kernel, count, ins, outs, scratch, flops, name):
    return pl.pallas_call(
        kernel,
        grid=(count,),
        in_specs=[spec for spec, _ in ins],
        out_specs=[spec for spec, _ in outs],
        out_shape=[shape for _, shape in outs],
        scratch_shapes=scratch,
        compiler_params=pltpu.CompilerParams(
            dimension_semantics=("arbitrary",), vmem_limit_bytes=56 * 1024 * 1024
        ),
        cost_estimate=pl.CostEstimate(
            flops=flops, bytes_accessed=8 * 1024 * 1024, transcendentals=0
        ),
        name=name,
    )(*[value for _, value in ins])


def shape(*dims, dtype=f32):
    return jax.ShapeDtypeStruct(dims, dtype)


def shifted(value, axis, steps):
    count = lax.axis_size(axis)
    leading, last = (max(0, -steps), min(count, count - steps))
    return lax.ppermute(value, axis, [(source, source + steps) for source in range(leading, last)])


def chain(part, axis, reverse):
    count = lax.axis_size(axis)
    place = lax.axis_index(axis)
    gathered = lax.all_gather(part, axis)
    decay = gathered[:, STATE]
    source = jnp.arange(count)[:, None, None]
    middle = jnp.arange(count)[None, :, None]
    if reverse:
        between = (middle < source) & (middle > place)
        ahead = jnp.arange(count) > place
    else:
        between = (middle > source) & (middle < place)
        ahead = jnp.arange(count) < place
    weight = jnp.prod(jnp.where(between, decay[None], 1.0), axis=1)
    weight = jnp.where(ahead[:, None], weight, 0.0)
    return jnp.sum(weight[:, None, :] * gathered[:, :STATE], axis=0)


def eight(row):
    return jnp.broadcast_to(row[None, :], (ROWS, row.shape[0]))


def pad_lanes(value):
    return jnp.pad(value, [(0, 0)] * (value.ndim - 1) + [(0, LANES - value.shape[-1])])


def shards(
    x_input,
    seg_ids,
    cotangent,
    norm_gain,
    w_z,
    w_x,
    w_bc,
    w_dt,
    conv_x,
    conv_bc,
    bias_x,
    bias_bc,
    dt_bias,
    a_log,
    d_skip,
    gate_gain,
    w_out,
):
    tok, width = x_input.shape
    inner = w_z.shape[2]
    heads = w_dt.shape[2]
    count = tok // GROUP
    conv_cols = inner + BC
    all_cols = 2 * inner + BC + LANES

    seg = seg_ids.astype(f32)
    edge_seg = shifted(seg[tok - ROWS :], "seq", 1)
    seg_ext = jnp.concatenate([edge_seg, seg])
    before = jnp.concatenate([edge_seg[ROWS - 1 :], seg[GROUP - 1 : tok - 1 : GROUP]])
    after = seg[GROUP - 1 :: GROUP]
    mask = jnp.stack(
        [
            (seg_ext[ROWS - CONV + 1 + k : ROWS - CONV + 1 + k + tok] == seg).astype(f32)
            for k in range(CONV - 1)
        ]
        + [
            (seg == jnp.repeat(before, GROUP)).astype(f32),
            (seg == jnp.repeat(after, GROUP)).astype(f32),
            seg,
            seg,
            seg,
        ],
        axis=1,
    )
    seg_col = seg[:, None]
    seg_row = eight(seg)
    expand = (jnp.arange(LANES)[:, None] == jnp.arange(inner)[None, :] // HEADDIM).astype(f32)
    position = jnp.arange(GROUP)
    tri = (position[:, None] >= position[None, :]).astype(f32)
    triback = (position[:, None] <= position[None, :]).astype(f32)

    matmul_flops = 2 * tok * width
    hidden = x_input
    stored = []
    for layer in range(LAYERS):
        wall = jnp.concatenate(
            [w_z[layer], w_x[layer], w_bc[layer], pad_lanes(w_dt[layer])], axis=1
        )
        taps = jnp.concatenate([conv_x[layer], conv_bc[layer]], axis=1)
        bias = eight(jnp.concatenate([bias_x[layer], bias_bc[layer]]))
        dtb = eight(pad_lanes(dt_bias[layer]))
        avec = eight(pad_lanes(-jnp.exp(a_log[layer])))
        dskip = eight(jnp.repeat(d_skip[layer], HEADDIM))
        ggain = eight(gate_gain[layer])
        ngain = norm_gain[layer][None, :]
        end = hidden[tok - 16 :].astype(f32)
        end = end * lax.rsqrt(jnp.mean(end * end, axis=1, keepdims=True) + epsilon) * ngain
        end = mm(end.astype(bf16), wall[:, inner : 2 * inner + BC])[ROWS:]
        halo = shifted(end, "seq", 1)
        normed, zval, cin, cpre, dtp, cum, dtv, xdt, bc, sloc, pref, send = call(
            in_kernel,
            count,
            [
                (by_rows(width, count), hidden),
                (whole((width, all_cols)), wall),
                (whole((1, width)), ngain),
                (whole((CONV, conv_cols)), taps),
                (whole((ROWS, conv_cols)), bias),
                (whole((ROWS, LANES)), dtb),
                (whole((ROWS, LANES)), avec),
                (by_rows(ROWS, count), mask),
                (whole((ROWS, conv_cols)), halo),
                (whole((LANES, inner)), expand),
                (whole((GROUP, GROUP)), tri),
            ],
            [
                (by_rows(width, count), shape(tok, width, dtype=bf16)),
                (by_rows(inner, count), shape(tok, inner)),
                (by_rows(conv_cols, count), shape(tok, conv_cols)),
                (by_rows(conv_cols, count), shape(tok, conv_cols)),
                (by_rows(LANES, count), shape(tok, LANES)),
                (by_rows(LANES, count), shape(tok, LANES)),
                (by_rows(LANES, count), shape(tok, LANES)),
                (by_rows(inner, count), shape(tok, inner, dtype=bf16)),
                (by_rows(BC, count), shape(tok, BC, dtype=bf16)),
                (by_group((STATE, inner), count), shape(count, STATE, inner)),
                (by_group((ROWS, inner), count), shape(count, ROWS, inner)),
                (whole((STATE + ROWS, inner)), shape(STATE + ROWS, inner)),
            ],
            [
                pltpu.VMEM((STATE, inner), f32),
                pltpu.VMEM((ROWS, inner), f32),
                pltpu.VMEM((ROWS, conv_cols), f32),
            ],
            matmul_flops * all_cols,
            "in_proj_conv",
        )
        (yin,) = call(
            intra_kernel,
            count,
            [
                (by_rows(LANES, count), cum),
                (by_rows(inner, count), xdt),
                (by_rows(BC, count), bc),
                (by_rows(1, count), seg_col),
                (by_cols(count), seg_row),
            ],
            [(by_rows(inner, count), shape(tok, inner))],
            [],
            matmul_flops * 512,
            "ssd_within",
        )
        entry = chain(send, "seq", False)
        y, gate_in, proj, sums = call(
            out_kernel,
            count,
            [
                (by_rows(inner, count), yin),
                (by_rows(inner, count), cpre),
                (by_rows(LANES, count), cum),
                (by_rows(BC, count), bc),
                (by_rows(ROWS, count), mask),
                (by_rows(inner, count), zval),
                (by_group((STATE, inner), count), sloc),
                (by_group((ROWS, inner), count), pref),
                (whole((STATE, inner)), entry),
                (whole((ROWS, inner)), dskip),
                (whole((ROWS, inner)), ggain),
                (whole((width, inner)), w_out[layer]),
                (whole((LANES, inner)), expand),
                (by_rows(width, count), cotangent),
            ],
            [
                (by_rows(inner, count), shape(tok, inner)),
                (by_rows(inner, count), shape(tok, inner, dtype=bf16)),
                (by_rows(width, count), shape(tok, width)),
                (by_cols(count), shape(ROWS, tok)),
            ],
            [],
            matmul_flops * 2 * inner,
            "gate_out_proj",
        )
        sums = lax.psum(sums, "head")
        proj_sum = lax.psum(proj, "head")
        gate_scale = lax.rsqrt(sums[0] / INNER + epsilon)
        stored.append(
            dict(
                hidden=hidden, normed=normed, zval=zval, cin=cin, cpre=cpre, dtp=dtp, cum=cum,
                dtv=dtv, xdt=xdt, bc=bc, sloc=sloc, pref=pref, entry=entry, y=y, gate_in=gate_in,
                proj_sum=proj_sum, gate_scale=gate_scale, dots=sums[1], halo=halo, wall=wall,
                taps=taps, dtb=dtb, avec=avec, dskip=dskip, ggain=ggain,
            )
        )
        hidden = hidden.astype(f32) + gate_scale[:, None] * proj_sum
    final_out = hidden.astype(bf16)

    grad_h = cotangent
    matrices = [None] * LAYERS
    vectors = [None] * LAYERS
    shared = [None] * LAYERS
    for layer in reversed(range(LAYERS)):
        kept = stored[layer]
        gate_scale = kept["gate_scale"]
        if layer == LAYERS - 1:
            grad_scale = kept["dots"]
        else:
            grad_scale = jnp.sum(grad_h * kept["proj_sum"], axis=1)
        gsq = -grad_scale * gate_scale**3 / INNER
        rev = functools.partial(by_rows, count=count, reverse=True)
        rev_group = functools.partial(by_group, count=count, reverse=True)
        gproj, dy, dz, gloc, suf, gsend, acc = call(
            gate_kernel,
            count,
            [
                (rev(width), grad_h),
                (rev(1), gate_scale[:, None]),
                (rev(1), gsq[:, None]),
                (rev(inner), kept["y"]),
                (rev(inner), kept["zval"]),
                (whole((ROWS, inner)), kept["ggain"]),
                (whole((width, inner)), w_out[layer]),
                (rev(LANES), kept["cum"]),
                (rev(BC), kept["bc"]),
                (rev(ROWS), mask),
                (whole((LANES, inner)), expand),
            ],
            [
                (rev(width), shape(tok, width, dtype=bf16)),
                (rev(inner), shape(tok, inner, dtype=bf16)),
                (rev(inner), shape(tok, inner, dtype=bf16)),
                (rev_group((STATE, inner)), shape(count, STATE, inner)),
                (rev_group((ROWS, inner)), shape(count, ROWS, inner)),
                (whole((STATE + ROWS, inner)), shape(STATE + ROWS, inner)),
                (whole((ROWS, inner)), shape(ROWS, inner)),
            ],
            [pltpu.VMEM((STATE, inner), f32), pltpu.VMEM((ROWS, inner), f32)],
            matmul_flops * inner,
            "gate_back",
        )
        u, dbc = call(
            intra_back_kernel,
            count,
            [
                (by_rows(LANES, count), kept["cum"]),
                (by_rows(inner, count), kept["xdt"]),
                (by_rows(BC, count), kept["bc"]),
                (by_rows(1, count), seg_col),
                (by_cols(count), seg_row),
                (by_rows(inner, count), dy),
            ],
            [
                (by_rows(inner, count), shape(tok, inner)),
                (by_rows(BC, count), shape(tok, BC)),
            ],
            [],
            matmul_flops * 1024,
            "ssd_within_back",
        )
        gout = chain(gsend, "seq", True)
        grad_wout = mm(gproj, kept["gate_in"], ((0,), (0,)))
        gall, last8, rim, gtaps, vecs, dsk = call(
            in_back_kernel,
            count,
            [
                (rev(inner), u),
                (rev(BC), dbc),
                (rev(inner), dy),
                (rev(inner), dz),
                (rev(inner), kept["y"]),
                (rev(conv_cols), kept["cpre"]),
                (rev(conv_cols), kept["cin"]),
                (rev(LANES), kept["dtp"]),
                (rev(LANES), kept["dtv"]),
                (rev(LANES), kept["cum"]),
                (rev(inner), kept["xdt"]),
                (rev(BC), kept["bc"]),
                (rev(ROWS), mask),
                (rev_group((STATE, inner)), kept["sloc"]),
                (rev_group((ROWS, inner)), kept["pref"]),
                (whole((STATE, inner)), kept["entry"]),
                (rev_group((STATE, inner)), gloc),
                (rev_group((ROWS, inner)), suf),
                (whole((STATE, inner)), gout),
                (whole((ROWS, conv_cols)), kept["halo"]),
                (whole((CONV, conv_cols)), kept["taps"]),
                (whole((ROWS, LANES)), kept["dtb"]),
                (whole((ROWS, LANES)), kept["avec"]),
                (whole((ROWS, inner)), kept["dskip"]),
                (whole((LANES, inner)), expand),
                (whole((GROUP, GROUP)), triback),
            ],
            [
                (rev(all_cols), shape(tok, all_cols, dtype=bf16)),
                (whole((ROWS, conv_cols)), shape(ROWS, conv_cols)),
                (whole((ROWS, conv_cols)), shape(ROWS, conv_cols)),
                (whole((ROWS, conv_cols)), shape(ROWS, conv_cols)),
                (whole((ROWS, LANES)), shape(ROWS, LANES)),
                (whole((ROWS, inner)), shape(ROWS, inner)),
            ],
            [pltpu.VMEM((CONV - 1, ROWS, conv_cols), f32)],
            matmul_flops * 1024,
            "in_proj_conv_back",
        )
        rim_back = shifted(rim, "seq", -1)
        gall = lax.dynamic_update_slice(
            gall, (last8 + rim_back).astype(bf16), (tok - ROWS, inner)
        )
        grad_normed = lax.psum(mm(gall, kept["wall"], ((1,), (1,))), "head")
        grad_win = mm(kept["normed"], gall, ((0,), (0,)))
        matrices[layer] = (
            lax.psum_scatter(grad_win, "seq", scatter_dimension=0, tiled=True),
            lax.psum_scatter(grad_wout, "seq", scatter_dimension=0, tiled=True),
        )
        hidden_in = kept["hidden"].astype(f32)
        inv = lax.rsqrt(jnp.mean(hidden_in * hidden_in, axis=1, keepdims=True) + epsilon)
        grad_ngain = jnp.sum(grad_normed * hidden_in * inv, axis=0)
        back = grad_normed * norm_gain[layer][None, :]
        grad_h = grad_h.astype(f32) + inv * (
            back - hidden_in * inv * inv * jnp.mean(back * hidden_in, axis=1, keepdims=True)
        )
        vectors[layer] = jnp.concatenate(
            [
                grad_ngain,
                gtaps[: CONV + 1, :inner].reshape(-1),
                acc[0],
                vecs[0],
                vecs[1],
                dsk[0],
            ]
        )
        shared[layer] = gtaps[: CONV + 1, inner:]
    vector = jnp.stack(vectors)
    share = jnp.stack(shared).reshape(LAYERS, -1)
    vector = lax.psum(jnp.concatenate([vector, share], axis=1), "seq")
    share = vector[:, -(CONV + 1) * BC :]
    grad_wbc = jnp.stack([m[0][:, 2 * inner : 2 * inner + BC] for m in matrices])
    share_all = lax.psum(
        jnp.concatenate([grad_wbc.reshape(LAYERS, -1), share], axis=1), "head"
    )
    grad_wbc = share_all[:, : -(CONV + 1) * BC].reshape(grad_wbc.shape)
    share = share_all[:, -(CONV + 1) * BC :].reshape(LAYERS, CONV + 1, BC)
    at = 0
    pieces = []
    for size in (width, CONV * inner, inner, inner, LANES, LANES, inner):
        pieces.append(vector[:, at : at + size])
        at += size
    g_ngain, g_conv, g_bias, g_ggain, g_alog, g_dtb, g_dsk = pieces
    g_win = jnp.stack([m[0] for m in matrices])
    return (
        final_out,
        grad_h,
        g_ngain,
        g_win[:, :, :inner],
        g_win[:, :, inner : 2 * inner],
        grad_wbc,
        g_win[:, :, 2 * inner + BC : 2 * inner + BC + heads],
        g_conv.reshape(LAYERS, CONV, inner),
        share[:, :CONV],
        g_bias,
        share[:, CONV],
        g_dtb[:, :heads],
        g_alog[:, :heads],
        jnp.sum(g_dsk.reshape(LAYERS, heads, HEADDIM), axis=2),
        g_ggain,
        jnp.stack([m[1] for m in matrices]),
    )


def solution(mesh):
    placed = (
        P("seq", None),
        P("seq"),
        P("seq", None),
        P(),
        P(None, None, "head"),
        P(None, None, "head"),
        P(),
        P(None, None, "head"),
        P(None, None, "head"),
        P(),
        P(None, "head"),
        P(),
        P(None, "head"),
        P(None, "head"),
        P(None, "head"),
        P(None, "head"),
        P(None, None, "head"),
    )
    return jax.shard_map(
        shards,
        mesh=mesh,
        in_specs=placed,
        out_specs=(
            P("seq", None),
            P("seq", None),
            P(),
            P(None, "seq", "head"),
            P(None, "seq", "head"),
            P(None, "seq", None),
            P(None, "seq", "head"),
            P(None, None, "head"),
            P(),
            P(None, "head"),
            P(),
            P(None, "head"),
            P(None, "head"),
            P(None, "head"),
            P(None, "head"),
            P(None, "seq", "head"),
        ),
        check_vma=False,
    )
```

time: 1520 us -> 1190 us (0.78)
  matrix products: 232 us -> 36.5 us
  Pallas kernels: 0 us -> 148 us
  other arithmetic: 181 us -> 61 us
  local copies, waits for them, and re-layouts: 128 us -> 41.3 us
  blocking collectives: 106 us -> 65.2 us
  waiting for transfers between devices: 830 us -> 801 us
    dot_general x54 -> x8, matrix products: 232 us -> 36.5 us  [mm(): lax.dot_general(left, right, (dims, ((), ())), preferred_element_type=f32...]
    pallas_call x0 -> x12, Pallas kernels: none -> 148 us  [call(): pl.pallas_call(kernel, grid=(count,), in_specs=[spec for spec, _ in ins],...]
    reduce_scatter x5 -> x4, waiting for transfers between devices: 207 us -> 123 us  [the longest x2 87.7 us: shards(): lax.psum_scatter(grad_wout, 'seq', scatter_dimension=0, tiled=True)]
    all_gather x4, waiting for transfers between devices: 0.01 us -> 74.9 us  [chain(): gathered = lax.all_gather(part, axis)]
    all_gather x4 -> x0, blocking collectives: 56.2 us -> none  [prefix(): gathered = jax.tree.map(lambda a: lax.all_gather(a, axis), part)]
    add x30 -> x1, other arithmetic: 48.1 us -> 6.46 us  [shards(): grad_h.astype(f32)]
    another operation x43 -> x5, other arithmetic: 28.8 us -> 3.05 us  [the longest x1 1.86 us: shards(): jnp.stack([m[1] for m in matrices])]
    reshape x18 -> x4, local copies, waits for them, and re-layouts: 26.2 us -> 0.72 us  [the longest x1 0.63 us: shards(): g_conv.reshape(LAYERS, CONV, inner)]
  transfers between devices with their start and end apart: 20 -> 17, of which waited for: 10 -> 15; matrix products, arithmetic and copies ran while one was open for 16% -> 7% of each run, Pallas kernels for 0% -> 4%
where the time goes in v1:
time: 1190 us; the launch traced here: 1180 us
  waiting for transfers between devices  801 us (67%)
  Pallas kernels  148 us (12%)
  blocking collectives  65.2 us (5%)
  other arithmetic  61 us (5%)
  local copies, waits for them, and re-layouts  41.3 us (3%)
  matrix products  36.5 us (3%)
  between operations  15.5 us (1%)
  starting transfers between devices  12.8 us (1%)
    psum x2, waiting for transfers between devices, shards(): grad_normed = lax.psum(mm(gall, kept['wall'], ((1,), (1,))), 'head')  314 us
    psum x2, waiting for transfers between devices, shards(): proj_sum = lax.psum(proj, 'head')  284 us
    pallas_call x12, Pallas kernels, call(): pl.pallas_call(kernel, grid=(count,), in_specs=[spec for spec, _ in ins],...  148 us
    reduce_scatter x2, waiting for transfers between devices, shards(): lax.psum_scatter(grad_wout, 'seq', scatter_dimension=0, tiled=True)  87.7 us
    all_gather x4, waiting for transfers between devices, chain(): gathered = lax.all_gather(part, axis)  74.9 us
    psum x2, blocking collectives, shards(): sums = lax.psum(sums, 'head')  40.7 us
    dot_general x8, matrix products, mm(): lax.dot_general(left, right, (dims, ((), ())), preferred_element_type=f32...  36.5 us
    reduce_scatter x2, waiting for transfers between devices, shards(): lax.psum_scatter(grad_win, 'seq', scatter_dimension=0, tiled=True)  35.6 us
  transfers between devices with their start and end apart: 17, of which 15 were waited for; matrix products, arithmetic and copies ran while one was open for 7% of the time, Pallas kernels for 4%

profile of v1, /device:TPU:0, one launch (start us, length us, event | category | flops | bytes accessed | tf_op | source)
XLA Modules:
  0.0 1181.4 jit_solution(12299700404661813443)
XLA Ops:
  31.8 17.0 %in_proj_conv.2 = (bf16[1024,1024]{1,0:T(8,128)(2,1)}, f32[1024,512]{1,0:T(8,128)}, f32[1024,768]{1,0:T(8,128)}, f32[1024,768]{1,0:T(8,128)}, f32[1024,128]{1,0:...) custom-call(bf16[1024,1024]{1,0:T(8,128)(2,1)} %hid.1, ...), custom_call_target="tpu_custom_call" | custom-call | flops 2952790016 | bytes 8388608 | tf_op jit(solution)/shard_map/in_proj_conv/pallas_call | solution.py:334
  52.2 5.5 ssd_within.2.yin
  57.7 20.1 %all-gather.9.cloned.1.call-done = f32[1088,512]{1,0:T(8,128)} async-done(((f32[136,512]{1,0:T(8,128)}), f32[1088,512]{1,0:T(8,128)}) %all-gather.9.cloned.1.call-update) | async-done | bytes 2228240 | tf_op jit(solution)/shard_map/all_gather | solution.py:364
  82.7 13.9 %gate_out_proj.2 = (f32[1024,512]{1,0:T(8,128)}, bf16[1024,512]{1,0:T(8,128)(2,1)}, f32[1024,1024]{1,0:T(8,128)}, f32[8,1024]{1,0:T(8,128)}) custom-call(f32[1024,512]{1,0:T(8,128)} %ssd_within.2.yin, f32[1024,768]{1,0:T(8,128)} %get-tuple-element.81.cpre, f32[1024,128]{1,0:T(8,128)} %get-tuple-element.78.cum, bf16[1024,256]{1,0:T(8,128)(2,1)} %get-tuple-element.80.bc, ...), custom_call_target="tpu_custom_call" | custom-call | flops 2147483648 | bytes 8388608 | tf_op jit(solution)/shard_map/gate_out_proj/pallas_call | solution.py:334
  101.2 21.0 %psum.56 = f32[8,1024]{1,0:T(8,128)S(1)} all-reduce(f32[8,1024]{1,0:T(8,128)S(1)} %copy-done.26), channel_id=1, replica_groups=mesh['seq'=8,'head'=4] {'head'}, use_global_device_ids=true, to_apply=%region_3.4 | all-reduce | flops 8192 | bytes 65536 | tf_op jit(solution)/shard_map/psum | solution.py:540
  122.2 130.6 %all-reduce.12.cloned.1.call-done = f32[1024,1024]{1,0:T(8,128)} async-done(((f32[1024,1024]{1,0:T(8,128)}), f32[1024,1024]{1,0:T(8,128)}) %all-reduce.12.cloned.1.call-update) | async-done | bytes 4194320 | tf_op jit(solution)/shard_map/psum | solution.py:541
  261.2 16.9 %in_proj_conv.3 = (bf16[1024,1024]{1,0:T(8,128)(2,1)}, f32[1024,512]{1,0:T(8,128)}, f32[1024,768]{1,0:T(8,128)}, f32[1024,768]{1,0:T(8,128)}, f32[1024,128]{1,0:...) custom-call(f32[1024,1024]{1,0:T(8,128)} %copy-done, ...), custom_call_target="tpu_custom_call" | custom-call | flops 2952790016 | bytes 8388608 | tf_op jit(solution)/shard_map/in_proj_conv/pallas_call | solution.py:334
  278.4 5.5 ssd_within.3.yin
  283.8 24.5 %all-gather.11.cloned.1.call-done = f32[1088,512]{1,0:T(8,128)} async-done(((f32[136,512]{1,0:T(8,128)}), f32[1088,512]{1,0:T(8,128)}) %all-gather.11.cloned.1.call-update) | async-done | bytes 2228240 | tf_op jit(solution)/shard_map/all_gather | solution.py:364
  313.3 13.9 %gate_out_proj.3 = (f32[1024,512]{1,0:T(8,128)}, bf16[1024,512]{1,0:T(8,128)(2,1)}, f32[1024,1024]{1,0:T(8,128)}, f32[8,1024]{1,0:T(8,128)}) custom-call(f32[1024,512]{1,0:T(8,128)} %ssd_within.3.yin, f32[1024,768]{1,0:T(8,128)} %get-tuple-element.91.cpre, f32[1024,128]{1,0:T(8,128)} %get-tuple-element.88.cum, bf16[1024,256]{1,0:T(8,128)(2,1)} %get-tuple-element.90.bc, ...), custom_call_target="tpu_custom_call" | custom-call | flops 2147483648 | bytes 8388608 | tf_op jit(solution)/shard_map/gate_out_proj/pallas_call | solution.py:334
  327.2 19.6 %psum.58 = f32[8,1024]{1,0:T(8,128)S(1)} all-reduce(f32[8,1024]{1,0:T(8,128)} %get-tuple-element.96), channel_id=1, replica_groups=mesh['seq'=8,'head'=4] {'head'}, use_global_device_ids=true, to_apply=%region_8.9 | all-reduce | flops 8192 | bytes 65536 | tf_op jit(solution)/shard_map/psum | solution.py:540
  348.5 9.6 gate_back.2
  359.1 7.5 ssd_within_back.2
  366.6 17.4 %all-gather.13.cloned.1.call-done = f32[1088,512]{1,0:T(8,128)} async-done(((f32[136,512]{1,0:T(8,128)}), f32[1088,512]{1,0:T(8,128)}) %all-gather.13.cloned.1.call-update) | async-done | bytes 2228240 | tf_op jit(solution)/shard_map/all_gather | solution.py:364
  387.7 20.5 %in_proj_conv_back.2 = (bf16[1024,1408]{1,0:T(8,128)(2,1)}, f32[8,768]{1,0:T(8,128)}, f32[8,768]{1,0:T(8,128)}, f32[8,768]{1,0:T(8,128)}, f32[8,128]{1,0:T(8,128)}, /*index=5*/f32[8,512]{1,0:T(8,128)}) custom-call(f32[1024,512]{1,0:T(8,128)} %get-tuple-element.100.uin, f32[1024,256]{1,0:T(8,128)} %get-tuple-element.101.dbc, ...), custom_call_target="tpu_custom_call" | custom-call | flops 2147483648 | bytes 8388608 | tf_op jit(solution)/shard_map/in_proj_conv_back/pallas_call | solution.py:334
  412.9 6.8 fusion.62
  420.3 157.5 %all-reduce.14.cloned.1.call-done = f32[1024,1024]{1,0:T(8,128)} async-done(((f32[1024,1024]{1,0:T(8,128)}), f32[1024,1024]{1,0:T(8,128)}) %all-reduce.14.cloned.1.call-update) | async-done | bytes 4194320 | tf_op jit(solution)/shard_map/psum | solution.py:665
  582.4 5.8 multiply_reduce_fusion.1
  589.3 10.0 gate_back.3
  599.6 6.9 fusion.76
  606.6 7.5 ssd_within_back.3
  614.1 12.8 %all-gather.15.cloned.1.call-done = f32[1088,512]{1,0:T(8,128)} async-done(((f32[136,512]{1,0:T(8,128)}), f32[1088,512]{1,0:T(8,128)}) %all-gather.15.cloned.1.call-update) | async-done | bytes 2228240 | tf_op jit(solution)/shard_map/all_gather | solution.py:364
  630.6 20.5 %in_proj_conv_back.3 = (bf16[1024,1408]{1,0:T(8,128)(2,1)}, f32[8,768]{1,0:T(8,128)}, f32[8,768]{1,0:T(8,128)}, f32[8,768]{1,0:T(8,128)}, f32[8,128]{1,0:T(8,128)}, /*index=5*/f32[8,512]{1,0:T(8,128)}) custom-call(f32[1024,512]{1,0:T(8,128)} %get-tuple-element.114.uin, f32[1024,256]{1,0:T(8,128)} %get-tuple-element.115.dbc, ...), custom_call_target="tpu_custom_call" | custom-call | flops 2147483648 | bytes 8388608 | tf_op jit(solution)/shard_map/in_proj_conv_back/pallas_call | solution.py:334
  655.8 6.9 fusion.64
  664.4 7.0 fusion.75
  690.6 156.4 %all-reduce.16.cloned.1.call-done = f32[1024,1024]{1,0:T(8,128)} async-done(((f32[1024,1024]{1,0:T(8,128)}), f32[1024,1024]{1,0:T(8,128)}) %all-reduce.16.cloned.1.call-update) | async-done | bytes 4194320 | tf_op jit(solution)/shard_map/psum | solution.py:665
  852.1 24.6 %psum.62 = f32[2,6144]{1,0:T(2,128)S(1)} all-reduce(f32[2,6144]{1,0:T(2,128)S(1)} %maximum_maximum_fusion), channel_id=1, replica_groups=mesh['seq'=8,'head'=4] {'seq'}, use_global_device_ids=true, to_apply=%region_23.24 | all-reduce | flops 12288 | bytes 98304 | tf_op jit(solution)/shard_map/psum | solution.py:691
  876.7 31.9 %reduce-scatter.5.cloned.1.call-done = f32[128,1408]{1,0:T(8,128)} async-done(((f32[1024,1408]{1,0:T(8,128)}), f32[128,1408]{1,0:T(8,128)}) %reduce-scatter.5.cloned.1.call-update) | async-done | bytes 720912 | tf_op jit(solution)/shard_map/reduce_scatter | solution.py:668
  910.7 43.2 %reduce-scatter.11.cloned.1.call-done = f32[128,512]{1,0:T(8,128)} async-done(((f32[1024,512]{1,0:T(8,128)}), f32[128,512]{1,0:T(8,128)}) %reduce-scatter.11.cloned.1.call-update) | async-done | bytes 262160 | tf_op jit(solution)/shard_map/reduce_scatter | solution.py:669
  953.9 44.5 %reduce-scatter.9.cloned.1.call-done = f32[128,512]{1,0:T(8,128)} async-done(((f32[1024,512]{1,0:T(8,128)}), f32[128,512]{1,0:T(8,128)}) %reduce-scatter.9.cloned.1.call-update) | async-done | bytes 262160 | tf_op jit(solution)/shard_map/reduce_scatter | solution.py:669
  1003.4 6.5 fusion.7
  1011.7 153.7 %all-reduce.18.cloned.1.call-done = (f32[1024,1024]{1,0:T(8,128)}, f32[2,34048]{1,0:T(2,128)}) async-done(((f32[1024,1024]{1,0:T(8,128)}, f32[2,34048]{1,0:T(2,128)}), (f32[1024,1024]{1,0:T(8,128)}, f32[2,34048]{1,0:T(2,128)})) %all-reduce.18.cloned.1.call-update) | async-done | bytes 4466704 | tf_op jit(solution)/shard_map/psum | solution.py:541
  (289 shorter events, 119.9 us)
Async XLA Ops:
  7.2 70.6 %all-gather.9.cloned.1.call-start = ((), (), s32[]{:S(2)}) async-start(), calls=%async_computation.11 | async-start | bytes 2506752 | tf_op jit(solution)/shard_map/all_gather | solution.py:364
  8.1 19.3 %collective-permute-start = (f32[8]{0:T(128)S(1)}, f32[8]{0:T(128)S(1)}, u32[]{:S(2)}, u32[]{:S(2)}) collective-permute-start(f32[8]{0:T(128)S(1)} %slice.260), channel_id=1, source_target_pairs={{0,4},{4,8},{8,12},{12,16},{16,20},{20,24},{24,28},{1,5},{5,9},{9,... | collective-permute-start | bytes 104 | tf_op jit(solution)/shard_map/ppermute | solution.py:358
  13.0 243.4 %copy-start.23 = (f32[1,1024]{1,0:T(1,128)}, f32[1,1024]{1,0:T(1,128)S(1)}, u32[]{:S(2)}) copy-start(f32[1,1024]{1,0:T(1,128)S(1)} %get-tuple-element.258.ngain) | copy-start | bytes 12292
  15.7 14.3 %collective-permute-start.1 = (f32[8,768]{1,0:T(8,128)S(1)}, f32[8,768]{1,0:T(8,128)S(1)}, u32[]{:S(2)}, u32[]{:S(2)}) collective-permute-start(f32[8,768]{1,0:T(8,128)S(1)} %fusion.17), channel_id=1, source_target_pairs={{0,4},{4,8},{8,12},{12,16},{16,20},{20,24},{24,28},{1,5},{5,9},{9,... | collective-permute-start | bytes 73736 | tf_op jit(solution)/shard_map/ppermute | solution.py:358
  31.8 18.3 %copy-start.35 = (f32[2,512]{1,0:T(2,128)S(1)}, f32[2,512]{1,0:T(2,128)}, u32[]{:S(2)}) copy-start(f32[2,512]{1,0:T(2,128)} %param.32) | copy-start | bytes 12292
  31.8 18.3 %copy-start.15 = (bf16[2,1024,512]{2,1,0:T(8,128)(2,1)S(1)}, bf16[2,1024,512]{2,1,0:T(8,128)(2,1)}, u32[]{:S(2)}) copy-start(bf16[2,1024,512]{2,1,0:T(8,128)(2,1)} %param.33) | copy-start | bytes 6291460
  48.8 204.0 %all-reduce.12.cloned.1.call-start = ((), (), s32[]{:S(2)}) async-start(), calls=%async_computation.4 | async-start | bytes 8388608 | tf_op jit(solution)/shard_map/psum | solution.py:541
  96.6 211.7 %all-gather.11.cloned.1.call-start = ((), (), s32[]{:S(2)}) async-start(), calls=%async_computation.12 | async-start | bytes 2506752 | tf_op jit(solution)/shard_map/all_gather | solution.py:364
  98.1 154.7 %copy-start.3 = (bf16[1024,1024]{1,0:T(8,128)(2,1)S(1)}, bf16[1024,1024]{1,0:T(8,128)(2,1)}, u32[]{:S(2)}) copy-start(bf16[1024,1024]{1,0:T(8,128)(2,1)} %hid.1) | copy-start | bytes 6291460
  256.8 2.6 collective-permute-start.2
  278.2 105.8 %all-gather.13.cloned.1.call-start = ((), (), s32[]{:S(2)}) async-start(), calls=%async_computation.13 | async-start | bytes 2506752 | tf_op jit(solution)/shard_map/all_gather | solution.py:364
  358.1 219.6 %all-reduce.14.cloned.1.call-start = ((), (), s32[]{:S(2)}) async-start(), calls=%async_computation.5 | async-start | bytes 8388608 | tf_op jit(solution)/shard_map/psum | solution.py:665
  387.7 25.2 %copy-start.11 = (bf16[1024,512]{1,0:T(8,128)(2,1)S(1)}, bf16[1024,512]{1,0:T(8,128)(2,1)}, u32[]{:S(2)}) copy-start(bf16[1024,512]{1,0:T(8,128)(2,1)} %get-tuple-element.239) | copy-start | bytes 3145732
  387.7 25.2 %copy-start.19 = (bf16[1024,256]{1,0:T(8,128)(2,1)S(1)}, bf16[1024,256]{1,0:T(8,128)(2,1)}, u32[]{:S(2)}) copy-start(bf16[1024,256]{1,0:T(8,128)(2,1)} %get-tuple-element.245) | copy-start | bytes 1572868
  387.7 25.2 %copy-start.20 = (bf16[1,1024,8]{2,1,0:T(8,128)(2,1)S(1)}, bf16[1,1024,8]{2,1,0:T(8,128)(2,1)}, u32[]{:S(2)}) copy-start(bf16[1,1024,8]{2,1,0:T(8,128)(2,1)} %copy.144) | copy-start | bytes 49156
  408.2 3.3 collective-permute-start.3
  419.7 158.0 %copy-start.24 = (f32[1,1024]{1,0:T(1,128)S(1)}, f32[1,1024]{1,0:T(1,128)}, u32[]{:S(2)}) copy-start(f32[1,1024]{1,0:T(1,128)} %copy-done.23) | copy-start | bytes 12292
  419.7 207.2 %all-gather.15.cloned.1.call-start = ((), (), s32[]{:S(2)}) async-start(), calls=%async_computation.14 | async-start | bytes 2506752 | tf_op jit(solution)/shard_map/all_gather | solution.py:364
  420.2 168.2 %copy-start.5 = (f32[1024,1]{1,0:T(8,128)}, f32[1024,1]{1,0:T(8,128)S(1)}, u32[]{:S(2)}) copy-start(f32[1024,1]{1,0:T(8,128)S(1)} %copy.133.scale) | copy-start | bytes 12292
  420.2 162.1 %copy-start.2 = (bf16[1024,1024]{1,0:T(8,128)(2,1)S(1)}, bf16[1024,1024]{1,0:T(8,128)(2,1)}, u32[]{:S(2)}) copy-start(bf16[1024,1024]{1,0:T(8,128)(2,1)} %gh.1) | copy-start | bytes 6291460
  599.3 90.3 %reduce-scatter.7.cloned.1.call-start = ((), (), s32[]{:S(2)}) async-start(), calls=%async_computation.8 | async-start | bytes 6488064 | tf_op jit(solution)/shard_map/reduce_scatter | solution.py:668
  606.5 240.5 %all-reduce.16.cloned.1.call-start = ((), (), s32[]{:S(2)}) async-start(), calls=%async_computation.6 | async-start | bytes 8388608 | tf_op jit(solution)/shard_map/psum | solution.py:665
  630.6 25.1 %copy-start.8 = (bf16[1024,512]{1,0:T(8,128)(2,1)S(1)}, bf16[1024,512]{1,0:T(8,128)(2,1)}, u32[]{:S(2)}) copy-start(bf16[1024,512]{1,0:T(8,128)(2,1)} %copy-done.7) | copy-start | bytes 3145732
  630.6 25.1 %copy-start.10 = (bf16[1024,512]{1,0:T(8,128)(2,1)S(1)}, bf16[1024,512]{1,0:T(8,128)(2,1)}, u32[]{:S(2)}) copy-start(bf16[1024,512]{1,0:T(8,128)(2,1)} %copy-done.9) | copy-start | bytes 3145732
  630.6 25.1 %copy-start.17 = (bf16[1024,256]{1,0:T(8,128)(2,1)S(1)}, bf16[1024,256]{1,0:T(8,128)(2,1)}, u32[]{:S(2)}) copy-start(bf16[1024,256]{1,0:T(8,128)(2,1)} %copy-done.16) | copy-start | bytes 1572868
  651.1 3.3 collective-permute-start.4
  662.7 246.0 %reduce-scatter.5.cloned.1.call-start = ((), (), s32[]{:S(2)}) async-start(), calls=%async_computation.7 | async-start | bytes 6488064 | tf_op jit(solution)/shard_map/reduce_scatter | solution.py:668
  671.5 282.5 %reduce-scatter.11.cloned.1.call-start = ((), (), s32[]{:S(2)}) async-start(), calls=%async_computation.10 | async-start | bytes 2359296 | tf_op jit(solution)/shard_map/reduce_scatter | solution.py:669
  677.0 321.5 %reduce-scatter.9.cloned.1.call-start = ((), (), s32[]{:S(2)}) async-start(), calls=%async_computation.9 | async-start | bytes 2359296 | tf_op jit(solution)/shard_map/reduce_scatter | solution.py:669
  680.7 166.4 %copy-start.22 = (f32[1,1024]{1,0:T(1,128)S(1)}, f32[1,1024]{1,0:T(1,128)}, u32[]{:S(2)}) copy-start(f32[1,1024]{1,0:T(1,128)} %copy-done.21) | copy-start | bytes 12292
  684.9 162.1 %copy-start.4 = (bf16[1024,1024]{1,0:T(8,128)(2,1)S(1)}, bf16[1024,1024]{1,0:T(8,128)(2,1)}, u32[]{:S(2)}) copy-start(bf16[1024,1024]{1,0:T(8,128)(2,1)} %hid.1) | copy-start | bytes 6291460
  685.0 480.4 %all-reduce.18.cloned.1.call-start = ((), (), s32[]{:S(2)}) async-start(), calls=%async_computation.15 | async-start | bytes 8933376 | tf_op jit(solution)/shard_map/psum | solution.py:541
  (29 other events, 162.6 us)
Sparse Core Ops, SparseCore 0:
  48.9 28.7 all-gather.8
  96.8 155.9 all-reduce.11
  278.3 30.0 all-gather.10
  358.2 25.7 all-gather.12
  419.8 157.8 all-reduce.13
  599.4 27.4 all-gather.14
  630.4 59.1 reduce-scatter.6
  692.1 154.9 all-reduce.15
  850.5 58.0 reduce-scatter.4
  912.7 41.2 reduce-scatter.10
  957.2 41.1 reduce-scatter.8
  1000.9 164.4 all-reduce.17

commit v2 on v1

--- a/solution.py
+++ b/solution.py
@@ -147,7 +147,7 @@
     proj[...] = mm(low, wout[...], ((1,), (1,)))
     ones = jnp.ones((ROWS, inner), f32)
     squares = mm(ones, gated * gated, ((1,), (1,)), precision=highest)
-    back = mm(cot[...], wout[...])
+    back = mm(cot[...].astype(bf16), wout[...])
     dots = mm(ones, low.astype(f32) * back, ((1,), (1,)), precision=highest)
     row = lax.broadcasted_iota(jnp.int32, squares.shape, 0)
     sums[...] = jnp.where(row == 0, squares, dots)
@@ -352,16 +352,26 @@
     return jax.ShapeDtypeStruct(dims, dtype)
 
 
-def shifted(value, axis, steps):
-    count = lax.axis_size(axis)
+SWAP = ((0, 1), (1, 0))
+CROSS = ((0, 1), (3, 2))
+CROSS_BACK = ((1, 0), (2, 3))
+CORE_OUT = ((0, 2), (3, 1))
+CORE_IN = ((2, 0), (1, 3))
+DIAGONAL = ((2, 1), (1, 2))
+BOTH = ("core", "zh")
+BLOCKS = ("chip", "zh")
+
+
+def shifted(value, steps):
+    count = lax.axis_size(BLOCKS)
     leading, last = (max(0, -steps), min(count, count - steps))
-    return lax.ppermute(value, axis, [(source, source + steps) for source in range(leading, last)])
-
-
-def chain(part, axis, reverse):
-    count = lax.axis_size(axis)
-    place = lax.axis_index(axis)
-    gathered = lax.all_gather(part, axis)
+    return lax.ppermute(value, BLOCKS, [(source, source + steps) for source in range(leading, last)])
+
+
+def chain(part, reverse):
+    count = lax.axis_size(BLOCKS)
+    place = lax.axis_index(BLOCKS)
+    gathered = lax.all_gather(part, BLOCKS)
     decay = gathered[:, STATE]
     source = jnp.arange(count)[:, None, None]
     middle = jnp.arange(count)[None, :, None]
@@ -376,12 +386,158 @@
     return jnp.sum(weight[:, None, :] * gathered[:, :STATE], axis=0)
 
 
+def swap(value, axis):
+    return lax.ppermute(value, axis, SWAP)
+
+
+def total(value, axes):
+    for axis in axes:
+        count = lax.axis_size(axis)
+        step = 1
+        while step < count:
+            value = value + lax.ppermute(value, axis, [(i, i ^ step) for i in range(count)])
+            step *= 2
+    return value
+
+
+def take(value, index, count):
+    size = value.shape[0] // count
+    return lax.dynamic_slice_in_dim(value, index * size, size)
+
+
+def ordered(place, mine, theirs):
+    return jnp.where(
+        place == 0, jnp.concatenate([mine, theirs]), jnp.concatenate([theirs, mine])
+    )
+
+
+def scatter_sum(part):
+    core, near = lax.axis_index("core"), lax.axis_index("zl")
+    half = take(part, core, 2) + swap(take(part, 1 - core, 2), "core")
+    if lax.axis_size("zl") == 2:
+        return take(half, near, 2) + swap(take(half, 1 - near, 2), "zl")
+    return lax.psum_scatter(half, "zl", scatter_dimension=0, tiled=True)
+
+
+def own_rows(value):
+    core, near = lax.axis_index("core"), lax.axis_index("zl")
+    return take(take(value, core, 2), near, lax.axis_size("zl"))
+
+
+def gather_near(value):
+    if lax.axis_size("zl") == 2:
+        return ordered(lax.axis_index("zl"), value, swap(value, "zl"))
+    return lax.all_gather(value, "zl", tiled=True)
+
+
+def gather_rows(value):
+    half = gather_near(value)
+    return ordered(lax.axis_index("core"), half, swap(half, "core"))
+
+
+def deliver(value):
+    core, far = lax.axis_index("core"), lax.axis_index("zh")
+    mine = lax.ppermute(value, BOTH, CROSS)
+    theirs = lax.ppermute(value, BOTH, DIAGONAL)
+    near = lax.ppermute(value, BOTH, CORE_IN)
+    held = core == far
+    mine = gather_near(jnp.where(held, value, mine))
+    theirs = gather_near(jnp.where(held, near, theirs))
+    return ordered(core, mine, theirs)
+
+
+def to_block(value):
+    got = lax.ppermute(value, BOTH, CORE_OUT)
+    return jnp.where(lax.axis_index("core") == lax.axis_index("zh"), value, got)
+
+
 def eight(row):
     return jnp.broadcast_to(row[None, :], (ROWS, row.shape[0]))
 
 
 def pad_lanes(value):
     return jnp.pad(value, [(0, 0)] * (value.ndim - 1) + [(0, LANES - value.shape[-1])])
+
+
+def weight_kernel(place, own_z, own_x, own_out, bc, dt, *refs):
+    parts, (wall, wout) = refs[:-2], refs[-2:]
+    block = pl.program_id(0)
+    inner = own_z.shape[1]
+    wall[:, 2 * inner : 2 * inner + BC] = bc[...]
+    wall[:, 2 * inner + BC :] = dt[...].astype(bf16)
+
+    @pl.when(place[1] == 1)
+    def _():
+        wall[:, :inner] = own_z[...]
+        wall[:, inner : 2 * inner] = own_x[...]
+        wout[...] = own_out[...]
+
+    for away in range(len(parts)):
+
+        @pl.when((place[1] == 0) & (lax.bitwise_xor(place[0], block) == away))
+        def _():
+            wall[:, : 2 * inner] = parts[away][:, : 2 * inner].astype(bf16)
+            wout[...] = parts[away][:, 2 * inner :].astype(bf16)
+
+
+def narrow_kernel(wide, narrow):
+    narrow[...] = wide[...].astype(bf16)
+
+
+def narrowed(value):
+    rows, cols = value.shape
+    return pl.pallas_call(
+        narrow_kernel,
+        grid=(rows // GROUP,),
+        in_specs=[by_rows(cols, 0)],
+        out_specs=by_rows(cols, 0),
+        out_shape=shape(rows, cols, dtype=bf16),
+        name="narrowed",
+    )(value)
+
+
+def gather_weights(own_z, own_x, own_out, bc, dt):
+    width, inner = own_z.shape
+    chips = lax.axis_size("chip")
+    chip = lax.axis_index("chip")
+    core, far = lax.axis_index("core"), lax.axis_index("zh")
+    size = width // chips
+    cut = functools.partial(lax.dynamic_slice_in_dim, start_index=chip * size, slice_size=size)
+    piece = jnp.concatenate(
+        [cut(own_z).astype(f32), cut(own_x).astype(f32), cut(own_out).astype(f32)], axis=1
+    )
+    piece = lax.ppermute(piece, ("core", "zh"), CROSS)
+    if chips == 4:
+        parts = [piece]
+        for away in range(1, chips):
+            pairs = [
+                (4 * c + kind, 4 * (c ^ away) + kind) for c in range(chips) for kind in (1, 2)
+            ]
+            parts.append(lax.ppermute(piece, ("chip", "core", "zh"), pairs))
+        place = jnp.stack([chip, (core == far).astype(jnp.int32)]).astype(jnp.int32)
+        blocks = chips
+    else:
+        parts = [lax.all_gather(piece, "chip", tiled=True)]
+        place = jnp.stack([0, (core == far).astype(jnp.int32)]).astype(jnp.int32)
+        blocks, size = 1, width
+    wall_cols = 2 * inner + BC + LANES
+
+    def rows(cols):
+        return pl.BlockSpec((size, cols), lambda c: (c, 0))
+
+    return pl.pallas_call(
+        weight_kernel,
+        grid=(blocks,),
+        in_specs=[pl.BlockSpec(memory_space=pltpu.SMEM)]
+        + [rows(inner), rows(inner), rows(inner), rows(BC), rows(LANES)]
+        + [whole((size, 3 * inner))] * len(parts),
+        out_specs=[rows(wall_cols), rows(inner)],
+        out_shape=[shape(width, wall_cols, dtype=bf16), shape(width, inner, dtype=bf16)],
+        compiler_params=pltpu.CompilerParams(
+            dimension_semantics=("arbitrary",), vmem_limit_bytes=56 * 1024 * 1024
+        ),
+        name="weights",
+    )(place, own_z, own_x, own_out, bc, dt, *parts)
 
 
 def shards(
@@ -405,13 +561,38 @@
 ):
     tok, width = x_input.shape
     inner = w_z.shape[2]
+    core, far = lax.axis_index("core"), lax.axis_index("zh")
+    held = core == far
     heads = w_dt.shape[2]
     count = tok // GROUP
     conv_cols = inner + BC
     all_cols = 2 * inner + BC + LANES
 
-    seg = seg_ids.astype(f32)
-    edge_seg = shifted(seg[tok - ROWS :], "seq", 1)
+    small = jnp.concatenate(
+        [
+            value.astype(f32).reshape(LAYERS, -1)
+            for value in (w_dt, conv_x, bias_x, dt_bias, a_log, d_skip, gate_gain)
+        ],
+        axis=1,
+    )
+    small = jnp.where(held, small, lax.ppermute(small, BOTH, CROSS))
+    sizes = (width * heads, CONV * inner, inner, heads, heads, heads, inner)
+    pieces, at = [], 0
+    for size in sizes:
+        pieces.append(small[:, at : at + size])
+        at += size
+    w_dt, conv_x, bias_x, dt_bias, a_log, d_skip, gate_gain = pieces
+    w_dt = w_dt.reshape(LAYERS, width, heads)
+    conv_x = conv_x.reshape(LAYERS, CONV, inner)
+    weights = [
+        gather_weights(w_z[layer], w_x[layer], w_out[layer], w_bc[layer], pad_lanes(w_dt[layer]))
+        for layer in range(LAYERS)
+    ]
+    seg = to_block(seg_ids.astype(f32))
+    hidden = to_block(x_input.astype(f32))
+    cotangent = to_block(cotangent.astype(f32))
+    hidden_own = own_rows(hidden)
+    edge_seg = shifted(seg[tok - ROWS :], 1)
     seg_ext = jnp.concatenate([edge_seg, seg])
     before = jnp.concatenate([edge_seg[ROWS - 1 :], seg[GROUP - 1 : tok - 1 : GROUP]])
     after = seg[GROUP - 1 :: GROUP]
@@ -437,12 +618,9 @@
     triback = (position[:, None] <= position[None, :]).astype(f32)
 
     matmul_flops = 2 * tok * width
-    hidden = x_input
     stored = []
     for layer in range(LAYERS):
-        wall = jnp.concatenate(
-            [w_z[layer], w_x[layer], w_bc[layer], pad_lanes(w_dt[layer])], axis=1
-        )
+        wall, wout = weights[layer]
         taps = jnp.concatenate([conv_x[layer], conv_bc[layer]], axis=1)
         bias = eight(jnp.concatenate([bias_x[layer], bias_bc[layer]]))
         dtb = eight(pad_lanes(dt_bias[layer]))
@@ -453,7 +631,7 @@
         end = hidden[tok - 16 :].astype(f32)
         end = end * lax.rsqrt(jnp.mean(end * end, axis=1, keepdims=True) + epsilon) * ngain
         end = mm(end.astype(bf16), wall[:, inner : 2 * inner + BC])[ROWS:]
-        halo = shifted(end, "seq", 1)
+        halo = shifted(end, 1)
         normed, zval, cin, cpre, dtp, cum, dtv, xdt, bc, sloc, pref, send = call(
             in_kernel,
             count,
@@ -507,7 +685,7 @@
             matmul_flops * 512,
             "ssd_within",
         )
-        entry = chain(send, "seq", False)
+        entry = chain(send, False)
         y, gate_in, proj, sums = call(
             out_kernel,
             count,
@@ -523,7 +701,7 @@
                 (whole((STATE, inner)), entry),
                 (whole((ROWS, inner)), dskip),
                 (whole((ROWS, inner)), ggain),
-                (whole((width, inner)), w_out[layer]),
+                (whole((width, inner)), wout),
                 (whole((LANES, inner)), expand),
                 (by_rows(width, count), cotangent),
             ],
@@ -537,21 +715,24 @@
             matmul_flops * 2 * inner,
             "gate_out_proj",
         )
-        sums = lax.psum(sums, "head")
-        proj_sum = lax.psum(proj, "head")
+        sums = total(sums, ("core", "zl"))
+        proj_sum = scatter_sum(proj)
         gate_scale = lax.rsqrt(sums[0] / INNER + epsilon)
         stored.append(
             dict(
-                hidden=hidden, normed=normed, zval=zval, cin=cin, cpre=cpre, dtp=dtp, cum=cum,
+                hidden=hidden_own, normed=normed, zval=zval, cin=cin, cpre=cpre, dtp=dtp, cum=cum,
                 dtv=dtv, xdt=xdt, bc=bc, sloc=sloc, pref=pref, entry=entry, y=y, gate_in=gate_in,
-                proj_sum=proj_sum, gate_scale=gate_scale, dots=sums[1], halo=halo, wall=wall,
+                proj_sum=proj_sum, gate_scale=gate_scale, dots=sums[1], halo=halo, wall=wall, wout=wout,
                 taps=taps, dtb=dtb, avec=avec, dskip=dskip, ggain=ggain,
             )
         )
-        hidden = hidden.astype(f32) + gate_scale[:, None] * proj_sum
-    final_out = hidden.astype(bf16)
+        hidden_own = hidden_own + own_rows(gate_scale)[:, None] * proj_sum
+        if layer < LAYERS - 1:
+            hidden = gather_rows(hidden_own)
+    final_out = narrowed(deliver(hidden_own))
 
     grad_h = cotangent
+    grad_own = own_rows(cotangent)
     matrices = [None] * LAYERS
     vectors = [None] * LAYERS
     shared = [None] * LAYERS
@@ -561,7 +742,7 @@
         if layer == LAYERS - 1:
             grad_scale = kept["dots"]
         else:
-            grad_scale = jnp.sum(grad_h * kept["proj_sum"], axis=1)
+            grad_scale = gather_rows(jnp.sum(grad_own * kept["proj_sum"], axis=1))
         gsq = -grad_scale * gate_scale**3 / INNER
         rev = functools.partial(by_rows, count=count, reverse=True)
         rev_group = functools.partial(by_group, count=count, reverse=True)
@@ -575,7 +756,7 @@
                 (rev(inner), kept["y"]),
                 (rev(inner), kept["zval"]),
                 (whole((ROWS, inner)), kept["ggain"]),
-                (whole((width, inner)), w_out[layer]),
+                (whole((width, inner)), kept["wout"]),
                 (rev(LANES), kept["cum"]),
                 (rev(BC), kept["bc"]),
                 (rev(ROWS), mask),
@@ -613,7 +794,7 @@
             matmul_flops * 1024,
             "ssd_within_back",
         )
-        gout = chain(gsend, "seq", True)
+        gout = chain(gsend, True)
         grad_wout = mm(gproj, kept["gate_in"], ((0,), (0,)))
         gall, last8, rim, gtaps, vecs, dsk = call(
             in_back_kernel,
@@ -658,112 +839,140 @@
             matmul_flops * 1024,
             "in_proj_conv_back",
         )
-        rim_back = shifted(rim, "seq", -1)
+        rim_back = shifted(rim, -1)
         gall = lax.dynamic_update_slice(
             gall, (last8 + rim_back).astype(bf16), (tok - ROWS, inner)
         )
-        grad_normed = lax.psum(mm(gall, kept["wall"], ((1,), (1,))), "head")
-        grad_win = mm(kept["normed"], gall, ((0,), (0,)))
-        matrices[layer] = (
-            lax.psum_scatter(grad_win, "seq", scatter_dimension=0, tiled=True),
-            lax.psum_scatter(grad_wout, "seq", scatter_dimension=0, tiled=True),
-        )
-        hidden_in = kept["hidden"].astype(f32)
+        grad_normed = scatter_sum(mm(gall, kept["wall"], ((1,), (1,))))
+        grad_win = mm(kept["normed"], gall[:, : 2 * inner + BC], ((0,), (0,)))
+        grad_wdt = mm(kept["normed"], gall[:, 2 * inner + BC :], ((0,), (0,)))
+        hidden_in = kept["hidden"]
         inv = lax.rsqrt(jnp.mean(hidden_in * hidden_in, axis=1, keepdims=True) + epsilon)
         grad_ngain = jnp.sum(grad_normed * hidden_in * inv, axis=0)
         back = grad_normed * norm_gain[layer][None, :]
-        grad_h = grad_h.astype(f32) + inv * (
+        grad_own = grad_own + inv * (
             back - hidden_in * inv * inv * jnp.mean(back * hidden_in, axis=1, keepdims=True)
         )
+        if layer > 0:
+            grad_h = gather_rows(grad_own)
+        grad_win = lax.psum_scatter(grad_win, "chip", scatter_dimension=0, tiled=True)
+        grad_wout = lax.psum_scatter(grad_wout, "chip", scatter_dimension=0, tiled=True)
+        matrices[layer] = (
+            place_rows(grad_win[:, : 2 * inner]),
+            place_rows(grad_wout),
+            shared_rows(grad_win[:, 2 * inner :]),
+        )
         vectors[layer] = jnp.concatenate(
             [
-                grad_ngain,
                 gtaps[: CONV + 1, :inner].reshape(-1),
                 acc[0],
-                vecs[0],
-                vecs[1],
+                vecs[0, :heads],
+                vecs[1, :heads],
                 dsk[0],
+                grad_wdt[:, :heads].reshape(-1),
+                gtaps[: CONV + 1, inner:].reshape(-1),
+                grad_ngain,
             ]
         )
-        shared[layer] = gtaps[: CONV + 1, inner:]
-    vector = jnp.stack(vectors)
-    share = jnp.stack(shared).reshape(LAYERS, -1)
-    vector = lax.psum(jnp.concatenate([vector, share], axis=1), "seq")
-    share = vector[:, -(CONV + 1) * BC :]
-    grad_wbc = jnp.stack([m[0][:, 2 * inner : 2 * inner + BC] for m in matrices])
-    share_all = lax.psum(
-        jnp.concatenate([grad_wbc.reshape(LAYERS, -1), share], axis=1), "head"
-    )
-    grad_wbc = share_all[:, : -(CONV + 1) * BC].reshape(grad_wbc.shape)
-    share = share_all[:, -(CONV + 1) * BC :].reshape(LAYERS, CONV + 1, BC)
+    vector = total(jnp.stack(vectors), ("zh", "chip"))
+    other = swap(vector, "core")
+    common = (CONV + 1) * BC + width
+    by_head = jnp.where(held, vector, other)[:, :-common]
+    shared = total((vector + other)[:, -common:], ("zl",))
+    g_bc = shared[:, :-width].reshape(LAYERS, CONV + 1, BC)
+    g_ngain = shared[:, -width:]
     at = 0
     pieces = []
-    for size in (width, CONV * inner, inner, inner, LANES, LANES, inner):
-        pieces.append(vector[:, at : at + size])
+    for size in (CONV * inner, inner, inner, heads, heads, inner, width * heads):
+        pieces.append(by_head[:, at : at + size])
         at += size
-    g_ngain, g_conv, g_bias, g_ggain, g_alog, g_dtb, g_dsk = pieces
+    g_conv, g_bias, g_ggain, g_alog, g_dtb, g_dsk, g_wdt = pieces
+    g_wdt = g_wdt.reshape(LAYERS, width, heads)
+    rows = width // lax.axis_size(("chip", "core"))
+    g_wdt = lax.dynamic_slice_in_dim(g_wdt, lax.axis_index(("chip", "core")) * rows, rows, axis=1)
     g_win = jnp.stack([m[0] for m in matrices])
     return (
         final_out,
-        grad_h,
+        deliver(grad_own),
         g_ngain,
         g_win[:, :, :inner],
-        g_win[:, :, inner : 2 * inner],
-        grad_wbc,
-        g_win[:, :, 2 * inner + BC : 2 * inner + BC + heads],
+        g_win[:, :, inner:],
+        jnp.stack([m[2] for m in matrices]),
+        g_wdt,
         g_conv.reshape(LAYERS, CONV, inner),
-        share[:, :CONV],
+        g_bc[:, :CONV],
         g_bias,
-        share[:, CONV],
-        g_dtb[:, :heads],
-        g_alog[:, :heads],
+        g_bc[:, CONV],
+        g_dtb,
+        g_alog,
         jnp.sum(g_dsk.reshape(LAYERS, heads, HEADDIM), axis=2),
         g_ggain,
         jnp.stack([m[1] for m in matrices]),
     )
 
 
+def place_rows(part):
+    core, far = lax.axis_index("core"), lax.axis_index("zh")
+    full = part + lax.ppermute(part, BOTH, CROSS_BACK)
+    sent = lax.ppermute(take(full, 1 - core, 2), BOTH, CORE_OUT)
+    return jnp.where(core == far, take(full, core, 2), sent)
+
+
+def shared_rows(part):
+    core = lax.axis_index("core")
+    part = take(part, core, 2) + swap(take(part, 1 - core, 2), "core")
+    return total(part, ("zl", "zh"))
+
+
 def solution(mesh):
+    seq, head = mesh.devices.shape
+    mesh = jax.sharding.Mesh(
+        mesh.devices.reshape(seq // 2, 2, 2, head // 2), ("chip", "core", "zh", "zl")
+    )
+    tokens, columns = ("chip", "core"), ("zh", "zl")
+    by_col = P(None, None, columns)
+    by_head = P(None, columns)
+    both = P(None, tokens, columns)
     placed = (
-        P("seq", None),
-        P("seq"),
-        P("seq", None),
+        P(tokens, None),
+        P(tokens),
+        P(tokens, None),
         P(),
-        P(None, None, "head"),
-        P(None, None, "head"),
+        by_col,
+        by_col,
         P(),
-        P(None, None, "head"),
-        P(None, None, "head"),
+        by_col,
+        by_col,
         P(),
-        P(None, "head"),
+        by_head,
         P(),
-        P(None, "head"),
-        P(None, "head"),
-        P(None, "head"),
-        P(None, "head"),
-        P(None, None, "head"),
+        by_head,
+        by_head,
+        by_head,
+        by_head,
+        by_col,
     )
     return jax.shard_map(
         shards,
         mesh=mesh,
         in_specs=placed,
         out_specs=(
-            P("seq", None),
-            P("seq", None),
+            P(tokens, None),
+            P(tokens, None),
             P(),
-            P(None, "seq", "head"),
-            P(None, "seq", "head"),
-            P(None, "seq", None),
-            P(None, "seq", "head"),
-            P(None, None, "head"),
+            both,
+            both,
+            P(None, tokens, None),
+            both,
+            by_col,
             P(),
-            P(None, "head"),
+            by_head,
             P(),
-            P(None, "head"),
-            P(None, "head"),
-            P(None, "head"),
-            P(None, "head"),
-            P(None, "seq", "head"),
+            by_head,
+            by_head,
+            by_head,
+            by_head,
+            both,
         ),
         check_vma=False,
     )

time: 1190 us -> 1090 us (0.916)
  waiting for transfers between devices: 801 us -> 490 us
  starting transfers between devices: 12.8 us -> 196 us
  blocking collectives: 65.2 us -> 0 us
  other arithmetic: 61 us -> 98.7 us
  local copies, waits for them, and re-layouts: 41.3 us -> 75.4 us
  Pallas kernels: 148 us -> 167 us
    psum x4 -> x0, waiting for transfers between devices: 598 us -> none  [the longest x2 314 us: shards(): grad_normed = lax.psum(mm(gall, kept['wall'], ((1,), (1,))), 'head')]
    ppermute x5 -> x64, waiting for transfers between devices: 4.33 us -> 272 us  [the longest x21 129 us: swap(): return lax.ppermute(value, axis, SWAP)]
    ppermute x5 -> x64, starting transfers between devices: 11.6 us -> 195 us  [the longest x5 78 us: shifted(): lax.ppermute(value, BLOCKS, [(source, source + steps) for source in range...]
    all_gather x4, waiting for transfers between devices: 74.9 us -> 178 us  [chain(): gathered = lax.all_gather(part, BLOCKS)]
    reduce_scatter x4, waiting for transfers between devices: 123 us -> 40.7 us  [the longest x2 36.6 us: shards(): lax.psum_scatter(grad_wout, 'chip', scatter_dimension=0, tiled=True)]
    psum x3 -> x0, blocking collectives: 65.2 us -> none  [the longest x2 40.7 us: shards(): sums = lax.psum(sums, 'head')]
    select_n x0 -> x20, other arithmetic: none -> 30.9 us  [the longest x11 24.8 us: ordered(): jnp.where(place == 0, jnp.concatenate([mine, theirs]), jnp.concatenate([t...]
    pallas_call x0 -> x3, Pallas kernels: none -> 18.2 us  [the longest x2 13.8 us: gather_weights(): pl.pallas_call(weight_kernel, grid=(blocks,), in_specs=[pl.BlockSpec(memo...]
  transfers between devices with their start and end apart: 17 -> 72, of which waited for: 15 -> 34; matrix products, arithmetic and copies ran while one was open for 7% -> 15% of each run, Pallas kernels for 4% -> 8%
where the time goes in v2:
time: 1090 us; the launch traced here: 1080 us
  waiting for transfers between devices  490 us (45%)
  starting transfers between devices  196 us (18%)
  Pallas kernels  167 us (15%)
  other arithmetic  98.7 us (9%)
  local copies, waits for them, and re-layouts  75.4 us (7%)
  matrix products  36.3 us (3%)
  between operations  16 us (1%)
    all_gather x4, waiting for transfers between devices, chain(): gathered = lax.all_gather(part, BLOCKS)  178 us
    pallas_call x12, Pallas kernels, call(): pl.pallas_call(kernel, grid=(count,), in_specs=[spec for spec, _ in ins],...  149 us
    ppermute x21, waiting for transfers between devices, swap(): return lax.ppermute(value, axis, SWAP)  129 us
    ppermute x12, waiting for transfers between devices, total(): lax.ppermute(value, axis, [(i, i ^ step) for i in range(count)])  79.3 us
    ppermute x5, starting transfers between devices, shifted(): lax.ppermute(value, BLOCKS, [(source, source + steps) for source in range...  78 us
    ppermute x21, starting transfers between devices, swap(): return lax.ppermute(value, axis, SWAP)  41.5 us
    reduce_scatter x2, waiting for transfers between devices, shards(): lax.psum_scatter(grad_wout, 'chip', scatter_dimension=0, tiled=True)  36.6 us
    ppermute x4, waiting for transfers between devices, place_rows(): full = part + lax.ppermute(part, BOTH, CROSS_BACK)  34.8 us
  transfers between devices with their start and end apart: 72, of which 34 were waited for; matrix products, arithmetic and copies ran while one was open for 15% of the time, Pallas kernels for 8%

profile of v2, /device:TPU:0, one launch (start us, length us, event | category | flops | bytes accessed | tf_op | source)
XLA Modules:
  0.0 1079.6 jit_solution(16973715948141446139)
XLA Ops:
  57.1 6.9 weights.2
  66.2 41.1 %collective-permute-start.8 = (f32[8,768]{1,0:T(8,128)S(1)}, f32[8,768]{1,0:T(8,128)S(1)}, u32[]{:S(2)}, u32[]{:S(2)}) collective-permute-start(f32[8,768]{1,0:T(8,128)S(1)} %fusion.10), channel_id=1, source_target_pairs={{0,2},{2,8},{8,10},{10,16},{16,18},{18,24},{24,26},{1,3},{3,9},{9,... | collective-permute-start | bytes 73736 | tf_op jit(solution)/shard_map/ppermute | solution.py:368
  110.6 17.0 %in_proj_conv.2 = (bf16[1024,1024]{1,0:T(8,128)(2,1)}, f32[1024,512]{1,0:T(8,128)}, f32[1024,768]{1,0:T(8,128)}, f32[1024,768]{1,0:T(8,128)}, f32[1024,128]{1,0:...) custom-call(f32[1024,1024]{1,0:T(8,128)} %copy-done, ...), custom_call_target="tpu_custom_call" | custom-call | flops 2952790016 | bytes 8388608 | tf_op jit(solution)/shard_map/in_proj_conv/pallas_call | solution.py:334
  138.2 61.4 %all-gather.9.cloned.1.call-done = f32[1088,512]{1,0:T(8,128)} async-done(((f32[136,512]{1,0:T(8,128)}), f32[1088,512]{1,0:T(8,128)}) %all-gather.9.cloned.1.call-update) | async-done | bytes 2228240 | tf_op jit(solution)/shard_map/all_gather | solution.py:374
  204.6 14.2 %gate_out_proj.2 = (f32[1024,512]{1,0:T(8,128)}, bf16[1024,512]{1,0:T(8,128)(2,1)}, f32[1024,1024]{1,0:T(8,128)}, f32[8,1024]{1,0:T(8,128)}) custom-call(f32[1024,512]{1,0:T(8,128)} %ssd_within.2.yin, f32[1024,768]{1,0:T(8,128)} %get-tuple-element.86.cpre, f32[1024,128]{1,0:T(8,128)} %get-tuple-element.83.cum, bf16[1024,256]{1,0:T(8,128)(2,1)} %get-tuple-element.85.bc, ...), custom_call_target="tpu_custom_call" | custom-call | flops 2147483648 | bytes 8388608 | tf_op jit(solution)/shard_map/gate_out_proj/pallas_call | solution.py:334
  233.6 21.2 %collective-permute-done.11 = f32[8,1024]{1,0:T(8,128)} collective-permute-done((f32[8,1024]{1,0:T(8,128)S(1)}, f32[8,1024]{1,0:T(8,128)}, u32[]{:S(2)}, u32[]{:S(2)}) %collective-permute-start.11) | collective-permute-done | bytes 32800 | tf_op jit(solution)/shard_map/ppermute | solution.py:398
  265.1 34.9 %collective-permute-done.14 = f32[256,1024]{1,0:T(8,128)} collective-permute-done((f32[256,1024]{1,0:T(8,128)S(1)}, f32[256,1024]{1,0:T(8,128)}, u32[]{:S(2)}, u32[]{:S(2)}) %collective-permute-start.14) | collective-permute-done | bytes 1048608 | tf_op jit(solution)/shard_map/ppermute | solution.py:390
  312.5 6.9 weights.3
  325.0 32.6 %collective-permute-start.20 = (f32[8,768]{1,0:T(8,128)S(1)}, f32[8,768]{1,0:T(8,128)S(1)}, u32[]{:S(2)}, u32[]{:S(2)}) collective-permute-start(f32[8,768]{1,0:T(8,128)S(1)} %fusion.8), channel_id=1, source_target_pairs={{0,2},{2,8},{8,10},{10,16},{16,18},{18,24},{24,26},{1,3},{3,9},{9,... | collective-permute-start | bytes 73736 | tf_op jit(solution)/shard_map/ppermute | solution.py:368
  360.9 16.9 %in_proj_conv.3 = (bf16[1024,1024]{1,0:T(8,128)(2,1)}, f32[1024,512]{1,0:T(8,128)}, f32[1024,768]{1,0:T(8,128)}, f32[1024,768]{1,0:T(8,128)}, f32[1024,128]{1,0:...) custom-call(f32[1024,1024]{1,0:T(8,128)} %copy-done.13, ...), custom_call_target="tpu_custom_call" | custom-call | flops 2952790016 | bytes 8388608 | tf_op jit(solution)/shard_map/in_proj_conv/pallas_call | solution.py:334
  383.9 52.2 %all-gather.11.cloned.1.call-done = f32[1088,512]{1,0:T(8,128)} async-done(((f32[136,512]{1,0:T(8,128)}), f32[1088,512]{1,0:T(8,128)}) %all-gather.11.cloned.1.call-update) | async-done | bytes 2228240 | tf_op jit(solution)/shard_map/all_gather | solution.py:374
  441.0 14.1 %gate_out_proj.3 = (f32[1024,512]{1,0:T(8,128)}, bf16[1024,512]{1,0:T(8,128)(2,1)}, f32[1024,1024]{1,0:T(8,128)}, f32[8,1024]{1,0:T(8,128)}) custom-call(f32[1024,512]{1,0:T(8,128)} %ssd_within.3.yin, f32[1024,768]{1,0:T(8,128)} %get-tuple-element.98.cpre, f32[1024,128]{1,0:T(8,128)} %get-tuple-element.95.cum, bf16[1024,256]{1,0:T(8,128)(2,1)} %get-tuple-element.97.bc, ...), custom_call_target="tpu_custom_call" | custom-call | flops 2147483648 | bytes 8388608 | tf_op jit(solution)/shard_map/gate_out_proj/pallas_call | solution.py:334
  466.6 9.9 gate_back.2
  477.3 7.5 ssd_within_back.2
  484.8 46.2 %all-gather.13.cloned.1.call-done = f32[1088,512]{1,0:T(8,128)} async-done(((f32[136,512]{1,0:T(8,128)}), f32[1088,512]{1,0:T(8,128)}) %all-gather.13.cloned.1.call-update) | async-done | bytes 2228240 | tf_op jit(solution)/shard_map/all_gather | solution.py:374
  534.8 20.5 %in_proj_conv_back.2 = (bf16[1024,1408]{1,0:T(8,128)(2,1)}, f32[8,768]{1,0:T(8,128)}, f32[8,768]{1,0:T(8,128)}, f32[8,768]{1,0:T(8,128)}, f32[8,128]{1,0:T(8,128)}, /*index=5*/f32[8,512]{1,0:T(8,128)}) custom-call(f32[1024,512]{1,0:T(8,128)} %get-tuple-element.108.uin, f32[1024,256]{1,0:T(8,128)} %get-tuple-element.109.dbc, ...), custom_call_target="tpu_custom_call" | custom-call | flops 2147483648 | bytes 8388608 | tf_op jit(solution)/shard_map/in_proj_conv_back/pallas_call | solution.py:334
  582.4 18.8 %collective-permute-done.32 = f32[256,1024]{1,0:T(8,128)} collective-permute-done((f32[256,1024]{1,0:T(8,128)}, f32[256,1024]{1,0:T(8,128)}, u32[]{:S(2)}, u32[]{:S(2)}) %collective-permute-start.32) | collective-permute-done | bytes 1048608 | tf_op jit(solution)/shard_map/ppermute | solution.py:390
  603.1 19.8 %collective-permute-done.24 = f32[256,1024]{1,0:T(8,128)} collective-permute-done((f32[256,1024]{1,0:T(8,128)}, f32[256,1024]{1,0:T(8,128)}, u32[]{:S(2)}, u32[]{:S(2)}) %collective-permute-start.24) | collective-permute-done | bytes 1048608 | tf_op jit(solution)/shard_map/ppermute | solution.py:390
  626.5 24.1 %collective-permute-done.33 = f32[256,1024]{1,0:T(8,128)S(1)} collective-permute-done((f32[256,1024]{1,0:T(8,128)S(1)}, f32[256,1024]{1,0:T(8,128)S(1)}, u32[]{:S(2)}, u32[]{:S(2)}) %collective-permute-start.33) | collective-permute-done | bytes 1048608 | tf_op jit(solution)/shard_map/ppermute | solution.py:390
  662.1 10.0 gate_back.3
  694.9 34.8 %collective-permute-done.62 = f32[256,512]{1,0:T(8,128)} collective-permute-done((f32[256,512]{1,0:T(8,128)}, f32[256,512]{1,0:T(8,128)}, u32[]{:S(2)}, u32[]{:S(2)}) %collective-permute-start.62) | collective-permute-done | bytes 524320 | tf_op jit(solution)/shard_map/ppermute | solution.py:916
  736.8 7.5 ssd_within_back.3
  744.3 17.8 %all-gather.15.cloned.1.call-done = f32[1088,512]{1,0:T(8,128)} async-done(((f32[136,512]{1,0:T(8,128)}), f32[1088,512]{1,0:T(8,128)}) %all-gather.15.cloned.1.call-update) | async-done | bytes 2228240 | tf_op jit(solution)/shard_map/all_gather | solution.py:374
  765.9 20.3 %in_proj_conv_back.3 = (bf16[1024,1408]{1,0:T(8,128)(2,1)}, f32[8,768]{1,0:T(8,128)}, f32[8,768]{1,0:T(8,128)}, f32[8,768]{1,0:T(8,128)}, f32[8,128]{1,0:T(8,128)}, /*index=5*/f32[8,512]{1,0:T(8,128)}) custom-call(f32[1024,512]{1,0:T(8,128)} %get-tuple-element.122.uin, f32[1024,256]{1,0:T(8,128)} %get-tuple-element.123.dbc, ...), custom_call_target="tpu_custom_call" | custom-call | flops 2147483648 | bytes 8388608 | tf_op jit(solution)/shard_map/in_proj_conv_back/pallas_call | solution.py:334
  804.8 9.2 collective-permute-done.26
  828.6 36.6 %reduce-scatter.9.cloned.1.call-done = f32[256,512]{1,0:T(8,128)} async-done(((f32[1024,512]{1,0:T(8,128)}), f32[256,512]{1,0:T(8,128)}) %reduce-scatter.9.cloned.1.call-update) | async-done | bytes 524304 | tf_op jit(solution)/shard_map/reduce_scatter | solution.py:859
  896.9 15.5 %collective-permute-done.59 = f32[128,256]{1,0:T(8,128)} collective-permute-done((f32[128,256]{1,0:T(8,128)}, f32[128,256]{1,0:T(8,128)}, u32[]{:S(2)}, u32[]{:S(2)}) %collective-permute-start.59) | collective-permute-done | bytes 131104 | tf_op jit(solution)/shard_map/ppermute | solution.py:398
  919.2 10.4 collective-permute-done.39
  965.3 14.1 %collective-permute-done.40 = f32[256,1024]{1,0:T(8,128)S(1)} collective-permute-done((f32[256,1024]{1,0:T(8,128)S(1)}, f32[256,1024]{1,0:T(8,128)S(1)}, u32[]{:S(2)}, u32[]{:S(2)}) %collective-permute-start.40) | collective-permute-done | bytes 1048608 | tf_op jit(solution)/shard_map/ppermute | solution.py:440
  979.6 24.0 %collective-permute-start.41 = (f32[256,1024]{1,0:T(8,128)S(1)}, f32[256,1024]{1,0:T(8,128)}, u32[]{:S(2)}, u32[]{:S(2)}) collective-permute-start(f32[256,1024]{1,0:T(8,128)S(1)} %broadcast_select_fusion.3), channel_id=1, source_target_pairs={{0,1},{1,0},{2,3},{3,2},{4,5},{5,4},{6,7},{7,6},{8,9},{9,8},{10,11... | collective-permute-start | bytes 3145736 | tf_op jit(solution)/shard_map/ppermute | solution.py:390
  1017.4 20.9 %collective-permute-done.49 = f32[2,2304]{1,0:T(2,128)} collective-permute-done((f32[2,2304]{1,0:T(2,128)}, f32[2,2304]{1,0:T(2,128)}, u32[]{:S(2)}, u32[]{:S(2)}) %collective-permute-start.49) | collective-permute-done | bytes 18464 | tf_op jit(solution)/shard_map/ppermute | solution.py:398
  1040.9 12.5 %collective-permute-start.54 = (f32[128,256]{1,0:T(8,128)S(1)}, f32[128,256]{1,0:T(8,128)S(1)}, u32[]{:S(2)}, u32[]{:S(2)}) collective-permute-start(f32[128,256]{1,0:T(8,128)S(1)} %constant_dynamic-slice_fusion.4), channel_id=1, source_target_pairs={{0,4},{4,0},{1,5},{5,1},{2,6},{6,2},{3,7},{7,3},{8,12},{12,8},{9,1... | collective-permute-start | bytes 393224 | tf_op jit(solution)/shard_map/ppermute | solution.py:390
  (494 shorter events, 363.7 us)
Async XLA Ops:
  7.2 192.4 %all-gather.9.cloned.1.call-start = ((), (), s32[]{:S(2)}) async-start(), calls=%async_computation.8 | async-start | bytes 2506752 | tf_op jit(solution)/shard_map/all_gather | solution.py:374
  8.1 35.9 %collective-permute-start.6 = (f32[1024]{0:T(1024)S(1)}, f32[1024]{0:T(1024)S(1)}, u32[]{:S(2)}, u32[]{:S(2)}) collective-permute-start(f32[1024]{0:T(1024)S(1)} %convert_element_type.92), channel_id=1, source_target_pairs={{0,4},{6,2},{1,5},{7,3},{8,12},{14,10},{9,13},{15,11},{16,20},{22,... | collective-permute-start | bytes 12296 | tf_op jit(solution)/shard_map/ppermute | solution.py:450
  12.9 40.2 %collective-permute-start.1 = (f32[2,11288]{1,0:T(2,128)S(1)}, f32[2,11288]{1,0:T(2,128)S(1)}, u32[]{:S(2)}, u32[]{:S(2)}) collective-permute-start(f32[2,11288]{1,0:T(2,128)S(1)} %concatenate.147), channel_id=1, source_target_pairs={{0,2},{6,4},{1,3},{7,5},{8,10},{14,12},{9,11},{15,13},{16,18},{22,... | collective-permute-start | bytes 270920 | tf_op jit(solution)/shard_map/ppermute | solution.py:578
  31.4 97.7 %collective-permute-start.9 = (f32[1024,1024]{1,0:T(8,128)}, f32[1024,1024]{1,0:T(8,128)}, u32[]{:S(2)}, u32[]{:S(2)}) collective-permute-start(f32[1024,1024]{1,0:T(8,128)} %convert_element_type.96), channel_id=1, source_target_pairs={{0,4},{6,2},{1,5},{7,3},{8,12},{14,10},{9,13},{15,11},{16,20},{22,... | collective-permute-start | bytes 12582920 | tf_op jit(solution)/shard_map/ppermute | solution.py:450
  66.2 42.6 %collective-permute-start.8 = (f32[8,768]{1,0:T(8,128)S(1)}, f32[8,768]{1,0:T(8,128)S(1)}, u32[]{:S(2)}, u32[]{:S(2)}) collective-permute-start(f32[8,768]{1,0:T(8,128)S(1)} %fusion.10), channel_id=1, source_target_pairs={{0,2},{2,8},{8,10},{10,16},{16,18},{18,24},{24,26},{1,3},{3,9},{9,... | collective-permute-start | bytes 73736 | tf_op jit(solution)/shard_map/ppermute | solution.py:368
  127.6 308.5 %all-gather.11.cloned.1.call-start = ((), (), s32[]{:S(2)}) async-start(), calls=%async_computation.9 | async-start | bytes 2506752 | tf_op jit(solution)/shard_map/all_gather | solution.py:374
  228.6 27.1 %collective-permute-start.13 = (f32[256,1024]{1,0:T(8,128)}, f32[256,1024]{1,0:T(8,128)S(1)}, u32[]{:S(2)}, u32[]{:S(2)}) collective-permute-start(f32[256,1024]{1,0:T(8,128)} %constant_dynamic-slice_fusion.14), channel_id=1, source_target_pairs={{0,1},{1,0},{2,3},{3,2},{4,5},{5,4},{6,7},{7,6},{8,9},{9,8},{10,11... | collective-permute-start | bytes 3145736 | tf_op jit(solution)/shard_map/ppermute | solution.py:390
  258.8 41.3 %collective-permute-start.14 = (f32[256,1024]{1,0:T(8,128)S(1)}, f32[256,1024]{1,0:T(8,128)}, u32[]{:S(2)}, u32[]{:S(2)}) collective-permute-start(f32[256,1024]{1,0:T(8,128)S(1)} %get-tuple-element.225), channel_id=1, source_target_pairs={{0,1},{1,0},{2,3},{3,2},{4,5},{5,4},{6,7},{7,6},{8,9},{9,8},{10,11... | collective-permute-start | bytes 3145736 | tf_op jit(solution)/shard_map/ppermute | solution.py:390
  260.5 42.9 %collective-permute-start.16 = (f32[256,1536]{1,0:T(8,128)}, f32[256,1536]{1,0:T(8,128)}, u32[]{:S(2)}, u32[]{:S(2)}) collective-permute-start(f32[256,1536]{1,0:T(8,128)} %maximum_convert_fusion.1), channel_id=1, source_target_pairs={{0,2},{6,4},{1,3},{7,5},{8,10},{14,12},{9,11},{15,13},{16,18},{22,... | collective-permute-start | bytes 4718600 | tf_op jit(solution)/shard_map/ppermute | solution.py:509
  325.0 34.1 %collective-permute-start.20 = (f32[8,768]{1,0:T(8,128)S(1)}, f32[8,768]{1,0:T(8,128)S(1)}, u32[]{:S(2)}, u32[]{:S(2)}) collective-permute-start(f32[8,768]{1,0:T(8,128)S(1)} %fusion.8), channel_id=1, source_target_pairs={{0,2},{2,8},{8,10},{10,16},{16,18},{18,24},{24,26},{1,3},{3,9},{9,... | collective-permute-start | bytes 73736 | tf_op jit(solution)/shard_map/ppermute | solution.py:368
  377.8 153.2 %all-gather.13.cloned.1.call-start = ((), (), s32[]{:S(2)}) async-start(), calls=%async_computation.10 | async-start | bytes 2506752 | tf_op jit(solution)/shard_map/all_gather | solution.py:374
  476.5 208.6 %reduce-scatter.11.cloned.1.call-start = ((), (), s32[]{:S(2)}) async-start(), calls=%async_computation.7 | async-start | bytes 2621440 | tf_op jit(solution)/shard_map/reduce_scatter | solution.py:859
  578.4 44.4 %collective-permute-start.24 = (f32[256,1024]{1,0:T(8,128)}, f32[256,1024]{1,0:T(8,128)}, u32[]{:S(2)}, u32[]{:S(2)}) collective-permute-start(f32[256,1024]{1,0:T(8,128)} %constant_dynamic-slice_fusion.11), channel_id=1, source_target_pairs={{0,1},{1,0},{2,3},{3,2},{4,5},{5,4},{6,7},{7,6},{8,9},{9,8},{10,11... | collective-permute-start | bytes 3145736 | tf_op jit(solution)/shard_map/ppermute | solution.py:390
  582.3 179.9 %all-gather.15.cloned.1.call-start = ((), (), s32[]{:S(2)}) async-start(), calls=%async_computation.11 | async-start | bytes 2506752 | tf_op jit(solution)/shard_map/all_gather | solution.py:374
  672.2 154.6 %reduce-scatter.7.cloned.1.call-start = ((), (), s32[]{:S(2)}) async-start(), calls=%async_computation.5 | async-start | bytes 6553600 | tf_op jit(solution)/shard_map/reduce_scatter | solution.py:858
  678.7 186.5 %reduce-scatter.9.cloned.1.call-start = ((), (), s32[]{:S(2)}) async-start(), calls=%async_computation.6 | async-start | bytes 2621440 | tf_op jit(solution)/shard_map/reduce_scatter | solution.py:859
  680.0 55.4 %collective-permute-start.28 = (f32[256,1024]{1,0:T(8,128)S(1)}, f32[256,1024]{1,0:T(8,128)}, u32[]{:S(2)}, u32[]{:S(2)}) collective-permute-start(f32[256,1024]{1,0:T(8,128)S(1)} %copy-done.22), channel_id=1, source_target_pairs={{4,2},{2,4},{5,3},{3,5},{12,10},{10,12},{13,11},{11,13},{20,18},{1... | collective-permute-start | bytes 3145736 | tf_op jit(solution)/shard_map/ppermute | solution.py:441
  681.6 53.7 %collective-permute-start.27 = (f32[256,1024]{1,0:T(8,128)S(1)}, f32[256,1024]{1,0:T(8,128)}, u32[]{:S(2)}, u32[]{:S(2)}) collective-permute-start(f32[256,1024]{1,0:T(8,128)S(1)} %copy-done.22), channel_id=1, source_target_pairs={{4,0},{2,6},{5,1},{3,7},{12,8},{10,14},{13,9},{11,15},{20,16},{18,... | collective-permute-start | bytes 3145736 | tf_op jit(solution)/shard_map/ppermute | solution.py:442
  685.2 44.6 %collective-permute-start.62 = (f32[256,512]{1,0:T(8,128)}, f32[256,512]{1,0:T(8,128)}, u32[]{:S(2)}, u32[]{:S(2)}) collective-permute-start(f32[256,512]{1,0:T(8,128)} %reduce-scatter.11.cloned.1.call-done), channel_id=1, source_target_pairs={{2,0},{4,6},{3,1},{5,7},{10,8},{12,14},{11,9},{13,15},{18,16},{20,... | collective-permute-start | bytes 1572872 | tf_op jit(solution)/shard_map/ppermute | solution.py:916
  690.9 312.6 %reduce-scatter.5.cloned.1.call-start = ((), (), s32[]{:S(2)}) async-start(), calls=%async_computation.4 | async-start | bytes 6553600 | tf_op jit(solution)/shard_map/reduce_scatter | solution.py:858
  731.0 71.0 %collective-permute-start.63 = (f32[128,512]{1,0:T(8,128)S(1)}, f32[128,512]{1,0:T(8,128)}, u32[]{:S(2)}, u32[]{:S(2)}) collective-permute-start(f32[128,512]{1,0:T(8,128)S(1)} %constant_dynamic-slice_fusion), channel_id=1, source_target_pairs={{0,4},{6,2},{1,5},{7,3},{8,12},{14,10},{9,13},{15,11},{16,20},{22,... | collective-permute-start | bytes 786440 | tf_op jit(solution)/shard_map/ppermute | solution.py:917
  733.1 54.8 %collective-permute-start.25 = (f32[256,1024]{1,0:T(8,128)S(1)}, f32[256,1024]{1,0:T(8,128)}, u32[]{:S(2)}, u32[]{:S(2)}) collective-permute-start(f32[256,1024]{1,0:T(8,128)S(1)} %copy-done.22), channel_id=1, source_target_pairs={{0,2},{6,4},{1,3},{7,5},{8,10},{14,12},{9,11},{15,13},{16,18},{22,... | collective-permute-start | bytes 3145736 | tf_op jit(solution)/shard_map/ppermute | solution.py:440
  736.7 66.2 %collective-permute-start.29 = (f32[256,1024]{1,0:T(8,128)S(1)}, f32[256,1024]{1,0:T(8,128)}, u32[]{:S(2)}, u32[]{:S(2)}) collective-permute-start(f32[256,1024]{1,0:T(8,128)S(1)} %broadcast_select_fusion.4), channel_id=1, source_target_pairs={{0,1},{1,0},{2,3},{3,2},{4,5},{5,4},{6,7},{7,6},{8,9},{9,8},{10,11... | collective-permute-start | bytes 3145736 | tf_op jit(solution)/shard_map/ppermute | solution.py:390
  802.0 87.1 %collective-permute-start.38 = (f32[512,1024]{1,0:T(8,128)}, f32[512,1024]{1,0:T(8,128)}, u32[]{:S(2)}, u32[]{:S(2)}) collective-permute-start(f32[512,1024]{1,0:T(8,128)} %constant_dynamic-slice_fusion.8), channel_id=1, source_target_pairs={{0,4},{4,0},{1,5},{5,1},{2,6},{6,2},{3,7},{7,3},{8,12},{12,8},{9,1... | collective-permute-start | bytes 6291464 | tf_op jit(solution)/shard_map/ppermute | solution.py:390
  827.8 39.0 %collective-permute-start.57 = (f32[128,256]{1,0:T(8,128)S(1)}, f32[128,256]{1,0:T(8,128)S(1)}, u32[]{:S(2)}, u32[]{:S(2)}) collective-permute-start(f32[128,256]{1,0:T(8,128)S(1)} %constant_dynamic-slice_fusion.3), channel_id=1, source_target_pairs={{0,4},{4,0},{1,5},{5,1},{2,6},{6,2},{3,7},{7,3},{8,12},{12,8},{9,1... | collective-permute-start | bytes 393224 | tf_op jit(solution)/shard_map/ppermute | solution.py:390
  876.6 40.2 %collective-permute-start.52 = (f32[256,1024]{1,0:T(8,128)}, f32[256,1024]{1,0:T(8,128)}, u32[]{:S(2)}, u32[]{:S(2)}) collective-permute-start(f32[256,1024]{1,0:T(8,128)} %slice.437), channel_id=1, source_target_pairs={{2,0},{4,6},{3,1},{5,7},{10,8},{12,14},{11,9},{13,15},{18,16},{20,... | collective-permute-start | bytes 3145736 | tf_op jit(solution)/shard_map/ppermute | solution.py:916
  879.7 32.7 %collective-permute-start.59 = (f32[128,256]{1,0:T(8,128)}, f32[128,256]{1,0:T(8,128)}, u32[]{:S(2)}, u32[]{:S(2)}) collective-permute-start(f32[128,256]{1,0:T(8,128)} %add.306), channel_id=1, source_target_pairs={{0,2},{2,0},{1,3},{3,1},{4,6},{6,4},{5,7},{7,5},{8,10},{10,8},{9,1... | collective-permute-start | bytes 393224 | tf_op jit(solution)/shard_map/ppermute | solution.py:398
  892.2 37.4 %collective-permute-start.39 = (f32[256,1024]{1,0:T(8,128)}, f32[256,1024]{1,0:T(8,128)}, u32[]{:S(2)}, u32[]{:S(2)}) collective-permute-start(f32[256,1024]{1,0:T(8,128)} %constant_dynamic-slice_fusion.7), channel_id=1, source_target_pairs={{0,1},{1,0},{2,3},{3,2},{4,5},{5,4},{6,7},{7,6},{8,9},{9,8},{10,11... | collective-permute-start | bytes 3145736 | tf_op jit(solution)/shard_map/ppermute | solution.py:390
  962.7 90.8 %collective-permute-start.44 = (f32[256,1024]{1,0:T(8,128)S(1)}, f32[256,1024]{1,0:T(8,128)}, u32[]{:S(2)}, u32[]{:S(2)}) collective-permute-start(f32[256,1024]{1,0:T(8,128)S(1)} %broadcast_select_fusion.2), channel_id=1, source_target_pairs={{0,1},{1,0},{2,3},{3,2},{4,5},{5,4},{6,7},{7,6},{8,9},{9,8},{10,11... | collective-permute-start | bytes 3145736 | tf_op jit(solution)/shard_map/ppermute | solution.py:390
  979.6 77.8 %collective-permute-start.41 = (f32[256,1024]{1,0:T(8,128)S(1)}, f32[256,1024]{1,0:T(8,128)}, u32[]{:S(2)}, u32[]{:S(2)}) collective-permute-start(f32[256,1024]{1,0:T(8,128)S(1)} %broadcast_select_fusion.3), channel_id=1, source_target_pairs={{0,1},{1,0},{2,3},{3,2},{4,5},{5,4},{6,7},{7,6},{8,9},{9,8},{10,11... | collective-permute-start | bytes 3145736 | tf_op jit(solution)/shard_map/ppermute | solution.py:390
  1006.0 58.3 %collective-permute-start.50 = (f32[256,1024]{1,0:T(8,128)}, f32[256,1024]{1,0:T(8,128)}, u32[]{:S(2)}, u32[]{:S(2)}) collective-permute-start(f32[256,1024]{1,0:T(8,128)} %slice.435), channel_id=1, source_target_pairs={{2,0},{4,6},{3,1},{5,7},{10,8},{12,14},{11,9},{13,15},{18,16},{20,... | collective-permute-start | bytes 3145736 | tf_op jit(solution)/shard_map/ppermute | solution.py:916
  1008.6 29.6 %collective-permute-start.49 = (f32[2,2304]{1,0:T(2,128)}, f32[2,2304]{1,0:T(2,128)}, u32[]{:S(2)}, u32[]{:S(2)}) collective-permute-start(f32[2,2304]{1,0:T(2,128)} %slice_add_fusion), channel_id=1, source_target_pairs={{0,1},{1,0},{2,3},{3,2},{4,5},{5,4},{6,7},{7,6},{8,9},{9,8},{10,11... | collective-permute-start | bytes 55304 | tf_op jit(solution)/shard_map/ppermute | solution.py:398
  (100 other events, 1384.8 us)
Sparse Core Ops, SparseCore 0:
  127.7 71.8 all-gather.8
  377.9 58.0 all-gather.10
  476.7 54.3 all-gather.12
  582.4 35.0 reduce-scatter.10
  672.3 89.8 all-gather.14
  765.3 61.4 reduce-scatter.6
  830.0 35.1 reduce-scatter.8
  897.0 61.5 reduce-scatter.4

commit v3 on v2

--- a/solution.py
+++ b/solution.py
@@ -47,11 +47,21 @@
     return mm(lanes, expand, ((1,), (1,)), precision=highest)
 
 
+def pick(place, pieces, held):
+    if len(pieces) == 1:
+        return pieces[0][...]
+    away = lax.bitwise_xor(pl.program_id(0) if held is None else held, place[0])
+    value = pieces[3][...]
+    for number in range(3):
+        value = jnp.where(away == number, pieces[number][...], value)
+    return value
+
+
 def in_kernel(
-    hid, wall, ngain, taps, bias, dtb, avec, mask, halo, expand, tri,
-    normed, zval, cin, cpre, dtp, cum, dtv, xdt, bc, sloc, pref, send,
-    state, thru, prev,
+    place, wall, ngain, taps, bias, dtb, avec, mask, halo, expand, tri, *refs
 ):
+    hid = refs[:-14]
+    normed, cin, cpre, dtp, cum, dtv, xdt, bc, sloc, pref, send, state, thru, prev = refs[-14:]
     step = pl.program_id(0)
     inner = expand.shape[1]
 
@@ -61,13 +71,12 @@
         thru[...] = jnp.ones_like(thru)
         prev[...] = halo[...]
 
-    h = hid[...].astype(f32)
+    h = pick(place, hid, None)
     inv = lax.rsqrt(jnp.mean(h * h, axis=1, keepdims=True) + epsilon)
     low = (h * inv * ngain[...]).astype(bf16)
     normed[...] = low
-    zval[...] = mm(low, wall[:, :inner])
-    rows = mm(low, wall[:, inner : 2 * inner + BC])
-    pre_dt = mm(low, wall[:, 2 * inner + BC :])
+    rows = mm(low, wall[:, : inner + BC])
+    pre_dt = mm(low, wall[:, inner + BC :])
     dtp[...] = pre_dt
     cin[...] = rows
     ext = jnp.concatenate([prev[...], rows], axis=0)
@@ -130,9 +139,9 @@
 
 
 def out_kernel(
-    yin, cpre, cum, bc, mask, zval, sloc, pref, entry, dskip, ggain, wout, expand, cot,
-    y, gate_in, proj, sums,
+    yin, cpre, cum, bc, mask, zval, sloc, pref, entry, dskip, ggain, wout, expand, *refs
 ):
+    cot, (y, gate_in, proj, sums) = refs[:-4], refs[-4:]
     inner = expand.shape[1]
     pre = cpre[...]
     x = pre * jax.nn.sigmoid(pre)
@@ -147,17 +156,19 @@
     proj[...] = mm(low, wout[...], ((1,), (1,)))
     ones = jnp.ones((ROWS, inner), f32)
     squares = mm(ones, gated * gated, ((1,), (1,)), precision=highest)
-    back = mm(cot[...].astype(bf16), wout[...])
-    dots = mm(ones, low.astype(f32) * back, ((1,), (1,)), precision=highest)
-    row = lax.broadcasted_iota(jnp.int32, squares.shape, 0)
-    sums[...] = jnp.where(row == 0, squares, dots)
+    if cot:
+        back = mm(cot[0][...].astype(bf16), wout[...])
+        dots = mm(ones, low.astype(f32) * back, ((1,), (1,)), precision=highest)
+        row = lax.broadcasted_iota(jnp.int32, squares.shape, 0)
+        squares = jnp.where(row == 0, squares, dots)
+    sums[...] = squares
 
 
 def gate_kernel(
-    gh, scale, gsq, y, zval, ggain, wout, cum, bc, mask, expand,
-    gproj, dy, dz, gloc, suf, send, acc,
-    carry, thru,
+    place, scale, gsq, y, zval, ggain, wout, cum, bc, mask, expand, *refs
 ):
+    gh = refs[:-9]
+    gproj, dy, dz, gloc, suf, send, acc, carry, thru = refs[-9:]
     step = pl.program_id(0)
 
     @pl.when(step == 0)
@@ -166,7 +177,7 @@
         thru[...] = jnp.ones_like(thru)
         acc[...] = jnp.zeros_like(acc)
 
-    gp = (scale[...] * gh[...].astype(f32)).astype(bf16)
+    gp = (scale[...] * pick(place, gh, pl.num_programs(0) - 1 - step)).astype(bf16)
     gproj[...] = gp
     ggi = mm(gp, wout[...])
     z = zval[...]
@@ -224,7 +235,7 @@
 
 
 def in_back_kernel(
-    uin, dbc, dy, dz, y, cpre, cin, dtp, dtv, cum, xdt, bc, mask, sloc, pref, entry, gloc, suf,
+    uin, dbc, dy, y, cpre, cin, dtp, dtv, cum, xdt, bc, mask, sloc, pref, entry, gloc, suf,
     gout, halo, taps, dtb, avec, dskip, expand, triback,
     gall, last8, rim, gtaps, vecs, dsk,
     nexts,
@@ -289,9 +300,8 @@
         gtaps[k : k + 1, :] += jnp.sum(rows * shifted, axis=0, keepdims=True)
     for k in range(CONV - 1):
         nexts[k] = masked[k]
-    gall[:, :inner] = dz[...]
-    gall[:, inner : 2 * inner + BC] = grad_rows.astype(bf16)
-    gall[:, 2 * inner + BC :] = grad_dtpre.astype(bf16)
+    gall[:, : inner + BC] = grad_rows.astype(bf16)
+    gall[:, inner + BC :] = grad_dtpre.astype(bf16)
 
     @pl.when(step == 0)
     def _():
@@ -324,6 +334,12 @@
     if reverse:
         return pl.BlockSpec((1,) + shape, lambda c: (count - 1 - c, 0, 0))
     return pl.BlockSpec((1,) + shape, lambda c: (c, 0, 0))
+
+
+def by_piece(pieces, count, reverse=False):
+    if len(pieces) == 1:
+        return [(by_rows(pieces[0].shape[1], count, reverse), pieces[0])]
+    return [(whole(piece.shape), piece) for piece in pieces]
 
 
 def by_cols(count):
@@ -371,19 +387,20 @@
 def chain(part, reverse):
     count = lax.axis_size(BLOCKS)
     place = lax.axis_index(BLOCKS)
-    gathered = lax.all_gather(part, BLOCKS)
-    decay = gathered[:, STATE]
-    source = jnp.arange(count)[:, None, None]
-    middle = jnp.arange(count)[None, :, None]
-    if reverse:
-        between = (middle < source) & (middle > place)
-        ahead = jnp.arange(count) > place
-    else:
-        between = (middle > source) & (middle < place)
-        ahead = jnp.arange(count) < place
-    weight = jnp.prod(jnp.where(between, decay[None], 1.0), axis=1)
-    weight = jnp.where(ahead[:, None], weight, 0.0)
-    return jnp.sum(weight[:, None, :] * gathered[:, :STATE], axis=0)
+    state, decay = part[:STATE], part[STATE : STATE + 1]
+    entry, reach = jnp.zeros_like(state), jnp.ones_like(decay)
+    step = 1
+    while step < count:
+        got = lax.ppermute(part, BLOCKS, [(i, i ^ step) for i in range(count)])
+        got_state, got_decay = got[:STATE], got[STATE : STATE + 1]
+        later = ((place & step) == 0) if reverse else ((place & step) != 0)
+        entry = jnp.where(later, entry + reach * got_state, entry)
+        reach = jnp.where(later, reach * got_decay, reach)
+        state = jnp.where(later, state + decay * got_state, got_state + got_decay * state)
+        decay = decay * got_decay
+        part = jnp.concatenate([state, jnp.broadcast_to(decay, (ROWS, decay.shape[1]))])
+        step *= 2
+    return entry
 
 
 def swap(value, axis):
@@ -411,11 +428,16 @@
     )
 
 
-def scatter_sum(part):
+def behind(value, *marks):
+    return lax.optimization_barrier((value, *marks))[0]
+
+
+def scatter_sum(part, first=(), second=(), third=()):
     core, near = lax.axis_index("core"), lax.axis_index("zl")
-    half = take(part, core, 2) + swap(take(part, 1 - core, 2), "core")
+    part = behind(part, *first)
+    half = take(part, core, 2) + behind(swap(take(part, 1 - core, 2), "core"), *second)
     if lax.axis_size("zl") == 2:
-        return take(half, near, 2) + swap(take(half, 1 - near, 2), "zl")
+        return take(half, near, 2) + behind(swap(take(half, 1 - near, 2), "zl"), *third)
     return lax.psum_scatter(half, "zl", scatter_dimension=0, tiled=True)
 
 
@@ -435,15 +457,65 @@
     return ordered(lax.axis_index("core"), half, swap(half, "core"))
 
 
-def deliver(value):
+def own_place():
+    return 2 * lax.axis_index("core") + lax.axis_index("zl")
+
+
+def gather_pieces(value):
+    if lax.axis_size("zl") != 2 or value.shape[0] != GROUP:
+        return [gather_rows(value)]
+    near = swap(value, "zl")
+    return [value, near, swap(value, "core"), swap(near, "core")]
+
+
+def place_kernel(place, value, mine, near, theirs, value_s, mine_s, near_s, theirs_s, out):
+    away = lax.bitwise_xor(pl.program_id(0), place[0])
+    pairs = ((value, mine), (value_s, mine_s), (near, theirs), (near_s, theirs_s))
+    for number, (here, there) in enumerate(pairs):
+
+        @pl.when((away == number) & (place[1] == 1))
+        def _():
+            out[...] = here[...].astype(out.dtype)
+
+        @pl.when((away == number) & (place[1] == 0))
+        def _():
+            out[...] = there[...].astype(out.dtype)
+
+
+def deliver(value, dtype, first=(), second=(), third=()):
     core, far = lax.axis_index("core"), lax.axis_index("zh")
+    held = core == far
+    value = behind(value, *first)
     mine = lax.ppermute(value, BOTH, CROSS)
     theirs = lax.ppermute(value, BOTH, DIAGONAL)
     near = lax.ppermute(value, BOTH, CORE_IN)
-    held = core == far
-    mine = gather_near(jnp.where(held, value, mine))
-    theirs = gather_near(jnp.where(held, near, theirs))
-    return ordered(core, mine, theirs)
+    if lax.axis_size("zl") != 2 or value.shape[0] != GROUP:
+        mine = gather_near(jnp.where(held, value, mine))
+        theirs = gather_near(jnp.where(held, near, theirs))
+        full = ordered(core, mine, theirs)
+        return narrowed(full) if dtype == bf16 else full
+    axes = ("core", "zh", "zl")
+    here = [(2 * kind + i, 2 * kind + 1 - i) for kind in (0, 3) for i in range(2)]
+    there = [(2 * kind + i, 2 * kind + 1 - i) for kind in (1, 2) for i in range(2)]
+    value_s = lax.ppermute(value, axes, here)
+    near_s = lax.ppermute(near, axes, here)
+    mine, theirs = behind(mine, *second), behind(theirs, *second)
+    mine_s = lax.ppermute(mine, axes, there)
+    theirs_s = lax.ppermute(theirs, axes, there)
+    place = jnp.stack([own_place(), held.astype(jnp.int32)]).astype(jnp.int32)
+    width = value.shape[1]
+    parts = (value, mine, near, theirs, value_s, mine_s, near_s, behind(theirs_s, *third))
+    return pl.pallas_call(
+        place_kernel,
+        grid=(4,),
+        in_specs=[pl.BlockSpec(memory_space=pltpu.SMEM)] + [whole((GROUP, width))] * 8,
+        out_specs=by_rows(width, 4),
+        out_shape=shape(4 * GROUP, width, dtype=dtype),
+        compiler_params=pltpu.CompilerParams(
+            dimension_semantics=("arbitrary",), vmem_limit_bytes=40 * 1024 * 1024
+        ),
+        name="place",
+    )(place, *parts)
 
 
 def to_block(value):
@@ -459,25 +531,24 @@
     return jnp.pad(value, [(0, 0)] * (value.ndim - 1) + [(0, LANES - value.shape[-1])])
 
 
-def weight_kernel(place, own_z, own_x, own_out, bc, dt, *refs):
-    parts, (wall, wout) = refs[:-2], refs[-2:]
+def weight_kernel(place, own, *refs):
+    parts, out = refs[:-1], refs[-1]
     block = pl.program_id(0)
-    inner = own_z.shape[1]
-    wall[:, 2 * inner : 2 * inner + BC] = bc[...]
-    wall[:, 2 * inner + BC :] = dt[...].astype(bf16)
+    cols = own.shape[1]
 
     @pl.when(place[1] == 1)
     def _():
-        wall[:, :inner] = own_z[...]
-        wall[:, inner : 2 * inner] = own_x[...]
-        wout[...] = own_out[...]
-
-    for away in range(len(parts)):
+        out[:, :cols] = own[...]
+
+    for away in range(len(parts) if out.shape[1] == cols else len(parts) - 2):
 
         @pl.when((place[1] == 0) & (lax.bitwise_xor(place[0], block) == away))
         def _():
-            wall[:, : 2 * inner] = parts[away][:, : 2 * inner].astype(bf16)
-            wout[...] = parts[away][:, 2 * inner :].astype(bf16)
+            out[:, :cols] = parts[away][...].astype(bf16)
+
+    if out.shape[1] > cols:
+        out[:, cols : cols + BC] = parts[-2][...]
+        out[:, cols + BC :] = parts[-1][...].astype(bf16)
 
 
 def narrow_kernel(wide, narrow):
@@ -496,17 +567,14 @@
     )(value)
 
 
-def gather_weights(own_z, own_x, own_out, bc, dt):
-    width, inner = own_z.shape
+def gather_weights(own, more=(), first=(), second=()):
+    width, cols = own.shape
     chips = lax.axis_size("chip")
     chip = lax.axis_index("chip")
-    core, far = lax.axis_index("core"), lax.axis_index("zh")
+    held = (lax.axis_index("core") == lax.axis_index("zh")).astype(jnp.int32)
     size = width // chips
-    cut = functools.partial(lax.dynamic_slice_in_dim, start_index=chip * size, slice_size=size)
-    piece = jnp.concatenate(
-        [cut(own_z).astype(f32), cut(own_x).astype(f32), cut(own_out).astype(f32)], axis=1
-    )
-    piece = lax.ppermute(piece, ("core", "zh"), CROSS)
+    piece = lax.dynamic_slice_in_dim(behind(own, *first), chip * size, size).astype(f32)
+    piece = behind(lax.ppermute(piece, BOTH, CROSS), *second)
     if chips == 4:
         parts = [piece]
         for away in range(1, chips):
@@ -514,13 +582,13 @@
                 (4 * c + kind, 4 * (c ^ away) + kind) for c in range(chips) for kind in (1, 2)
             ]
             parts.append(lax.ppermute(piece, ("chip", "core", "zh"), pairs))
-        place = jnp.stack([chip, (core == far).astype(jnp.int32)]).astype(jnp.int32)
+        place = jnp.stack([chip, held]).astype(jnp.int32)
         blocks = chips
     else:
         parts = [lax.all_gather(piece, "chip", tiled=True)]
-        place = jnp.stack([0, (core == far).astype(jnp.int32)]).astype(jnp.int32)
+        place = jnp.stack([0, held]).astype(jnp.int32)
         blocks, size = 1, width
-    wall_cols = 2 * inner + BC + LANES
+    all_cols = cols + sum(value.shape[1] for value in more)
 
     def rows(cols):
         return pl.BlockSpec((size, cols), lambda c: (c, 0))
@@ -528,16 +596,16 @@
     return pl.pallas_call(
         weight_kernel,
         grid=(blocks,),
-        in_specs=[pl.BlockSpec(memory_space=pltpu.SMEM)]
-        + [rows(inner), rows(inner), rows(inner), rows(BC), rows(LANES)]
-        + [whole((size, 3 * inner))] * len(parts),
-        out_specs=[rows(wall_cols), rows(inner)],
-        out_shape=[shape(width, wall_cols, dtype=bf16), shape(width, inner, dtype=bf16)],
+        in_specs=[pl.BlockSpec(memory_space=pltpu.SMEM), rows(cols)]
+        + [whole((size, cols))] * len(parts)
+        + [rows(value.shape[1]) for value in more],
+        out_specs=rows(all_cols),
+        out_shape=shape(width, all_cols, dtype=bf16),
         compiler_params=pltpu.CompilerParams(
-            dimension_semantics=("arbitrary",), vmem_limit_bytes=56 * 1024 * 1024
+            dimension_semantics=("arbitrary",), vmem_limit_bytes=40 * 1024 * 1024
         ),
         name="weights",
-    )(place, own_z, own_x, own_out, bc, dt, *parts)
+    )(place, own, *parts, *more)
 
 
 def shards(
@@ -566,32 +634,33 @@
     heads = w_dt.shape[2]
     count = tok // GROUP
     conv_cols = inner + BC
-    all_cols = 2 * inner + BC + LANES
-
+    all_cols = inner + BC + LANES
+
+    dt_own = w_dt.astype(f32).reshape(LAYERS, width * heads // LANES, LANES)
+    dt_sent = lax.ppermute(dt_own, BOTH, CROSS)
+    dt_all = pad_lanes(jnp.where(held, dt_own, dt_sent).reshape(LAYERS, width, heads))
+    wall = gather_weights(w_x[0], (w_bc[0], dt_all[0]))
+    hidden = to_block(x_input.astype(f32))
+    seg = to_block(seg_ids.astype(f32))
     small = jnp.concatenate(
         [
-            value.astype(f32).reshape(LAYERS, -1)
-            for value in (w_dt, conv_x, bias_x, dt_bias, a_log, d_skip, gate_gain)
+            value.reshape(LAYERS, -1)
+            for value in (conv_x, bias_x, dt_bias, a_log, d_skip, gate_gain)
         ],
         axis=1,
     )
     small = jnp.where(held, small, lax.ppermute(small, BOTH, CROSS))
-    sizes = (width * heads, CONV * inner, inner, heads, heads, heads, inner)
+    sizes = (CONV * inner, inner, heads, heads, heads, inner)
     pieces, at = [], 0
     for size in sizes:
         pieces.append(small[:, at : at + size])
         at += size
-    w_dt, conv_x, bias_x, dt_bias, a_log, d_skip, gate_gain = pieces
-    w_dt = w_dt.reshape(LAYERS, width, heads)
+    conv_x, bias_x, dt_bias, a_log, d_skip, gate_gain = pieces
     conv_x = conv_x.reshape(LAYERS, CONV, inner)
-    weights = [
-        gather_weights(w_z[layer], w_x[layer], w_out[layer], w_bc[layer], pad_lanes(w_dt[layer]))
-        for layer in range(LAYERS)
-    ]
-    seg = to_block(seg_ids.astype(f32))
-    hidden = to_block(x_input.astype(f32))
-    cotangent = to_block(cotangent.astype(f32))
     hidden_own = own_rows(hidden)
+    hidden = [hidden]
+    place = jnp.stack([own_place(), own_place()]).astype(jnp.int32)
+    smem = pl.BlockSpec(memory_space=pltpu.SMEM)
     edge_seg = shifted(seg[tok - ROWS :], 1)
     seg_ext = jnp.concatenate([edge_seg, seg])
     before = jnp.concatenate([edge_seg[ROWS - 1 :], seg[GROUP - 1 : tok - 1 : GROUP]])
@@ -620,7 +689,8 @@
     matmul_flops = 2 * tok * width
     stored = []
     for layer in range(LAYERS):
-        wall, wout = weights[layer]
+        if layer > 0:
+            wall = next_wall
         taps = jnp.concatenate([conv_x[layer], conv_bc[layer]], axis=1)
         bias = eight(jnp.concatenate([bias_x[layer], bias_bc[layer]]))
         dtb = eight(pad_lanes(dt_bias[layer]))
@@ -628,15 +698,19 @@
         dskip = eight(jnp.repeat(d_skip[layer], HEADDIM))
         ggain = eight(gate_gain[layer])
         ngain = norm_gain[layer][None, :]
-        end = hidden[tok - 16 :].astype(f32)
+        if len(hidden) == 1:
+            end = hidden[0][tok - 16 :]
+        else:
+            ends = jnp.stack([piece[GROUP - 16 :] for piece in hidden])
+            end = lax.dynamic_index_in_dim(ends, 3 ^ own_place(), 0, False)
         end = end * lax.rsqrt(jnp.mean(end * end, axis=1, keepdims=True) + epsilon) * ngain
-        end = mm(end.astype(bf16), wall[:, inner : 2 * inner + BC])[ROWS:]
+        end = mm(end.astype(bf16), wall[:, : inner + BC])[ROWS:]
         halo = shifted(end, 1)
-        normed, zval, cin, cpre, dtp, cum, dtv, xdt, bc, sloc, pref, send = call(
+        normed, cin, cpre, dtp, cum, dtv, xdt, bc, sloc, pref, send = call(
             in_kernel,
             count,
             [
-                (by_rows(width, count), hidden),
+                (smem, place),
                 (whole((width, all_cols)), wall),
                 (whole((1, width)), ngain),
                 (whole((CONV, conv_cols)), taps),
@@ -647,10 +721,10 @@
                 (whole((ROWS, conv_cols)), halo),
                 (whole((LANES, inner)), expand),
                 (whole((GROUP, GROUP)), tri),
-            ],
+            ]
+            + by_piece(hidden, count),
             [
                 (by_rows(width, count), shape(tok, width, dtype=bf16)),
-                (by_rows(inner, count), shape(tok, inner)),
                 (by_rows(conv_cols, count), shape(tok, conv_cols)),
                 (by_rows(conv_cols, count), shape(tok, conv_cols)),
                 (by_rows(LANES, count), shape(tok, LANES)),
@@ -670,6 +744,16 @@
             matmul_flops * all_cols,
             "in_proj_conv",
         )
+        if layer == 0:
+            wz = gather_weights(w_z[0], first=(wall,))
+            wout = gather_weights(w_out[0], first=(wall,))
+            cotangent = to_block(behind(cotangent.astype(f32), wall))
+            next_wall = gather_weights(w_x[1], (w_bc[1], dt_all[1]), (send,))
+            next_wz = gather_weights(w_z[1], first=(send,))
+            next_wout = gather_weights(w_out[1], first=(send,))
+        else:
+            wz, wout = next_wz, next_wout
+        zval = mm(normed, wz)
         (yin,) = call(
             intra_kernel,
             count,
@@ -703,8 +787,8 @@
                 (whole((ROWS, inner)), ggain),
                 (whole((width, inner)), wout),
                 (whole((LANES, inner)), expand),
-                (by_rows(width, count), cotangent),
-            ],
+            ]
+            + ([(by_rows(width, count), cotangent)] if layer == LAYERS - 1 else []),
             [
                 (by_rows(inner, count), shape(tok, inner)),
                 (by_rows(inner, count), shape(tok, inner, dtype=bf16)),
@@ -716,22 +800,22 @@
             "gate_out_proj",
         )
         sums = total(sums, ("core", "zl"))
-        proj_sum = scatter_sum(proj)
         gate_scale = lax.rsqrt(sums[0] / INNER + epsilon)
         stored.append(
             dict(
                 hidden=hidden_own, normed=normed, zval=zval, cin=cin, cpre=cpre, dtp=dtp, cum=cum,
                 dtv=dtv, xdt=xdt, bc=bc, sloc=sloc, pref=pref, entry=entry, y=y, gate_in=gate_in,
-                proj_sum=proj_sum, gate_scale=gate_scale, dots=sums[1], halo=halo, wall=wall, wout=wout,
+                proj=proj, gate_scale=gate_scale, dots=sums[1], halo=halo, wall=wall, wz=wz, wout=wout,
                 taps=taps, dtb=dtb, avec=avec, dskip=dskip, ggain=ggain,
             )
         )
-        hidden_own = hidden_own + own_rows(gate_scale)[:, None] * proj_sum
         if layer < LAYERS - 1:
-            hidden = gather_rows(hidden_own)
-    final_out = narrowed(deliver(hidden_own))
-
-    grad_h = cotangent
+            proj_sum = scatter_sum(proj)
+            stored[layer]["proj_sum"] = proj_sum
+            hidden_own = hidden_own + own_rows(gate_scale)[:, None] * proj_sum
+            hidden = gather_pieces(hidden_own)
+
+    grad_h = [cotangent]
     grad_own = own_rows(cotangent)
     matrices = [None] * LAYERS
     vectors = [None] * LAYERS
@@ -750,7 +834,7 @@
             gate_kernel,
             count,
             [
-                (rev(width), grad_h),
+                (smem, place),
                 (rev(1), gate_scale[:, None]),
                 (rev(1), gsq[:, None]),
                 (rev(inner), kept["y"]),
@@ -761,7 +845,8 @@
                 (rev(BC), kept["bc"]),
                 (rev(ROWS), mask),
                 (whole((LANES, inner)), expand),
-            ],
+            ]
+            + by_piece(grad_h, count, True),
             [
                 (rev(width), shape(tok, width, dtype=bf16)),
                 (rev(inner), shape(tok, inner, dtype=bf16)),
@@ -796,6 +881,8 @@
         )
         gout = chain(gsend, True)
         grad_wout = mm(gproj, kept["gate_in"], ((0,), (0,)))
+        grad_wz = mm(kept["normed"], dz, ((0,), (0,)))
+        partial_z = mm(dz, kept["wz"], ((1,), (1,)))
         gall, last8, rim, gtaps, vecs, dsk = call(
             in_back_kernel,
             count,
@@ -803,7 +890,6 @@
                 (rev(inner), u),
                 (rev(BC), dbc),
                 (rev(inner), dy),
-                (rev(inner), dz),
                 (rev(inner), kept["y"]),
                 (rev(conv_cols), kept["cpre"]),
                 (rev(conv_cols), kept["cin"]),
@@ -841,11 +927,13 @@
         )
         rim_back = shifted(rim, -1)
         gall = lax.dynamic_update_slice(
-            gall, (last8 + rim_back).astype(bf16), (tok - ROWS, inner)
+            gall, (last8 + rim_back).astype(bf16), (tok - ROWS, 0)
         )
-        grad_normed = scatter_sum(mm(gall, kept["wall"], ((1,), (1,))))
-        grad_win = mm(kept["normed"], gall[:, : 2 * inner + BC], ((0,), (0,)))
-        grad_wdt = mm(kept["normed"], gall[:, 2 * inner + BC :], ((0,), (0,)))
+        partial = partial_z + mm(gall, kept["wall"], ((1,), (1,)))
+        grad_normed = scatter_sum(partial)
+        late = behind(gall, partial)
+        grad_win = mm(kept["normed"], late[:, : inner + BC], ((0,), (0,)))
+        grad_wdt = mm(kept["normed"], late[:, inner + BC :], ((0,), (0,)))
         hidden_in = kept["hidden"]
         inv = lax.rsqrt(jnp.mean(hidden_in * hidden_in, axis=1, keepdims=True) + epsilon)
         grad_ngain = jnp.sum(grad_normed * hidden_in * inv, axis=0)
@@ -854,14 +942,27 @@
             back - hidden_in * inv * inv * jnp.mean(back * hidden_in, axis=1, keepdims=True)
         )
         if layer > 0:
-            grad_h = gather_rows(grad_own)
-        grad_win = lax.psum_scatter(grad_win, "chip", scatter_dimension=0, tiled=True)
-        grad_wout = lax.psum_scatter(grad_wout, "chip", scatter_dimension=0, tiled=True)
-        matrices[layer] = (
-            place_rows(grad_win[:, : 2 * inner]),
-            place_rows(grad_wout),
-            shared_rows(grad_win[:, 2 * inner :]),
-        )
+            grad_h = gather_pieces(grad_own)
+        matrices[layer] = [
+            lax.psum_scatter(value, "chip", scatter_dimension=0, tiled=True)
+            for value in (grad_wout, grad_wz, grad_win)
+        ]
+        if layer == LAYERS - 1:
+            last_sum = scatter_sum(kept["proj"], (dy,), (u,), (gall,))
+            hidden_own = hidden_own + own_rows(gate_scale)[:, None] * last_sum
+        else:
+            marks = ((dy,), (u,), (partial,))
+            final_out = deliver(hidden_own, bf16, *marks)
+            input_grad = deliver(grad_own, f32)
+            matrices[1] = [behind(value, u) for value in matrices[1]]
+            matrices[0] = [behind(value, grad_own) for value in matrices[0]]
+            for number, (g_out, g_z, g_in) in enumerate(matrices):
+                matrices[number] = (
+                    place_rows(g_out),
+                    place_rows(g_z),
+                    place_rows(g_in[:, :inner]),
+                    shared_rows(g_in[:, inner:]),
+                )
         vectors[layer] = jnp.concatenate(
             [
                 gtaps[: CONV + 1, :inner].reshape(-1),
@@ -890,14 +991,13 @@
     g_wdt = g_wdt.reshape(LAYERS, width, heads)
     rows = width // lax.axis_size(("chip", "core"))
     g_wdt = lax.dynamic_slice_in_dim(g_wdt, lax.axis_index(("chip", "core")) * rows, rows, axis=1)
-    g_win = jnp.stack([m[0] for m in matrices])
     return (
         final_out,
-        deliver(grad_own),
+        input_grad,
         g_ngain,
-        g_win[:, :, :inner],
-        g_win[:, :, inner:],
+        jnp.stack([m[1] for m in matrices]),
         jnp.stack([m[2] for m in matrices]),
+        jnp.stack([m[3] for m in matrices]),
         g_wdt,
         g_conv.reshape(LAYERS, CONV, inner),
         g_bc[:, :CONV],
@@ -907,7 +1007,7 @@
         g_alog,
         jnp.sum(g_dsk.reshape(LAYERS, heads, HEADDIM), axis=2),
         g_ggain,
-        jnp.stack([m[1] for m in matrices]),
+        jnp.stack([m[0] for m in matrices]),
     )
 
 

time: 1090 us -> 967 us (0.89)
  waiting for transfers between devices: 490 us -> 331 us
  starting transfers between devices: 196 us -> 241 us
  other arithmetic: 98.7 us -> 78.9 us
    all_gather x4 -> x0, waiting for transfers between devices: 178 us -> none  [chain(): gathered = lax.all_gather(part, BLOCKS)]
    ppermute x2 -> x27, waiting for transfers between devices: 0.01 us -> 108 us  [the longest x12 65.6 us: chain(): got = lax.ppermute(part, BLOCKS, [(i, i ^ step) for i in range(count)])]
    ppermute x2 -> x27, starting transfers between devices: 7.17 us -> 109 us  [the longest x6 46.3 us: gather_weights(): piece = behind(lax.ppermute(piece, BOTH, CROSS), *second)]
    ppermute x5, starting transfers between devices: 78 us -> 7.69 us  [shifted(): lax.ppermute(value, BLOCKS, [(source, source + steps) for source in range...]
    reduce_scatter x4 -> x6, waiting for transfers between devices: 40.7 us -> 0.05 us  [shards(): lax.psum_scatter(value, 'chip', scatter_dimension=0, tiled=True)]
    ppermute x21 -> x19, waiting for transfers between devices: 129 us -> 95.5 us  [swap(): return lax.ppermute(value, axis, SWAP)]
    ppermute x12, waiting for transfers between devices: 79.3 us -> 50.2 us  [total(): lax.ppermute(value, axis, [(i, i ^ step) for i in range(count)])]
    ppermute x4 -> x6, waiting for transfers between devices: 34.8 us -> 63.2 us  [place_rows(): full = part + lax.ppermute(part, BOTH, CROSS_BACK)]
  transfers between devices with their start and end apart: 72 -> 109, of which waited for: 34 -> 37; matrix products, arithmetic and copies ran while one was open for 15% -> 16% of each run, Pallas kernels for 8% -> 14%
where the time goes in v3:
time: 967 us; the launch traced here: 956 us
  waiting for transfers between devices  331 us (34%)
  starting transfers between devices  241 us (25%)
  Pallas kernels  165 us (17%)
  local copies, waits for them, and re-layouts  82.4 us (9%)
  other arithmetic  78.9 us (8%)
  matrix products  40.8 us (4%)
  between operations  16.5 us (2%)
    pallas_call x12, Pallas kernels, call(): pl.pallas_call(kernel, grid=(count,), in_specs=[spec for spec, _ in ins],...  146 us
    ppermute x19, waiting for transfers between devices, swap(): return lax.ppermute(value, axis, SWAP)  95.5 us
    ppermute x12, waiting for transfers between devices, chain(): got = lax.ppermute(part, BLOCKS, [(i, i ^ step) for i in range(count)])  65.6 us
    ppermute x6, waiting for transfers between devices, place_rows(): full = part + lax.ppermute(part, BOTH, CROSS_BACK)  63.2 us
    ppermute x12, waiting for transfers between devices, total(): lax.ppermute(value, axis, [(i, i ^ step) for i in range(count)])  50.2 us
    ppermute x6, starting transfers between devices, gather_weights(): piece = behind(lax.ppermute(piece, BOTH, CROSS), *second)  46.3 us
    dot_general x14, matrix products, mm(): lax.dot_general(left, right, (dims, ((), ())), preferred_element_type=f32...  36.8 us
    ppermute x12, starting transfers between devices, total(): lax.ppermute(value, axis, [(i, i ^ step) for i in range(count)])  30.3 us
  transfers between devices with their start and end apart: 109, of which 37 were waited for; matrix products, arithmetic and copies ran while one was open for 16% of the time, Pallas kernels for 14%

profile of v3, /device:TPU:0, one launch (start us, length us, event | category | flops | bytes accessed | tf_op | source)
XLA Modules:
  0.0 955.5 jit_solution(13554170077552739850)
XLA Ops:
  59.3 19.2 %collective-permute-start.10 = (f32[256,512]{1,0:T(8,128)S(1)}, f32[256,512]{1,0:T(8,128)}, u32[]{:S(2)}, u32[]{:S(2)}) collective-permute-start(f32[256,512]{1,0:T(8,128)S(1)} %dynamic-slice_convert_fusion.4), channel_id=1, source_target_pairs={{0,2},{6,4},{1,3},{7,5},{8,10},{14,12},{9,11},{15,13},{16,18},{22,... | collective-permute-start | bytes 1572872 | tf_op jit(solution)/shard_map/ppermute | solution.py:577
  92.4 15.6 %in_proj_conv.2 = (bf16[1024,1024]{1,0:T(8,128)(2,1)}, f32[1024,768]{1,0:T(8,128)}, f32[1024,768]{1,0:T(8,128)}, f32[1024,128]{1,0:T(8,128)}, f32[1024,128]{1,0:...) custom-call(s32[2]{0:T(128)} %pad_add_fusion.place, ...), custom_call_target="tpu_custom_call" | custom-call | flops 1879048192 | bytes 8388608 | tf_op jit(solution)/shard_map/in_proj_conv/pallas_call | solution.py:350
  152.2 11.1 %gate_out_proj.2 = (f32[1024,512]{1,0:T(8,128)}, bf16[1024,512]{1,0:T(8,128)(2,1)}, f32[1024,1024]{1,0:T(8,128)}, f32[8,1024]{1,0:T(8,128)}) custom-call(f32[1024,512]{1,0:T(8,128)} %ssd_within.2.yin, f32[1024,768]{1,0:T(8,128)} %get-tuple-element.100.cpre, f32[1024,128]{1,0:T(8,128)} %get-tuple-element.97.cum, bf16[1024,256]{1,0:T(8,128)(2,1)} %get-tuple-element.99.bc, ...), custom_call_target="tpu_custom_call" | custom-call | flops 2147483648 | bytes 8388608 | tf_op jit(solution)/shard_map/gate_out_proj/pallas_call | solution.py:350
  166.5 13.1 %collective-permute-start.23 = (f32[512,1024]{1,0:T(8,128)}, f32[512,1024]{1,0:T(8,128)}, u32[]{:S(2)}, u32[]{:S(2)}) collective-permute-start(f32[512,1024]{1,0:T(8,128)} %constant_dynamic-slice_fusion.17), channel_id=1, source_target_pairs={{0,4},{4,0},{1,5},{5,1},{2,6},{6,2},{3,7},{7,3},{8,12},{12,8},{9,1... | collective-permute-start | bytes 6291464 | tf_op jit(solution)/shard_map/ppermute | solution.py:407
  207.0 13.6 %collective-permute-done.22 = f32[8,1024]{1,0:T(8,128)S(1)} collective-permute-done((f32[8,1024]{1,0:T(8,128)S(1)}, f32[8,1024]{1,0:T(8,128)S(1)}, u32[]{:S(2)}, u32[]{:S(2)}) %collective-permute-start.22) | collective-permute-done | bytes 32800 | tf_op jit(solution)/shard_map/ppermute | solution.py:415
  228.4 20.6 %collective-permute-done.29.refs_1_ = f32[256,1024]{1,0:T(8,128)} collective-permute-done((f32[256,1024]{1,0:T(8,128)}, f32[256,1024]{1,0:T(8,128)}, u32[]{:S(2)}, u32[]{:S(2)}) %collective-permute-start.29) | collective-permute-done | bytes 1048608 | tf_op jit(solution)/shard_map/ppermute | solution.py:407
  253.0 10.2 %collective-permute-start.33 = (f32[256,512]{1,0:T(8,128)}, f32[256,512]{1,0:T(8,128)}, u32[]{:S(2)}, u32[]{:S(2)}) collective-permute-start(f32[256,512]{1,0:T(8,128)} %dynamic-slice_convert_fusion.1), channel_id=1, source_target_pairs={{0,2},{6,4},{1,3},{7,5},{8,10},{14,12},{9,11},{15,13},{16,18},{22,... | collective-permute-start | bytes 1572872 | tf_op jit(solution)/shard_map/ppermute | solution.py:577
  280.8 17.1 %in_proj_conv.3 = (bf16[1024,1024]{1,0:T(8,128)(2,1)}, f32[1024,768]{1,0:T(8,128)}, f32[1024,768]{1,0:T(8,128)}, f32[1024,128]{1,0:T(8,128)}, f32[1024,128]{1,0:...) custom-call(s32[2]{0:T(128)} %pad_add_fusion.place, ...), custom_call_target="tpu_custom_call" | custom-call | flops 1879048192 | bytes 8388608 | tf_op jit(solution)/shard_map/in_proj_conv/pallas_call | solution.py:350
  304.6 11.1 %collective-permute-done.37 = f32[136,512]{1,0:T(8,128)S(1)} collective-permute-done((f32[136,512]{1,0:T(8,128)}, f32[136,512]{1,0:T(8,128)S(1)}, u32[]{:S(2)}, u32[]{:S(2)}) %collective-permute-start.37) | collective-permute-done | bytes 278560 | tf_op jit(solution)/shard_map/ppermute | solution.py:394
  344.1 14.1 %gate_out_proj.3 = (f32[1024,512]{1,0:T(8,128)}, bf16[1024,512]{1,0:T(8,128)(2,1)}, f32[1024,1024]{1,0:T(8,128)}, f32[8,1024]{1,0:T(8,128)}) custom-call(f32[1024,512]{1,0:T(8,128)} %ssd_within.3.yin, f32[1024,768]{1,0:T(8,128)} %get-tuple-element.113.cpre, f32[1024,128]{1,0:T(8,128)} %get-tuple-element.110.cum, bf16[1024,256]{1,0:T(8,128)(2,1)} %get-tuple-element.112.bc, ...), custom_call_target="tpu_custom_call" | custom-call | flops 2147483648 | bytes 8388608 | tf_op jit(solution)/shard_map/gate_out_proj/pallas_call | solution.py:350
  358.2 9.0 collective-permute-start.45
  374.6 10.1 %gate_back.2 = (bf16[1024,1024]{1,0:T(8,128)(2,1)}, bf16[1024,512]{1,0:T(8,128)(2,1)}, bf16[1024,512]{1,0:T(8,128)(2,1)}, f32[4,128,512]{2,1,0:T(8,128)}, f32[4,...) custom-call(s32[2]{0:T(128)} %pad_add_fusion.place, f32[1024,1]{1,0:T(8,128)} %copy-done.48, ...), custom_call_target="tpu_custom_call" | custom-call | flops 1073741824 | bytes 8388608 | tf_op jit(solution)/shard_map/gate_back/pallas_call | solution.py:350
  399.3 7.4 collective-permute-done.49
  407.8 10.4 %collective-permute-done.50 = f32[136,512]{1,0:T(8,128)S(1)} collective-permute-done((f32[136,512]{1,0:T(8,128)S(1)}, f32[136,512]{1,0:T(8,128)S(1)}, u32[]{:S(2)}, u32[]{:S(2)}) %collective-permute-start.50) | collective-permute-done | bytes 278560 | tf_op jit(solution)/shard_map/ppermute | solution.py:394
  420.5 7.5 ssd_within_back.2
  429.6 20.5 %in_proj_conv_back.2 = (bf16[1024,896]{1,0:T(8,128)(2,1)}, f32[8,768]{1,0:T(8,128)}, f32[8,768]{1,0:T(8,128)}, f32[8,768]{1,0:T(8,128)}, f32[8,128]{1,0:T(8,128)}, /*index=5*/f32[8,512]{1,0:T(8,128)}) custom-call(f32[1024,512]{1,0:T(8,128)} %get-tuple-element.126.uin, f32[1024,256]{1,0:T(8,128)} %get-tuple-element.128.dbc, ...), custom_call_target="tpu_custom_call" | custom-call | flops 2147483648 | bytes 8388608 | tf_op jit(solution)/shard_map/in_proj_conv_back/pallas_call | solution.py:350
  473.8 23.1 %collective-permute-done.48 = f32[256,1024]{1,0:T(8,128)S(1)} collective-permute-done((f32[256,1024]{1,0:T(8,128)S(1)}, f32[256,1024]{1,0:T(8,128)S(1)}, u32[]{:S(2)}, u32[]{:S(2)}) %collective-permute-start.48) | collective-permute-done | bytes 1048608 | tf_op jit(solution)/shard_map/ppermute | solution.py:407
  496.9 21.8 %collective-permute-done.54 = f32[256,1024]{1,0:T(8,128)S(1)} collective-permute-done((f32[256,1024]{1,0:T(8,128)S(1)}, f32[256,1024]{1,0:T(8,128)S(1)}, u32[]{:S(2)}, u32[]{:S(2)}) %collective-permute-start.54) | collective-permute-done | bytes 1048608 | tf_op jit(solution)/shard_map/ppermute | solution.py:407
  524.5 22.9 %collective-permute-done.57.refs_1_ = f32[256,1024]{1,0:T(8,128)} collective-permute-done((f32[256,1024]{1,0:T(8,128)S(1)}, f32[256,1024]{1,0:T(8,128)}, u32[]{:S(2)}, u32[]{:S(2)}) %collective-permute-start.57) | collective-permute-done | bytes 1048608 | tf_op jit(solution)/shard_map/ppermute | solution.py:407
  553.3 11.0 %gate_back.3 = (bf16[1024,1024]{1,0:T(8,128)(2,1)}, bf16[1024,512]{1,0:T(8,128)(2,1)}, bf16[1024,512]{1,0:T(8,128)(2,1)}, f32[4,128,512]{2,1,0:T(8,128)}, f32[4,...) custom-call(s32[2]{0:T(128)} %pad_add_fusion.place, f32[1024,1]{1,0:T(8,128)} %copy-done.47, ...), custom_call_target="tpu_custom_call" | custom-call | flops 1073741824 | bytes 8388608 | tf_op jit(solution)/shard_map/gate_back/pallas_call | solution.py:350
  572.6 13.0 %collective-permute-done.67 = f32[136,512]{1,0:T(8,128)S(1)} collective-permute-done((f32[136,512]{1,0:T(8,128)S(1)}, f32[136,512]{1,0:T(8,128)S(1)}, u32[]{:S(2)}, u32[]{:S(2)}) %collective-permute-start.67) | collective-permute-done | bytes 278560 | tf_op jit(solution)/shard_map/ppermute | solution.py:394
  586.4 9.5 collective-permute-done.68
  597.6 7.5 ssd_within_back.3
  609.5 20.4 %in_proj_conv_back.3 = (bf16[1024,896]{1,0:T(8,128)(2,1)}, f32[8,768]{1,0:T(8,128)}, f32[8,768]{1,0:T(8,128)}, f32[8,768]{1,0:T(8,128)}, f32[8,128]{1,0:T(8,128)}, /*index=5*/f32[8,512]{1,0:T(8,128)}) custom-call(f32[1024,512]{1,0:T(8,128)} %get-tuple-element.143.uin, f32[1024,256]{1,0:T(8,128)} %get-tuple-element.147.dbc, ...), custom_call_target="tpu_custom_call" | custom-call | flops 2147483648 | bytes 8388608 | tf_op jit(solution)/shard_map/in_proj_conv_back/pallas_call | solution.py:350
  699.1 9.9 %collective-permute-start.98 = (f32[128,256]{1,0:T(8,128)}, f32[128,256]{1,0:T(8,128)}, u32[]{:S(2)}, u32[]{:S(2)}) collective-permute-start(f32[128,256]{1,0:T(8,128)} %add.437), channel_id=1, source_target_pairs={{0,2},{2,0},{1,3},{3,1},{4,6},{6,4},{5,7},{7,5},{8,10},{10,8},{9,1... | collective-permute-start | bytes 393224 | tf_op jit(solution)/shard_map/ppermute | solution.py:415
  711.6 14.3 %collective-permute-start.63 = (f32[256,1024]{1,0:T(8,128)S(1)}, f32[256,1024]{1,0:T(8,128)}, u32[]{:S(2)}, u32[]{:S(2)}) collective-permute-start(f32[256,1024]{1,0:T(8,128)S(1)} %get-tuple-element.142.value), channel_id=1, source_target_pairs={{0,1},{1,0},{6,7},{7,6},{8,9},{9,8},{14,15},{15,14},{16,17},{17,16... | collective-permute-start | bytes 3145736 | tf_op jit(solution)/shard_map/ppermute | solution.py:500
  734.7 11.4 %collective-permute-start.65 = (f32[256,1024]{1,0:T(8,128)}, f32[256,1024]{1,0:T(8,128)}, u32[]{:S(2)}, u32[]{:S(2)}) collective-permute-start(f32[256,1024]{1,0:T(8,128)} %collective-permute-done.61.near), channel_id=1, source_target_pairs={{0,1},{1,0},{6,7},{7,6},{8,9},{9,8},{14,15},{15,14},{16,17},{17,16... | collective-permute-start | bytes 3145736 | tf_op jit(solution)/shard_map/ppermute | solution.py:501
  751.6 20.7 %collective-permute-done.80 = f32[2,14096]{1,0:T(2,128)S(1)} collective-permute-done((f32[2,14096]{1,0:T(2,128)S(1)}, f32[2,14096]{1,0:T(2,128)S(1)}, u32[]{:S(2)}, u32[]{:S(2)}) %collective-permute-start.80) | collective-permute-done | bytes 112800 | tf_op jit(solution)/shard_map/ppermute | solution.py:415
  782.8 8.7 collective-permute-done.65.near_s
  818.7 52.6 %collective-permute-done.85 = f32[256,512]{1,0:T(8,128)} collective-permute-done((f32[256,512]{1,0:T(8,128)}, f32[256,512]{1,0:T(8,128)}, u32[]{:S(2)}, u32[]{:S(2)}) %collective-permute-start.85) | collective-permute-done | bytes 524320 | tf_op jit(solution)/shard_map/ppermute | solution.py:1016
  900.9 20.0 %collective-permute-done.76.value_s = f32[256,1024]{1,0:T(8,128)} collective-permute-done((f32[256,1024]{1,0:T(8,128)S(1)}, f32[256,1024]{1,0:T(8,128)}, u32[]{:S(2)}, u32[]{:S(2)}) %collective-permute-start.76) | collective-permute-done | bytes 1048608 | tf_op jit(solution)/shard_map/ppermute | solution.py:500
  920.9 13.5 %collective-permute-done.78.near_s = f32[256,1024]{1,0:T(8,128)S(1)} collective-permute-done((f32[256,1024]{1,0:T(8,128)S(1)}, f32[256,1024]{1,0:T(8,128)S(1)}, u32[]{:S(2)}, u32[]{:S(2)}) %collective-permute-start.78) | collective-permute-done | bytes 1048608 | tf_op jit(solution)/shard_map/ppermute | solution.py:501
  (666 shorter events, 448.4 us)
Async XLA Ops:
  7.2 597.9 %reduce-scatter.9.cloned.1.call-start = ((), (), s32[]{:S(2)}) async-start(), calls=%async_computation.7 | async-start | bytes 2621440 | tf_op jit(solution)/shard_map/reduce_scatter | solution.py:947
  25.9 56.6 %collective-permute-start = (f32[1024,1024]{1,0:T(8,128)}, f32[1024,1024]{1,0:T(8,128)}, u32[]{:S(2)}, u32[]{:S(2)}) collective-permute-start(f32[1024,1024]{1,0:T(8,128)} %convert_element_type.87), channel_id=1, source_target_pairs={{0,4},{6,2},{1,5},{7,3},{8,12},{14,10},{9,13},{15,11},{16,20},{22,... | collective-permute-start | bytes 12582920 | tf_op jit(solution)/shard_map/ppermute | solution.py:522
  86.1 37.1 %collective-permute-start.11 = (f32[256,512]{1,0:T(8,128)}, f32[256,512]{1,0:T(8,128)S(1)}, u32[]{:S(2)}, u32[]{:S(2)}) collective-permute-start(f32[256,512]{1,0:T(8,128)} %collective-permute-done.10.refs_0_), channel_id=1, source_target_pairs={{2,10},{4,12},{10,2},{12,4},{18,26},{20,28},{26,18},{28,20},{3,11}... | collective-permute-start | bytes 1572872 | tf_op jit(solution)/shard_map/ppermute | solution.py:584
  193.2 125.0 %collective-permute-start.44 = (f32[1024,1024]{1,0:T(8,128)}, f32[1024,1024]{1,0:T(8,128)}, u32[]{:S(2)}, u32[]{:S(2)}) collective-permute-start(f32[1024,1024]{1,0:T(8,128)} %convert_element_type.99), channel_id=1, source_target_pairs={{0,4},{6,2},{1,5},{7,3},{8,12},{14,10},{9,13},{15,11},{16,20},{22,... | collective-permute-start | bytes 12582920 | tf_op jit(solution)/shard_map/ppermute | solution.py:522
  224.7 49.2 %collective-permute-start.30 = (f32[256,1024]{1,0:T(8,128)}, f32[256,1024]{1,0:T(8,128)}, u32[]{:S(2)}, u32[]{:S(2)}) collective-permute-start(f32[256,1024]{1,0:T(8,128)} %get-tuple-element.239.refs_0_), channel_id=1, source_target_pairs={{0,4},{4,0},{1,5},{5,1},{2,6},{6,2},{3,7},{7,3},{8,12},{12,8},{9,1... | collective-permute-start | bytes 3145736 | tf_op jit(solution)/shard_map/ppermute | solution.py:407
  226.9 36.4 %collective-permute-start.28 = (f32[256,512]{1,0:T(8,128)S(1)}, f32[256,512]{1,0:T(8,128)}, u32[]{:S(2)}, u32[]{:S(2)}) collective-permute-start(f32[256,512]{1,0:T(8,128)S(1)} %collective-permute-done.25.refs_0_), channel_id=1, source_target_pairs={{2,26},{4,28},{10,18},{12,20},{18,10},{20,12},{26,2},{28,4},{3,27}... | collective-permute-start | bytes 1572872 | tf_op jit(solution)/shard_map/ppermute | solution.py:584
  253.0 49.5 %collective-permute-start.33 = (f32[256,512]{1,0:T(8,128)}, f32[256,512]{1,0:T(8,128)}, u32[]{:S(2)}, u32[]{:S(2)}) collective-permute-start(f32[256,512]{1,0:T(8,128)} %dynamic-slice_convert_fusion.1), channel_id=1, source_target_pairs={{0,2},{6,4},{1,3},{7,5},{8,10},{14,12},{9,11},{15,13},{16,18},{22,... | collective-permute-start | bytes 1572872 | tf_op jit(solution)/shard_map/ppermute | solution.py:577
  263.2 40.7 %collective-permute-start.40 = (f32[256,512]{1,0:T(8,128)}, f32[256,512]{1,0:T(8,128)}, u32[]{:S(2)}, u32[]{:S(2)}) collective-permute-start(f32[256,512]{1,0:T(8,128)} %dynamic-slice_convert_fusion), channel_id=1, source_target_pairs={{0,2},{6,4},{1,3},{7,5},{8,10},{14,12},{9,11},{15,13},{16,18},{22,... | collective-permute-start | bytes 1572872 | tf_op jit(solution)/shard_map/ppermute | solution.py:577
  388.6 256.9 %reduce-scatter.17.cloned.1.call-start = ((), (), s32[]{:S(2)}) async-start(), calls=%async_computation.11 | async-start | bytes 2621440 | tf_op jit(solution)/shard_map/reduce_scatter | solution.py:947
  399.1 277.6 %reduce-scatter.13.cloned.1.call-start = ((), (), s32[]{:S(2)}) async-start(), calls=%async_computation.9 | async-start | bytes 3932160 | tf_op jit(solution)/shard_map/reduce_scatter | solution.py:947
  467.7 342.2 %reduce-scatter.7.cloned.1.call-start = ((), (), s32[]{:S(2)}) async-start(), calls=%async_computation.6 | async-start | bytes 2621440 | tf_op jit(solution)/shard_map/reduce_scatter | solution.py:947
  473.1 45.6 %collective-permute-start.54 = (f32[256,1024]{1,0:T(8,128)S(1)}, f32[256,1024]{1,0:T(8,128)S(1)}, u32[]{:S(2)}, u32[]{:S(2)}) collective-permute-start(f32[256,1024]{1,0:T(8,128)S(1)} %constant_dynamic-slice_fusion.11), channel_id=1, source_target_pairs={{0,1},{1,0},{2,3},{3,2},{4,5},{5,4},{6,7},{7,6},{8,9},{9,8},{10,11... | collective-permute-start | bytes 3145736 | tf_op jit(solution)/shard_map/ppermute | solution.py:407
  568.2 243.0 %reduce-scatter.15.cloned.1.call-start = ((), (), s32[]{:S(2)}) async-start(), calls=%async_computation.10 | async-start | bytes 2621440 | tf_op jit(solution)/shard_map/reduce_scatter | solution.py:947
  605.1 44.1 %collective-permute-start.87 = (f32[256,512]{1,0:T(8,128)}, f32[256,512]{1,0:T(8,128)S(1)}, u32[]{:S(2)}, u32[]{:S(2)}) collective-permute-start(f32[256,512]{1,0:T(8,128)} %reduce-scatter.9.cloned.1.call-done), channel_id=1, source_target_pairs={{2,0},{4,6},{3,1},{5,7},{10,8},{12,14},{11,9},{13,15},{18,16},{20,... | collective-permute-start | bytes 1572872 | tf_op jit(solution)/shard_map/ppermute | solution.py:1016
  634.3 255.5 %reduce-scatter.11.cloned.1.call-start = ((), (), s32[]{:S(2)}) async-start(), calls=%async_computation.8 | async-start | bytes 3932160 | tf_op jit(solution)/shard_map/reduce_scatter | solution.py:947
  645.4 41.2 %collective-permute-start.71 = (f32[512,1024]{1,0:T(8,128)}, f32[512,1024]{1,0:T(8,128)}, u32[]{:S(2)}, u32[]{:S(2)}) collective-permute-start(f32[512,1024]{1,0:T(8,128)} %constant_dynamic-slice_fusion.10), channel_id=1, source_target_pairs={{0,4},{4,0},{1,5},{5,1},{2,6},{6,2},{3,7},{7,3},{8,12},{12,8},{9,1... | collective-permute-start | bytes 6291464 | tf_op jit(solution)/shard_map/ppermute | solution.py:407
  670.8 62.2 %collective-permute-start.61 = (f32[256,1024]{1,0:T(8,128)S(1)}, f32[256,1024]{1,0:T(8,128)}, u32[]{:S(2)}, u32[]{:S(2)}) collective-permute-start(f32[256,1024]{1,0:T(8,128)S(1)} %get-tuple-element.142.value), channel_id=1, source_target_pairs={{4,0},{2,6},{5,1},{3,7},{12,8},{10,14},{13,9},{11,15},{20,16},{18,... | collective-permute-start | bytes 3145736 | tf_op jit(solution)/shard_map/ppermute | solution.py:491
  672.9 38.8 %collective-permute-start.62 = (f32[256,1024]{1,0:T(8,128)S(1)}, f32[256,1024]{1,0:T(8,128)}, u32[]{:S(2)}, u32[]{:S(2)}) collective-permute-start(f32[256,1024]{1,0:T(8,128)S(1)} %get-tuple-element.142.value), channel_id=1, source_target_pairs={{4,2},{2,4},{5,3},{3,5},{12,10},{10,12},{13,11},{11,13},{20,18},{1... | collective-permute-start | bytes 3145736 | tf_op jit(solution)/shard_map/ppermute | solution.py:490
  691.9 56.1 %collective-permute-start.72 = (f32[256,1024]{1,0:T(8,128)}, f32[256,1024]{1,0:T(8,128)}, u32[]{:S(2)}, u32[]{:S(2)}) collective-permute-start(f32[256,1024]{1,0:T(8,128)} %constant_dynamic-slice_fusion.9), channel_id=1, source_target_pairs={{0,1},{1,0},{2,3},{3,2},{4,5},{5,4},{6,7},{7,6},{8,9},{9,8},{10,11... | collective-permute-start | bytes 3145736 | tf_op jit(solution)/shard_map/ppermute | solution.py:407
  697.2 37.5 %collective-permute-start.91 = (f32[256,512]{1,0:T(8,128)}, f32[256,512]{1,0:T(8,128)}, u32[]{:S(2)}, u32[]{:S(2)}) collective-permute-start(f32[256,512]{1,0:T(8,128)} %slice.453), channel_id=1, source_target_pairs={{2,0},{4,6},{3,1},{5,7},{10,8},{12,14},{11,9},{13,15},{18,16},{20,... | collective-permute-start | bytes 1572872 | tf_op jit(solution)/shard_map/ppermute | solution.py:1016
  711.6 71.2 %collective-permute-start.63 = (f32[256,1024]{1,0:T(8,128)S(1)}, f32[256,1024]{1,0:T(8,128)}, u32[]{:S(2)}, u32[]{:S(2)}) collective-permute-start(f32[256,1024]{1,0:T(8,128)S(1)} %get-tuple-element.142.value), channel_id=1, source_target_pairs={{0,1},{1,0},{6,7},{7,6},{8,9},{9,8},{14,15},{15,14},{16,17},{17,16... | collective-permute-start | bytes 3145736 | tf_op jit(solution)/shard_map/ppermute | solution.py:500
  729.7 53.1 %collective-permute-start.64 = (f32[256,1024]{1,0:T(8,128)S(1)}, f32[256,1024]{1,0:T(8,128)}, u32[]{:S(2)}, u32[]{:S(2)}) collective-permute-start(f32[256,1024]{1,0:T(8,128)S(1)} %collective-permute-done.60.mine), channel_id=1, source_target_pairs={{2,3},{3,2},{4,5},{5,4},{10,11},{11,10},{12,13},{13,12},{18,19},{1... | collective-permute-start | bytes 3145736 | tf_op jit(solution)/shard_map/ppermute | solution.py:503
  733.0 49.8 %collective-permute-start.66 = (f32[256,1024]{1,0:T(8,128)}, f32[256,1024]{1,0:T(8,128)}, u32[]{:S(2)}, u32[]{:S(2)}) collective-permute-start(f32[256,1024]{1,0:T(8,128)} %collective-permute-done.62.theirs), channel_id=1, source_target_pairs={{2,3},{3,2},{4,5},{5,4},{10,11},{11,10},{12,13},{13,12},{18,19},{1... | collective-permute-start | bytes 3145736 | tf_op jit(solution)/shard_map/ppermute | solution.py:504
  734.7 56.8 %collective-permute-start.65 = (f32[256,1024]{1,0:T(8,128)}, f32[256,1024]{1,0:T(8,128)}, u32[]{:S(2)}, u32[]{:S(2)}) collective-permute-start(f32[256,1024]{1,0:T(8,128)} %collective-permute-done.61.near), channel_id=1, source_target_pairs={{0,1},{1,0},{6,7},{7,6},{8,9},{9,8},{14,15},{15,14},{16,17},{17,16... | collective-permute-start | bytes 3145736 | tf_op jit(solution)/shard_map/ppermute | solution.py:501
  803.6 83.6 %collective-permute-start.73 = (f32[256,1024]{1,0:T(8,128)S(1)}, f32[256,1024]{1,0:T(8,128)S(1)}, u32[]{:S(2)}, u32[]{:S(2)}) collective-permute-start(f32[256,1024]{1,0:T(8,128)S(1)} %multiply_add_fusion.value), channel_id=1, source_target_pairs={{0,2},{6,4},{1,3},{7,5},{8,10},{14,12},{9,11},{15,13},{16,18},{22,... | collective-permute-start | bytes 3145736 | tf_op jit(solution)/shard_map/ppermute | solution.py:489
  806.9 84.6 %collective-permute-start.74 = (f32[256,1024]{1,0:T(8,128)S(1)}, f32[256,1024]{1,0:T(8,128)S(1)}, u32[]{:S(2)}, u32[]{:S(2)}) collective-permute-start(f32[256,1024]{1,0:T(8,128)S(1)} %multiply_add_fusion.value), channel_id=1, source_target_pairs={{4,0},{2,6},{5,1},{3,7},{12,8},{10,14},{13,9},{11,15},{20,16},{18,... | collective-permute-start | bytes 3145736 | tf_op jit(solution)/shard_map/ppermute | solution.py:491
  808.2 72.0 %collective-permute-start.75 = (f32[256,1024]{1,0:T(8,128)S(1)}, f32[256,1024]{1,0:T(8,128)}, u32[]{:S(2)}, u32[]{:S(2)}) collective-permute-start(f32[256,1024]{1,0:T(8,128)S(1)} %multiply_add_fusion.value), channel_id=1, source_target_pairs={{4,2},{2,4},{5,3},{3,5},{12,10},{10,12},{13,11},{11,13},{20,18},{1... | collective-permute-start | bytes 3145736 | tf_op jit(solution)/shard_map/ppermute | solution.py:490
  809.9 61.4 %collective-permute-start.85 = (f32[256,512]{1,0:T(8,128)}, f32[256,512]{1,0:T(8,128)}, u32[]{:S(2)}, u32[]{:S(2)}) collective-permute-start(f32[256,512]{1,0:T(8,128)} %reduce-scatter.7.cloned.1.call-done), channel_id=1, source_target_pairs={{2,0},{4,6},{3,1},{5,7},{10,8},{12,14},{11,9},{13,15},{18,16},{20,... | collective-permute-start | bytes 1572872 | tf_op jit(solution)/shard_map/ppermute | solution.py:1016
  811.2 65.8 %collective-permute-start.99 = (f32[256,512]{1,0:T(8,128)}, f32[256,512]{1,0:T(8,128)}, u32[]{:S(2)}, u32[]{:S(2)}) collective-permute-start(f32[256,512]{1,0:T(8,128)} %reduce-scatter.15.cloned.1.call-done), channel_id=1, source_target_pairs={{2,0},{4,6},{3,1},{5,7},{10,8},{12,14},{11,9},{13,15},{18,16},{20,... | collective-permute-start | bytes 1572872 | tf_op jit(solution)/shard_map/ppermute | solution.py:1016
  891.6 42.9 %collective-permute-start.78 = (f32[256,1024]{1,0:T(8,128)S(1)}, f32[256,1024]{1,0:T(8,128)S(1)}, u32[]{:S(2)}, u32[]{:S(2)}) collective-permute-start(f32[256,1024]{1,0:T(8,128)S(1)} %collective-permute-done.74.near), channel_id=1, source_target_pairs={{0,1},{1,0},{6,7},{7,6},{8,9},{9,8},{14,15},{15,14},{16,17},{17,16... | collective-permute-start | bytes 3145736 | tf_op jit(solution)/shard_map/ppermute | solution.py:501
  897.1 41.9 %collective-permute-start.89 = (f32[256,512]{1,0:T(8,128)S(1)}, f32[256,512]{1,0:T(8,128)S(1)}, u32[]{:S(2)}, u32[]{:S(2)}) collective-permute-start(f32[256,512]{1,0:T(8,128)S(1)} %slice.451), channel_id=1, source_target_pairs={{2,0},{4,6},{3,1},{5,7},{10,8},{12,14},{11,9},{13,15},{18,16},{20,... | collective-permute-start | bytes 1572872 | tf_op jit(solution)/shard_map/ppermute | solution.py:1016
  898.5 40.4 %collective-permute-start.94 = (f32[128,256]{1,0:T(8,128)S(1)}, f32[128,256]{1,0:T(8,128)S(1)}, u32[]{:S(2)}, u32[]{:S(2)}) collective-permute-start(f32[128,256]{1,0:T(8,128)S(1)} %dynamic-slice_add_fusion.8), channel_id=1, source_target_pairs={{0,1},{1,0},{2,3},{3,2},{4,5},{5,4},{6,7},{7,6},{8,9},{9,8},{10,11... | collective-permute-start | bytes 393224 | tf_op jit(solution)/shard_map/ppermute | solution.py:415
  (177 other events, 2434.4 us)
Sparse Core Ops, SparseCore 0:
  388.7 44.2 reduce-scatter.8
  436.3 35.8 reduce-scatter.16
  475.2 43.9 reduce-scatter.12
  568.3 42.7 reduce-scatter.6
  634.4 37.9 reduce-scatter.14
  711.8 54.9 reduce-scatter.10

commit v4 on v3

--- a/solution.py
+++ b/solution.py
@@ -432,12 +432,11 @@
     return lax.optimization_barrier((value, *marks))[0]
 
 
-def scatter_sum(part, first=(), second=(), third=()):
+def scatter_sum(part, mark=()):
     core, near = lax.axis_index("core"), lax.axis_index("zl")
-    part = behind(part, *first)
-    half = take(part, core, 2) + behind(swap(take(part, 1 - core, 2), "core"), *second)
+    half = take(part, core, 2) + behind(swap(take(part, 1 - core, 2), "core"), *mark)
     if lax.axis_size("zl") == 2:
-        return take(half, near, 2) + behind(swap(take(half, 1 - near, 2), "zl"), *third)
+        return take(half, near, 2) + swap(take(half, 1 - near, 2), "zl")
     return lax.psum_scatter(half, "zl", scatter_dimension=0, tiled=True)
 
 
@@ -482,13 +481,13 @@
             out[...] = there[...].astype(out.dtype)
 
 
-def deliver(value, dtype, first=(), second=(), third=()):
+def cross_over(value):
+    return [lax.ppermute(value, BOTH, pairs) for pairs in (CROSS, DIAGONAL, CORE_IN)]
+
+
+def deliver(value, mine, theirs, near, dtype):
     core, far = lax.axis_index("core"), lax.axis_index("zh")
     held = core == far
-    value = behind(value, *first)
-    mine = lax.ppermute(value, BOTH, CROSS)
-    theirs = lax.ppermute(value, BOTH, DIAGONAL)
-    near = lax.ppermute(value, BOTH, CORE_IN)
     if lax.axis_size("zl") != 2 or value.shape[0] != GROUP:
         mine = gather_near(jnp.where(held, value, mine))
         theirs = gather_near(jnp.where(held, near, theirs))
@@ -499,12 +498,11 @@
     there = [(2 * kind + i, 2 * kind + 1 - i) for kind in (1, 2) for i in range(2)]
     value_s = lax.ppermute(value, axes, here)
     near_s = lax.ppermute(near, axes, here)
-    mine, theirs = behind(mine, *second), behind(theirs, *second)
     mine_s = lax.ppermute(mine, axes, there)
     theirs_s = lax.ppermute(theirs, axes, there)
     place = jnp.stack([own_place(), held.astype(jnp.int32)]).astype(jnp.int32)
     width = value.shape[1]
-    parts = (value, mine, near, theirs, value_s, mine_s, near_s, behind(theirs_s, *third))
+    parts = (value, mine, near, theirs, value_s, mine_s, near_s, theirs_s)
     return pl.pallas_call(
         place_kernel,
         grid=(4,),
@@ -531,24 +529,30 @@
     return jnp.pad(value, [(0, 0)] * (value.ndim - 1) + [(0, LANES - value.shape[-1])])
 
 
-def weight_kernel(place, own, *refs):
-    parts, out = refs[:-1], refs[-1]
+def weight_kernel(count, extra, place, *refs):
+    own, rest = refs[:count], refs[count:]
+    outs, rest = rest[-count:], rest[:-count]
+    parts, more = (rest[:-2], rest[-2:]) if extra else (rest, ())
     block = pl.program_id(0)
-    cols = own.shape[1]
-
-    @pl.when(place[1] == 1)
-    def _():
-        out[:, :cols] = own[...]
-
-    for away in range(len(parts) if out.shape[1] == cols else len(parts) - 2):
-
-        @pl.when((place[1] == 0) & (lax.bitwise_xor(place[0], block) == away))
+    at = 0
+    for source, out in zip(own, outs):
+        cols = source.shape[1]
+
+        @pl.when(place[1] == 1)
         def _():
-            out[:, :cols] = parts[away][...].astype(bf16)
-
-    if out.shape[1] > cols:
-        out[:, cols : cols + BC] = parts[-2][...]
-        out[:, cols + BC :] = parts[-1][...].astype(bf16)
+            out[:, :cols] = source[...]
+
+        for away, part in enumerate(parts):
+
+            @pl.when((place[1] == 0) & (lax.bitwise_xor(place[0], block) == away))
+            def _():
+                out[:, :cols] = part[:, at : at + cols].astype(bf16)
+
+        at += cols
+    if more:
+        cols = own[0].shape[1]
+        outs[0][:, cols : cols + BC] = more[0][...]
+        outs[0][:, cols + BC :] = more[1][...].astype(bf16)
 
 
 def narrow_kernel(wide, narrow):
@@ -567,13 +571,19 @@
     )(value)
 
 
-def gather_weights(own, more=(), first=(), second=()):
-    width, cols = own.shape
+def gather_weights(own, more=(), first=(), second=(), third=()):
+    width = own[0].shape[0]
     chips = lax.axis_size("chip")
     chip = lax.axis_index("chip")
     held = (lax.axis_index("core") == lax.axis_index("zh")).astype(jnp.int32)
     size = width // chips
-    piece = lax.dynamic_slice_in_dim(behind(own, *first), chip * size, size).astype(f32)
+    piece = jnp.concatenate(
+        [
+            lax.dynamic_slice_in_dim(value, chip * size, size).astype(f32)
+            for value in behind(own, *first)
+        ],
+        axis=1,
+    )
     piece = behind(lax.ppermute(piece, BOTH, CROSS), *second)
     if chips == 4:
         parts = [piece]
@@ -588,24 +598,27 @@
         parts = [lax.all_gather(piece, "chip", tiled=True)]
         place = jnp.stack([0, held]).astype(jnp.int32)
         blocks, size = 1, width
-    all_cols = cols + sum(value.shape[1] for value in more)
+    parts = behind(parts, *third)
+    out_cols = [value.shape[1] for value in own]
+    out_cols[0] += sum(value.shape[1] for value in more)
 
     def rows(cols):
         return pl.BlockSpec((size, cols), lambda c: (c, 0))
 
     return pl.pallas_call(
-        weight_kernel,
+        functools.partial(weight_kernel, len(own), bool(more)),
         grid=(blocks,),
-        in_specs=[pl.BlockSpec(memory_space=pltpu.SMEM), rows(cols)]
-        + [whole((size, cols))] * len(parts)
+        in_specs=[pl.BlockSpec(memory_space=pltpu.SMEM)]
+        + [rows(value.shape[1]) for value in own]
+        + [whole(piece.shape if chips == 4 else parts[0].shape)] * len(parts)
         + [rows(value.shape[1]) for value in more],
-        out_specs=rows(all_cols),
-        out_shape=shape(width, all_cols, dtype=bf16),
+        out_specs=[rows(cols) for cols in out_cols],
+        out_shape=[shape(width, cols, dtype=bf16) for cols in out_cols],
         compiler_params=pltpu.CompilerParams(
             dimension_semantics=("arbitrary",), vmem_limit_bytes=40 * 1024 * 1024
         ),
         name="weights",
-    )(place, own, *parts, *more)
+    )(place, *own, *parts, *more)
 
 
 def shards(
@@ -639,8 +652,9 @@
     dt_own = w_dt.astype(f32).reshape(LAYERS, width * heads // LANES, LANES)
     dt_sent = lax.ppermute(dt_own, BOTH, CROSS)
     dt_all = pad_lanes(jnp.where(held, dt_own, dt_sent).reshape(LAYERS, width, heads))
-    wall = gather_weights(w_x[0], (w_bc[0], dt_all[0]))
+    (wall,) = gather_weights([w_x[0]], (w_bc[0], dt_all[0]))
     hidden = to_block(x_input.astype(f32))
+    cotangent = to_block(behind(cotangent.astype(f32), hidden))
     seg = to_block(seg_ids.astype(f32))
     small = jnp.concatenate(
         [
@@ -745,12 +759,9 @@
             "in_proj_conv",
         )
         if layer == 0:
-            wz = gather_weights(w_z[0], first=(wall,))
-            wout = gather_weights(w_out[0], first=(wall,))
-            cotangent = to_block(behind(cotangent.astype(f32), wall))
-            next_wall = gather_weights(w_x[1], (w_bc[1], dt_all[1]), (send,))
-            next_wz = gather_weights(w_z[1], first=(send,))
-            next_wout = gather_weights(w_out[1], first=(send,))
+            wz, wout = gather_weights(
+                [w_z[0], w_out[0]], first=(hidden[0],), second=(wall,), third=(send,)
+            )
         else:
             wz, wout = next_wz, next_wout
         zval = mm(normed, wz)
@@ -810,6 +821,13 @@
             )
         )
         if layer < LAYERS - 1:
+            next_wall, next_wz, next_wout = gather_weights(
+                [w_x[1], w_z[1], w_out[1]],
+                (w_bc[1], dt_all[1]),
+                first=(yin,),
+                second=(proj,),
+                third=(gate_scale,),
+            )
             proj_sum = scatter_sum(proj)
             stored[layer]["proj_sum"] = proj_sum
             hidden_own = hidden_own + own_rows(gate_scale)[:, None] * proj_sum
@@ -880,6 +898,13 @@
             "ssd_within_back",
         )
         gout = chain(gsend, True)
+        if layer == LAYERS - 1:
+            last_sum = scatter_sum(kept["proj"], (dy,))
+            hidden_own = hidden_own + own_rows(gate_scale)[:, None] * last_sum
+            u = behind(u, hidden_own)
+        else:
+            out_parts = cross_over(behind(hidden_own, gout))
+            first_sums = join_halves(behind(matrices[LAYERS - 1], dy))
         grad_wout = mm(gproj, kept["gate_in"], ((0,), (0,)))
         grad_wz = mm(kept["normed"], dz, ((0,), (0,)))
         partial_z = mm(dz, kept["wz"], ((1,), (1,)))
@@ -926,11 +951,15 @@
             "in_proj_conv_back",
         )
         rim_back = shifted(rim, -1)
+        if layer == 0:
+            last8 = behind(last8, first_sums)
         gall = lax.dynamic_update_slice(
             gall, (last8 + rim_back).astype(bf16), (tok - ROWS, 0)
         )
         partial = partial_z + mm(gall, kept["wall"], ((1,), (1,)))
         grad_normed = scatter_sum(partial)
+        if layer == 0:
+            grad_normed = behind(grad_normed, *out_parts)
         late = behind(gall, partial)
         grad_win = mm(kept["normed"], late[:, : inner + BC], ((0,), (0,)))
         grad_wdt = mm(kept["normed"], late[:, inner + BC :], ((0,), (0,)))
@@ -947,22 +976,6 @@
             lax.psum_scatter(value, "chip", scatter_dimension=0, tiled=True)
             for value in (grad_wout, grad_wz, grad_win)
         ]
-        if layer == LAYERS - 1:
-            last_sum = scatter_sum(kept["proj"], (dy,), (u,), (gall,))
-            hidden_own = hidden_own + own_rows(gate_scale)[:, None] * last_sum
-        else:
-            marks = ((dy,), (u,), (partial,))
-            final_out = deliver(hidden_own, bf16, *marks)
-            input_grad = deliver(grad_own, f32)
-            matrices[1] = [behind(value, u) for value in matrices[1]]
-            matrices[0] = [behind(value, grad_own) for value in matrices[0]]
-            for number, (g_out, g_z, g_in) in enumerate(matrices):
-                matrices[number] = (
-                    place_rows(g_out),
-                    place_rows(g_z),
-                    place_rows(g_in[:, :inner]),
-                    shared_rows(g_in[:, inner:]),
-                )
         vectors[layer] = jnp.concatenate(
             [
                 gtaps[: CONV + 1, :inner].reshape(-1),
@@ -975,7 +988,17 @@
                 grad_ngain,
             ]
         )
-    vector = total(jnp.stack(vectors), ("zh", "chip"))
+    grad_parts = cross_over(grad_own)
+    near = grad_parts[2]
+    early = join_halves(behind(matrices[0][:2], near))
+    vector = total(behind(jnp.stack(vectors), near), ("zh", "chip"))
+    final_out = deliver(hidden_own, *out_parts, bf16)
+    input_grad = deliver(grad_own, *grad_parts, f32)
+    late = join_halves(matrices[0][2:])
+    g_cols = [place_rows(early, late), place_rows(first_sums)]
+    grad_wbc = shared_rows(
+        jnp.stack([matrices[layer][2][:, inner:] for layer in range(LAYERS)], axis=1)
+    )
     other = swap(vector, "core")
     common = (CONV + 1) * BC + width
     by_head = jnp.where(held, vector, other)[:, :-common]
@@ -995,9 +1018,9 @@
         final_out,
         input_grad,
         g_ngain,
-        jnp.stack([m[1] for m in matrices]),
-        jnp.stack([m[2] for m in matrices]),
-        jnp.stack([m[3] for m in matrices]),
+        jnp.stack([g[:, inner : 2 * inner] for g in g_cols]),
+        jnp.stack([g[:, 2 * inner :] for g in g_cols]),
+        jnp.stack([grad_wbc[:, layer] for layer in range(LAYERS)]),
         g_wdt,
         g_conv.reshape(LAYERS, CONV, inner),
         g_bc[:, :CONV],
@@ -1007,15 +1030,25 @@
         g_alog,
         jnp.sum(g_dsk.reshape(LAYERS, heads, HEADDIM), axis=2),
         g_ggain,
-        jnp.stack([m[0] for m in matrices]),
+        jnp.stack([g[:, :inner] for g in g_cols]),
     )
 
 
-def place_rows(part):
+def join_halves(parts):
+    inner = parts[0].shape[1]
+    part = jnp.concatenate([value[:, :inner] for value in parts], axis=1)
+    if len(parts) == 1:
+        part = part[:, : inner - BC]
+    return part + lax.ppermute(part, BOTH, CROSS_BACK)
+
+
+def place_rows(*parts):
     core, far = lax.axis_index("core"), lax.axis_index("zh")
-    full = part + lax.ppermute(part, BOTH, CROSS_BACK)
-    sent = lax.ppermute(take(full, 1 - core, 2), BOTH, CORE_OUT)
-    return jnp.where(core == far, take(full, core, 2), sent)
+    sent = [lax.ppermute(take(full, 1 - core, 2), BOTH, CORE_OUT) for full in parts]
+    rows = [
+        jnp.where(core == far, take(full, core, 2), got) for full, got in zip(parts, sent)
+    ]
+    return jnp.concatenate(rows, axis=1)
 
 
 def shared_rows(part):

time: 967 us -> 932 us (0.964)
  waiting for transfers between devices: 331 us -> 307 us
  starting transfers between devices: 241 us -> 220 us
    ppermute x18 -> x12, waiting for transfers between devices: 64.1 us -> 20.5 us  [the longest x3 19.4 us: join_halves(): return part + lax.ppermute(part, BOTH, CROSS_BACK)]
    ppermute x6 -> x3, starting transfers between devices: 46.3 us -> 4.82 us  [gather_weights(): piece = behind(lax.ppermute(piece, BOTH, CROSS), *second)]
    ppermute x19 -> x18, starting transfers between devices: 25.2 us -> 51.8 us  [swap(): return lax.ppermute(value, axis, SWAP)]
    ppermute x12 -> x10, waiting for transfers between devices: 50.2 us -> 76.6 us  [total(): lax.ppermute(value, axis, [(i, i ^ step) for i in range(count)])]
    ppermute x6 -> x3, waiting for transfers between devices: 0.02 us -> 24.9 us  [gather_weights(): piece = behind(lax.ppermute(piece, BOTH, CROSS), *second)]
    ppermute x5, starting transfers between devices: 7.69 us -> 30.5 us  [shifted(): lax.ppermute(value, BLOCKS, [(source, source + steps) for source in range...]
    ppermute x2, waiting for transfers between devices: 22.2 us -> 0.01 us  [deliver(): near_s = lax.ppermute(near, axes, here)]
    ppermute x2, waiting for transfers between devices: 20 us -> 0.01 us  [deliver(): value_s = lax.ppermute(value, axes, here)]
  transfers between devices with their start and end apart: 109 -> 88, of which waited for: 37 -> 34; matrix products, arithmetic and copies ran while one was open for 16% -> 19% of each run, Pallas kernels for 14% -> 12%
where the time goes in v4:
time: 932 us; the launch traced here: 921 us
  waiting for transfers between devices  307 us (33%)
  starting transfers between devices  220 us (24%)
  Pallas kernels  163 us (17%)
  local copies, waits for them, and re-layouts  91.3 us (10%)
  other arithmetic  77.7 us (8%)
  matrix products  44.8 us (5%)
  between operations  16.4 us (2%)
    pallas_call x12, Pallas kernels, call(): pl.pallas_call(kernel, grid=(count,), in_specs=[spec for spec, _ in ins],...  146 us
    ppermute x18, waiting for transfers between devices, swap(): return lax.ppermute(value, axis, SWAP)  90.5 us
    ppermute x12, waiting for transfers between devices, chain(): got = lax.ppermute(part, BLOCKS, [(i, i ^ step) for i in range(count)])  83.6 us
    ppermute x10, waiting for transfers between devices, total(): lax.ppermute(value, axis, [(i, i ^ step) for i in range(count)])  76.6 us
    ppermute x18, starting transfers between devices, swap(): return lax.ppermute(value, axis, SWAP)  51.8 us
    dot_general x14, matrix products, mm(): lax.dot_general(left, right, (dims, ((), ())), preferred_element_type=f32...  39.2 us
    ppermute x6, starting transfers between devices, cross_over(): lax.ppermute(value, BOTH, pairs)  32.5 us
    ppermute x5, starting transfers between devices, shifted(): lax.ppermute(value, BLOCKS, [(source, source + steps) for source in range...  30.5 us
  transfers between devices with their start and end apart: 88, of which 34 were waited for; matrix products, arithmetic and copies ran while one was open for 19% of the time, Pallas kernels for 12%

profile of v4, /device:TPU:0, one launch (start us, length us, event | category | flops | bytes accessed | tf_op | source)
XLA Modules:
  0.0 921.1 jit_solution(871736379611933309)
XLA Ops:
  60.5 18.3 %collective-permute-start.9 = (f32[8,768]{1,0:T(8,128)S(1)}, f32[8,768]{1,0:T(8,128)S(1)}, u32[]{:S(2)}, u32[]{:S(2)}) collective-permute-start(f32[8,768]{1,0:T(8,128)S(1)} %fusion), channel_id=1, source_target_pairs={{0,2},{2,8},{8,10},{10,16},{16,18},{18,24},{24,26},{1,3},{3,9},{9,... | collective-permute-start | bytes 73736 | tf_op jit(solution)/shard_map/ppermute | solution.py:384
  82.1 15.6 %in_proj_conv.2 = (bf16[1024,1024]{1,0:T(8,128)(2,1)}, f32[1024,768]{1,0:T(8,128)}, f32[1024,768]{1,0:T(8,128)}, f32[1024,128]{1,0:T(8,128)}, f32[1024,128]{1,0:...) custom-call(s32[2]{0:T(128)} %pad_add_fusion.place, ...), custom_call_target="tpu_custom_call" | custom-call | flops 1879048192 | bytes 8388608 | tf_op jit(solution)/shard_map/in_proj_conv/pallas_call | solution.py:350
  103.1 19.3 %collective-permute-done.14 = f32[136,512]{1,0:T(8,128)} collective-permute-done((f32[136,512]{1,0:T(8,128)}, f32[136,512]{1,0:T(8,128)}, u32[]{:S(2)}, u32[]{:S(2)}) %collective-permute-start.14) | collective-permute-done | bytes 278560 | tf_op jit(solution)/shard_map/ppermute | solution.py:394
  145.7 10.5 %collective-permute-done.16 = f32[136,512]{1,0:T(8,128)S(1)} collective-permute-done((f32[136,512]{1,0:T(8,128)S(1)}, f32[136,512]{1,0:T(8,128)S(1)}, u32[]{:S(2)}, u32[]{:S(2)}) %collective-permute-start.16) | collective-permute-done | bytes 278560 | tf_op jit(solution)/shard_map/ppermute | solution.py:394
  164.5 11.1 %gate_out_proj.2 = (f32[1024,512]{1,0:T(8,128)}, bf16[1024,512]{1,0:T(8,128)(2,1)}, f32[1024,1024]{1,0:T(8,128)}, f32[8,1024]{1,0:T(8,128)}) custom-call(f32[1024,512]{1,0:T(8,128)} %ssd_within.2.yin, f32[1024,768]{1,0:T(8,128)} %get-tuple-element.121.cpre, f32[1024,128]{1,0:T(8,128)} %get-tuple-element.118.cum, bf16[1024,256]{1,0:T(8,128)(2,1)} %get-tuple-element.120.bc, ...), custom_call_target="tpu_custom_call" | custom-call | flops 2147483648 | bytes 8388608 | tf_op jit(solution)/shard_map/gate_out_proj/pallas_call | solution.py:350
  179.0 11.9 %collective-permute-start.19 = (f32[512,1024]{1,0:T(8,128)}, f32[512,1024]{1,0:T(8,128)}, u32[]{:S(2)}, u32[]{:S(2)}) collective-permute-start(f32[512,1024]{1,0:T(8,128)} %constant_dynamic-slice_fusion.15), channel_id=1, source_target_pairs={{0,4},{4,0},{1,5},{5,1},{2,6},{6,2},{3,7},{7,3},{8,12},{12,8},{9,1... | collective-permute-start | bytes 6291464 | tf_op jit(solution)/shard_map/ppermute | solution.py:407
  199.2 24.9 %collective-permute-done.21.refs_3_ = f32[256,1536]{1,0:T(8,128)S(1)} collective-permute-done((f32[256,1536]{1,0:T(8,128)}, f32[256,1536]{1,0:T(8,128)S(1)}, u32[]{:S(2)}, u32[]{:S(2)}) %collective-permute-start.21) | collective-permute-done | bytes 1572896 | tf_op jit(solution)/shard_map/ppermute | solution.py:587
  251.5 22.3 %collective-permute-done.25.refs_1_ = f32[256,1024]{1,0:T(8,128)} collective-permute-done((f32[256,1024]{1,0:T(8,128)}, f32[256,1024]{1,0:T(8,128)}, u32[]{:S(2)}, u32[]{:S(2)}) %collective-permute-start.25) | collective-permute-done | bytes 1048608 | tf_op jit(solution)/shard_map/ppermute | solution.py:407
  288.6 7.9 collective-permute-start.28
  299.6 17.1 %in_proj_conv.3 = (bf16[1024,1024]{1,0:T(8,128)(2,1)}, f32[1024,768]{1,0:T(8,128)}, f32[1024,768]{1,0:T(8,128)}, f32[1024,128]{1,0:T(8,128)}, f32[1024,128]{1,0:...) custom-call(s32[2]{0:T(128)} %pad_add_fusion.place, ...), custom_call_target="tpu_custom_call" | custom-call | flops 1879048192 | bytes 8388608 | tf_op jit(solution)/shard_map/in_proj_conv/pallas_call | solution.py:350
  320.1 11.8 %collective-permute-done.29 = f32[136,512]{1,0:T(8,128)S(1)} collective-permute-done((f32[136,512]{1,0:T(8,128)}, f32[136,512]{1,0:T(8,128)S(1)}, u32[]{:S(2)}, u32[]{:S(2)}) %collective-permute-start.29) | collective-permute-done | bytes 278560 | tf_op jit(solution)/shard_map/ppermute | solution.py:394
  356.9 14.1 %gate_out_proj.3 = (f32[1024,512]{1,0:T(8,128)}, bf16[1024,512]{1,0:T(8,128)(2,1)}, f32[1024,1024]{1,0:T(8,128)}, f32[8,1024]{1,0:T(8,128)}) custom-call(f32[1024,512]{1,0:T(8,128)} %ssd_within.3.yin, f32[1024,768]{1,0:T(8,128)} %get-tuple-element.149.cpre, f32[1024,128]{1,0:T(8,128)} %get-tuple-element.146.cum, bf16[1024,256]{1,0:T(8,128)(2,1)} %get-tuple-element.148.bc, ...), custom_call_target="tpu_custom_call" | custom-call | flops 2147483648 | bytes 8388608 | tf_op jit(solution)/shard_map/gate_out_proj/pallas_call | solution.py:350
  378.9 10.0 %gate_back.2 = (bf16[1024,1024]{1,0:T(8,128)(2,1)}, bf16[1024,512]{1,0:T(8,128)(2,1)}, bf16[1024,512]{1,0:T(8,128)(2,1)}, f32[4,128,512]{2,1,0:T(8,128)}, f32[4,...) custom-call(s32[2]{0:T(128)} %pad_add_fusion.place, f32[1024,1]{1,0:T(8,128)} %copy-done.43, ...), custom_call_target="tpu_custom_call" | custom-call | flops 1073741824 | bytes 8388608 | tf_op jit(solution)/shard_map/gate_back/pallas_call | solution.py:350
  402.1 11.1 %collective-permute-done.37 = f32[136,512]{1,0:T(8,128)S(1)} collective-permute-done((f32[136,512]{1,0:T(8,128)S(1)}, f32[136,512]{1,0:T(8,128)S(1)}, u32[]{:S(2)}, u32[]{:S(2)}) %collective-permute-start.37) | collective-permute-done | bytes 278560 | tf_op jit(solution)/shard_map/ppermute | solution.py:394
  416.8 8.4 collective-permute-done.38
  426.3 7.5 ssd_within_back.2
  443.1 20.6 %in_proj_conv_back.2 = (bf16[1024,896]{1,0:T(8,128)(2,1)}, f32[8,768]{1,0:T(8,128)}, f32[8,768]{1,0:T(8,128)}, f32[8,768]{1,0:T(8,128)}, f32[8,128]{1,0:T(8,128)}, /*index=5*/f32[8,512]{1,0:T(8,128)}) custom-call(f32[1024,512]{1,0:T(8,128)} %get-tuple-element.164.uin, f32[1024,256]{1,0:T(8,128)} %get-tuple-element.165.dbc, ...), custom_call_target="tpu_custom_call" | custom-call | flops 2147483648 | bytes 8388608 | tf_op jit(solution)/shard_map/in_proj_conv_back/pallas_call | solution.py:350
  487.3 24.6 %collective-permute-done.42 = f32[256,1024]{1,0:T(8,128)S(1)} collective-permute-done((f32[256,1024]{1,0:T(8,128)S(1)}, f32[256,1024]{1,0:T(8,128)S(1)}, u32[]{:S(2)}, u32[]{:S(2)}) %collective-permute-start.42) | collective-permute-done | bytes 1048608 | tf_op jit(solution)/shard_map/ppermute | solution.py:407
  516.5 23.7 %collective-permute-done.45.refs_1_ = f32[256,1024]{1,0:T(8,128)} collective-permute-done((f32[256,1024]{1,0:T(8,128)S(1)}, f32[256,1024]{1,0:T(8,128)}, u32[]{:S(2)}, u32[]{:S(2)}) %collective-permute-start.45) | collective-permute-done | bytes 1048608 | tf_op jit(solution)/shard_map/ppermute | solution.py:407
  546.1 11.0 %gate_back.3 = (bf16[1024,1024]{1,0:T(8,128)(2,1)}, bf16[1024,512]{1,0:T(8,128)(2,1)}, bf16[1024,512]{1,0:T(8,128)(2,1)}, f32[4,128,512]{2,1,0:T(8,128)}, f32[4,...) custom-call(s32[2]{0:T(128)} %pad_add_fusion.place, f32[1024,1]{1,0:T(8,128)} %copy-done.42, ...), custom_call_target="tpu_custom_call" | custom-call | flops 1073741824 | bytes 8388608 | tf_op jit(solution)/shard_map/gate_back/pallas_call | solution.py:350
  563.7 14.1 %collective-permute-done.48 = f32[136,512]{1,0:T(8,128)S(1)} collective-permute-done((f32[136,512]{1,0:T(8,128)S(1)}, f32[136,512]{1,0:T(8,128)S(1)}, u32[]{:S(2)}, u32[]{:S(2)}) %collective-permute-start.48) | collective-permute-done | bytes 278560 | tf_op jit(solution)/shard_map/ppermute | solution.py:394
  594.0 7.5 ssd_within_back.3
  603.8 20.3 %in_proj_conv_back.3 = (bf16[1024,896]{1,0:T(8,128)(2,1)}, f32[8,768]{1,0:T(8,128)}, f32[8,768]{1,0:T(8,128)}, f32[8,768]{1,0:T(8,128)}, f32[8,128]{1,0:T(8,128)}, /*index=5*/f32[8,512]{1,0:T(8,128)}) custom-call(f32[1024,512]{1,0:T(8,128)} %get-tuple-element.180.uin, f32[1024,256]{1,0:T(8,128)} %get-tuple-element.181.dbc, ...), custom_call_target="tpu_custom_call" | custom-call | flops 2147483648 | bytes 8388608 | tf_op jit(solution)/shard_map/in_proj_conv_back/pallas_call | solution.py:350
  672.8 23.9 %collective-permute-start.61 = (f32[256,1024]{1,0:T(8,128)}, f32[256,1024]{1,0:T(8,128)}, u32[]{:S(2)}, u32[]{:S(2)}) collective-permute-start(f32[256,1024]{1,0:T(8,128)} %constant_dynamic-slice_fusion.4), channel_id=1, source_target_pairs={{0,1},{1,0},{2,3},{3,2},{4,5},{5,4},{6,7},{7,6},{8,9},{9,8},{10,11... | collective-permute-start | bytes 3145736 | tf_op jit(solution)/shard_map/ppermute | solution.py:407
  709.8 7.9 collective-permute-start.76
  722.4 8.5 collective-permute-done.61
  735.2 21.1 %collective-permute-start.62 = (f32[256,1024]{1,0:T(8,128)S(1)}, f32[256,1024]{1,0:T(8,128)}, u32[]{:S(2)}, u32[]{:S(2)}) collective-permute-start(f32[256,1024]{1,0:T(8,128)S(1)} %multiply_add_fusion.value), channel_id=1, source_target_pairs={{0,2},{6,4},{1,3},{7,5},{8,10},{14,12},{9,11},{15,13},{16,18},{22,... | collective-permute-start | bytes 3145736 | tf_op jit(solution)/shard_map/ppermute | solution.py:485
  758.7 44.5 %collective-permute-done.69 = f32[2,14096]{1,0:T(2,128)S(1)} collective-permute-done((f32[2,14096]{1,0:T(2,128)S(1)}, f32[2,14096]{1,0:T(2,128)S(1)}, u32[]{:S(2)}, u32[]{:S(2)}) %collective-permute-start.69) | collective-permute-done | bytes 112800 | tf_op jit(solution)/shard_map/ppermute | solution.py:415
  825.0 19.4 %collective-permute-done.74 = f32[256,1024]{1,0:T(8,128)S(1)} collective-permute-done((f32[256,1024]{1,0:T(8,128)S(1)}, f32[256,1024]{1,0:T(8,128)S(1)}, u32[]{:S(2)}, u32[]{:S(2)}) %collective-permute-start.74) | collective-permute-done | bytes 1048608 | tf_op jit(solution)/shard_map/ppermute | solution.py:1042
  857.6 11.5 %collective-permute-start.79 = (f32[128,2,256]{2,0,1:T(8,128)}, f32[128,2,256]{2,0,1:T(8,128)}, u32[]{:S(2)}, u32[]{:S(2)}) collective-permute-start(f32[128,2,256]{2,0,1:T(8,128)} %fusion.12), channel_id=1, source_target_pairs={{0,4},{4,0},{1,5},{5,1},{2,6},{6,2},{3,7},{7,3},{8,12},{12,8},{9,1... | collective-permute-start | bytes 786440 | tf_op jit(solution)/shard_map/ppermute | solution.py:407
  886.4 9.3 %collective-permute-done.80 = f32[128,2,256]{2,0,1:T(8,128)S(1)} collective-permute-done((f32[128,2,256]{2,0,1:T(8,128)S(1)}, f32[128,2,256]{2,0,1:T(8,128)S(1)}, u32[]{:S(2)}, u32[]{:S(2)}) %collective-permute-start.80) | collective-permute-done | bytes 262176 | tf_op jit(solution)/shard_map/ppermute | solution.py:415
  901.8 10.3 %collective-permute-done.81 = f32[128,2,256]{2,0,1:T(8,128)S(1)} collective-permute-done((f32[128,2,256]{2,0,1:T(8,128)S(1)}, f32[128,2,256]{2,0,1:T(8,128)S(1)}, u32[]{:S(2)}, u32[]{:S(2)}) %collective-permute-start.81) | collective-permute-done | bytes 262176 | tf_op jit(solution)/shard_map/ppermute | solution.py:415
  (588 shorter events, 404.7 us)
Async XLA Ops:
  7.2 572.9 %reduce-scatter.7.cloned.1.call-start = ((), (), s32[]{:S(2)}) async-start(), calls=%async_computation.6 | async-start | bytes 2621440 | tf_op jit(solution)/shard_map/reduce_scatter | solution.py:976
  8.1 29.8 %collective-permute-start.7 = (f32[1024]{0:T(1024)S(1)}, f32[1024]{0:T(1024)S(1)}, u32[]{:S(2)}, u32[]{:S(2)}) collective-permute-start(f32[1024]{0:T(1024)S(1)} %convert_element_type.76), channel_id=1, source_target_pairs={{0,4},{6,2},{1,5},{7,3},{8,12},{14,10},{9,13},{15,11},{16,20},{22,... | collective-permute-start | bytes 12296 | tf_op jit(solution)/shard_map/ppermute | solution.py:520
  12.0 31.3 %collective-permute-start.6 = (f32[2,3096]{1,0:T(2,128)S(1)}, f32[2,3096]{1,0:T(2,128)S(1)}, u32[]{:S(2)}, u32[]{:S(2)}) collective-permute-start(f32[2,3096]{1,0:T(2,128)S(1)} %concatenate.117), channel_id=1, source_target_pairs={{0,2},{6,4},{1,3},{7,5},{8,10},{14,12},{9,11},{15,13},{16,18},{22,... | collective-permute-start | bytes 74312 | tf_op jit(solution)/shard_map/ppermute | solution.py:666
  27.2 31.1 %collective-permute-start = (f32[1024,1024]{1,0:T(8,128)}, f32[1024,1024]{1,0:T(8,128)}, u32[]{:S(2)}, u32[]{:S(2)}) collective-permute-start(f32[1024,1024]{1,0:T(8,128)} %convert_element_type.74), channel_id=1, source_target_pairs={{0,4},{6,2},{1,5},{7,3},{8,12},{14,10},{9,13},{15,11},{16,20},{22,... | collective-permute-start | bytes 12582920 | tf_op jit(solution)/shard_map/ppermute | solution.py:520
  127.8 30.2 %collective-permute-start.13 = (f32[256,1024]{1,0:T(8,128)S(1)}, f32[256,1024]{1,0:T(8,128)}, u32[]{:S(2)}, u32[]{:S(2)}) collective-permute-start(f32[256,1024]{1,0:T(8,128)S(1)} %collective-permute-done.10.refs_2_), channel_id=1, source_target_pairs={{2,26},{4,28},{10,18},{12,20},{18,10},{20,12},{26,2},{28,4},{3,27}... | collective-permute-start | bytes 3145736 | tf_op jit(solution)/shard_map/ppermute | solution.py:594
  193.3 30.8 %collective-permute-start.21 = (f32[256,1536]{1,0:T(8,128)}, f32[256,1536]{1,0:T(8,128)S(1)}, u32[]{:S(2)}, u32[]{:S(2)}) collective-permute-start(f32[256,1536]{1,0:T(8,128)} %maximum_convert_fusion), channel_id=1, source_target_pairs={{0,2},{6,4},{1,3},{7,5},{8,10},{14,12},{9,11},{15,13},{16,18},{22,... | collective-permute-start | bytes 4718600 | tf_op jit(solution)/shard_map/ppermute | solution.py:587
  198.7 46.9 %collective-permute-start.20 = (f32[256,1024]{1,0:T(8,128)}, f32[256,1024]{1,0:T(8,128)}, u32[]{:S(2)}, u32[]{:S(2)}) collective-permute-start(f32[256,1024]{1,0:T(8,128)} %constant_dynamic-slice_fusion.14), channel_id=1, source_target_pairs={{0,1},{1,0},{2,3},{3,2},{4,5},{5,4},{6,7},{7,6},{8,9},{9,8},{10,11... | collective-permute-start | bytes 3145736 | tf_op jit(solution)/shard_map/ppermute | solution.py:407
  237.6 97.6 %collective-permute-start.32 = (f32[1024,1024]{1,0:T(8,128)}, f32[1024,1024]{1,0:T(8,128)}, u32[]{:S(2)}, u32[]{:S(2)}) collective-permute-start(f32[1024,1024]{1,0:T(8,128)} %convert_element_type.81), channel_id=1, source_target_pairs={{0,4},{6,2},{1,5},{7,3},{8,12},{14,10},{9,13},{15,11},{16,20},{22,... | collective-permute-start | bytes 12582920 | tf_op jit(solution)/shard_map/ppermute | solution.py:520
  241.9 32.6 %collective-permute-start.23 = (f32[256,1536]{1,0:T(8,128)S(1)}, f32[256,1536]{1,0:T(8,128)}, u32[]{:S(2)}, u32[]{:S(2)}) collective-permute-start(f32[256,1536]{1,0:T(8,128)S(1)} %collective-permute-done.21.refs_3_), channel_id=1, source_target_pairs={{2,18},{4,20},{10,26},{12,28},{18,2},{20,4},{26,10},{28,12},{3,19}... | collective-permute-start | bytes 4718600 | tf_op jit(solution)/shard_map/ppermute | solution.py:594
  243.7 30.8 %collective-permute-start.22 = (f32[256,1536]{1,0:T(8,128)S(1)}, f32[256,1536]{1,0:T(8,128)}, u32[]{:S(2)}, u32[]{:S(2)}) collective-permute-start(f32[256,1536]{1,0:T(8,128)S(1)} %collective-permute-done.21.refs_3_), channel_id=1, source_target_pairs={{2,10},{4,12},{10,2},{12,4},{18,26},{20,28},{26,18},{28,20},{3,11}... | collective-permute-start | bytes 4718600 | tf_op jit(solution)/shard_map/ppermute | solution.py:594
  250.6 35.8 %collective-permute-start.26 = (f32[256,1024]{1,0:T(8,128)}, f32[256,1024]{1,0:T(8,128)}, u32[]{:S(2)}, u32[]{:S(2)}) collective-permute-start(f32[256,1024]{1,0:T(8,128)} %get-tuple-element.272.refs_0_), channel_id=1, source_target_pairs={{0,4},{4,0},{1,5},{5,1},{2,6},{6,2},{3,7},{7,3},{8,12},{12,8},{9,1... | collective-permute-start | bytes 3145736 | tf_op jit(solution)/shard_map/ppermute | solution.py:407
  393.2 186.9 %reduce-scatter.9.cloned.1.call-start = ((), (), s32[]{:S(2)}) async-start(), calls=%async_computation.7 | async-start | bytes 2621440 | tf_op jit(solution)/shard_map/reduce_scatter | solution.py:976
  402.0 178.1 %reduce-scatter.11.cloned.1.call-start = ((), (), s32[]{:S(2)}) async-start(), calls=%async_computation.8 | async-start | bytes 3932160 | tf_op jit(solution)/shard_map/reduce_scatter | solution.py:976
  485.0 323.7 %reduce-scatter.13.cloned.1.call-start = ((), (), s32[]{:S(2)}) async-start(), calls=%async_computation.9 | async-start | bytes 2621440 | tf_op jit(solution)/shard_map/reduce_scatter | solution.py:976
  561.3 247.4 %reduce-scatter.15.cloned.1.call-start = ((), (), s32[]{:S(2)}) async-start(), calls=%async_computation.10 | async-start | bytes 2621440 | tf_op jit(solution)/shard_map/reduce_scatter | solution.py:976
  582.7 42.9 %collective-permute-start.58 = (f32[256,1536]{1,0:T(8,128)S(1)}, f32[256,1536]{1,0:T(8,128)}, u32[]{:S(2)}, u32[]{:S(2)}) collective-permute-start(f32[256,1536]{1,0:T(8,128)S(1)} %pad_maximum_fusion), channel_id=1, source_target_pairs={{2,0},{4,6},{3,1},{5,7},{10,8},{12,14},{11,9},{13,15},{18,16},{20,... | collective-permute-start | bytes 4718600 | tf_op jit(solution)/shard_map/ppermute | solution.py:1042
  593.8 257.1 %reduce-scatter.17.cloned.1.call-start = ((), (), s32[]{:S(2)}) async-start(), calls=%async_computation.11 | async-start | bytes 3932160 | tf_op jit(solution)/shard_map/reduce_scatter | solution.py:976
  637.7 30.1 %collective-permute-start.60 = (f32[512,1024]{1,0:T(8,128)}, f32[512,1024]{1,0:T(8,128)}, u32[]{:S(2)}, u32[]{:S(2)}) collective-permute-start(f32[512,1024]{1,0:T(8,128)} %constant_dynamic-slice_fusion.5), channel_id=1, source_target_pairs={{0,4},{4,0},{1,5},{5,1},{2,6},{6,2},{3,7},{7,3},{8,12},{12,8},{9,1... | collective-permute-start | bytes 6291464 | tf_op jit(solution)/shard_map/ppermute | solution.py:407
  648.0 61.9 %collective-permute-start.54 = (f32[256,1024]{1,0:T(8,128)S(1)}, f32[256,1024]{1,0:T(8,128)}, u32[]{:S(2)}, u32[]{:S(2)}) collective-permute-start(f32[256,1024]{1,0:T(8,128)S(1)} %multiply_add_fusion.2.value), channel_id=1, source_target_pairs={{0,1},{1,0},{6,7},{7,6},{8,9},{9,8},{14,15},{15,14},{16,17},{17,16... | collective-permute-start | bytes 3145736 | tf_op jit(solution)/shard_map/ppermute | solution.py:499
  660.9 56.8 %collective-permute-start.57 = (f32[256,1024]{1,0:T(8,128)S(1)}, f32[256,1024]{1,0:T(8,128)}, u32[]{:S(2)}, u32[]{:S(2)}) collective-permute-start(f32[256,1024]{1,0:T(8,128)S(1)} %collective-permute-done.53.theirs), channel_id=1, source_target_pairs={{2,3},{3,2},{4,5},{5,4},{10,11},{11,10},{12,13},{13,12},{18,19},{1... | collective-permute-start | bytes 3145736 | tf_op jit(solution)/shard_map/ppermute | solution.py:502
  662.6 55.1 %collective-permute-start.56 = (f32[256,1024]{1,0:T(8,128)S(1)}, f32[256,1024]{1,0:T(8,128)}, u32[]{:S(2)}, u32[]{:S(2)}) collective-permute-start(f32[256,1024]{1,0:T(8,128)S(1)} %collective-permute-done.52.near), channel_id=1, source_target_pairs={{0,1},{1,0},{6,7},{7,6},{8,9},{9,8},{14,15},{15,14},{16,17},{17,16... | collective-permute-start | bytes 3145736 | tf_op jit(solution)/shard_map/ppermute | solution.py:500
  665.9 51.9 %collective-permute-start.55 = (f32[256,1024]{1,0:T(8,128)}, f32[256,1024]{1,0:T(8,128)}, u32[]{:S(2)}, u32[]{:S(2)}) collective-permute-start(f32[256,1024]{1,0:T(8,128)} %collective-permute-done.51.mine), channel_id=1, source_target_pairs={{2,3},{3,2},{4,5},{5,4},{10,11},{11,10},{12,13},{13,12},{18,19},{1... | collective-permute-start | bytes 3145736 | tf_op jit(solution)/shard_map/ppermute | solution.py:501
  672.8 58.1 %collective-permute-start.61 = (f32[256,1024]{1,0:T(8,128)}, f32[256,1024]{1,0:T(8,128)}, u32[]{:S(2)}, u32[]{:S(2)}) collective-permute-start(f32[256,1024]{1,0:T(8,128)} %constant_dynamic-slice_fusion.4), channel_id=1, source_target_pairs={{0,1},{1,0},{2,3},{3,2},{4,5},{5,4},{6,7},{7,6},{8,9},{9,8},{10,11... | collective-permute-start | bytes 3145736 | tf_op jit(solution)/shard_map/ppermute | solution.py:407
  709.8 47.6 %collective-permute-start.76 = (f32[128,1536]{1,0:T(8,128)}, f32[128,1536]{1,0:T(8,128)}, u32[]{:S(2)}, u32[]{:S(2)}) collective-permute-start(f32[128,1536]{1,0:T(8,128)} %constant_dynamic-slice_fusion.2), channel_id=1, source_target_pairs={{0,4},{6,2},{1,5},{7,3},{8,12},{14,10},{9,13},{15,11},{16,20},{22,... | collective-permute-start | bytes 2359304 | tf_op jit(solution)/shard_map/ppermute | solution.py:1047
  733.2 84.5 %collective-permute-start.64 = (f32[256,1024]{1,0:T(8,128)S(1)}, f32[256,1024]{1,0:T(8,128)S(1)}, u32[]{:S(2)}, u32[]{:S(2)}) collective-permute-start(f32[256,1024]{1,0:T(8,128)S(1)} %multiply_add_fusion.value), channel_id=1, source_target_pairs={{4,2},{2,4},{5,3},{3,5},{12,10},{10,12},{13,11},{11,13},{20,18},{1... | collective-permute-start | bytes 3145736 | tf_op jit(solution)/shard_map/ppermute | solution.py:485
  735.2 85.8 %collective-permute-start.62 = (f32[256,1024]{1,0:T(8,128)S(1)}, f32[256,1024]{1,0:T(8,128)}, u32[]{:S(2)}, u32[]{:S(2)}) collective-permute-start(f32[256,1024]{1,0:T(8,128)S(1)} %multiply_add_fusion.value), channel_id=1, source_target_pairs={{0,2},{6,4},{1,3},{7,5},{8,10},{14,12},{9,11},{15,13},{16,18},{22,... | collective-permute-start | bytes 3145736 | tf_op jit(solution)/shard_map/ppermute | solution.py:485
  757.3 45.8 %collective-permute-start.69 = (f32[2,14096]{1,0:T(2,128)S(1)}, f32[2,14096]{1,0:T(2,128)S(1)}, u32[]{:S(2)}, u32[]{:S(2)}) collective-permute-start(f32[2,14096]{1,0:T(2,128)S(1)} %pad_maximum_fusion.13), channel_id=1, source_target_pairs={{0,2},{2,0},{1,3},{3,1},{4,6},{6,4},{5,7},{7,5},{8,10},{10,8},{9,1... | collective-permute-start | bytes 338312 | tf_op jit(solution)/shard_map/ppermute | solution.py:415
  806.7 45.1 %collective-permute-start.65 = (f32[256,1024]{1,0:T(8,128)S(1)}, f32[256,1024]{1,0:T(8,128)}, u32[]{:S(2)}, u32[]{:S(2)}) collective-permute-start(f32[256,1024]{1,0:T(8,128)S(1)} %multiply_add_fusion.value), channel_id=1, source_target_pairs={{0,1},{1,0},{6,7},{7,6},{8,9},{9,8},{14,15},{15,14},{16,17},{17,16... | collective-permute-start | bytes 3145736 | tf_op jit(solution)/shard_map/ppermute | solution.py:499
  817.7 59.0 %collective-permute-start.67 = (f32[256,1024]{1,0:T(8,128)S(1)}, f32[256,1024]{1,0:T(8,128)}, u32[]{:S(2)}, u32[]{:S(2)}) collective-permute-start(f32[256,1024]{1,0:T(8,128)S(1)} %collective-permute-done.63.near), channel_id=1, source_target_pairs={{0,1},{1,0},{6,7},{7,6},{8,9},{9,8},{14,15},{15,14},{16,17},{17,16... | collective-permute-start | bytes 3145736 | tf_op jit(solution)/shard_map/ppermute | solution.py:500
  821.0 55.7 %collective-permute-start.68 = (f32[256,1024]{1,0:T(8,128)S(1)}, f32[256,1024]{1,0:T(8,128)}, u32[]{:S(2)}, u32[]{:S(2)}) collective-permute-start(f32[256,1024]{1,0:T(8,128)S(1)} %collective-permute-done.64.theirs), channel_id=1, source_target_pairs={{2,3},{3,2},{4,5},{5,4},{10,11},{11,10},{12,13},{13,12},{18,19},{1... | collective-permute-start | bytes 3145736 | tf_op jit(solution)/shard_map/ppermute | solution.py:502
  822.6 54.1 %collective-permute-start.66 = (f32[256,1024]{1,0:T(8,128)}, f32[256,1024]{1,0:T(8,128)}, u32[]{:S(2)}, u32[]{:S(2)}) collective-permute-start(f32[256,1024]{1,0:T(8,128)} %collective-permute-done.62.mine), channel_id=1, source_target_pairs={{2,3},{3,2},{4,5},{5,4},{10,11},{11,10},{12,13},{13,12},{18,19},{1... | collective-permute-start | bytes 3145736 | tf_op jit(solution)/shard_map/ppermute | solution.py:501
  846.4 35.5 %collective-permute-start.75 = (f32[128,1024]{1,0:T(8,128)}, f32[128,1024]{1,0:T(8,128)}, u32[]{:S(2)}, u32[]{:S(2)}) collective-permute-start(f32[128,1024]{1,0:T(8,128)} %constant_dynamic-slice_fusion.3), channel_id=1, source_target_pairs={{0,4},{6,2},{1,5},{7,3},{8,12},{14,10},{9,13},{15,11},{16,20},{22,... | collective-permute-start | bytes 1572872 | tf_op jit(solution)/shard_map/ppermute | solution.py:1047
  (142 other events, 1860.7 us)
Sparse Core Ops, SparseCore 0:
  393.3 35.3 reduce-scatter.6
  432.0 36.5 reduce-scatter.8
  485.1 43.0 reduce-scatter.10
  561.4 39.2 reduce-scatter.12
  603.8 36.3 reduce-scatter.14
  707.8 50.6 reduce-scatter.16

commit v5 on v4

--- a/solution.py
+++ b/solution.py
@@ -346,7 +346,7 @@
     return pl.BlockSpec((ROWS, GROUP), lambda c: (0, c))
 
 
-def call(kernel, count, ins, outs, scratch, flops, name):
+def call(kernel, count, ins, outs, scratch, micros, name):
     return pl.pallas_call(
         kernel,
         grid=(count,),
@@ -358,7 +358,7 @@
             dimension_semantics=("arbitrary",), vmem_limit_bytes=56 * 1024 * 1024
         ),
         cost_estimate=pl.CostEstimate(
-            flops=flops, bytes_accessed=8 * 1024 * 1024, transcendentals=0
+            flops=micros * 1_150_000_000, bytes_accessed=1024 * 1024, transcendentals=0
         ),
         name=name,
     )(*[value for _, value in ins])
@@ -571,20 +571,21 @@
     )(value)
 
 
-def gather_weights(own, more=(), first=(), second=(), third=()):
+def weights_over(own, *marks):
+    chips = lax.axis_size("chip")
+    piece = jnp.concatenate(
+        [take(value, lax.axis_index("chip"), chips).astype(f32) for value in behind(own, *marks)],
+        axis=1,
+    )
+    return lax.ppermute(piece, BOTH, CROSS)
+
+
+def gather_weights(piece, own, more=(), third=()):
     width = own[0].shape[0]
     chips = lax.axis_size("chip")
     chip = lax.axis_index("chip")
     held = (lax.axis_index("core") == lax.axis_index("zh")).astype(jnp.int32)
     size = width // chips
-    piece = jnp.concatenate(
-        [
-            lax.dynamic_slice_in_dim(value, chip * size, size).astype(f32)
-            for value in behind(own, *first)
-        ],
-        axis=1,
-    )
-    piece = behind(lax.ppermute(piece, BOTH, CROSS), *second)
     if chips == 4:
         parts = [piece]
         for away in range(1, chips):
@@ -652,9 +653,13 @@
     dt_own = w_dt.astype(f32).reshape(LAYERS, width * heads // LANES, LANES)
     dt_sent = lax.ppermute(dt_own, BOTH, CROSS)
     dt_all = pad_lanes(jnp.where(held, dt_own, dt_sent).reshape(LAYERS, width, heads))
-    (wall,) = gather_weights([w_x[0]], (w_bc[0], dt_all[0]))
     hidden = to_block(x_input.astype(f32))
+    first_x = weights_over([w_x[0]])
+    first_rest = weights_over([w_z[0], w_out[0]], dt_sent)
+    second_all = weights_over([w_x[1], w_z[1], w_out[1]], hidden)
+    (wall,) = gather_weights(first_x, [w_x[0]], (w_bc[0], dt_all[0]))
     cotangent = to_block(behind(cotangent.astype(f32), hidden))
+    hidden = behind(hidden, first_rest, cotangent)
     seg = to_block(seg_ids.astype(f32))
     small = jnp.concatenate(
         [
@@ -672,6 +677,7 @@
     conv_x, bias_x, dt_bias, a_log, d_skip, gate_gain = pieces
     conv_x = conv_x.reshape(LAYERS, CONV, inner)
     hidden_own = own_rows(hidden)
+    hidden_block = hidden
     hidden = [hidden]
     place = jnp.stack([own_place(), own_place()]).astype(jnp.int32)
     smem = pl.BlockSpec(memory_space=pltpu.SMEM)
@@ -700,7 +706,6 @@
     tri = (position[:, None] >= position[None, :]).astype(f32)
     triback = (position[:, None] <= position[None, :]).astype(f32)
 
-    matmul_flops = 2 * tok * width
     stored = []
     for layer in range(LAYERS):
         if layer > 0:
@@ -755,13 +760,14 @@
                 pltpu.VMEM((ROWS, inner), f32),
                 pltpu.VMEM((ROWS, conv_cols), f32),
             ],
-            matmul_flops * all_cols,
+            16,
             "in_proj_conv",
         )
         if layer == 0:
             wz, wout = gather_weights(
-                [w_z[0], w_out[0]], first=(hidden[0],), second=(wall,), third=(send,)
+                behind(first_rest, wall), [w_z[0], w_out[0]], third=(send,)
             )
+            send = behind(send, second_all)
         else:
             wz, wout = next_wz, next_wout
         zval = mm(normed, wz)
@@ -777,7 +783,7 @@
             ],
             [(by_rows(inner, count), shape(tok, inner))],
             [],
-            matmul_flops * 512,
+            6,
             "ssd_within",
         )
         entry = chain(send, False)
@@ -807,7 +813,7 @@
                 (by_cols(count), shape(ROWS, tok)),
             ],
             [],
-            matmul_flops * 2 * inner,
+            12,
             "gate_out_proj",
         )
         sums = total(sums, ("core", "zl"))
@@ -822,10 +828,9 @@
         )
         if layer < LAYERS - 1:
             next_wall, next_wz, next_wout = gather_weights(
+                behind(second_all, entry),
                 [w_x[1], w_z[1], w_out[1]],
                 (w_bc[1], dt_all[1]),
-                first=(yin,),
-                second=(proj,),
                 third=(gate_scale,),
             )
             proj_sum = scatter_sum(proj)
@@ -875,9 +880,12 @@
                 (whole((ROWS, inner)), shape(ROWS, inner)),
             ],
             [pltpu.VMEM((STATE, inner), f32), pltpu.VMEM((ROWS, inner), f32)],
-            matmul_flops * inner,
+            10,
             "gate_back",
         )
+        if layer == 0:
+            out_parts = cross_over(behind(hidden_own, *grad_h))
+            dy = behind(dy, *out_parts)
         u, dbc = call(
             intra_back_kernel,
             count,
@@ -894,7 +902,7 @@
                 (by_rows(BC, count), shape(tok, BC)),
             ],
             [],
-            matmul_flops * 1024,
+            8,
             "ssd_within_back",
         )
         gout = chain(gsend, True)
@@ -903,8 +911,7 @@
             hidden_own = hidden_own + own_rows(gate_scale)[:, None] * last_sum
             u = behind(u, hidden_own)
         else:
-            out_parts = cross_over(behind(hidden_own, gout))
-            first_sums = join_halves(behind(matrices[LAYERS - 1], dy))
+            first_sums = join_halves(behind(matrices[LAYERS - 1], u))
         grad_wout = mm(gproj, kept["gate_in"], ((0,), (0,)))
         grad_wz = mm(kept["normed"], dz, ((0,), (0,)))
         partial_z = mm(dz, kept["wz"], ((1,), (1,)))
@@ -947,7 +954,7 @@
                 (whole((ROWS, inner)), shape(ROWS, inner)),
             ],
             [pltpu.VMEM((CONV - 1, ROWS, conv_cols), f32)],
-            matmul_flops * 1024,
+            20,
             "in_proj_conv_back",
         )
         rim_back = shifted(rim, -1)
@@ -958,14 +965,20 @@
         )
         partial = partial_z + mm(gall, kept["wall"], ((1,), (1,)))
         grad_normed = scatter_sum(partial)
-        if layer == 0:
-            grad_normed = behind(grad_normed, *out_parts)
         late = behind(gall, partial)
         grad_win = mm(kept["normed"], late[:, : inner + BC], ((0,), (0,)))
         grad_wdt = mm(kept["normed"], late[:, inner + BC :], ((0,), (0,)))
         hidden_in = kept["hidden"]
         inv = lax.rsqrt(jnp.mean(hidden_in * hidden_in, axis=1, keepdims=True) + epsilon)
-        grad_ngain = jnp.sum(grad_normed * hidden_in * inv, axis=0)
+        if layer == 0:
+            full = hidden_block
+            grad_ngain = jnp.sum(
+                partial
+                * (full * lax.rsqrt(jnp.mean(full * full, axis=1, keepdims=True) + epsilon)),
+                axis=0,
+            )
+        else:
+            grad_ngain = jnp.sum(grad_normed * hidden_in * inv, axis=0)
         back = grad_normed * norm_gain[layer][None, :]
         grad_own = grad_own + inv * (
             back - hidden_in * inv * inv * jnp.mean(back * hidden_in, axis=1, keepdims=True)
@@ -988,12 +1001,12 @@
                 grad_ngain,
             ]
         )
+    vector = total(jnp.stack(vectors), ("chip", "zh"))
     grad_parts = cross_over(grad_own)
     near = grad_parts[2]
+    input_grad = deliver(grad_own, *grad_parts, f32)
+    final_out = deliver(hidden_own, *out_parts, bf16)
     early = join_halves(behind(matrices[0][:2], near))
-    vector = total(behind(jnp.stack(vectors), near), ("zh", "chip"))
-    final_out = deliver(hidden_own, *out_parts, bf16)
-    input_grad = deliver(grad_own, *grad_parts, f32)
     late = join_halves(matrices[0][2:])
     g_cols = [place_rows(early, late), place_rows(first_sums)]
     grad_wbc = shared_rows(

time: 932 us -> 904 us (0.970)
  waiting for transfers between devices: 307 us -> 275 us
    ppermute x10, waiting for transfers between devices: 76.6 us -> 31.8 us  [total(): lax.ppermute(value, axis, [(i, i ^ step) for i in range(count)])]
    ppermute x3, waiting for transfers between devices: 19.4 us -> 52.6 us  [join_halves(): return part + lax.ppermute(part, BOTH, CROSS_BACK)]
    ppermute x3, waiting for transfers between devices: 24.9 us -> 0.01 us  [weights_over(): return lax.ppermute(piece, BOTH, CROSS)]
    ppermute x2, starting transfers between devices: 5.51 us -> 28.4 us  [deliver(): near_s = lax.ppermute(near, axes, here)]
    ppermute x12, waiting for transfers between devices: 83.6 us -> 62.8 us  [chain(): got = lax.ppermute(part, BLOCKS, [(i, i ^ step) for i in range(count)])]
    ppermute x10, starting transfers between devices: 15.8 us -> 33 us  [total(): lax.ppermute(value, axis, [(i, i ^ step) for i in range(count)])]
    ppermute x6, starting transfers between devices: 32.5 us -> 16.5 us  [cross_over(): lax.ppermute(value, BOTH, pairs)]
    ppermute x3, starting transfers between devices: 4.82 us -> 20 us  [weights_over(): return lax.ppermute(piece, BOTH, CROSS)]
  transfers between devices with their start and end apart: 88 -> 88, of which waited for: 34 -> 33; matrix products, arithmetic and copies ran while one was open for 19% -> 19% of each run, Pallas kernels for 12% -> 12%
where the time goes in v5:
time: 904 us; the launch traced here: 893 us
  waiting for transfers between devices  275 us (30%)
  starting transfers between devices  228 us (25%)
  Pallas kernels  163 us (18%)
  local copies, waits for them, and re-layouts  86.4 us (10%)
  other arithmetic  80.4 us (9%)
  matrix products  43.3 us (5%)
  between operations  16.3 us (2%)
    pallas_call x12, Pallas kernels, call(): pl.pallas_call(kernel, grid=(count,), in_specs=[spec for spec, _ in ins],...  146 us
    ppermute x18, waiting for transfers between devices, swap(): return lax.ppermute(value, axis, SWAP)  103 us
    ppermute x12, waiting for transfers between devices, chain(): got = lax.ppermute(part, BLOCKS, [(i, i ^ step) for i in range(count)])  62.8 us
    ppermute x3, waiting for transfers between devices, join_halves(): return part + lax.ppermute(part, BOTH, CROSS_BACK)  52.6 us
    dot_general x14, matrix products, mm(): lax.dot_general(left, right, (dims, ((), ())), preferred_element_type=f32...  39.4 us
    ppermute x18, starting transfers between devices, swap(): return lax.ppermute(value, axis, SWAP)  38.5 us
    ppermute x10, starting transfers between devices, total(): lax.ppermute(value, axis, [(i, i ^ step) for i in range(count)])  33 us
    ppermute x10, waiting for transfers between devices, total(): lax.ppermute(value, axis, [(i, i ^ step) for i in range(count)])  31.8 us
  transfers between devices with their start and end apart: 88, of which 33 were waited for; matrix products, arithmetic and copies ran while one was open for 19% of the time, Pallas kernels for 12%

profile of v5, /device:TPU:0, one launch (start us, length us, event | category | flops | bytes accessed | tf_op | source)
XLA Modules:
  0.0 893.2 jit_solution(12741103887424448254)
XLA Ops:
  57.1 12.2 %collective-permute-start.2 = (f32[256,1024]{1,0:T(8,128)}, f32[256,1024]{1,0:T(8,128)}, u32[]{:S(2)}, u32[]{:S(2)}) collective-permute-start(f32[256,1024]{1,0:T(8,128)} %maximum_convert_fusion.1), channel_id=1, source_target_pairs={{0,2},{6,4},{1,3},{7,5},{8,10},{14,12},{9,11},{15,13},{16,18},{22,... | collective-permute-start | bytes 3145736 | tf_op jit(solution)/shard_map/ppermute | solution.py:580
  96.0 15.6 %in_proj_conv.2 = (bf16[1024,1024]{1,0:T(8,128)(2,1)}, f32[1024,768]{1,0:T(8,128)}, f32[1024,768]{1,0:T(8,128)}, f32[1024,128]{1,0:T(8,128)}, f32[1024,128]{1,0:...) custom-call(s32[2]{0:T(128)} %pad_add_fusion.place, ...), custom_call_target="tpu_custom_call" | custom-call | flops 18400000000 | bytes 1048576 | tf_op jit(solution)/shard_map/in_proj_conv/pallas_call | solution.py:350
  138.5 14.2 %collective-permute-done.18 = f32[136,512]{1,0:T(8,128)S(1)} collective-permute-done((f32[136,512]{1,0:T(8,128)S(1)}, f32[136,512]{1,0:T(8,128)S(1)}, u32[]{:S(2)}, u32[]{:S(2)}) %collective-permute-start.18) | collective-permute-done | bytes 278560 | tf_op jit(solution)/shard_map/ppermute | solution.py:394
  154.8 11.1 %gate_out_proj.2 = (f32[1024,512]{1,0:T(8,128)}, bf16[1024,512]{1,0:T(8,128)(2,1)}, f32[1024,1024]{1,0:T(8,128)}, f32[8,1024]{1,0:T(8,128)}) custom-call(f32[1024,512]{1,0:T(8,128)} %ssd_within.2.yin, f32[1024,768]{1,0:T(8,128)} %get-tuple-element.126.cpre, f32[1024,128]{1,0:T(8,128)} %get-tuple-element.123.cum, bf16[1024,256]{1,0:T(8,128)(2,1)} %get-tuple-element.125.bc, ...), custom_call_target="tpu_custom_call" | custom-call | flops 13799999488 | bytes 1048576 | tf_op jit(solution)/shard_map/gate_out_proj/pallas_call | solution.py:350
  169.1 19.1 %collective-permute-start.21 = (f32[512,1024]{1,0:T(8,128)}, f32[512,1024]{1,0:T(8,128)S(1)}, u32[]{:S(2)}, u32[]{:S(2)}) collective-permute-start(f32[512,1024]{1,0:T(8,128)} %constant_dynamic-slice_fusion.12), channel_id=1, source_target_pairs={{0,4},{4,0},{1,5},{5,1},{2,6},{6,2},{3,7},{7,3},{8,12},{12,8},{9,1... | collective-permute-start | bytes 6291464 | tf_op jit(solution)/shard_map/ppermute | solution.py:407
  204.3 17.4 %collective-permute-done.20 = f32[8,1024]{1,0:T(8,128)S(1)} collective-permute-done((f32[8,1024]{1,0:T(8,128)S(1)}, f32[8,1024]{1,0:T(8,128)S(1)}, u32[]{:S(2)}, u32[]{:S(2)}) %collective-permute-start.20) | collective-permute-done | bytes 32800 | tf_op jit(solution)/shard_map/ppermute | solution.py:415
  226.5 24.6 %collective-permute-done.26.refs_1_ = f32[256,1024]{1,0:T(8,128)} collective-permute-done((f32[256,1024]{1,0:T(8,128)}, f32[256,1024]{1,0:T(8,128)}, u32[]{:S(2)}, u32[]{:S(2)}) %collective-permute-start.26) | collective-permute-done | bytes 1048608 | tf_op jit(solution)/shard_map/ppermute | solution.py:407
  263.6 13.2 %collective-permute-start.29 = (f32[8,768]{1,0:T(8,128)S(1)}, f32[8,768]{1,0:T(8,128)S(1)}, u32[]{:S(2)}, u32[]{:S(2)}) collective-permute-start(f32[8,768]{1,0:T(8,128)S(1)} %fusion.6), channel_id=1, source_target_pairs={{0,2},{2,8},{8,10},{10,16},{16,18},{18,24},{24,26},{1,3},{3,9},{9,... | collective-permute-start | bytes 73736 | tf_op jit(solution)/shard_map/ppermute | solution.py:384
  279.9 17.1 %in_proj_conv.3 = (bf16[1024,1024]{1,0:T(8,128)(2,1)}, f32[1024,768]{1,0:T(8,128)}, f32[1024,768]{1,0:T(8,128)}, f32[1024,128]{1,0:T(8,128)}, f32[1024,128]{1,0:...) custom-call(s32[2]{0:T(128)} %pad_add_fusion.place, ...), custom_call_target="tpu_custom_call" | custom-call | flops 18400000000 | bytes 1048576 | tf_op jit(solution)/shard_map/in_proj_conv/pallas_call | solution.py:350
  300.4 12.2 %collective-permute-done.30 = f32[136,512]{1,0:T(8,128)S(1)} collective-permute-done((f32[136,512]{1,0:T(8,128)}, f32[136,512]{1,0:T(8,128)S(1)}, u32[]{:S(2)}, u32[]{:S(2)}) %collective-permute-start.30) | collective-permute-done | bytes 278560 | tf_op jit(solution)/shard_map/ppermute | solution.py:394
  330.9 14.1 %gate_out_proj.3 = (f32[1024,512]{1,0:T(8,128)}, bf16[1024,512]{1,0:T(8,128)(2,1)}, f32[1024,1024]{1,0:T(8,128)}, f32[8,1024]{1,0:T(8,128)}) custom-call(f32[1024,512]{1,0:T(8,128)} %ssd_within.3.yin, f32[1024,768]{1,0:T(8,128)} %get-tuple-element.153.cpre, f32[1024,128]{1,0:T(8,128)} %get-tuple-element.150.cum, bf16[1024,256]{1,0:T(8,128)(2,1)} %get-tuple-element.152.bc, ...), custom_call_target="tpu_custom_call" | custom-call | flops 13799999488 | bytes 1048576 | tf_op jit(solution)/shard_map/gate_out_proj/pallas_call | solution.py:350
  353.6 10.0 %gate_back.2 = (bf16[1024,1024]{1,0:T(8,128)(2,1)}, bf16[1024,512]{1,0:T(8,128)(2,1)}, bf16[1024,512]{1,0:T(8,128)(2,1)}, f32[4,128,512]{2,1,0:T(8,128)}, f32[4,...) custom-call(s32[2]{0:T(128)} %pad_add_fusion.place, f32[1024,1]{1,0:T(8,128)} %copy-done.41, ...), custom_call_target="tpu_custom_call" | custom-call | flops 11500000256 | bytes 1048576 | tf_op jit(solution)/shard_map/gate_back/pallas_call | solution.py:350
  375.7 12.6 %collective-permute-done.37 = f32[136,512]{1,0:T(8,128)S(1)} collective-permute-done((f32[136,512]{1,0:T(8,128)S(1)}, f32[136,512]{1,0:T(8,128)S(1)}, u32[]{:S(2)}, u32[]{:S(2)}) %collective-permute-start.37) | collective-permute-done | bytes 278560 | tf_op jit(solution)/shard_map/ppermute | solution.py:394
  388.8 7.7 ssd_within_back.2
  414.3 12.3 %collective-permute-done.36 = f32[256,1024]{1,0:T(8,128)S(1)} collective-permute-done((f32[256,1024]{1,0:T(8,128)}, f32[256,1024]{1,0:T(8,128)S(1)}, u32[]{:S(2)}, u32[]{:S(2)}) %collective-permute-start.36) | collective-permute-done | bytes 1048608 | tf_op jit(solution)/shard_map/ppermute | solution.py:407
  429.7 20.4 %in_proj_conv_back.2 = (bf16[1024,896]{1,0:T(8,128)(2,1)}, f32[8,768]{1,0:T(8,128)}, f32[8,768]{1,0:T(8,128)}, f32[8,768]{1,0:T(8,128)}, f32[8,128]{1,0:T(8,128)}, /*index=5*/f32[8,512]{1,0:T(8,128)}) custom-call(f32[1024,512]{1,0:T(8,128)} %get-tuple-element.167.uin, f32[1024,256]{1,0:T(8,128)} %get-tuple-element.168.dbc, ...), custom_call_target="tpu_custom_call" | custom-call | flops 23000000512 | bytes 1048576 | tf_op jit(solution)/shard_map/in_proj_conv_back/pallas_call | solution.py:350
  474.9 23.4 %collective-permute-done.42 = f32[256,1024]{1,0:T(8,128)S(1)} collective-permute-done((f32[256,1024]{1,0:T(8,128)S(1)}, f32[256,1024]{1,0:T(8,128)S(1)}, u32[]{:S(2)}, u32[]{:S(2)}) %collective-permute-start.42) | collective-permute-done | bytes 1048608 | tf_op jit(solution)/shard_map/ppermute | solution.py:407
  503.7 22.7 %collective-permute-done.43.refs_1_ = f32[256,1024]{1,0:T(8,128)} collective-permute-done((f32[256,1024]{1,0:T(8,128)S(1)}, f32[256,1024]{1,0:T(8,128)}, u32[]{:S(2)}, u32[]{:S(2)}) %collective-permute-start.43) | collective-permute-done | bytes 1048608 | tf_op jit(solution)/shard_map/ppermute | solution.py:407
  532.2 10.9 %gate_back.3 = (bf16[1024,1024]{1,0:T(8,128)(2,1)}, bf16[1024,512]{1,0:T(8,128)(2,1)}, bf16[1024,512]{1,0:T(8,128)(2,1)}, f32[4,128,512]{2,1,0:T(8,128)}, f32[4,...) custom-call(s32[2]{0:T(128)} %pad_add_fusion.place, f32[1024,1]{1,0:T(8,128)} %copy-done.40, ...), custom_call_target="tpu_custom_call" | custom-call | flops 11500000256 | bytes 1048576 | tf_op jit(solution)/shard_map/gate_back/pallas_call | solution.py:350
  559.5 7.2 collective-permute-done.55
  574.8 7.1 collective-permute-start.46
  597.1 7.5 ssd_within_back.3
  610.3 20.3 %in_proj_conv_back.3 = (bf16[1024,896]{1,0:T(8,128)(2,1)}, f32[8,768]{1,0:T(8,128)}, f32[8,768]{1,0:T(8,128)}, f32[8,768]{1,0:T(8,128)}, f32[8,128]{1,0:T(8,128)}, /*index=5*/f32[8,512]{1,0:T(8,128)}) custom-call(f32[1024,512]{1,0:T(8,128)} %get-tuple-element.183.uin, f32[1024,256]{1,0:T(8,128)} %get-tuple-element.184.dbc, ...), custom_call_target="tpu_custom_call" | custom-call | flops 23000000512 | bytes 1048576 | tf_op jit(solution)/shard_map/in_proj_conv_back/pallas_call | solution.py:350
  635.8 25.7 %collective-permute-start.51 = (f32[256,1024]{1,0:T(8,128)}, f32[256,1024]{1,0:T(8,128)}, u32[]{:S(2)}, u32[]{:S(2)}) collective-permute-start(f32[256,1024]{1,0:T(8,128)} %collective-permute-done.47.near), channel_id=1, source_target_pairs={{0,1},{1,0},{6,7},{7,6},{8,9},{9,8},{14,15},{15,14},{16,17},{17,16... | collective-permute-start | bytes 3145736 | tf_op jit(solution)/shard_map/ppermute | solution.py:500
  662.2 8.1 collective-permute-done.58
  697.3 11.4 %collective-permute-start.60 = (f32[512,1024]{1,0:T(8,128)S(1)}, f32[512,1024]{1,0:T(8,128)S(1)}, u32[]{:S(2)}, u32[]{:S(2)}) collective-permute-start(f32[512,1024]{1,0:T(8,128)S(1)} %constant_dynamic-slice_fusion.5), channel_id=1, source_target_pairs={{0,4},{4,0},{1,5},{5,1},{2,6},{6,2},{3,7},{7,3},{8,12},{12,8},{9,1... | collective-permute-start | bytes 6291464 | tf_op jit(solution)/shard_map/ppermute | solution.py:407
  728.9 12.6 %collective-permute-done.61 = f32[256,1024]{1,0:T(8,128)S(1)} collective-permute-done((f32[256,1024]{1,0:T(8,128)}, f32[256,1024]{1,0:T(8,128)S(1)}, u32[]{:S(2)}, u32[]{:S(2)}) %collective-permute-start.61) | collective-permute-done | bytes 1048608 | tf_op jit(solution)/shard_map/ppermute | solution.py:407
  780.7 37.2 %collective-permute-done.74 = f32[256,1024]{1,0:T(8,128)} collective-permute-done((f32[256,1024]{1,0:T(8,128)}, f32[256,1024]{1,0:T(8,128)}, u32[]{:S(2)}, u32[]{:S(2)}) %collective-permute-start.74) | collective-permute-done | bytes 1048608 | tf_op jit(solution)/shard_map/ppermute | solution.py:1055
  825.8 8.7 collective-permute-done.67.near_s
  842.8 7.5 collective-permute-done.80
  850.4 22.4 %collective-permute-start.81 = (f32[128,2,256]{2,0,1:T(8,128)S(1)}, f32[128,2,256]{2,0,1:T(8,128)S(1)}, u32[]{:S(2)}, u32[]{:S(2)}) collective-permute-start(f32[128,2,256]{2,0,1:T(8,128)S(1)} %fusion.103), channel_id=1, source_target_pairs={{0,2},{2,0},{1,3},{3,1},{4,6},{6,4},{5,7},{7,5},{8,10},{10,8},{9,1... | collective-permute-start | bytes 786440 | tf_op jit(solution)/shard_map/ppermute | solution.py:415
  872.8 7.3 collective-permute-done.77
  (572 shorter events, 402.9 us)
Async XLA Ops:
  7.3 597.4 %reduce-scatter.7.cloned.1.call-start = ((), (), s32[]{:S(2)}) async-start(), calls=%async_computation.6 | async-start | bytes 2621440 | tf_op jit(solution)/shard_map/reduce_scatter | solution.py:989
  15.7 29.4 %collective-permute-start.9 = (f32[1024]{0:T(1024)S(1)}, f32[1024]{0:T(1024)S(1)}, u32[]{:S(2)}, u32[]{:S(2)}) collective-permute-start(f32[1024]{0:T(1024)S(1)} %convert_element_type.77), channel_id=1, source_target_pairs={{0,4},{6,2},{1,5},{7,3},{8,12},{14,10},{9,13},{15,11},{16,20},{22,... | collective-permute-start | bytes 12296 | tf_op jit(solution)/shard_map/ppermute | solution.py:520
  17.2 33.4 %collective-permute-start.8 = (f32[2,3096]{1,0:T(2,128)S(1)}, f32[2,3096]{1,0:T(2,128)S(1)}, u32[]{:S(2)}, u32[]{:S(2)}) collective-permute-start(f32[2,3096]{1,0:T(2,128)S(1)} %concatenate.119), channel_id=1, source_target_pairs={{0,2},{6,4},{1,3},{7,5},{8,10},{14,12},{9,11},{15,13},{16,18},{22,... | collective-permute-start | bytes 74312 | tf_op jit(solution)/shard_map/ppermute | solution.py:671
  20.8 30.7 %collective-permute-start.1 = (f32[2,64,128]{2,1,0:T(8,128)S(1)}, f32[2,64,128]{2,1,0:T(8,128)S(1)}, u32[]{:S(2)}, u32[]{:S(2)}) collective-permute-start(f32[2,64,128]{2,1,0:T(8,128)S(1)} %reshape.406), channel_id=1, source_target_pairs={{0,2},{6,4},{1,3},{7,5},{8,10},{14,12},{9,11},{15,13},{16,18},{22,... | collective-permute-start | bytes 196616 | tf_op jit(solution)/shard_map/ppermute | solution.py:654
  39.0 39.1 %collective-permute-start.3 = (f32[1024,1024]{1,0:T(8,128)}, f32[1024,1024]{1,0:T(8,128)}, u32[]{:S(2)}, u32[]{:S(2)}) collective-permute-start(f32[1024,1024]{1,0:T(8,128)} %convert_element_type.75), channel_id=1, source_target_pairs={{0,4},{6,2},{1,5},{7,3},{8,12},{14,10},{9,13},{15,11},{16,20},{22,... | collective-permute-start | bytes 12582920 | tf_op jit(solution)/shard_map/ppermute | solution.py:520
  57.1 26.7 %collective-permute-start.2 = (f32[256,1024]{1,0:T(8,128)}, f32[256,1024]{1,0:T(8,128)}, u32[]{:S(2)}, u32[]{:S(2)}) collective-permute-start(f32[256,1024]{1,0:T(8,128)} %maximum_convert_fusion.1), channel_id=1, source_target_pairs={{0,2},{6,4},{1,3},{7,5},{8,10},{14,12},{9,11},{15,13},{16,18},{22,... | collective-permute-start | bytes 3145736 | tf_op jit(solution)/shard_map/ppermute | solution.py:580
  198.9 52.9 %collective-permute-start.25 = (f32[256,1536]{1,0:T(8,128)}, f32[256,1536]{1,0:T(8,128)}, u32[]{:S(2)}, u32[]{:S(2)}) collective-permute-start(f32[256,1536]{1,0:T(8,128)} %collective-permute-done.15.refs_3_), channel_id=1, source_target_pairs={{2,26},{4,28},{10,18},{12,20},{18,10},{20,12},{26,2},{28,4},{3,27}... | collective-permute-start | bytes 4718600 | tf_op jit(solution)/shard_map/ppermute | solution.py:595
  200.7 51.0 %collective-permute-start.24 = (f32[256,1536]{1,0:T(8,128)}, f32[256,1536]{1,0:T(8,128)}, u32[]{:S(2)}, u32[]{:S(2)}) collective-permute-start(f32[256,1536]{1,0:T(8,128)} %collective-permute-done.15.refs_3_), channel_id=1, source_target_pairs={{2,18},{4,20},{10,26},{12,28},{18,2},{20,4},{26,10},{28,12},{3,19}... | collective-permute-start | bytes 4718600 | tf_op jit(solution)/shard_map/ppermute | solution.py:595
  202.5 49.2 %collective-permute-start.23 = (f32[256,1536]{1,0:T(8,128)}, f32[256,1536]{1,0:T(8,128)}, u32[]{:S(2)}, u32[]{:S(2)}) collective-permute-start(f32[256,1536]{1,0:T(8,128)} %collective-permute-done.15.refs_3_), channel_id=1, source_target_pairs={{2,10},{4,12},{10,2},{12,4},{18,26},{20,28},{26,18},{28,20},{3,11}... | collective-permute-start | bytes 4718600 | tf_op jit(solution)/shard_map/ppermute | solution.py:595
  226.5 34.9 %collective-permute-start.27 = (f32[256,1024]{1,0:T(8,128)}, f32[256,1024]{1,0:T(8,128)}, u32[]{:S(2)}, u32[]{:S(2)}) collective-permute-start(f32[256,1024]{1,0:T(8,128)} %get-tuple-element.274.refs_0_), channel_id=1, source_target_pairs={{0,4},{4,0},{1,5},{5,1},{2,6},{6,2},{3,7},{7,3},{8,12},{12,8},{9,1... | collective-permute-start | bytes 3145736 | tf_op jit(solution)/shard_map/ppermute | solution.py:407
  367.9 236.7 %reduce-scatter.9.cloned.1.call-start = ((), (), s32[]{:S(2)}) async-start(), calls=%async_computation.7 | async-start | bytes 2621440 | tf_op jit(solution)/shard_map/reduce_scatter | solution.py:989
  407.6 197.1 %reduce-scatter.11.cloned.1.call-start = ((), (), s32[]{:S(2)}) async-start(), calls=%async_computation.8 | async-start | bytes 3932160 | tf_op jit(solution)/shard_map/reduce_scatter | solution.py:989
  471.4 281.7 %reduce-scatter.13.cloned.1.call-start = ((), (), s32[]{:S(2)}) async-start(), calls=%async_computation.9 | async-start | bytes 2621440 | tf_op jit(solution)/shard_map/reduce_scatter | solution.py:989
  503.7 28.5 %collective-permute-start.44 = (f32[256,1024]{1,0:T(8,128)S(1)}, f32[256,1024]{1,0:T(8,128)}, u32[]{:S(2)}, u32[]{:S(2)}) collective-permute-start(f32[256,1024]{1,0:T(8,128)S(1)} %get-tuple-element.271.refs_0_), channel_id=1, source_target_pairs={{0,4},{4,0},{1,5},{5,1},{2,6},{6,2},{3,7},{7,3},{8,12},{12,8},{9,1... | collective-permute-start | bytes 3145736 | tf_op jit(solution)/shard_map/ppermute | solution.py:407
  547.4 205.7 %reduce-scatter.15.cloned.1.call-start = ((), (), s32[]{:S(2)}) async-start(), calls=%async_computation.10 | async-start | bytes 2621440 | tf_op jit(solution)/shard_map/reduce_scatter | solution.py:989
  554.3 132.5 %collective-permute-start.49 = (f32[256,1024]{1,0:T(8,128)S(1)}, f32[256,1024]{1,0:T(8,128)S(1)}, u32[]{:S(2)}, u32[]{:S(2)}) collective-permute-start(f32[256,1024]{1,0:T(8,128)S(1)} %multiply_add_fusion.2.value), channel_id=1, source_target_pairs={{0,1},{1,0},{6,7},{7,6},{8,9},{9,8},{14,15},{15,14},{16,17},{17,16... | collective-permute-start | bytes 3145736 | tf_op jit(solution)/shard_map/ppermute | solution.py:499
  589.7 233.8 %reduce-scatter.17.cloned.1.call-start = ((), (), s32[]{:S(2)}) async-start(), calls=%async_computation.11 | async-start | bytes 3932160 | tf_op jit(solution)/shard_map/reduce_scatter | solution.py:989
  609.0 61.3 %collective-permute-start.58 = (f32[256,1536]{1,0:T(8,128)}, f32[256,1536]{1,0:T(8,128)}, u32[]{:S(2)}, u32[]{:S(2)}) collective-permute-start(f32[256,1536]{1,0:T(8,128)} %pad_maximum_fusion), channel_id=1, source_target_pairs={{2,0},{4,6},{3,1},{5,7},{10,8},{12,14},{11,9},{13,15},{18,16},{20,... | collective-permute-start | bytes 4718600 | tf_op jit(solution)/shard_map/ppermute | solution.py:1055
  632.8 42.5 %collective-permute-start.59 = (f32[8,768]{1,0:T(8,128)}, f32[8,768]{1,0:T(8,128)S(1)}, u32[]{:S(2)}, u32[]{:S(2)}) collective-permute-start(f32[8,768]{1,0:T(8,128)} %get-tuple-element.200), channel_id=1, source_target_pairs={{2,0},{8,2},{10,8},{16,10},{18,16},{24,18},{26,24},{3,1},{9,3},{11... | collective-permute-start | bytes 73736 | tf_op jit(solution)/shard_map/ppermute | solution.py:384
  634.1 52.8 %collective-permute-start.52 = (f32[256,1024]{1,0:T(8,128)S(1)}, f32[256,1024]{1,0:T(8,128)}, u32[]{:S(2)}, u32[]{:S(2)}) collective-permute-start(f32[256,1024]{1,0:T(8,128)S(1)} %collective-permute-done.48.theirs), channel_id=1, source_target_pairs={{2,3},{3,2},{4,5},{5,4},{10,11},{11,10},{12,13},{13,12},{18,19},{1... | collective-permute-start | bytes 3145736 | tf_op jit(solution)/shard_map/ppermute | solution.py:502
  635.8 56.6 %collective-permute-start.51 = (f32[256,1024]{1,0:T(8,128)}, f32[256,1024]{1,0:T(8,128)}, u32[]{:S(2)}, u32[]{:S(2)}) collective-permute-start(f32[256,1024]{1,0:T(8,128)} %collective-permute-done.47.near), channel_id=1, source_target_pairs={{0,1},{1,0},{6,7},{7,6},{8,9},{9,8},{14,15},{15,14},{16,17},{17,16... | collective-permute-start | bytes 3145736 | tf_op jit(solution)/shard_map/ppermute | solution.py:500
  724.4 48.2 %collective-permute-start.76 = (f32[128,1536]{1,0:T(8,128)}, f32[128,1536]{1,0:T(8,128)}, u32[]{:S(2)}, u32[]{:S(2)}) collective-permute-start(f32[128,1536]{1,0:T(8,128)} %constant_dynamic-slice_fusion.2), channel_id=1, source_target_pairs={{0,4},{6,2},{1,5},{7,3},{8,12},{14,10},{9,13},{15,11},{16,20},{22,... | collective-permute-start | bytes 2359304 | tf_op jit(solution)/shard_map/ppermute | solution.py:1060
  727.7 37.5 %collective-permute-start.73 = (f32[2,2304]{1,0:T(2,128)S(1)}, f32[2,2304]{1,0:T(2,128)}, u32[]{:S(2)}, u32[]{:S(2)}) collective-permute-start(f32[2,2304]{1,0:T(2,128)S(1)} %slice_add_fusion), channel_id=1, source_target_pairs={{0,1},{1,0},{2,3},{3,2},{4,5},{5,4},{6,7},{7,6},{8,9},{9,8},{10,11... | collective-permute-start | bytes 55304 | tf_op jit(solution)/shard_map/ppermute | solution.py:415
  745.6 29.6 %collective-permute-start.64 = (f32[256,1024]{1,0:T(8,128)S(1)}, f32[256,1024]{1,0:T(8,128)S(1)}, u32[]{:S(2)}, u32[]{:S(2)}) collective-permute-start(f32[256,1024]{1,0:T(8,128)S(1)} %multiply_add_fusion.value), channel_id=1, source_target_pairs={{4,2},{2,4},{5,3},{3,5},{12,10},{10,12},{13,11},{11,13},{20,18},{1... | collective-permute-start | bytes 3145736 | tf_op jit(solution)/shard_map/ppermute | solution.py:485
  747.7 29.3 %collective-permute-start.62 = (f32[256,1024]{1,0:T(8,128)S(1)}, f32[256,1024]{1,0:T(8,128)}, u32[]{:S(2)}, u32[]{:S(2)}) collective-permute-start(f32[256,1024]{1,0:T(8,128)S(1)} %multiply_add_fusion.value), channel_id=1, source_target_pairs={{0,2},{6,4},{1,3},{7,5},{8,10},{14,12},{9,11},{15,13},{16,18},{22,... | collective-permute-start | bytes 3145736 | tf_op jit(solution)/shard_map/ppermute | solution.py:485
  756.9 61.0 %collective-permute-start.74 = (f32[256,1024]{1,0:T(8,128)}, f32[256,1024]{1,0:T(8,128)}, u32[]{:S(2)}, u32[]{:S(2)}) collective-permute-start(f32[256,1024]{1,0:T(8,128)} %constant_dynamic-update-slice_fusion), channel_id=1, source_target_pairs={{2,0},{4,6},{3,1},{5,7},{10,8},{12,14},{11,9},{13,15},{18,16},{20,... | collective-permute-start | bytes 3145736 | tf_op jit(solution)/shard_map/ppermute | solution.py:1055
  765.2 59.3 %collective-permute-start.65 = (f32[256,1024]{1,0:T(8,128)S(1)}, f32[256,1024]{1,0:T(8,128)}, u32[]{:S(2)}, u32[]{:S(2)}) collective-permute-start(f32[256,1024]{1,0:T(8,128)S(1)} %multiply_add_fusion.value), channel_id=1, source_target_pairs={{0,1},{1,0},{6,7},{7,6},{8,9},{9,8},{14,15},{15,14},{16,17},{17,16... | collective-permute-start | bytes 3145736 | tf_op jit(solution)/shard_map/ppermute | solution.py:499
  772.5 61.9 %collective-permute-start.67 = (f32[256,1024]{1,0:T(8,128)S(1)}, f32[256,1024]{1,0:T(8,128)}, u32[]{:S(2)}, u32[]{:S(2)}) collective-permute-start(f32[256,1024]{1,0:T(8,128)S(1)} %collective-permute-done.63.near), channel_id=1, source_target_pairs={{0,1},{1,0},{6,7},{7,6},{8,9},{9,8},{14,15},{15,14},{16,17},{17,16... | collective-permute-start | bytes 3145736 | tf_op jit(solution)/shard_map/ppermute | solution.py:500
  775.2 50.5 %collective-permute-start.68 = (f32[256,1024]{1,0:T(8,128)S(1)}, f32[256,1024]{1,0:T(8,128)}, u32[]{:S(2)}, u32[]{:S(2)}) collective-permute-start(f32[256,1024]{1,0:T(8,128)S(1)} %collective-permute-done.64.theirs), channel_id=1, source_target_pairs={{2,3},{3,2},{4,5},{5,4},{10,11},{11,10},{12,13},{13,12},{18,19},{1... | collective-permute-start | bytes 3145736 | tf_op jit(solution)/shard_map/ppermute | solution.py:502
  776.9 57.5 %collective-permute-start.66 = (f32[256,1024]{1,0:T(8,128)}, f32[256,1024]{1,0:T(8,128)}, u32[]{:S(2)}, u32[]{:S(2)}) collective-permute-start(f32[256,1024]{1,0:T(8,128)} %collective-permute-done.62.mine), channel_id=1, source_target_pairs={{2,3},{3,2},{4,5},{5,4},{10,11},{11,10},{12,13},{13,12},{18,19},{1... | collective-permute-start | bytes 3145736 | tf_op jit(solution)/shard_map/ppermute | solution.py:501
  839.7 40.5 %collective-permute-start.77 = (f32[256,512]{1,0:T(8,128)S(1)}, f32[256,512]{1,0:T(8,128)S(1)}, u32[]{:S(2)}, u32[]{:S(2)}) collective-permute-start(f32[256,512]{1,0:T(8,128)S(1)} %slice.560), channel_id=1, source_target_pairs={{2,0},{4,6},{3,1},{5,7},{10,8},{12,14},{11,9},{13,15},{18,16},{20,... | collective-permute-start | bytes 1572872 | tf_op jit(solution)/shard_map/ppermute | solution.py:1055
  850.4 33.8 %collective-permute-start.81 = (f32[128,2,256]{2,0,1:T(8,128)S(1)}, f32[128,2,256]{2,0,1:T(8,128)S(1)}, u32[]{:S(2)}, u32[]{:S(2)}) collective-permute-start(f32[128,2,256]{2,0,1:T(8,128)S(1)} %fusion.103), channel_id=1, source_target_pairs={{0,2},{2,0},{1,3},{3,1},{4,6},{6,4},{5,7},{7,5},{8,10},{10,8},{9,1... | collective-permute-start | bytes 786440 | tf_op jit(solution)/shard_map/ppermute | solution.py:415
  (133 other events, 1728.6 us)
Sparse Core Ops, SparseCore 0:
  368.0 36.1 reduce-scatter.6
  407.7 35.9 reduce-scatter.8
  471.5 46.2 reduce-scatter.10
  547.5 40.6 reduce-scatter.12
  591.3 35.8 reduce-scatter.14
  721.2 41.6 reduce-scatter.16

commit v6 on v5

--- a/solution.py
+++ b/solution.py
@@ -432,9 +432,11 @@
     return lax.optimization_barrier((value, *marks))[0]
 
 
-def scatter_sum(part, mark=()):
+def scatter_sum(part, mark=(), stages=None):
     core, near = lax.axis_index("core"), lax.axis_index("zl")
     half = take(part, core, 2) + behind(swap(take(part, 1 - core, 2), "core"), *mark)
+    if stages is not None:
+        stages.append(half)
     if lax.axis_size("zl") == 2:
         return take(half, near, 2) + swap(take(half, 1 - near, 2), "zl")
     return lax.psum_scatter(half, "zl", scatter_dimension=0, tiled=True)
@@ -485,7 +487,27 @@
     return [lax.ppermute(value, BOTH, pairs) for pairs in (CROSS, DIAGONAL, CORE_IN)]
 
 
-def deliver(value, mine, theirs, near, dtype):
+def near_swap(value):
+    if lax.axis_size("zl") != 2 or value.shape[0] != GROUP:
+        return None
+    here = [(2 * kind + i, 2 * kind + 1 - i) for kind in (0, 3) for i in range(2)]
+    return lax.ppermute(value, ("core", "zh", "zl"), here)
+
+
+def near_swaps(value, mine, theirs, near, value_s=None):
+    if lax.axis_size("zl") != 2 or value.shape[0] != GROUP:
+        return None
+    axes = ("core", "zh", "zl")
+    there = [(2 * kind + i, 2 * kind + 1 - i) for kind in (1, 2) for i in range(2)]
+    return (
+        near_swap(value) if value_s is None else value_s,
+        lax.ppermute(mine, axes, there),
+        lax.ppermute(theirs, axes, there),
+        near_swap(near),
+    )
+
+
+def deliver(value, mine, theirs, near, dtype, swaps=None, mark=()):
     core, far = lax.axis_index("core"), lax.axis_index("zh")
     held = core == far
     if lax.axis_size("zl") != 2 or value.shape[0] != GROUP:
@@ -493,16 +515,12 @@
         theirs = gather_near(jnp.where(held, near, theirs))
         full = ordered(core, mine, theirs)
         return narrowed(full) if dtype == bf16 else full
-    axes = ("core", "zh", "zl")
-    here = [(2 * kind + i, 2 * kind + 1 - i) for kind in (0, 3) for i in range(2)]
-    there = [(2 * kind + i, 2 * kind + 1 - i) for kind in (1, 2) for i in range(2)]
-    value_s = lax.ppermute(value, axes, here)
-    near_s = lax.ppermute(near, axes, here)
-    mine_s = lax.ppermute(mine, axes, there)
-    theirs_s = lax.ppermute(theirs, axes, there)
+    if swaps is None:
+        swaps = near_swaps(value, mine, theirs, near)
+    value_s, mine_s, theirs_s, near_s = swaps
     place = jnp.stack([own_place(), held.astype(jnp.int32)]).astype(jnp.int32)
     width = value.shape[1]
-    parts = (value, mine, near, theirs, value_s, mine_s, near_s, theirs_s)
+    parts = behind((value, mine, near, theirs, value_s, mine_s, near_s, theirs_s), *mark)
     return pl.pallas_call(
         place_kernel,
         grid=(4,),
@@ -656,10 +674,9 @@
     hidden = to_block(x_input.astype(f32))
     first_x = weights_over([w_x[0]])
     first_rest = weights_over([w_z[0], w_out[0]], dt_sent)
-    second_all = weights_over([w_x[1], w_z[1], w_out[1]], hidden)
+    second_all = weights_over([w_x[1], w_z[1], w_out[1]], dt_sent)
+    first_x, first_rest, second_all = behind((first_x, first_rest, second_all))
     (wall,) = gather_weights(first_x, [w_x[0]], (w_bc[0], dt_all[0]))
-    cotangent = to_block(behind(cotangent.astype(f32), hidden))
-    hidden = behind(hidden, first_rest, cotangent)
     seg = to_block(seg_ids.astype(f32))
     small = jnp.concatenate(
         [
@@ -767,7 +784,7 @@
             wz, wout = gather_weights(
                 behind(first_rest, wall), [w_z[0], w_out[0]], third=(send,)
             )
-            send = behind(send, second_all)
+            cotangent = to_block(behind(cotangent, send).astype(f32))
         else:
             wz, wout = next_wz, next_wout
         zval = mm(normed, wz)
@@ -883,9 +900,6 @@
             10,
             "gate_back",
         )
-        if layer == 0:
-            out_parts = cross_over(behind(hidden_own, *grad_h))
-            dy = behind(dy, *out_parts)
         u, dbc = call(
             intra_back_kernel,
             count,
@@ -910,11 +924,19 @@
             last_sum = scatter_sum(kept["proj"], (dy,))
             hidden_own = hidden_own + own_rows(gate_scale)[:, None] * last_sum
             u = behind(u, hidden_own)
+            out_parts = cross_over(hidden_own)
         else:
-            first_sums = join_halves(behind(matrices[LAYERS - 1], u))
+            out_swaps = near_swaps(behind(hidden_own, dy), *out_parts)
+            g_out, g_z, _, g_x = behind(matrices[LAYERS - 1], u)
+            first_sums = join_halves([g_out, g_z, g_x])
         grad_wout = mm(gproj, kept["gate_in"], ((0,), (0,)))
         grad_wz = mm(kept["normed"], dz, ((0,), (0,)))
         partial_z = mm(dz, kept["wz"], ((1,), (1,)))
+        u = behind(u, grad_wout, grad_wz, partial_z)
+        matrices[layer] = [
+            lax.psum_scatter(value, "chip", scatter_dimension=0, tiled=True)
+            for value in (grad_wout, grad_wz)
+        ]
         gall, last8, rim, gtaps, vecs, dsk = call(
             in_back_kernel,
             count,
@@ -959,15 +981,22 @@
         )
         rim_back = shifted(rim, -1)
         if layer == 0:
-            last8 = behind(last8, first_sums)
+            last8 = behind(last8, first_sums, *(out_swaps or ()))
+        else:
+            last8 = behind(last8, out_parts[0], out_parts[2])
         gall = lax.dynamic_update_slice(
             gall, (last8 + rim_back).astype(bf16), (tok - ROWS, 0)
         )
         partial = partial_z + mm(gall, kept["wall"], ((1,), (1,)))
-        grad_normed = scatter_sum(partial)
-        late = behind(gall, partial)
-        grad_win = mm(kept["normed"], late[:, : inner + BC], ((0,), (0,)))
+        if layer > 0:
+            partial = behind(partial, *out_parts)
+        stages = []
+        grad_normed = scatter_sum(partial, stages=stages)
+        late = behind(gall, *stages)
+        partial = behind(partial, *stages)
+        grad_wbc = mm(kept["normed"], late[:, inner : inner + BC], ((0,), (0,)))
         grad_wdt = mm(kept["normed"], late[:, inner + BC :], ((0,), (0,)))
+        grad_win = mm(kept["normed"], behind(late, grad_wbc, grad_wdt)[:, :inner], ((0,), (0,)))
         hidden_in = kept["hidden"]
         inv = lax.rsqrt(jnp.mean(hidden_in * hidden_in, axis=1, keepdims=True) + epsilon)
         if layer == 0:
@@ -985,9 +1014,9 @@
         )
         if layer > 0:
             grad_h = gather_pieces(grad_own)
-        matrices[layer] = [
+        matrices[layer] += [
             lax.psum_scatter(value, "chip", scatter_dimension=0, tiled=True)
-            for value in (grad_wout, grad_wz, grad_win)
+            for value in (grad_wbc, grad_win)
         ]
         vectors[layer] = jnp.concatenate(
             [
@@ -1001,21 +1030,22 @@
                 grad_ngain,
             ]
         )
-    vector = total(jnp.stack(vectors), ("chip", "zh"))
-    grad_parts = cross_over(grad_own)
-    near = grad_parts[2]
-    input_grad = deliver(grad_own, *grad_parts, f32)
-    final_out = deliver(hidden_own, *out_parts, bf16)
-    early = join_halves(behind(matrices[0][:2], near))
-    late = join_halves(matrices[0][2:])
-    g_cols = [place_rows(early, late), place_rows(first_sums)]
-    grad_wbc = shared_rows(
-        jnp.stack([matrices[layer][2][:, inner:] for layer in range(LAYERS)], axis=1)
-    )
+    vector = total(jnp.stack(vectors), ("zh", "chip"))
     other = swap(vector, "core")
     common = (CONV + 1) * BC + width
+    shared = total((vector + other)[:, -common:], ("zl",))
+    grad_wbc = half_rows(jnp.stack([matrices[1][2], matrices[0][2]], axis=1)[:, ::-1])
+    grad_parts = cross_over(grad_own)
+    own_s = near_swap(grad_own)
+    grad_parts, own_s, shared, grad_wbc = behind((grad_parts, own_s, shared, grad_wbc))
+    mark = grad_parts[0]
+    input_grad = deliver(grad_own, *grad_parts, f32, near_swaps(grad_own, *grad_parts, own_s))
+    final_out = deliver(hidden_own, *out_parts, bf16, out_swaps, (mark,))
+    grad_wbc = total(grad_wbc, ("zh",))
+    g_out, g_z, g_x = behind((matrices[0][0], matrices[0][1], matrices[0][3]), mark)
+    early, late = join_halves([g_out, g_z]), join_halves([g_x])
+    g_cols = [place_rows(early, late), place_rows(behind(first_sums, mark))]
     by_head = jnp.where(held, vector, other)[:, :-common]
-    shared = total((vector + other)[:, -common:], ("zl",))
     g_bc = shared[:, :-width].reshape(LAYERS, CONV + 1, BC)
     g_ngain = shared[:, -width:]
     at = 0
@@ -1048,10 +1078,7 @@
 
 
 def join_halves(parts):
-    inner = parts[0].shape[1]
-    part = jnp.concatenate([value[:, :inner] for value in parts], axis=1)
-    if len(parts) == 1:
-        part = part[:, : inner - BC]
+    part = jnp.concatenate(parts, axis=1)
     return part + lax.ppermute(part, BOTH, CROSS_BACK)
 
 
@@ -1064,10 +1091,10 @@
     return jnp.concatenate(rows, axis=1)
 
 
-def shared_rows(part):
+def half_rows(part):
     core = lax.axis_index("core")
     part = take(part, core, 2) + swap(take(part, 1 - core, 2), "core")
-    return total(part, ("zl", "zh"))
+    return total(part, ("zl",))
 
 
 def solution(mesh):

time: 904 us -> 937 us (1.037)
  waiting for transfers between devices: 275 us -> 308 us
    reduce_scatter x6 -> x8, waiting for transfers between devices: 0.07 us -> 28.2 us  [shards(): lax.psum_scatter(value, 'chip', scatter_dimension=0, tiled=True)]
    ppermute x12, waiting for transfers between devices: 62.8 us -> 36.7 us  [chain(): got = lax.ppermute(part, BLOCKS, [(i, i ^ step) for i in range(count)])]
    ppermute x3, starting transfers between devices: 6.6 us -> 32.3 us  [place_rows(): lax.ppermute(take(full, 1 - core, 2), BOTH, CORE_OUT)]
    ppermute x3, waiting for transfers between devices: 0.01 us -> 25.4 us  [weights_over(): return lax.ppermute(piece, BOTH, CROSS)]
    ppermute x8, starting transfers between devices: 41.9 us -> 16.9 us  [the longest x4 11.9 us: near_swap(): return lax.ppermute(value, ('core', 'zh', 'zl'), here)]
    ppermute x10, waiting for transfers between devices: 31.8 us -> 54.1 us  [total(): lax.ppermute(value, axis, [(i, i ^ step) for i in range(count)])]
    ppermute x3, waiting for transfers between devices: 52.6 us -> 30.8 us  [join_halves(): return part + lax.ppermute(part, BOTH, CROSS_BACK)]
    ppermute x5, waiting for transfers between devices: 7.85 us -> 25.8 us  [shifted(): lax.ppermute(value, BLOCKS, [(source, source + steps) for source in range...]
  transfers between devices with their start and end apart: 88 -> 90, of which waited for: 33 -> 33; matrix products, arithmetic and copies ran while one was open for 19% -> 20% of each run, Pallas kernels for 12% -> 13%
where the time goes in v6:
time: 937 us; the launch traced here: 925 us
  waiting for transfers between devices  308 us (33%)
  starting transfers between devices  220 us (23%)
  Pallas kernels  163 us (17%)
  local copies, waits for them, and re-layouts  91 us (10%)
  other arithmetic  75.8 us (8%)
  matrix products  50.3 us (5%)
  between operations  16.3 us (2%)
    pallas_call x12, Pallas kernels, call(): pl.pallas_call(kernel, grid=(count,), in_specs=[spec for spec, _ in ins],...  146 us
    ppermute x18, waiting for transfers between devices, swap(): return lax.ppermute(value, axis, SWAP)  106 us
    ppermute x10, waiting for transfers between devices, total(): lax.ppermute(value, axis, [(i, i ^ step) for i in range(count)])  54.1 us
    dot_general x18, matrix products, mm(): lax.dot_general(left, right, (dims, ((), ())), preferred_element_type=f32...  50.3 us
    ppermute x18, starting transfers between devices, swap(): return lax.ppermute(value, axis, SWAP)  37.5 us
    ppermute x12, waiting for transfers between devices, chain(): got = lax.ppermute(part, BLOCKS, [(i, i ^ step) for i in range(count)])  36.7 us
    ppermute x5, starting transfers between devices, shifted(): lax.ppermute(value, BLOCKS, [(source, source + steps) for source in range...  36.5 us
    ppermute x3, starting transfers between devices, place_rows(): lax.ppermute(take(full, 1 - core, 2), BOTH, CORE_OUT)  32.3 us
  transfers between devices with their start and end apart: 90, of which 33 were waited for; matrix products, arithmetic and copies ran while one was open for 20% of the time, Pallas kernels for 13%

profile of v6, /device:TPU:0, one launch (start us, length us, event | category | flops | bytes accessed | tf_op | source)
XLA Modules:
  0.0 925.0 jit_solution(1826604734823093777)
XLA Ops:
  8.7 5.9 collective-permute-start.2
  47.0 7.6 collective-permute-start.4
  57.1 25.4 %collective-permute-done.3.refs_2_ = f32[256,1024]{1,0:T(8,128)} collective-permute-done((f32[256,1024]{1,0:T(8,128)S(1)}, f32[256,1024]{1,0:T(8,128)}, u32[]{:S(2)}, u32[]{:S(2)}) %collective-permute-start.3) | collective-permute-done | bytes 1048608 | tf_op jit(solution)/shard_map/ppermute | solution.py:598
  95.4 19.8 %collective-permute-start.11 = (f32[8,768]{1,0:T(8,128)S(1)}, f32[8,768]{1,0:T(8,128)S(1)}, u32[]{:S(2)}, u32[]{:S(2)}) collective-permute-start(f32[8,768]{1,0:T(8,128)S(1)} %fusion), channel_id=1, source_target_pairs={{0,2},{2,8},{8,10},{10,16},{16,18},{18,24},{24,26},{1,3},{3,9},{9,... | collective-permute-start | bytes 73736 | tf_op jit(solution)/shard_map/ppermute | solution.py:384
  118.5 15.5 %in_proj_conv.2 = (bf16[1024,1024]{1,0:T(8,128)(2,1)}, f32[1024,768]{1,0:T(8,128)}, f32[1024,768]{1,0:T(8,128)}, f32[1024,128]{1,0:T(8,128)}, f32[1024,128]{1,0:...) custom-call(s32[2]{0:T(128)} %pad_add_fusion.place, ...), custom_call_target="tpu_custom_call" | custom-call | flops 18400000000 | bytes 1048576 | tf_op jit(solution)/shard_map/in_proj_conv/pallas_call | solution.py:350
  163.2 11.1 %gate_out_proj.2 = (f32[1024,512]{1,0:T(8,128)}, bf16[1024,512]{1,0:T(8,128)(2,1)}, f32[1024,1024]{1,0:T(8,128)}, f32[8,1024]{1,0:T(8,128)}) custom-call(f32[1024,512]{1,0:T(8,128)} %ssd_within.2.yin, f32[1024,768]{1,0:T(8,128)} %get-tuple-element.159.cpre, f32[1024,128]{1,0:T(8,128)} %get-tuple-element.156.cum, bf16[1024,256]{1,0:T(8,128)(2,1)} %get-tuple-element.158.bc, ...), custom_call_target="tpu_custom_call" | custom-call | flops 13799999488 | bytes 1048576 | tf_op jit(solution)/shard_map/gate_out_proj/pallas_call | solution.py:350
  176.0 35.7 %collective-permute-start.20 = (f32[512,1024]{1,0:T(8,128)S(1)}, f32[512,1024]{1,0:T(8,128)}, u32[]{:S(2)}, u32[]{:S(2)}) collective-permute-start(f32[512,1024]{1,0:T(8,128)S(1)} %constant_dynamic-slice_fusion.13), channel_id=1, source_target_pairs={{0,4},{4,0},{1,5},{5,1},{2,6},{6,2},{3,7},{7,3},{8,12},{12,8},{9,1... | collective-permute-start | bytes 6291464 | tf_op jit(solution)/shard_map/ppermute | solution.py:407
  229.5 16.3 %collective-permute-done.19 = f32[8,1024]{1,0:T(8,128)S(1)} collective-permute-done((f32[8,1024]{1,0:T(8,128)S(1)}, f32[8,1024]{1,0:T(8,128)S(1)}, u32[]{:S(2)}, u32[]{:S(2)}) %collective-permute-start.19) | collective-permute-done | bytes 32800 | tf_op jit(solution)/shard_map/ppermute | solution.py:415
  255.3 18.7 %collective-permute-done.25.refs_1_ = f32[256,1024]{1,0:T(8,128)} collective-permute-done((f32[256,1024]{1,0:T(8,128)}, f32[256,1024]{1,0:T(8,128)}, u32[]{:S(2)}, u32[]{:S(2)}) %collective-permute-start.25) | collective-permute-done | bytes 1048608 | tf_op jit(solution)/shard_map/ppermute | solution.py:407
  284.6 12.5 %collective-permute-start.28 = (f32[8,768]{1,0:T(8,128)S(1)}, f32[8,768]{1,0:T(8,128)S(1)}, u32[]{:S(2)}, u32[]{:S(2)}) collective-permute-start(f32[8,768]{1,0:T(8,128)S(1)} %fusion.2), channel_id=1, source_target_pairs={{0,2},{2,8},{8,10},{10,16},{16,18},{18,24},{24,26},{1,3},{3,9},{9,... | collective-permute-start | bytes 73736 | tf_op jit(solution)/shard_map/ppermute | solution.py:384
  300.2 17.2 %in_proj_conv.3 = (bf16[1024,1024]{1,0:T(8,128)(2,1)}, f32[1024,768]{1,0:T(8,128)}, f32[1024,768]{1,0:T(8,128)}, f32[1024,128]{1,0:T(8,128)}, f32[1024,128]{1,0:...) custom-call(s32[2]{0:T(128)} %pad_add_fusion.place, ...), custom_call_target="tpu_custom_call" | custom-call | flops 18400000000 | bytes 1048576 | tf_op jit(solution)/shard_map/in_proj_conv/pallas_call | solution.py:350
  323.8 9.2 collective-permute-done.29
  349.7 14.1 %gate_out_proj.3 = (f32[1024,512]{1,0:T(8,128)}, bf16[1024,512]{1,0:T(8,128)(2,1)}, f32[1024,1024]{1,0:T(8,128)}, f32[8,1024]{1,0:T(8,128)}) custom-call(f32[1024,512]{1,0:T(8,128)} %ssd_within.3.yin, f32[1024,768]{1,0:T(8,128)} %get-tuple-element.184.cpre, f32[1024,128]{1,0:T(8,128)} %get-tuple-element.181.cum, bf16[1024,256]{1,0:T(8,128)(2,1)} %get-tuple-element.183.bc, ...), custom_call_target="tpu_custom_call" | custom-call | flops 13799999488 | bytes 1048576 | tf_op jit(solution)/shard_map/gate_out_proj/pallas_call | solution.py:350
  377.4 10.0 %gate_back.2 = (bf16[1024,1024]{1,0:T(8,128)(2,1)}, bf16[1024,512]{1,0:T(8,128)(2,1)}, bf16[1024,512]{1,0:T(8,128)(2,1)}, f32[4,128,512]{2,1,0:T(8,128)}, f32[4,...) custom-call(s32[2]{0:T(128)} %pad_add_fusion.place, f32[1024,1]{1,0:T(8,128)} %copy.107.scale, ...), custom_call_target="tpu_custom_call" | custom-call | flops 11500000256 | bytes 1048576 | tf_op jit(solution)/shard_map/gate_back/pallas_call | solution.py:350
  395.2 7.7 ssd_within_back.2
  410.7 7.2 collective-permute-done.41
  422.9 6.7 collective-permute-done.42
  443.2 20.3 %in_proj_conv_back.2 = (bf16[1024,896]{1,0:T(8,128)(2,1)}, f32[8,768]{1,0:T(8,128)}, f32[8,768]{1,0:T(8,128)}, f32[8,768]{1,0:T(8,128)}, f32[8,128]{1,0:T(8,128)}, /*index=5*/f32[8,512]{1,0:T(8,128)}) custom-call(f32[1024,512]{1,0:T(8,128)} %get-tuple-element.202.uin, f32[1024,256]{1,0:T(8,128)} %get-tuple-element.203.dbc, ...), custom_call_target="tpu_custom_call" | custom-call | flops 23000000512 | bytes 1048576 | tf_op jit(solution)/shard_map/in_proj_conv_back/pallas_call | solution.py:350
  465.0 22.0 %collective-permute-done.43 = f32[8,768]{1,0:T(8,128)S(1)} collective-permute-done((f32[8,768]{1,0:T(8,128)}, f32[8,768]{1,0:T(8,128)S(1)}, u32[]{:S(2)}, u32[]{:S(2)}) %collective-permute-start.43) | collective-permute-done | bytes 24608 | tf_op jit(solution)/shard_map/ppermute | solution.py:384
  503.9 21.7 %collective-permute-done.45 = f32[256,1024]{1,0:T(8,128)} collective-permute-done((f32[256,1024]{1,0:T(8,128)}, f32[256,1024]{1,0:T(8,128)}, u32[]{:S(2)}, u32[]{:S(2)}) %collective-permute-start.45) | collective-permute-done | bytes 1048608 | tf_op jit(solution)/shard_map/ppermute | solution.py:407
  537.0 20.3 %collective-permute-done.48.refs_1_ = f32[256,1024]{1,0:T(8,128)} collective-permute-done((f32[256,1024]{1,0:T(8,128)}, f32[256,1024]{1,0:T(8,128)}, u32[]{:S(2)}, u32[]{:S(2)}) %collective-permute-start.48) | collective-permute-done | bytes 1048608 | tf_op jit(solution)/shard_map/ppermute | solution.py:407
  560.2 17.8 %collective-permute-done.46 = f32[256]{0:T(256)S(1)} collective-permute-done((f32[256]{0:T(256)S(1)}, f32[256]{0:T(256)S(1)}, u32[]{:S(2)}, u32[]{:S(2)}) %collective-permute-start.46) | collective-permute-done | bytes 1056 | tf_op jit(solution)/shard_map/ppermute | solution.py:407
  585.6 11.2 %gate_back.3 = (bf16[1024,1024]{1,0:T(8,128)(2,1)}, bf16[1024,512]{1,0:T(8,128)(2,1)}, bf16[1024,512]{1,0:T(8,128)(2,1)}, f32[4,128,512]{2,1,0:T(8,128)}, f32[4,...) custom-call(s32[2]{0:T(128)} %pad_add_fusion.place, f32[1024,1]{1,0:T(8,128)} %copy.115.scale, ...), custom_call_target="tpu_custom_call" | custom-call | flops 11500000256 | bytes 1048576 | tf_op jit(solution)/shard_map/gate_back/pallas_call | solution.py:350
  601.0 7.7 ssd_within_back.3
  639.8 20.3 %in_proj_conv_back.3 = (bf16[1024,896]{1,0:T(8,128)(2,1)}, f32[8,768]{1,0:T(8,128)}, f32[8,768]{1,0:T(8,128)}, f32[8,768]{1,0:T(8,128)}, f32[8,128]{1,0:T(8,128)}, /*index=5*/f32[8,512]{1,0:T(8,128)}) custom-call(f32[1024,512]{1,0:T(8,128)} %get-tuple-element.222.uin, f32[1024,256]{1,0:T(8,128)} %get-tuple-element.223.dbc, ...), custom_call_target="tpu_custom_call" | custom-call | flops 23000000512 | bytes 1048576 | tf_op jit(solution)/shard_map/in_proj_conv_back/pallas_call | solution.py:350
  660.0 19.0 %collective-permute-done.58 = f32[256,1536]{1,0:T(8,128)S(1)} collective-permute-done((f32[256,1536]{1,0:T(8,128)S(1)}, f32[256,1536]{1,0:T(8,128)S(1)}, u32[]{:S(2)}, u32[]{:S(2)}) %collective-permute-start.58) | collective-permute-done | bytes 1572896 | tf_op jit(solution)/shard_map/ppermute | solution.py:1082
  744.3 10.6 %collective-permute-done.61 = f32[256,1024]{1,0:T(8,128)} collective-permute-done((f32[256,1024]{1,0:T(8,128)}, f32[256,1024]{1,0:T(8,128)}, u32[]{:S(2)}, u32[]{:S(2)}) %collective-permute-start.61) | collective-permute-done | bytes 1048608 | tf_op jit(solution)/shard_map/ppermute | solution.py:407
  775.6 27.7 %collective-permute-done.72 = f32[128,2,256]{2,0,1:T(8,128)} collective-permute-done((f32[128,2,256]{2,0,1:T(8,128)S(1)}, f32[128,2,256]{2,0,1:T(8,128)}, u32[]{:S(2)}, u32[]{:S(2)}) %collective-permute-start.72) | collective-permute-done | bytes 262176 | tf_op jit(solution)/shard_map/ppermute | solution.py:415
  806.6 10.2 %collective-permute-start.78 = (f32[128,1536]{1,0:T(8,128)}, f32[128,1536]{1,0:T(8,128)}, u32[]{:S(2)}, u32[]{:S(2)}) collective-permute-start(f32[128,1536]{1,0:T(8,128)} %constant_dynamic-slice_fusion.2), channel_id=1, source_target_pairs={{0,4},{6,2},{1,5},{7,3},{8,12},{14,10},{9,13},{15,11},{16,20},{22,... | collective-permute-start | bytes 2359304 | tf_op jit(solution)/shard_map/ppermute | solution.py:1087
  818.2 28.2 %reduce-scatter.23.cloned.1.call-done = f32[256,512]{1,0:T(8,128)} async-done(((f32[1024,512]{1,0:T(8,128)}), f32[256,512]{1,0:T(8,128)}) %reduce-scatter.23.cloned.1.call-update) | async-done | bytes 524304 | tf_op jit(solution)/shard_map/reduce_scatter | solution.py:1018
  874.5 11.8 %collective-permute-done.79 = f32[256,512]{1,0:T(8,128)S(1)} collective-permute-done((f32[256,512]{1,0:T(8,128)S(1)}, f32[256,512]{1,0:T(8,128)S(1)}, u32[]{:S(2)}, u32[]{:S(2)}) %collective-permute-start.79) | collective-permute-done | bytes 524320 | tf_op jit(solution)/shard_map/ppermute | solution.py:1082
  886.4 20.8 %collective-permute-start.80 = (f32[128,512]{1,0:T(8,128)S(1)}, f32[128,512]{1,0:T(8,128)S(1)}, u32[]{:S(2)}, u32[]{:S(2)}) collective-permute-start(f32[128,512]{1,0:T(8,128)S(1)} %constant_dynamic-slice_fusion.1), channel_id=1, source_target_pairs={{0,4},{6,2},{1,5},{7,3},{8,12},{14,10},{9,13},{15,11},{16,20},{22,... | collective-permute-start | bytes 786440 | tf_op jit(solution)/shard_map/ppermute | solution.py:1087
  (601 shorter events, 398.4 us)
Async XLA Ops:
  7.2 629.0 %reduce-scatter.11.cloned.1.call-start = ((), (), s32[]{:S(2)}) async-start(), calls=%async_computation.9 | async-start | bytes 2621440 | tf_op jit(solution)/shard_map/reduce_scatter | solution.py:937
  18.2 38.9 %collective-permute-start.1 = (f32[256,512]{1,0:T(8,128)}, f32[256,512]{1,0:T(8,128)}, u32[]{:S(2)}, u32[]{:S(2)}) collective-permute-start(f32[256,512]{1,0:T(8,128)} %dynamic-slice_convert_fusion), channel_id=1, source_target_pairs={{0,2},{6,4},{1,3},{7,5},{8,10},{14,12},{9,11},{15,13},{16,18},{22,... | collective-permute-start | bytes 1572872 | tf_op jit(solution)/shard_map/ppermute | solution.py:598
  24.5 68.9 %collective-permute-start = (f32[1024,1024]{1,0:T(8,128)}, f32[1024,1024]{1,0:T(8,128)}, u32[]{:S(2)}, u32[]{:S(2)}) collective-permute-start(f32[1024,1024]{1,0:T(8,128)} %convert_element_type.74), channel_id=1, source_target_pairs={{0,4},{6,2},{1,5},{7,3},{8,12},{14,10},{9,13},{15,11},{16,20},{22,... | collective-permute-start | bytes 12582920 | tf_op jit(solution)/shard_map/ppermute | solution.py:538
  176.0 39.6 %collective-permute-start.20 = (f32[512,1024]{1,0:T(8,128)S(1)}, f32[512,1024]{1,0:T(8,128)}, u32[]{:S(2)}, u32[]{:S(2)}) collective-permute-start(f32[512,1024]{1,0:T(8,128)S(1)} %constant_dynamic-slice_fusion.13), channel_id=1, source_target_pairs={{0,4},{4,0},{1,5},{5,1},{2,6},{6,2},{3,7},{7,3},{8,12},{12,8},{9,1... | collective-permute-start | bytes 6291464 | tf_op jit(solution)/shard_map/ppermute | solution.py:407
  225.8 48.8 %collective-permute-start.23 = (f32[256,1536]{1,0:T(8,128)}, f32[256,1536]{1,0:T(8,128)}, u32[]{:S(2)}, u32[]{:S(2)}) collective-permute-start(f32[256,1536]{1,0:T(8,128)} %collective-permute-done.4.refs_3_), channel_id=1, source_target_pairs={{2,18},{4,20},{10,26},{12,28},{18,2},{20,4},{26,10},{28,12},{3,19}... | collective-permute-start | bytes 4718600 | tf_op jit(solution)/shard_map/ppermute | solution.py:613
  227.7 46.9 %collective-permute-start.24 = (f32[256,1536]{1,0:T(8,128)}, f32[256,1536]{1,0:T(8,128)}, u32[]{:S(2)}, u32[]{:S(2)}) collective-permute-start(f32[256,1536]{1,0:T(8,128)} %collective-permute-done.4.refs_3_), channel_id=1, source_target_pairs={{2,26},{4,28},{10,18},{12,20},{18,10},{20,12},{26,2},{28,4},{3,27}... | collective-permute-start | bytes 4718600 | tf_op jit(solution)/shard_map/ppermute | solution.py:613
  251.8 68.8 %collective-permute-start.32 = (f32[1024,1024]{1,0:T(8,128)}, f32[1024,1024]{1,0:T(8,128)}, u32[]{:S(2)}, u32[]{:S(2)}) collective-permute-start(f32[1024,1024]{1,0:T(8,128)} %convert_element_type.81), channel_id=1, source_target_pairs={{0,4},{6,2},{1,5},{7,3},{8,12},{14,10},{9,13},{15,11},{16,20},{22,... | collective-permute-start | bytes 12582920 | tf_op jit(solution)/shard_map/ppermute | solution.py:538
  394.6 241.5 %reduce-scatter.9.cloned.1.call-start = ((), (), s32[]{:S(2)}) async-start(), calls=%async_computation.8 | async-start | bytes 2621440 | tf_op jit(solution)/shard_map/reduce_scatter | solution.py:937
  441.5 51.3 %collective-permute-start.39 = (f32[256,1024]{1,0:T(8,128)S(1)}, f32[256,1024]{1,0:T(8,128)}, u32[]{:S(2)}, u32[]{:S(2)}) collective-permute-start(f32[256,1024]{1,0:T(8,128)S(1)} %multiply_add_fusion.2.value), channel_id=1, source_target_pairs={{4,2},{2,4},{5,3},{3,5},{12,10},{10,12},{13,11},{11,13},{20,18},{1... | collective-permute-start | bytes 3145736 | tf_op jit(solution)/shard_map/ppermute | solution.py:487
  464.9 171.2 %reduce-scatter.13.cloned.1.call-start = ((), (), s32[]{:S(2)}) async-start(), calls=%async_computation.10 | async-start | bytes 1310720 | tf_op jit(solution)/shard_map/reduce_scatter | solution.py:1018
  503.8 132.3 %reduce-scatter.15.cloned.1.call-start = ((), (), s32[]{:S(2)}) async-start(), calls=%async_computation.11 | async-start | bytes 2621440 | tf_op jit(solution)/shard_map/reduce_scatter | solution.py:1018
  532.2 158.3 %collective-permute-start.52 = (f32[256,1024]{1,0:T(8,128)}, f32[256,1024]{1,0:T(8,128)S(1)}, u32[]{:S(2)}, u32[]{:S(2)}) collective-permute-start(f32[256,1024]{1,0:T(8,128)} %collective-permute-done.37.mine), channel_id=1, source_target_pairs={{2,3},{3,2},{4,5},{5,4},{10,11},{11,10},{12,13},{13,12},{18,19},{1... | collective-permute-start | bytes 3145736 | tf_op jit(solution)/shard_map/ppermute | solution.py:504
  532.9 157.6 %collective-permute-start.53 = (f32[256,1024]{1,0:T(8,128)}, f32[256,1024]{1,0:T(8,128)S(1)}, u32[]{:S(2)}, u32[]{:S(2)}) collective-permute-start(f32[256,1024]{1,0:T(8,128)} %collective-permute-done.38.near), channel_id=1, source_target_pairs={{0,1},{1,0},{6,7},{7,6},{8,9},{9,8},{14,15},{15,14},{16,17},{17,16... | collective-permute-start | bytes 3145736 | tf_op jit(solution)/shard_map/ppermute | solution.py:494
  536.6 49.0 %collective-permute-start.49 = (f32[256,1024]{1,0:T(8,128)}, f32[256,1024]{1,0:T(8,128)}, u32[]{:S(2)}, u32[]{:S(2)}) collective-permute-start(f32[256,1024]{1,0:T(8,128)} %get-tuple-element.335.refs_0_), channel_id=1, source_target_pairs={{0,4},{4,0},{1,5},{5,1},{2,6},{6,2},{3,7},{7,3},{8,12},{12,8},{9,1... | collective-permute-start | bytes 3145736 | tf_op jit(solution)/shard_map/ppermute | solution.py:407
  536.7 41.3 %collective-permute-start.46 = (f32[256]{0:T(256)S(1)}, f32[256]{0:T(256)S(1)}, u32[]{:S(2)}, u32[]{:S(2)}) collective-permute-start(f32[256]{0:T(256)S(1)} %get-tuple-element.334), channel_id=1, source_target_pairs={{0,1},{1,0},{2,3},{3,2},{4,5},{5,4},{6,7},{7,6},{8,9},{9,8},{10,11... | collective-permute-start | bytes 3080 | tf_op jit(solution)/shard_map/ppermute | solution.py:407
  580.7 176.2 %reduce-scatter.17.cloned.1.call-start = ((), (), s32[]{:S(2)}) async-start(), calls=%async_computation.12 | async-start | bytes 1310720 | tf_op jit(solution)/shard_map/reduce_scatter | solution.py:1018
  580.7 109.8 %collective-permute-start.54 = (f32[256,1024]{1,0:T(8,128)}, f32[256,1024]{1,0:T(8,128)}, u32[]{:S(2)}, u32[]{:S(2)}) collective-permute-start(f32[256,1024]{1,0:T(8,128)} %collective-permute-done.39.theirs), channel_id=1, source_target_pairs={{2,3},{3,2},{4,5},{5,4},{10,11},{11,10},{12,13},{13,12},{18,19},{1... | collective-permute-start | bytes 3145736 | tf_op jit(solution)/shard_map/ppermute | solution.py:505
  631.9 58.6 %collective-permute-start.51 = (f32[256,1024]{1,0:T(8,128)S(1)}, f32[256,1024]{1,0:T(8,128)}, u32[]{:S(2)}, u32[]{:S(2)}) collective-permute-start(f32[256,1024]{1,0:T(8,128)S(1)} %multiply_add_fusion.2.value), channel_id=1, source_target_pairs={{0,1},{1,0},{6,7},{7,6},{8,9},{9,8},{14,15},{15,14},{16,17},{17,16... | collective-permute-start | bytes 3145736 | tf_op jit(solution)/shard_map/ppermute | solution.py:494
  638.5 40.6 %collective-permute-start.58 = (f32[256,1536]{1,0:T(8,128)S(1)}, f32[256,1536]{1,0:T(8,128)S(1)}, u32[]{:S(2)}, u32[]{:S(2)}) collective-permute-start(f32[256,1536]{1,0:T(8,128)S(1)} %constant_dynamic-update-slice_fusion), channel_id=1, source_target_pairs={{2,0},{4,6},{3,1},{5,7},{10,8},{12,14},{11,9},{13,15},{18,16},{20,... | collective-permute-start | bytes 4718600 | tf_op jit(solution)/shard_map/ppermute | solution.py:1082
  702.0 116.1 %reduce-scatter.21.cloned.1.call-start = ((), (), s32[]{:S(2)}) async-start(), calls=%async_computation.14 | async-start | bytes 2621440 | tf_op jit(solution)/shard_map/reduce_scatter | solution.py:937
  702.6 115.5 %reduce-scatter.19.cloned.1.call-start = ((), (), s32[]{:S(2)}) async-start(), calls=%async_computation.13 | async-start | bytes 2621440 | tf_op jit(solution)/shard_map/reduce_scatter | solution.py:937
  721.9 124.5 %reduce-scatter.23.cloned.1.call-start = ((), (), s32[]{:S(2)}) async-start(), calls=%async_computation.15 | async-start | bytes 2621440 | tf_op jit(solution)/shard_map/reduce_scatter | solution.py:1018
  761.5 42.9 %collective-permute-start.62 = (f32[256,1024]{1,0:T(8,128)S(1)}, f32[256,1024]{1,0:T(8,128)S(1)}, u32[]{:S(2)}, u32[]{:S(2)}) collective-permute-start(f32[256,1024]{1,0:T(8,128)S(1)} %multiply_add_fusion.value), channel_id=1, source_target_pairs={{0,2},{6,4},{1,3},{7,5},{8,10},{14,12},{9,11},{15,13},{16,18},{22,... | collective-permute-start | bytes 3145736 | tf_op jit(solution)/shard_map/ppermute | solution.py:487
  763.0 41.5 %collective-permute-start.63 = (f32[256,1024]{1,0:T(8,128)S(1)}, f32[256,1024]{1,0:T(8,128)}, u32[]{:S(2)}, u32[]{:S(2)}) collective-permute-start(f32[256,1024]{1,0:T(8,128)S(1)} %multiply_add_fusion.value), channel_id=1, source_target_pairs={{4,2},{2,4},{5,3},{3,5},{12,10},{10,12},{13,11},{11,13},{20,18},{1... | collective-permute-start | bytes 3145736 | tf_op jit(solution)/shard_map/ppermute | solution.py:487
  764.6 39.8 %collective-permute-start.64 = (f32[256,1024]{1,0:T(8,128)S(1)}, f32[256,1024]{1,0:T(8,128)}, u32[]{:S(2)}, u32[]{:S(2)}) collective-permute-start(f32[256,1024]{1,0:T(8,128)S(1)} %multiply_add_fusion.value), channel_id=1, source_target_pairs={{4,0},{2,6},{5,1},{3,7},{12,8},{10,14},{13,9},{11,15},{20,16},{18,... | collective-permute-start | bytes 3145736 | tf_op jit(solution)/shard_map/ppermute | solution.py:487
  765.9 38.5 %collective-permute-start.65 = (f32[256,1024]{1,0:T(8,128)S(1)}, f32[256,1024]{1,0:T(8,128)}, u32[]{:S(2)}, u32[]{:S(2)}) collective-permute-start(f32[256,1024]{1,0:T(8,128)S(1)} %multiply_add_fusion.value), channel_id=1, source_target_pairs={{0,1},{1,0},{6,7},{7,6},{8,9},{9,8},{14,15},{15,14},{16,17},{17,16... | collective-permute-start | bytes 3145736 | tf_op jit(solution)/shard_map/ppermute | solution.py:494
  806.6 65.8 %collective-permute-start.78 = (f32[128,1536]{1,0:T(8,128)}, f32[128,1536]{1,0:T(8,128)}, u32[]{:S(2)}, u32[]{:S(2)}) collective-permute-start(f32[128,1536]{1,0:T(8,128)} %constant_dynamic-slice_fusion.2), channel_id=1, source_target_pairs={{0,4},{6,2},{1,5},{7,3},{8,12},{14,10},{9,13},{15,11},{16,20},{22,... | collective-permute-start | bytes 2359304 | tf_op jit(solution)/shard_map/ppermute | solution.py:1087
  818.1 52.4 %collective-permute-start.81 = (f32[128,2,256]{2,0,1:T(8,128)S(1)}, f32[128,2,256]{2,0,1:T(8,128)}, u32[]{:S(2)}, u32[]{:S(2)}) collective-permute-start(f32[128,2,256]{2,0,1:T(8,128)S(1)} %add.419), channel_id=1, source_target_pairs={{0,2},{2,0},{1,3},{3,1},{4,6},{6,4},{5,7},{7,5},{8,10},{10,8},{9,1... | collective-permute-start | bytes 786440 | tf_op jit(solution)/shard_map/ppermute | solution.py:415
  850.1 57.2 %collective-permute-start.76 = (f32[256,1024]{1,0:T(8,128)}, f32[256,1024]{1,0:T(8,128)}, u32[]{:S(2)}, u32[]{:S(2)}) collective-permute-start(f32[256,1024]{1,0:T(8,128)} %constant_dynamic-update-slice_fusion.3), channel_id=1, source_target_pairs={{2,0},{4,6},{3,1},{5,7},{10,8},{12,14},{11,9},{13,15},{18,16},{20,... | collective-permute-start | bytes 3145736 | tf_op jit(solution)/shard_map/ppermute | solution.py:1082
  855.7 54.7 %collective-permute-start.73 = (f32[256,1024]{1,0:T(8,128)S(1)}, f32[256,1024]{1,0:T(8,128)}, u32[]{:S(2)}, u32[]{:S(2)}) collective-permute-start(f32[256,1024]{1,0:T(8,128)S(1)} %collective-permute-done.62.mine), channel_id=1, source_target_pairs={{2,3},{3,2},{4,5},{5,4},{10,11},{11,10},{12,13},{13,12},{18,19},{1... | collective-permute-start | bytes 3145736 | tf_op jit(solution)/shard_map/ppermute | solution.py:504
  859.3 51.2 %collective-permute-start.74 = (f32[256,1024]{1,0:T(8,128)}, f32[256,1024]{1,0:T(8,128)S(1)}, u32[]{:S(2)}, u32[]{:S(2)}) collective-permute-start(f32[256,1024]{1,0:T(8,128)} %collective-permute-done.64.near), channel_id=1, source_target_pairs={{0,1},{1,0},{6,7},{7,6},{8,9},{9,8},{14,15},{15,14},{16,17},{17,16... | collective-permute-start | bytes 3145736 | tf_op jit(solution)/shard_map/ppermute | solution.py:494
  870.5 40.0 %collective-permute-start.75 = (f32[256,1024]{1,0:T(8,128)}, f32[256,1024]{1,0:T(8,128)S(1)}, u32[]{:S(2)}, u32[]{:S(2)}) collective-permute-start(f32[256,1024]{1,0:T(8,128)} %collective-permute-done.63.theirs), channel_id=1, source_target_pairs={{2,3},{3,2},{4,5},{5,4},{10,11},{11,10},{12,13},{13,12},{18,19},{1... | collective-permute-start | bytes 3145736 | tf_op jit(solution)/shard_map/ppermute | solution.py:505
  (144 other events, 2073.8 us)
Sparse Core Ops, SparseCore 0:
  394.7 39.4 reduce-scatter.10
  465.0 39.4 reduce-scatter.8
  507.4 27.7 reduce-scatter.12
  580.8 35.4 reduce-scatter.14
  702.2 28.1 reduce-scatter.16
  733.5 36.1 reduce-scatter.20
  772.7 35.1 reduce-scatter.18
  811.1 35.1 reduce-scatter.22

commit v7 on v6

--- a/solution.py
+++ b/solution.py
@@ -384,7 +384,7 @@
     return lax.ppermute(value, BLOCKS, [(source, source + steps) for source in range(leading, last)])
 
 
-def chain(part, reverse):
+def chain(part, reverse, stages):
     count = lax.axis_size(BLOCKS)
     place = lax.axis_index(BLOCKS)
     state, decay = part[:STATE], part[STATE : STATE + 1]
@@ -394,6 +394,7 @@
         got = lax.ppermute(part, BLOCKS, [(i, i ^ step) for i in range(count)])
         got_state, got_decay = got[:STATE], got[STATE : STATE + 1]
         later = ((place & step) == 0) if reverse else ((place & step) != 0)
+        stages.append(got)
         entry = jnp.where(later, entry + reach * got_state, entry)
         reach = jnp.where(later, reach * got_decay, reach)
         state = jnp.where(later, state + decay * got_state, got_state + got_decay * state)
@@ -432,11 +433,9 @@
     return lax.optimization_barrier((value, *marks))[0]
 
 
-def scatter_sum(part, mark=(), stages=None):
+def scatter_sum(part, mark=()):
     core, near = lax.axis_index("core"), lax.axis_index("zl")
     half = take(part, core, 2) + behind(swap(take(part, 1 - core, 2), "core"), *mark)
-    if stages is not None:
-        stages.append(half)
     if lax.axis_size("zl") == 2:
         return take(half, near, 2) + swap(take(half, 1 - near, 2), "zl")
     return lax.psum_scatter(half, "zl", scatter_dimension=0, tiled=True)
@@ -671,12 +670,10 @@
     dt_own = w_dt.astype(f32).reshape(LAYERS, width * heads // LANES, LANES)
     dt_sent = lax.ppermute(dt_own, BOTH, CROSS)
     dt_all = pad_lanes(jnp.where(held, dt_own, dt_sent).reshape(LAYERS, width, heads))
+    first_x = weights_over([w_x[0]])
     hidden = to_block(x_input.astype(f32))
-    first_x = weights_over([w_x[0]])
-    first_rest = weights_over([w_z[0], w_out[0]], dt_sent)
-    second_all = weights_over([w_x[1], w_z[1], w_out[1]], dt_sent)
-    first_x, first_rest, second_all = behind((first_x, first_rest, second_all))
-    (wall,) = gather_weights(first_x, [w_x[0]], (w_bc[0], dt_all[0]))
+    first_rest = weights_over([w_z[0], w_out[0]], first_x)
+    (wall,) = gather_weights(first_x, [w_x[0]], (w_bc[0], dt_all[0]), (first_rest,))
     seg = to_block(seg_ids.astype(f32))
     small = jnp.concatenate(
         [
@@ -784,7 +781,8 @@
             wz, wout = gather_weights(
                 behind(first_rest, wall), [w_z[0], w_out[0]], third=(send,)
             )
-            cotangent = to_block(behind(cotangent, send).astype(f32))
+            cotangent = behind(cotangent, send).astype(f32)
+            cot_sent = lax.ppermute(cotangent, BOTH, CORE_OUT)
         else:
             wz, wout = next_wz, next_wout
         zval = mm(normed, wz)
@@ -803,7 +801,12 @@
             6,
             "ssd_within",
         )
-        entry = chain(send, False)
+        stages = []
+        entry = chain(send, False, stages)
+        if layer == 0:
+            second_all = weights_over([w_x[1], w_z[1], w_out[1]], stages[0])
+            entry = behind(entry, second_all, cot_sent)
+            cotangent = jnp.where(held, cotangent, cot_sent)
         y, gate_in, proj, sums = call(
             out_kernel,
             count,
@@ -844,15 +847,15 @@
             )
         )
         if layer < LAYERS - 1:
-            next_wall, next_wz, next_wout = gather_weights(
-                behind(second_all, entry),
-                [w_x[1], w_z[1], w_out[1]],
-                (w_bc[1], dt_all[1]),
-                third=(gate_scale,),
-            )
             proj_sum = scatter_sum(proj)
             stored[layer]["proj_sum"] = proj_sum
             hidden_own = hidden_own + own_rows(gate_scale)[:, None] * proj_sum
+            next_wall, next_wz, next_wout = gather_weights(
+                behind(second_all, proj),
+                [w_x[1], w_z[1], w_out[1]],
+                (w_bc[1], dt_all[1]),
+                third=(hidden_own,),
+            )
             hidden = gather_pieces(hidden_own)
 
     grad_h = [cotangent]
@@ -900,6 +903,10 @@
             10,
             "gate_back",
         )
+        if layer == LAYERS - 1:
+            last_sum = scatter_sum(kept["proj"], (gate_scale,))
+            hidden_own = hidden_own + own_rows(gate_scale)[:, None] * last_sum
+            dz, gproj = behind((dz, gproj), hidden_own)
         u, dbc = call(
             intra_back_kernel,
             count,
@@ -919,24 +926,19 @@
             8,
             "ssd_within_back",
         )
-        gout = chain(gsend, True)
+        stages = []
+        gout = chain(gsend, True, stages)
+        round_one = stages[0]
         if layer == LAYERS - 1:
-            last_sum = scatter_sum(kept["proj"], (dy,))
-            hidden_own = hidden_own + own_rows(gate_scale)[:, None] * last_sum
+            out_parts = cross_over(hidden_own)
             u = behind(u, hidden_own)
-            out_parts = cross_over(hidden_own)
         else:
-            out_swaps = near_swaps(behind(hidden_own, dy), *out_parts)
-            g_out, g_z, _, g_x = behind(matrices[LAYERS - 1], u)
-            first_sums = join_halves([g_out, g_z, g_x])
+            out_swaps = near_swaps(*behind((hidden_own, *out_parts), round_one))
+            first_sums = join_halves(behind(matrices[1][:, : 3 * inner], round_one))
         grad_wout = mm(gproj, kept["gate_in"], ((0,), (0,)))
         grad_wz = mm(kept["normed"], dz, ((0,), (0,)))
         partial_z = mm(dz, kept["wz"], ((1,), (1,)))
         u = behind(u, grad_wout, grad_wz, partial_z)
-        matrices[layer] = [
-            lax.psum_scatter(value, "chip", scatter_dimension=0, tiled=True)
-            for value in (grad_wout, grad_wz)
-        ]
         gall, last8, rim, gtaps, vecs, dsk = call(
             in_back_kernel,
             count,
@@ -983,20 +985,18 @@
         if layer == 0:
             last8 = behind(last8, first_sums, *(out_swaps or ()))
         else:
-            last8 = behind(last8, out_parts[0], out_parts[2])
+            last8 = behind(last8, *out_parts)
         gall = lax.dynamic_update_slice(
             gall, (last8 + rim_back).astype(bf16), (tok - ROWS, 0)
         )
         partial = partial_z + mm(gall, kept["wall"], ((1,), (1,)))
-        if layer > 0:
-            partial = behind(partial, *out_parts)
-        stages = []
-        grad_normed = scatter_sum(partial, stages=stages)
-        late = behind(gall, *stages)
-        partial = behind(partial, *stages)
+        grad_normed = scatter_sum(partial)
+        late = behind(gall, partial)
         grad_wbc = mm(kept["normed"], late[:, inner : inner + BC], ((0,), (0,)))
+        grad_win = mm(kept["normed"], behind(late, grad_wbc)[:, :inner], ((0,), (0,)))
+        partial = behind(partial, grad_normed)
+        late = behind(gall, grad_normed)
         grad_wdt = mm(kept["normed"], late[:, inner + BC :], ((0,), (0,)))
-        grad_win = mm(kept["normed"], behind(late, grad_wbc, grad_wdt)[:, :inner], ((0,), (0,)))
         hidden_in = kept["hidden"]
         inv = lax.rsqrt(jnp.mean(hidden_in * hidden_in, axis=1, keepdims=True) + epsilon)
         if layer == 0:
@@ -1014,10 +1014,12 @@
         )
         if layer > 0:
             grad_h = gather_pieces(grad_own)
-        matrices[layer] += [
-            lax.psum_scatter(value, "chip", scatter_dimension=0, tiled=True)
-            for value in (grad_wbc, grad_win)
-        ]
+        matrices[layer] = lax.psum_scatter(
+            jnp.concatenate([grad_wout, grad_wz, grad_win, grad_wbc], axis=1),
+            "chip",
+            scatter_dimension=0,
+            tiled=True,
+        )
         vectors[layer] = jnp.concatenate(
             [
                 gtaps[: CONV + 1, :inner].reshape(-1),
@@ -1030,21 +1032,23 @@
                 grad_ngain,
             ]
         )
-    vector = total(jnp.stack(vectors), ("zh", "chip"))
+    vector = total(jnp.stack(vectors), ("chip",))
+    grad_parts = cross_over(grad_own)
+    own_s = near_swap(grad_own)
+    grad_parts, own_s, vector, _ = behind((grad_parts, own_s, vector, grad_win))
+    mark = grad_parts[0]
+    grad_swaps = near_swaps(grad_own, *grad_parts, own_s)
+    input_grad = deliver(grad_own, *grad_parts, f32, grad_swaps)
+    final_out = deliver(hidden_own, *out_parts, bf16, out_swaps, (mark,))
+    g_last = behind(matrices[0], *(grad_swaps or (mark,)))
+    last_sums = join_halves(g_last[:, : 3 * inner])
+    grad_wbc = jnp.stack([g_last[:, 3 * inner :], matrices[1][:, 3 * inner :]], axis=1)
+    grad_wbc = total(half_rows(grad_wbc), ("zh",))
+    g_cols = [place_rows(last_sums), place_rows(behind(first_sums, mark))]
+    vector = total(vector, ("zh",))
     other = swap(vector, "core")
     common = (CONV + 1) * BC + width
     shared = total((vector + other)[:, -common:], ("zl",))
-    grad_wbc = half_rows(jnp.stack([matrices[1][2], matrices[0][2]], axis=1)[:, ::-1])
-    grad_parts = cross_over(grad_own)
-    own_s = near_swap(grad_own)
-    grad_parts, own_s, shared, grad_wbc = behind((grad_parts, own_s, shared, grad_wbc))
-    mark = grad_parts[0]
-    input_grad = deliver(grad_own, *grad_parts, f32, near_swaps(grad_own, *grad_parts, own_s))
-    final_out = deliver(hidden_own, *out_parts, bf16, out_swaps, (mark,))
-    grad_wbc = total(grad_wbc, ("zh",))
-    g_out, g_z, g_x = behind((matrices[0][0], matrices[0][1], matrices[0][3]), mark)
-    early, late = join_halves([g_out, g_z]), join_halves([g_x])
-    g_cols = [place_rows(early, late), place_rows(behind(first_sums, mark))]
     by_head = jnp.where(held, vector, other)[:, :-common]
     g_bc = shared[:, :-width].reshape(LAYERS, CONV + 1, BC)
     g_ngain = shared[:, -width:]
@@ -1077,18 +1081,14 @@
     )
 
 
-def join_halves(parts):
-    part = jnp.concatenate(parts, axis=1)
+def join_halves(part):
     return part + lax.ppermute(part, BOTH, CROSS_BACK)
 
 
-def place_rows(*parts):
+def place_rows(full):
     core, far = lax.axis_index("core"), lax.axis_index("zh")
-    sent = [lax.ppermute(take(full, 1 - core, 2), BOTH, CORE_OUT) for full in parts]
-    rows = [
-        jnp.where(core == far, take(full, core, 2), got) for full, got in zip(parts, sent)
-    ]
-    return jnp.concatenate(rows, axis=1)
+    sent = lax.ppermute(take(full, 1 - core, 2), BOTH, CORE_OUT)
+    return jnp.where(core == far, take(full, core, 2), sent)
 
 
 def half_rows(part):

time: 937 us -> 901 us (0.962)
  starting transfers between devices: 220 us -> 200 us
    ppermute x4, waiting for transfers between devices: 0.01 us -> 45.8 us  [near_swap(): return lax.ppermute(value, ('core', 'zh', 'zl'), here)]
    reduce_scatter x8 -> x2, waiting for transfers between devices: 28.2 us -> 0.01 us  [shards(): lax.psum_scatter(jnp.concatenate([grad_wout, grad_wz, grad_win, grad_wbc]...]
    ppermute x10, waiting for transfers between devices: 54.1 us -> 30.3 us  [total(): lax.ppermute(value, axis, [(i, i ^ step) for i in range(count)])]
    ppermute x3, waiting for transfers between devices: 25.4 us -> 2.74 us  [weights_over(): return lax.ppermute(piece, BOTH, CROSS)]
    ppermute x3, starting transfers between devices: 32.3 us -> 9.72 us  [the longest x2 5.94 us: place_rows(): sent = lax.ppermute(take(full, 1 - core, 2), BOTH, CORE_OUT)]
    ppermute x6, waiting for transfers between devices: 0.02 us -> 17.1 us  [cross_over(): lax.ppermute(value, BOTH, pairs)]
    ppermute x10, starting transfers between devices: 17.7 us -> 34.8 us  [total(): lax.ppermute(value, axis, [(i, i ^ step) for i in range(count)])]
    ppermute x12, waiting for transfers between devices: 36.7 us -> 52 us  [chain(): got = lax.ppermute(part, BLOCKS, [(i, i ^ step) for i in range(count)])]
  transfers between devices with their start and end apart: 90 -> 82, of which waited for: 33 -> 35; matrix products, arithmetic and copies ran while one was open for 20% -> 16% of each run, Pallas kernels for 13% -> 12%
where the time goes in v7:
time: 901 us; the launch traced here: 891 us
  waiting for transfers between devices  299 us (33%)
  starting transfers between devices  200 us (22%)
  Pallas kernels  162 us (18%)
  local copies, waits for them, and re-layouts  96.1 us (11%)
  other arithmetic  74.1 us (8%)
  matrix products  43.5 us (5%)
  between operations  16.2 us (2%)
    pallas_call x12, Pallas kernels, call(): pl.pallas_call(kernel, grid=(count,), in_specs=[spec for spec, _ in ins],...  146 us
    ppermute x18, waiting for transfers between devices, swap(): return lax.ppermute(value, axis, SWAP)  114 us
    ppermute x12, waiting for transfers between devices, chain(): got = lax.ppermute(part, BLOCKS, [(i, i ^ step) for i in range(count)])  52 us
    ppermute x4, waiting for transfers between devices, near_swap(): return lax.ppermute(value, ('core', 'zh', 'zl'), here)  45.8 us
    dot_general x16, matrix products, mm(): lax.dot_general(left, right, (dims, ((), ())), preferred_element_type=f32...  38 us
    ppermute x18, starting transfers between devices, swap(): return lax.ppermute(value, axis, SWAP)  35.3 us
    ppermute x10, starting transfers between devices, total(): lax.ppermute(value, axis, [(i, i ^ step) for i in range(count)])  34.8 us
    ppermute x10, waiting for transfers between devices, total(): lax.ppermute(value, axis, [(i, i ^ step) for i in range(count)])  30.3 us
  transfers between devices with their start and end apart: 82, of which 35 were waited for; matrix products, arithmetic and copies ran while one was open for 16% of the time, Pallas kernels for 12%

profile of v7, /device:TPU:0, one launch (start us, length us, event | category | flops | bytes accessed | tf_op | source)
XLA Modules:
  0.0 891.2 jit_solution(2149613966745834334)
XLA Ops:
  45.4 7.3 collective-permute-start.5
  68.5 12.0 %collective-permute-start.10 = (f32[8,768]{1,0:T(8,128)S(1)}, f32[8,768]{1,0:T(8,128)S(1)}, u32[]{:S(2)}, u32[]{:S(2)}) collective-permute-start(f32[8,768]{1,0:T(8,128)S(1)} %fusion), channel_id=1, source_target_pairs={{0,2},{2,8},{8,10},{10,16},{16,18},{18,24},{24,26},{1,3},{3,9},{9,... | collective-permute-start | bytes 73736 | tf_op jit(solution)/shard_map/ppermute | solution.py:384
  83.8 15.6 %in_proj_conv.2 = (bf16[1024,1024]{1,0:T(8,128)(2,1)}, f32[1024,768]{1,0:T(8,128)}, f32[1024,768]{1,0:T(8,128)}, f32[1024,128]{1,0:T(8,128)}, f32[1024,128]{1,0:...) custom-call(s32[2]{0:T(128)} %pad_add_fusion.place, ...), custom_call_target="tpu_custom_call" | custom-call | flops 18400000000 | bytes 1048576 | tf_op jit(solution)/shard_map/in_proj_conv/pallas_call | solution.py:350
  120.3 12.1 %collective-permute-start.17 = (f32[256,1536]{1,0:T(8,128)}, f32[256,1536]{1,0:T(8,128)}, u32[]{:S(2)}, u32[]{:S(2)}) collective-permute-start(f32[256,1536]{1,0:T(8,128)} %maximum_convert_fusion), channel_id=1, source_target_pairs={{0,2},{6,4},{1,3},{7,5},{8,10},{14,12},{9,11},{15,13},{16,18},{22,... | collective-permute-start | bytes 4718600 | tf_op jit(solution)/shard_map/ppermute | solution.py:597
  157.7 11.1 %gate_out_proj.2 = (f32[1024,512]{1,0:T(8,128)}, bf16[1024,512]{1,0:T(8,128)(2,1)}, f32[1024,1024]{1,0:T(8,128)}, f32[8,1024]{1,0:T(8,128)}) custom-call(f32[1024,512]{1,0:T(8,128)} %ssd_within.2.yin, f32[1024,768]{1,0:T(8,128)} %get-tuple-element.153.cpre, f32[1024,128]{1,0:T(8,128)} %get-tuple-element.150.cum, bf16[1024,256]{1,0:T(8,128)(2,1)} %get-tuple-element.152.bc, ...), custom_call_target="tpu_custom_call" | custom-call | flops 13799999488 | bytes 1048576 | tf_op jit(solution)/shard_map/gate_out_proj/pallas_call | solution.py:350
  198.3 16.8 %collective-permute-done.20 = f32[8,1024]{1,0:T(8,128)S(1)} collective-permute-done((f32[8,1024]{1,0:T(8,128)S(1)}, f32[8,1024]{1,0:T(8,128)S(1)}, u32[]{:S(2)}, u32[]{:S(2)}) %collective-permute-start.20) | collective-permute-done | bytes 32800 | tf_op jit(solution)/shard_map/ppermute | solution.py:416
  220.2 23.3 %collective-permute-done.26.refs_1_ = f32[256,1024]{1,0:T(8,128)} collective-permute-done((f32[256,1024]{1,0:T(8,128)}, f32[256,1024]{1,0:T(8,128)}, u32[]{:S(2)}, u32[]{:S(2)}) %collective-permute-start.26) | collective-permute-done | bytes 1048608 | tf_op jit(solution)/shard_map/ppermute | solution.py:408
  264.1 17.2 %in_proj_conv.3 = (bf16[1024,1024]{1,0:T(8,128)(2,1)}, f32[1024,768]{1,0:T(8,128)}, f32[1024,768]{1,0:T(8,128)}, f32[1024,128]{1,0:T(8,128)}, f32[1024,128]{1,0:...) custom-call(s32[2]{0:T(128)} %pad_add_fusion.place, ...), custom_call_target="tpu_custom_call" | custom-call | flops 18400000000 | bytes 1048576 | tf_op jit(solution)/shard_map/in_proj_conv/pallas_call | solution.py:350
  287.7 9.2 %collective-permute-done.30 = f32[136,512]{1,0:T(8,128)S(1)} collective-permute-done((f32[136,512]{1,0:T(8,128)}, f32[136,512]{1,0:T(8,128)S(1)}, u32[]{:S(2)}, u32[]{:S(2)}) %collective-permute-start.30) | collective-permute-done | bytes 278560 | tf_op jit(solution)/shard_map/ppermute | solution.py:394
  314.9 14.1 %gate_out_proj.3 = (f32[1024,512]{1,0:T(8,128)}, bf16[1024,512]{1,0:T(8,128)(2,1)}, f32[1024,1024]{1,0:T(8,128)}, f32[8,1024]{1,0:T(8,128)}) custom-call(f32[1024,512]{1,0:T(8,128)} %ssd_within.3.yin, f32[1024,768]{1,0:T(8,128)} %get-tuple-element.181.cpre, f32[1024,128]{1,0:T(8,128)} %get-tuple-element.178.cum, bf16[1024,256]{1,0:T(8,128)(2,1)} %get-tuple-element.180.bc, ...), custom_call_target="tpu_custom_call" | custom-call | flops 13799999488 | bytes 1048576 | tf_op jit(solution)/shard_map/gate_out_proj/pallas_call | solution.py:350
  337.8 9.9 %gate_back.2 = (bf16[1024,1024]{1,0:T(8,128)(2,1)}, bf16[1024,512]{1,0:T(8,128)(2,1)}, bf16[1024,512]{1,0:T(8,128)(2,1)}, f32[4,128,512]{2,1,0:T(8,128)}, f32[4,...) custom-call(s32[2]{0:T(128)} %pad_add_fusion.place, f32[1024,1]{1,0:T(8,128)} %copy-done.61, ...), custom_call_target="tpu_custom_call" | custom-call | flops 11500000256 | bytes 1048576 | tf_op jit(solution)/shard_map/gate_back/pallas_call | solution.py:350
  351.1 12.9 %collective-permute-done.40 = f32[136,512]{1,0:T(8,128)S(1)} collective-permute-done((f32[136,512]{1,0:T(8,128)}, f32[136,512]{1,0:T(8,128)S(1)}, u32[]{:S(2)}, u32[]{:S(2)}) %collective-permute-start.40) | collective-permute-done | bytes 278560 | tf_op jit(solution)/shard_map/ppermute | solution.py:394
  367.2 7.4 collective-permute-done.41
  379.4 7.7 ssd_within_back.2
  388.0 15.5 %collective-permute-done.36 = f32[256,1024]{1,0:T(8,128)S(1)} collective-permute-done((f32[256,1024]{1,0:T(8,128)S(1)}, f32[256,1024]{1,0:T(8,128)S(1)}, u32[]{:S(2)}, u32[]{:S(2)}) %collective-permute-start.36) | collective-permute-done | bytes 1048608 | tf_op jit(solution)/shard_map/ppermute | solution.py:408
  419.7 20.3 %in_proj_conv_back.2 = (bf16[1024,896]{1,0:T(8,128)(2,1)}, f32[8,768]{1,0:T(8,128)}, f32[8,768]{1,0:T(8,128)}, f32[8,768]{1,0:T(8,128)}, f32[8,128]{1,0:T(8,128)}, /*index=5*/f32[8,512]{1,0:T(8,128)}) custom-call(f32[1024,512]{1,0:T(8,128)} %get-tuple-element.199.uin, f32[1024,256]{1,0:T(8,128)} %get-tuple-element.200.dbc, ...), custom_call_target="tpu_custom_call" | custom-call | flops 23000000512 | bytes 1048576 | tf_op jit(solution)/shard_map/in_proj_conv_back/pallas_call | solution.py:350
  446.9 14.2 %collective-permute-done.43 = f32[8,768]{1,0:T(8,128)S(1)} collective-permute-done((f32[8,768]{1,0:T(8,128)}, f32[8,768]{1,0:T(8,128)S(1)}, u32[]{:S(2)}, u32[]{:S(2)}) %collective-permute-start.43) | collective-permute-done | bytes 24608 | tf_op jit(solution)/shard_map/ppermute | solution.py:384
  461.7 7.2 convolution_add_fusion
  482.2 25.2 %collective-permute-done.45 = f32[256,1024]{1,0:T(8,128)S(1)} collective-permute-done((f32[256,1024]{1,0:T(8,128)S(1)}, f32[256,1024]{1,0:T(8,128)S(1)}, u32[]{:S(2)}, u32[]{:S(2)}) %collective-permute-start.45) | collective-permute-done | bytes 1048608 | tf_op jit(solution)/shard_map/ppermute | solution.py:408
  511.6 24.4 %collective-permute-done.48.refs_1_ = f32[256,1024]{1,0:T(8,128)} collective-permute-done((f32[256,1024]{1,0:T(8,128)S(1)}, f32[256,1024]{1,0:T(8,128)}, u32[]{:S(2)}, u32[]{:S(2)}) %collective-permute-start.48) | collective-permute-done | bytes 1048608 | tf_op jit(solution)/shard_map/ppermute | solution.py:408
  541.9 11.5 %gate_back.3 = (bf16[1024,1024]{1,0:T(8,128)(2,1)}, bf16[1024,512]{1,0:T(8,128)(2,1)}, bf16[1024,512]{1,0:T(8,128)(2,1)}, f32[4,128,512]{2,1,0:T(8,128)}, f32[4,...) custom-call(s32[2]{0:T(128)} %pad_add_fusion.place, f32[1024,1]{1,0:T(8,128)} %copy-done.59, ...), custom_call_target="tpu_custom_call" | custom-call | flops 11500000256 | bytes 1048576 | tf_op jit(solution)/shard_map/gate_back/pallas_call | solution.py:350
  555.4 7.7 ssd_within_back.3
  592.6 20.3 %in_proj_conv_back.3 = (bf16[1024,896]{1,0:T(8,128)(2,1)}, f32[8,768]{1,0:T(8,128)}, f32[8,768]{1,0:T(8,128)}, f32[8,768]{1,0:T(8,128)}, f32[8,128]{1,0:T(8,128)}, /*index=5*/f32[8,512]{1,0:T(8,128)}) custom-call(f32[1024,512]{1,0:T(8,128)} %get-tuple-element.222.uin, f32[1024,256]{1,0:T(8,128)} %get-tuple-element.223.dbc, ...), custom_call_target="tpu_custom_call" | custom-call | flops 23000000512 | bytes 1048576 | tf_op jit(solution)/shard_map/in_proj_conv_back/pallas_call | solution.py:350
  626.1 20.8 %collective-permute-done.54.near_s = f32[256,1024]{1,0:T(8,128)} collective-permute-done((f32[256,1024]{1,0:T(8,128)}, f32[256,1024]{1,0:T(8,128)}, u32[]{:S(2)}, u32[]{:S(2)}) %collective-permute-start.54) | collective-permute-done | bytes 1048608 | tf_op jit(solution)/shard_map/ppermute | solution.py:493
  655.5 9.9 %collective-permute-start.60 = (f32[512,1024]{1,0:T(8,128)}, f32[512,1024]{1,0:T(8,128)}, u32[]{:S(2)}, u32[]{:S(2)}) collective-permute-start(f32[512,1024]{1,0:T(8,128)} %constant_dynamic-slice_fusion.4), channel_id=1, source_target_pairs={{0,4},{4,0},{1,5},{5,1},{2,6},{6,2},{3,7},{7,3},{8,12},{12,8},{9,1... | collective-permute-start | bytes 6291464 | tf_op jit(solution)/shard_map/ppermute | solution.py:408
  690.6 13.5 %collective-permute-done.61 = f32[256,1024]{1,0:T(8,128)} collective-permute-done((f32[256,1024]{1,0:T(8,128)}, f32[256,1024]{1,0:T(8,128)}, u32[]{:S(2)}, u32[]{:S(2)}) %collective-permute-start.61) | collective-permute-done | bytes 1048608 | tf_op jit(solution)/shard_map/ppermute | solution.py:408
  736.5 17.1 %collective-permute-done.62.mine = f32[256,1024]{1,0:T(8,128)S(1)} collective-permute-done((f32[256,1024]{1,0:T(8,128)S(1)}, f32[256,1024]{1,0:T(8,128)S(1)}, u32[]{:S(2)}, u32[]{:S(2)}) %collective-permute-start.62) | collective-permute-done | bytes 1048608 | tf_op jit(solution)/shard_map/ppermute | solution.py:486
  753.6 11.9 %collective-permute-done.65.value_s = f32[256,1024]{1,0:T(8,128)S(1)} collective-permute-done((f32[256,1024]{1,0:T(8,128)S(1)}, f32[256,1024]{1,0:T(8,128)S(1)}, u32[]{:S(2)}, u32[]{:S(2)}) %collective-permute-start.65) | collective-permute-done | bytes 1048608 | tf_op jit(solution)/shard_map/ppermute | solution.py:493
  765.5 11.1 %collective-permute-start.71 = (f32[2,14096]{1,0:T(2,128)S(1)}, f32[2,14096]{1,0:T(2,128)S(1)}, u32[]{:S(2)}, u32[]{:S(2)}) collective-permute-start(f32[2,14096]{1,0:T(2,128)S(1)} %fusion.110), channel_id=1, source_target_pairs={{0,2},{2,0},{1,3},{3,1},{4,6},{6,4},{5,7},{7,5},{8,10},{10,8},{9,1... | collective-permute-start | bytes 338312 | tf_op jit(solution)/shard_map/ppermute | solution.py:416
  796.2 13.1 %collective-permute-done.69.near_s = f32[256,1024]{1,0:T(8,128)S(1)} collective-permute-done((f32[256,1024]{1,0:T(8,128)S(1)}, f32[256,1024]{1,0:T(8,128)S(1)}, u32[]{:S(2)}, u32[]{:S(2)}) %collective-permute-start.69) | collective-permute-done | bytes 1048608 | tf_op jit(solution)/shard_map/ppermute | solution.py:493
  839.4 12.3 %collective-permute-start.79 = (f32[128,2,256]{0,2,1:T(8,128)S(1)}, f32[128,2,256]{0,2,1:T(8,128)S(1)}, u32[]{:S(2)}, u32[]{:S(2)}) collective-permute-start(f32[128,2,256]{0,2,1:T(8,128)S(1)} %fusion.109), channel_id=1, source_target_pairs={{0,2},{2,0},{1,3},{3,1},{4,6},{6,4},{5,7},{7,5},{8,10},{10,8},{9,1... | collective-permute-start | bytes 786440 | tf_op jit(solution)/shard_map/ppermute | solution.py:416
  851.7 17.6 %collective-permute-done.74 = f32[256,1536]{0,1:T(8,128)} collective-permute-done((f32[256,1536]{0,1:T(8,128)}, f32[256,1536]{0,1:T(8,128)}, u32[]{:S(2)}, u32[]{:S(2)}) %collective-permute-start.74) | collective-permute-done | bytes 1572896 | tf_op jit(solution)/shard_map/ppermute | solution.py:1085
  (613 shorter events, 425.1 us)
Async XLA Ops:
  7.2 582.6 %reduce-scatter.3.cloned.1.call-start = ((), (), s32[]{:S(2)}) async-start(), calls=%async_computation.2 | async-start | bytes 9175040 | tf_op jit(solution)/shard_map/reduce_scatter | solution.py:1017
  10.8 33.5 %collective-permute-start.1 = (f32[256,512]{1,0:T(8,128)}, f32[256,512]{1,0:T(8,128)}, u32[]{:S(2)}, u32[]{:S(2)}) collective-permute-start(f32[256,512]{1,0:T(8,128)} %dynamic-slice_convert_fusion), channel_id=1, source_target_pairs={{0,2},{6,4},{1,3},{7,5},{8,10},{14,12},{9,11},{15,13},{16,18},{22,... | collective-permute-start | bytes 1572872 | tf_op jit(solution)/shard_map/ppermute | solution.py:597
  20.4 35.5 %collective-permute-start.6 = (f32[2,64,128]{2,1,0:T(8,128)S(1)}, f32[2,64,128]{2,1,0:T(8,128)S(1)}, u32[]{:S(2)}, u32[]{:S(2)}) collective-permute-start(f32[2,64,128]{2,1,0:T(8,128)S(1)} %reshape.406), channel_id=1, source_target_pairs={{0,2},{6,4},{1,3},{7,5},{8,10},{14,12},{9,11},{15,13},{16,18},{22,... | collective-permute-start | bytes 196616 | tf_op jit(solution)/shard_map/ppermute | solution.py:671
  24.3 42.2 %collective-permute-start = (f32[1024,1024]{1,0:T(8,128)}, f32[1024,1024]{1,0:T(8,128)}, u32[]{:S(2)}, u32[]{:S(2)}) collective-permute-start(f32[1024,1024]{1,0:T(8,128)} %convert_element_type.74), channel_id=1, source_target_pairs={{0,4},{6,2},{1,5},{7,3},{8,12},{14,10},{9,13},{15,11},{16,20},{22,... | collective-permute-start | bytes 12582920 | tf_op jit(solution)/shard_map/ppermute | solution.py:537
  103.6 52.9 %collective-permute-start.18 = (f32[1024,1024]{1,0:T(8,128)}, f32[1024,1024]{1,0:T(8,128)}, u32[]{:S(2)}, u32[]{:S(2)}) collective-permute-start(f32[1024,1024]{1,0:T(8,128)} %convert_element_type.80), channel_id=1, source_target_pairs={{0,4},{6,2},{1,5},{7,3},{8,12},{14,10},{9,13},{15,11},{16,20},{22,... | collective-permute-start | bytes 12582920 | tf_op jit(solution)/shard_map/ppermute | solution.py:785
  109.4 25.5 %collective-permute-start.11 = (f32[256,1024]{1,0:T(8,128)}, f32[256,1024]{1,0:T(8,128)S(1)}, u32[]{:S(2)}, u32[]{:S(2)}) collective-permute-start(f32[256,1024]{1,0:T(8,128)} %collective-permute-done.5.refs_2_), channel_id=1, source_target_pairs={{2,10},{4,12},{10,2},{12,4},{18,26},{20,28},{26,18},{28,20},{3,11}... | collective-permute-start | bytes 3145736 | tf_op jit(solution)/shard_map/ppermute | solution.py:612
  110.1 31.4 %collective-permute-start.12 = (f32[256,1024]{1,0:T(8,128)}, f32[256,1024]{1,0:T(8,128)S(1)}, u32[]{:S(2)}, u32[]{:S(2)}) collective-permute-start(f32[256,1024]{1,0:T(8,128)} %collective-permute-done.5.refs_2_), channel_id=1, source_target_pairs={{2,18},{4,20},{10,26},{12,28},{18,2},{20,4},{26,10},{28,12},{3,19}... | collective-permute-start | bytes 3145736 | tf_op jit(solution)/shard_map/ppermute | solution.py:612
  110.9 30.7 %collective-permute-start.13 = (f32[256,1024]{1,0:T(8,128)}, f32[256,1024]{1,0:T(8,128)S(1)}, u32[]{:S(2)}, u32[]{:S(2)}) collective-permute-start(f32[256,1024]{1,0:T(8,128)} %collective-permute-done.5.refs_2_), channel_id=1, source_target_pairs={{2,26},{4,28},{10,18},{12,20},{18,10},{20,12},{26,2},{28,4},{3,27}... | collective-permute-start | bytes 3145736 | tf_op jit(solution)/shard_map/ppermute | solution.py:612
  120.3 36.2 %collective-permute-start.17 = (f32[256,1536]{1,0:T(8,128)}, f32[256,1536]{1,0:T(8,128)}, u32[]{:S(2)}, u32[]{:S(2)}) collective-permute-start(f32[256,1536]{1,0:T(8,128)} %maximum_convert_fusion), channel_id=1, source_target_pairs={{0,2},{6,4},{1,3},{7,5},{8,10},{14,12},{9,11},{15,13},{16,18},{22,... | collective-permute-start | bytes 4718600 | tf_op jit(solution)/shard_map/ppermute | solution.py:597
  186.0 29.2 %collective-permute-start.22 = (f32[256,1024]{1,0:T(8,128)S(1)}, f32[256,1024]{1,0:T(8,128)S(1)}, u32[]{:S(2)}, u32[]{:S(2)}) collective-permute-start(f32[256,1024]{1,0:T(8,128)S(1)} %constant_dynamic-slice_fusion.10), channel_id=1, source_target_pairs={{0,1},{1,0},{2,3},{3,2},{4,5},{5,4},{6,7},{7,6},{8,9},{9,8},{10,11... | collective-permute-start | bytes 3145736 | tf_op jit(solution)/shard_map/ppermute | solution.py:408
  192.7 51.3 %collective-permute-start.23 = (f32[256,1536]{1,0:T(8,128)}, f32[256,1536]{1,0:T(8,128)}, u32[]{:S(2)}, u32[]{:S(2)}) collective-permute-start(f32[256,1536]{1,0:T(8,128)} %collective-permute-done.17.refs_3_), channel_id=1, source_target_pairs={{2,10},{4,12},{10,2},{12,4},{18,26},{20,28},{26,18},{28,20},{3,11}... | collective-permute-start | bytes 4718600 | tf_op jit(solution)/shard_map/ppermute | solution.py:612
  194.5 49.5 %collective-permute-start.24 = (f32[256,1536]{1,0:T(8,128)}, f32[256,1536]{1,0:T(8,128)}, u32[]{:S(2)}, u32[]{:S(2)}) collective-permute-start(f32[256,1536]{1,0:T(8,128)} %collective-permute-done.17.refs_3_), channel_id=1, source_target_pairs={{2,18},{4,20},{10,26},{12,28},{18,2},{20,4},{26,10},{28,12},{3,19}... | collective-permute-start | bytes 4718600 | tf_op jit(solution)/shard_map/ppermute | solution.py:612
  196.4 47.6 %collective-permute-start.25 = (f32[256,1536]{1,0:T(8,128)}, f32[256,1536]{1,0:T(8,128)}, u32[]{:S(2)}, u32[]{:S(2)}) collective-permute-start(f32[256,1536]{1,0:T(8,128)} %collective-permute-done.17.refs_3_), channel_id=1, source_target_pairs={{2,26},{4,28},{10,18},{12,20},{18,10},{20,12},{26,2},{28,4},{3,27}... | collective-permute-start | bytes 4718600 | tf_op jit(solution)/shard_map/ppermute | solution.py:612
  220.2 32.8 %collective-permute-start.27 = (f32[256,1024]{1,0:T(8,128)}, f32[256,1024]{1,0:T(8,128)}, u32[]{:S(2)}, u32[]{:S(2)}) collective-permute-start(f32[256,1024]{1,0:T(8,128)} %get-tuple-element.351.refs_0_), channel_id=1, source_target_pairs={{0,4},{4,0},{1,5},{5,1},{2,6},{6,2},{3,7},{7,3},{8,12},{12,8},{9,1... | collective-permute-start | bytes 3145736 | tf_op jit(solution)/shard_map/ppermute | solution.py:408
  336.2 40.3 %collective-permute-start.35 = (f32[512,1024]{1,0:T(8,128)}, f32[512,1024]{1,0:T(8,128)}, u32[]{:S(2)}, u32[]{:S(2)}) collective-permute-start(f32[512,1024]{1,0:T(8,128)} %constant_dynamic-slice_fusion.8), channel_id=1, source_target_pairs={{0,4},{4,0},{1,5},{5,1},{2,6},{6,2},{3,7},{7,3},{8,12},{12,8},{9,1... | collective-permute-start | bytes 6291464 | tf_op jit(solution)/shard_map/ppermute | solution.py:408
  411.6 35.3 %collective-permute-start.37 = (f32[256,1024]{1,0:T(8,128)S(1)}, f32[256,1024]{1,0:T(8,128)}, u32[]{:S(2)}, u32[]{:S(2)}) collective-permute-start(f32[256,1024]{1,0:T(8,128)S(1)} %multiply_add_fusion.2.value), channel_id=1, source_target_pairs={{0,2},{6,4},{1,3},{7,5},{8,10},{14,12},{9,11},{15,13},{16,18},{22,... | collective-permute-start | bytes 3145736 | tf_op jit(solution)/shard_map/ppermute | solution.py:486
  414.2 32.7 %collective-permute-start.38 = (f32[256,1024]{1,0:T(8,128)S(1)}, f32[256,1024]{1,0:T(8,128)}, u32[]{:S(2)}, u32[]{:S(2)}) collective-permute-start(f32[256,1024]{1,0:T(8,128)S(1)} %multiply_add_fusion.2.value), channel_id=1, source_target_pairs={{4,0},{2,6},{5,1},{3,7},{12,8},{10,14},{13,9},{11,15},{20,16},{18,... | collective-permute-start | bytes 3145736 | tf_op jit(solution)/shard_map/ppermute | solution.py:486
  415.5 31.4 %collective-permute-start.39 = (f32[256,1024]{1,0:T(8,128)S(1)}, f32[256,1024]{1,0:T(8,128)}, u32[]{:S(2)}, u32[]{:S(2)}) collective-permute-start(f32[256,1024]{1,0:T(8,128)S(1)} %multiply_add_fusion.2.value), channel_id=1, source_target_pairs={{4,2},{2,4},{5,3},{3,5},{12,10},{10,12},{13,11},{11,13},{20,18},{1... | collective-permute-start | bytes 3145736 | tf_op jit(solution)/shard_map/ppermute | solution.py:486
  475.4 335.9 %reduce-scatter.5.cloned.1.call-start = ((), (), s32[]{:S(2)}) async-start(), calls=%async_computation.3 | async-start | bytes 9175040 | tf_op jit(solution)/shard_map/reduce_scatter | solution.py:1017
  482.1 25.3 %collective-permute-start.45 = (f32[256,1024]{1,0:T(8,128)S(1)}, f32[256,1024]{1,0:T(8,128)S(1)}, u32[]{:S(2)}, u32[]{:S(2)}) collective-permute-start(f32[256,1024]{1,0:T(8,128)S(1)} %constant_dynamic-slice_fusion.5), channel_id=1, source_target_pairs={{0,1},{1,0},{2,3},{3,2},{4,5},{5,4},{6,7},{7,6},{8,9},{9,8},{10,11... | collective-permute-start | bytes 3145736 | tf_op jit(solution)/shard_map/ppermute | solution.py:408
  511.6 30.3 %collective-permute-start.49 = (f32[256,1024]{1,0:T(8,128)S(1)}, f32[256,1024]{1,0:T(8,128)}, u32[]{:S(2)}, u32[]{:S(2)}) collective-permute-start(f32[256,1024]{1,0:T(8,128)S(1)} %get-tuple-element.348.refs_0_), channel_id=1, source_target_pairs={{0,4},{4,0},{1,5},{5,1},{2,6},{6,2},{3,7},{7,3},{8,12},{12,8},{9,1... | collective-permute-start | bytes 3145736 | tf_op jit(solution)/shard_map/ppermute | solution.py:408
  580.8 45.3 %collective-permute-start.52 = (f32[256,1024]{1,0:T(8,128)S(1)}, f32[256,1024]{1,0:T(8,128)S(1)}, u32[]{:S(2)}, u32[]{:S(2)}) collective-permute-start(f32[256,1024]{1,0:T(8,128)S(1)} %multiply_add_fusion.2.value), channel_id=1, source_target_pairs={{0,1},{1,0},{6,7},{7,6},{8,9},{9,8},{14,15},{15,14},{16,17},{17,16... | collective-permute-start | bytes 3145736 | tf_op jit(solution)/shard_map/ppermute | solution.py:493
  583.1 43.0 %collective-permute-start.53 = (f32[256,1024]{1,0:T(8,128)}, f32[256,1024]{1,0:T(8,128)S(1)}, u32[]{:S(2)}, u32[]{:S(2)}) collective-permute-start(f32[256,1024]{1,0:T(8,128)} %collective-permute-done.37.mine), channel_id=1, source_target_pairs={{2,3},{3,2},{4,5},{5,4},{10,11},{11,10},{12,13},{13,12},{18,19},{1... | collective-permute-start | bytes 3145736 | tf_op jit(solution)/shard_map/ppermute | solution.py:503
  583.8 63.1 %collective-permute-start.54 = (f32[256,1024]{1,0:T(8,128)}, f32[256,1024]{1,0:T(8,128)}, u32[]{:S(2)}, u32[]{:S(2)}) collective-permute-start(f32[256,1024]{1,0:T(8,128)} %collective-permute-done.38.near), channel_id=1, source_target_pairs={{0,1},{1,0},{6,7},{7,6},{8,9},{9,8},{14,15},{15,14},{16,17},{17,16... | collective-permute-start | bytes 3145736 | tf_op jit(solution)/shard_map/ppermute | solution.py:493
  587.3 59.6 %collective-permute-start.55 = (f32[256,1024]{1,0:T(8,128)}, f32[256,1024]{1,0:T(8,128)}, u32[]{:S(2)}, u32[]{:S(2)}) collective-permute-start(f32[256,1024]{1,0:T(8,128)} %collective-permute-done.39.theirs), channel_id=1, source_target_pairs={{2,3},{3,2},{4,5},{5,4},{10,11},{11,10},{12,13},{13,12},{18,19},{1... | collective-permute-start | bytes 3145736 | tf_op jit(solution)/shard_map/ppermute | solution.py:504
  615.8 31.1 %collective-permute-start.59 = (f32[8,768]{1,0:T(8,128)}, f32[8,768]{1,0:T(8,128)S(1)}, u32[]{:S(2)}, u32[]{:S(2)}) collective-permute-start(f32[8,768]{1,0:T(8,128)} %get-tuple-element.235), channel_id=1, source_target_pairs={{2,0},{8,2},{10,8},{16,10},{18,16},{24,18},{26,24},{3,1},{9,3},{11... | collective-permute-start | bytes 73736 | tf_op jit(solution)/shard_map/ppermute | solution.py:384
  676.7 27.4 %collective-permute-start.61 = (f32[256,1024]{1,0:T(8,128)}, f32[256,1024]{1,0:T(8,128)}, u32[]{:S(2)}, u32[]{:S(2)}) collective-permute-start(f32[256,1024]{1,0:T(8,128)} %constant_dynamic-slice_fusion.3), channel_id=1, source_target_pairs={{0,1},{1,0},{2,3},{3,2},{4,5},{5,4},{6,7},{7,6},{8,9},{9,8},{10,11... | collective-permute-start | bytes 3145736 | tf_op jit(solution)/shard_map/ppermute | solution.py:408
  732.8 32.7 %collective-permute-start.65 = (f32[256,1024]{1,0:T(8,128)S(1)}, f32[256,1024]{1,0:T(8,128)S(1)}, u32[]{:S(2)}, u32[]{:S(2)}) collective-permute-start(f32[256,1024]{1,0:T(8,128)S(1)} %multiply_add_fusion.value), channel_id=1, source_target_pairs={{0,1},{1,0},{6,7},{7,6},{8,9},{9,8},{14,15},{15,14},{16,17},{17,16... | collective-permute-start | bytes 3145736 | tf_op jit(solution)/shard_map/ppermute | solution.py:493
  778.3 31.0 %collective-permute-start.69 = (f32[256,1024]{1,0:T(8,128)S(1)}, f32[256,1024]{1,0:T(8,128)S(1)}, u32[]{:S(2)}, u32[]{:S(2)}) collective-permute-start(f32[256,1024]{1,0:T(8,128)S(1)} %collective-permute-done.64.near), channel_id=1, source_target_pairs={{0,1},{1,0},{6,7},{7,6},{8,9},{9,8},{14,15},{15,14},{16,17},{17,16... | collective-permute-start | bytes 3145736 | tf_op jit(solution)/shard_map/ppermute | solution.py:493
  787.1 87.8 %collective-permute-start.76 = (f32[128,1536]{0,1:T(8,128)}, f32[128,1536]{0,1:T(8,128)}, u32[]{:S(2)}, u32[]{:S(2)}) collective-permute-start(f32[128,1536]{0,1:T(8,128)} %constant_dynamic-slice_fusion.1), channel_id=1, source_target_pairs={{0,4},{6,2},{1,5},{7,3},{8,12},{14,10},{9,13},{15,11},{16,20},{22,... | collective-permute-start | bytes 2359304 | tf_op jit(solution)/shard_map/ppermute | solution.py:1090
  814.9 54.4 %collective-permute-start.74 = (f32[256,1536]{0,1:T(8,128)}, f32[256,1536]{0,1:T(8,128)}, u32[]{:S(2)}, u32[]{:S(2)}) collective-permute-start(f32[256,1536]{0,1:T(8,128)} %slice.491), channel_id=1, source_target_pairs={{2,0},{4,6},{3,1},{5,7},{10,8},{12,14},{11,9},{13,15},{18,16},{20,... | collective-permute-start | bytes 4718600 | tf_op jit(solution)/shard_map/ppermute | solution.py:1085
  839.4 39.6 %collective-permute-start.79 = (f32[128,2,256]{0,2,1:T(8,128)S(1)}, f32[128,2,256]{0,2,1:T(8,128)S(1)}, u32[]{:S(2)}, u32[]{:S(2)}) collective-permute-start(f32[128,2,256]{0,2,1:T(8,128)S(1)} %fusion.109), channel_id=1, source_target_pairs={{0,2},{2,0},{1,3},{3,1},{4,6},{6,4},{5,7},{7,5},{8,10},{10,8},{9,1... | collective-permute-start | bytes 786440 | tf_op jit(solution)/shard_map/ppermute | solution.py:416
  (153 other events, 2050.5 us)
Sparse Core Ops, SparseCore 0:
  475.5 77.9 reduce-scatter.2
  673.1 85.7 reduce-scatter.4

commit v8 on v7

--- a/solution.py
+++ b/solution.py
@@ -207,7 +207,7 @@
         send[STATE:] = thru[...]
 
 
-def intra_back_kernel(cum, xdt, bc, seg, segrow, dy, u, dbc):
+def intra_back_kernel(cum, xdt, bc, seg, segrow, dy, dz, wz, u, dbc, part):
     inner = xdt.shape[1]
     run = cum[...]
     run_t = run.T
@@ -229,6 +229,7 @@
             grad_base = grad_base + decay * mm(xs, pair_lanes(ds, which), ((1,), (1,)))
         lane = lax.broadcasted_iota(jnp.int32, (GROUP, LANES), 1)
         u[:, cols] = jnp.where(lane < HEADDIM, parts[0], parts[1])
+    part[...] = mm(dz[...], wz[...], ((1,), (1,)))
     low = grad_base.astype(bf16)
     dbc[:, :STATE] = mm(low, bc[:, STATE:])
     dbc[:, STATE:] = mm(low, bc[:, :STATE], ((0,), (0,)))
@@ -493,7 +494,7 @@
     return lax.ppermute(value, ("core", "zh", "zl"), here)
 
 
-def near_swaps(value, mine, theirs, near, value_s=None):
+def near_swaps(value, mine, theirs, near, value_s=None, near_s=None):
     if lax.axis_size("zl") != 2 or value.shape[0] != GROUP:
         return None
     axes = ("core", "zh", "zl")
@@ -502,7 +503,7 @@
         near_swap(value) if value_s is None else value_s,
         lax.ppermute(mine, axes, there),
         lax.ppermute(theirs, axes, there),
-        near_swap(near),
+        near_swap(near) if near_s is None else near_s,
     )
 
 
@@ -906,8 +907,10 @@
         if layer == LAYERS - 1:
             last_sum = scatter_sum(kept["proj"], (gate_scale,))
             hidden_own = hidden_own + own_rows(gate_scale)[:, None] * last_sum
-            dz, gproj = behind((dz, gproj), hidden_own)
-        u, dbc = call(
+            dy = behind(dy, hidden_own)
+            out_parts = cross_over(hidden_own)
+            out_held = (near_swap(hidden_own), near_swap(out_parts[2]))
+        u, dbc, partial_z = call(
             intra_back_kernel,
             count,
             [
@@ -917,10 +920,13 @@
                 (by_rows(1, count), seg_col),
                 (by_cols(count), seg_row),
                 (by_rows(inner, count), dy),
+                (by_rows(inner, count), dz),
+                (whole((width, inner)), kept["wz"]),
             ],
             [
                 (by_rows(inner, count), shape(tok, inner)),
                 (by_rows(BC, count), shape(tok, BC)),
+                (by_rows(width, count), shape(tok, width)),
             ],
             [],
             8,
@@ -929,16 +935,11 @@
         stages = []
         gout = chain(gsend, True, stages)
         round_one = stages[0]
-        if layer == LAYERS - 1:
-            out_parts = cross_over(hidden_own)
-            u = behind(u, hidden_own)
-        else:
-            out_swaps = near_swaps(*behind((hidden_own, *out_parts), round_one))
-            first_sums = join_halves(behind(matrices[1][:, : 3 * inner], round_one))
+        if layer == 0:
+            out_swaps = near_swaps(hidden_own, *behind(out_parts, round_one), *out_held)
         grad_wout = mm(gproj, kept["gate_in"], ((0,), (0,)))
         grad_wz = mm(kept["normed"], dz, ((0,), (0,)))
-        partial_z = mm(dz, kept["wz"], ((1,), (1,)))
-        u = behind(u, grad_wout, grad_wz, partial_z)
+        u = behind(u, grad_wout, grad_wz)
         gall, last8, rim, gtaps, vecs, dsk = call(
             in_back_kernel,
             count,
@@ -983,9 +984,9 @@
         )
         rim_back = shifted(rim, -1)
         if layer == 0:
-            last8 = behind(last8, first_sums, *(out_swaps or ()))
+            last8 = behind(last8, matrices[1], *(out_swaps or ()))
         else:
-            last8 = behind(last8, *out_parts)
+            last8 = behind(last8, *out_parts, *(out_held if out_held[0] is not None else ()))
         gall = lax.dynamic_update_slice(
             gall, (last8 + rim_back).astype(bf16), (tok - ROWS, 0)
         )
@@ -994,8 +995,14 @@
         late = behind(gall, partial)
         grad_wbc = mm(kept["normed"], late[:, inner : inner + BC], ((0,), (0,)))
         grad_win = mm(kept["normed"], behind(late, grad_wbc)[:, :inner], ((0,), (0,)))
-        partial = behind(partial, grad_normed)
-        late = behind(gall, grad_normed)
+        if layer == 0:
+            grad_own = input_gradient(grad_own, grad_normed, kept["hidden"], norm_gain[layer])
+            grad_parts = cross_over(grad_own)
+            own_s = near_swap(grad_own)
+            late, partial = behind((gall, partial), grad_parts[2])
+            grad_parts, own_s, _ = behind((grad_parts, own_s, grad_win))
+            mark = grad_parts[0]
+            grad_swaps = near_swaps(grad_own, *grad_parts, own_s)
         grad_wdt = mm(kept["normed"], late[:, inner + BC :], ((0,), (0,)))
         hidden_in = kept["hidden"]
         inv = lax.rsqrt(jnp.mean(hidden_in * hidden_in, axis=1, keepdims=True) + epsilon)
@@ -1008,11 +1015,8 @@
             )
         else:
             grad_ngain = jnp.sum(grad_normed * hidden_in * inv, axis=0)
-        back = grad_normed * norm_gain[layer][None, :]
-        grad_own = grad_own + inv * (
-            back - hidden_in * inv * inv * jnp.mean(back * hidden_in, axis=1, keepdims=True)
-        )
         if layer > 0:
+            grad_own = input_gradient(grad_own, grad_normed, hidden_in, norm_gain[layer])
             grad_h = gather_pieces(grad_own)
         matrices[layer] = lax.psum_scatter(
             jnp.concatenate([grad_wout, grad_wz, grad_win, grad_wbc], axis=1),
@@ -1032,20 +1036,16 @@
                 grad_ngain,
             ]
         )
-    vector = total(jnp.stack(vectors), ("chip",))
-    grad_parts = cross_over(grad_own)
-    own_s = near_swap(grad_own)
-    grad_parts, own_s, vector, _ = behind((grad_parts, own_s, vector, grad_win))
-    mark = grad_parts[0]
-    grad_swaps = near_swaps(grad_own, *grad_parts, own_s)
+    vector = total(behind(jnp.stack(vectors), mark), ("chip",))
     input_grad = deliver(grad_own, *grad_parts, f32, grad_swaps)
     final_out = deliver(hidden_own, *out_parts, bf16, out_swaps, (mark,))
     g_last = behind(matrices[0], *(grad_swaps or (mark,)))
     last_sums = join_halves(g_last[:, : 3 * inner])
     grad_wbc = jnp.stack([g_last[:, 3 * inner :], matrices[1][:, 3 * inner :]], axis=1)
     grad_wbc = total(half_rows(grad_wbc), ("zh",))
-    g_cols = [place_rows(last_sums), place_rows(behind(first_sums, mark))]
-    vector = total(vector, ("zh",))
+    first_sums = join_halves(behind(matrices[1][:, : 3 * inner], mark))
+    g_cols = [place_rows(last_sums), place_rows(first_sums)]
+    vector = total(behind(vector, first_sums, *(grad_swaps or (mark,))), ("zh",))
     other = swap(vector, "core")
     common = (CONV + 1) * BC + width
     shared = total((vector + other)[:, -common:], ("zl",))
@@ -1083,6 +1083,14 @@
 
 def join_halves(part):
     return part + lax.ppermute(part, BOTH, CROSS_BACK)
+
+
+def input_gradient(grad_out, grad_normed, hidden, gain):
+    inv = lax.rsqrt(jnp.mean(hidden * hidden, axis=1, keepdims=True) + epsilon)
+    back = grad_normed * gain[None, :]
+    return grad_out + inv * (
+        back - hidden * inv * inv * jnp.mean(back * hidden, axis=1, keepdims=True)
+    )
 
 
 def place_rows(full):

time: 901 us -> 858 us (0.952)
  local copies, waits for them, and re-layouts: 96.1 us -> 76.4 us
  waiting for transfers between devices: 299 us -> 287 us
  starting transfers between devices: 200 us -> 189 us
    ppermute x10, starting transfers between devices: 34.8 us -> 18 us  [total(): lax.ppermute(value, axis, [(i, i ^ step) for i in range(count)])]
    ppermute x18, waiting for transfers between devices: 114 us -> 127 us  [swap(): return lax.ppermute(value, axis, SWAP)]
    ppermute x6, waiting for transfers between devices: 17.1 us -> 5.09 us  [cross_over(): lax.ppermute(value, BOTH, pairs)]
    dot_general x2 -> x0, local copies, waits for them, and re-layouts: 11 us -> none  [mm(): lax.dot_general(left, right, (dims, ((), ())), preferred_element_type=f32...]
    ppermute x5, waiting for transfers between devices: 17.7 us -> 8.32 us  [shifted(): lax.ppermute(value, BLOCKS, [(source, source + steps) for source in range...]
    unnamed x217 -> x185, local copies, waits for them, and re-layouts: 21.7 us -> 14.1 us
    dot_general x16 -> x14, matrix products: 38 us -> 31.3 us  [mm(): lax.dot_general(left, right, (dims, ((), ())), preferred_element_type=f32...]
  transfers between devices with their start and end apart: 82 -> 82, of which waited for: 35 -> 39; matrix products, arithmetic and copies ran while one was open for 16% -> 14% of each run, Pallas kernels for 12% -> 13%
where the time goes in v8:
time: 858 us; the launch traced here: 847 us
  waiting for transfers between devices  287 us (33%)
  starting transfers between devices  189 us (22%)
  Pallas kernels  167 us (19%)
  local copies, waits for them, and re-layouts  76.4 us (9%)
  other arithmetic  75.5 us (9%)
  matrix products  35.3 us (4%)
  between operations  16.2 us (2%)
    pallas_call x12, Pallas kernels, call(): pl.pallas_call(kernel, grid=(count,), in_specs=[spec for spec, _ in ins],...  150 us
    ppermute x18, waiting for transfers between devices, swap(): return lax.ppermute(value, axis, SWAP)  127 us
    ppermute x12, waiting for transfers between devices, chain(): got = lax.ppermute(part, BLOCKS, [(i, i ^ step) for i in range(count)])  48.4 us
    ppermute x4, waiting for transfers between devices, near_swap(): return lax.ppermute(value, ('core', 'zh', 'zl'), here)  40.8 us
    ppermute x10, waiting for transfers between devices, total(): lax.ppermute(value, axis, [(i, i ^ step) for i in range(count)])  32.7 us
    dot_general x14, matrix products, mm(): lax.dot_general(left, right, (dims, ((), ())), preferred_element_type=f32...  31.3 us
    ppermute x18, starting transfers between devices, swap(): return lax.ppermute(value, axis, SWAP)  26.3 us
    ppermute x3, starting transfers between devices, weights_over(): return lax.ppermute(piece, BOTH, CROSS)  26.2 us
  transfers between devices with their start and end apart: 82, of which 39 were waited for; matrix products, arithmetic and copies ran while one was open for 14% of the time, Pallas kernels for 13%

profile of v8, /device:TPU:0, one launch (start us, length us, event | category | flops | bytes accessed | tf_op | source)
XLA Modules:
  0.0 846.6 jit_solution(10438226878395399140)
XLA Ops:
  10.8 6.7 collective-permute-start.1
  45.5 7.4 collective-permute-start.5
  68.5 12.0 %collective-permute-start.10 = (f32[8,768]{1,0:T(8,128)S(1)}, f32[8,768]{1,0:T(8,128)S(1)}, u32[]{:S(2)}, u32[]{:S(2)}) collective-permute-start(f32[8,768]{1,0:T(8,128)S(1)} %fusion), channel_id=1, source_target_pairs={{0,2},{2,8},{8,10},{10,16},{16,18},{18,24},{24,26},{1,3},{3,9},{9,... | collective-permute-start | bytes 73736 | tf_op jit(solution)/shard_map/ppermute | solution.py:385
  83.9 15.6 %in_proj_conv.2 = (bf16[1024,1024]{1,0:T(8,128)(2,1)}, f32[1024,768]{1,0:T(8,128)}, f32[1024,768]{1,0:T(8,128)}, f32[1024,128]{1,0:T(8,128)}, f32[1024,128]{1,0:...) custom-call(s32[2]{0:T(128)} %pad_add_fusion.place, ...), custom_call_target="tpu_custom_call" | custom-call | flops 18400000000 | bytes 1048576 | tf_op jit(solution)/shard_map/in_proj_conv/pallas_call | solution.py:351
  111.6 6.2 collective-permute-done.14
  120.4 12.1 %collective-permute-start.17 = (f32[256,1536]{1,0:T(8,128)}, f32[256,1536]{1,0:T(8,128)}, u32[]{:S(2)}, u32[]{:S(2)}) collective-permute-start(f32[256,1536]{1,0:T(8,128)} %maximum_convert_fusion), channel_id=1, source_target_pairs={{0,2},{6,4},{1,3},{7,5},{8,10},{14,12},{9,11},{15,13},{16,18},{22,... | collective-permute-start | bytes 4718600 | tf_op jit(solution)/shard_map/ppermute | solution.py:598
  157.9 11.1 %gate_out_proj.2 = (f32[1024,512]{1,0:T(8,128)}, bf16[1024,512]{1,0:T(8,128)(2,1)}, f32[1024,1024]{1,0:T(8,128)}, f32[8,1024]{1,0:T(8,128)}) custom-call(f32[1024,512]{1,0:T(8,128)} %ssd_within.2.yin, f32[1024,768]{1,0:T(8,128)} %get-tuple-element.150.cpre, f32[1024,128]{1,0:T(8,128)} %get-tuple-element.147.cum, bf16[1024,256]{1,0:T(8,128)(2,1)} %get-tuple-element.149.bc, ...), custom_call_target="tpu_custom_call" | custom-call | flops 13799999488 | bytes 1048576 | tf_op jit(solution)/shard_map/gate_out_proj/pallas_call | solution.py:351
  170.8 6.5 collective-permute-start.21
  196.6 17.6 %collective-permute-done.20 = f32[8,1024]{1,0:T(8,128)S(1)} collective-permute-done((f32[8,1024]{1,0:T(8,128)S(1)}, f32[8,1024]{1,0:T(8,128)S(1)}, u32[]{:S(2)}, u32[]{:S(2)}) %collective-permute-start.20) | collective-permute-done | bytes 32800 | tf_op jit(solution)/shard_map/ppermute | solution.py:417
  219.3 23.4 %collective-permute-done.26.refs_1_ = f32[256,1024]{1,0:T(8,128)} collective-permute-done((f32[256,1024]{1,0:T(8,128)}, f32[256,1024]{1,0:T(8,128)}, u32[]{:S(2)}, u32[]{:S(2)}) %collective-permute-start.26) | collective-permute-done | bytes 1048608 | tf_op jit(solution)/shard_map/ppermute | solution.py:409
  263.3 17.2 %in_proj_conv.3 = (bf16[1024,1024]{1,0:T(8,128)(2,1)}, f32[1024,768]{1,0:T(8,128)}, f32[1024,768]{1,0:T(8,128)}, f32[1024,128]{1,0:T(8,128)}, f32[1024,128]{1,0:...) custom-call(s32[2]{0:T(128)} %pad_add_fusion.place, ...), custom_call_target="tpu_custom_call" | custom-call | flops 18400000000 | bytes 1048576 | tf_op jit(solution)/shard_map/in_proj_conv/pallas_call | solution.py:351
  286.9 9.2 %collective-permute-done.30 = f32[136,512]{1,0:T(8,128)S(1)} collective-permute-done((f32[136,512]{1,0:T(8,128)}, f32[136,512]{1,0:T(8,128)S(1)}, u32[]{:S(2)}, u32[]{:S(2)}) %collective-permute-start.30) | collective-permute-done | bytes 278560 | tf_op jit(solution)/shard_map/ppermute | solution.py:395
  314.1 14.1 %gate_out_proj.3 = (f32[1024,512]{1,0:T(8,128)}, bf16[1024,512]{1,0:T(8,128)(2,1)}, f32[1024,1024]{1,0:T(8,128)}, f32[8,1024]{1,0:T(8,128)}) custom-call(f32[1024,512]{1,0:T(8,128)} %ssd_within.3.yin, f32[1024,768]{1,0:T(8,128)} %get-tuple-element.178.cpre, f32[1024,128]{1,0:T(8,128)} %get-tuple-element.175.cum, bf16[1024,256]{1,0:T(8,128)(2,1)} %get-tuple-element.177.bc, ...), custom_call_target="tpu_custom_call" | custom-call | flops 13799999488 | bytes 1048576 | tf_op jit(solution)/shard_map/gate_out_proj/pallas_call | solution.py:351
  338.8 10.1 %gate_back.2 = (bf16[1024,1024]{1,0:T(8,128)(2,1)}, bf16[1024,512]{1,0:T(8,128)(2,1)}, bf16[1024,512]{1,0:T(8,128)(2,1)}, f32[4,128,512]{2,1,0:T(8,128)}, f32[4,...) custom-call(s32[2]{0:T(128)} %pad_add_fusion.place, f32[1024,1]{1,0:T(8,128)} %copy-done.53, ...), custom_call_target="tpu_custom_call" | custom-call | flops 11500000256 | bytes 1048576 | tf_op jit(solution)/shard_map/gate_back/pallas_call | solution.py:351
  356.4 8.8 %collective-permute-done.41 = f32[136,512]{1,0:T(8,128)S(1)} collective-permute-done((f32[136,512]{1,0:T(8,128)}, f32[136,512]{1,0:T(8,128)S(1)}, u32[]{:S(2)}, u32[]{:S(2)}) %collective-permute-start.41) | collective-permute-done | bytes 278560 | tf_op jit(solution)/shard_map/ppermute | solution.py:395
  378.2 14.5 %collective-permute-done.36 = f32[256,1024]{1,0:T(8,128)S(1)} collective-permute-done((f32[256,1024]{1,0:T(8,128)S(1)}, f32[256,1024]{1,0:T(8,128)S(1)}, u32[]{:S(2)}, u32[]{:S(2)}) %collective-permute-start.36) | collective-permute-done | bytes 1048608 | tf_op jit(solution)/shard_map/ppermute | solution.py:409
  404.8 9.3 %ssd_within_back.2 = (f32[1024,512]{1,0:T(8,128)}, f32[1024,256]{1,0:T(8,128)}, f32[1024,1024]{1,0:T(8,128)}) custom-call(f32[1024,128]{1,0:T(8,128)} %get-tuple-element.175.cum, bf16[1024,512]{1,0:T(8,128)(2,1)} %get-tuple-element.176.xdt, bf16[1024,256]{1,0:T(8,128)(2,1)} %get-tuple-element.177.bc, f32[1024,1]{1,0:T(8,128)} %copy.111.seg, ...), custom_call_target="tpu_custom_call" | custom-call | flops 9200000000 | bytes 1048576 | tf_op jit(solution)/shard_map/ssd_within_back/pallas_call | solution.py:351
  416.3 20.4 %in_proj_conv_back.2 = (bf16[1024,896]{1,0:T(8,128)(2,1)}, f32[8,768]{1,0:T(8,128)}, f32[8,768]{1,0:T(8,128)}, f32[8,768]{1,0:T(8,128)}, f32[8,128]{1,0:T(8,128)}, /*index=5*/f32[8,512]{1,0:T(8,128)}) custom-call(f32[1024,512]{1,0:T(8,128)} %get-tuple-element.195.uin, f32[1024,256]{1,0:T(8,128)} %get-tuple-element.196.dbc, ...), custom_call_target="tpu_custom_call" | custom-call | flops 23000000512 | bytes 1048576 | tf_op jit(solution)/shard_map/in_proj_conv_back/pallas_call | solution.py:351
  438.3 15.4 %collective-permute-done.44.near_s = f32[256,1024]{1,0:T(8,128)S(1)} collective-permute-done((f32[256,1024]{1,0:T(8,128)S(1)}, f32[256,1024]{1,0:T(8,128)S(1)}, u32[]{:S(2)}, u32[]{:S(2)}) %collective-permute-start.44) | collective-permute-done | bytes 1048608 | tf_op jit(solution)/shard_map/ppermute | solution.py:494
  475.5 25.2 %collective-permute-done.47 = f32[256,1024]{1,0:T(8,128)S(1)} collective-permute-done((f32[256,1024]{1,0:T(8,128)S(1)}, f32[256,1024]{1,0:T(8,128)S(1)}, u32[]{:S(2)}, u32[]{:S(2)}) %collective-permute-start.47) | collective-permute-done | bytes 1048608 | tf_op jit(solution)/shard_map/ppermute | solution.py:409
  505.3 24.2 %collective-permute-done.50.refs_1_ = f32[256,1024]{1,0:T(8,128)} collective-permute-done((f32[256,1024]{1,0:T(8,128)S(1)}, f32[256,1024]{1,0:T(8,128)}, u32[]{:S(2)}, u32[]{:S(2)}) %collective-permute-start.50) | collective-permute-done | bytes 1048608 | tf_op jit(solution)/shard_map/ppermute | solution.py:409
  535.4 11.0 %gate_back.3 = (bf16[1024,1024]{1,0:T(8,128)(2,1)}, bf16[1024,512]{1,0:T(8,128)(2,1)}, bf16[1024,512]{1,0:T(8,128)(2,1)}, f32[4,128,512]{2,1,0:T(8,128)}, f32[4,...) custom-call(s32[2]{0:T(128)} %pad_add_fusion.place, f32[1024,1]{1,0:T(8,128)} %copy-done.51, ...), custom_call_target="tpu_custom_call" | custom-call | flops 11500000256 | bytes 1048576 | tf_op jit(solution)/shard_map/gate_back/pallas_call | solution.py:351
  547.0 9.4 %ssd_within_back.3 = (f32[1024,512]{1,0:T(8,128)}, f32[1024,256]{1,0:T(8,128)}, f32[1024,1024]{1,0:T(8,128)}) custom-call(f32[1024,128]{1,0:T(8,128)} %get-tuple-element.147.cum, bf16[1024,512]{1,0:T(8,128)(2,1)} %get-tuple-element.148.xdt, bf16[1024,256]{1,0:T(8,128)(2,1)} %get-tuple-element.149.bc, f32[1024,1]{1,0:T(8,128)} %copy.111.seg, ...), custom_call_target="tpu_custom_call" | custom-call | flops 9200000000 | bytes 1048576 | tf_op jit(solution)/shard_map/ssd_within_back/pallas_call | solution.py:351
  579.1 20.3 %in_proj_conv_back.3 = (bf16[1024,896]{1,0:T(8,128)(2,1)}, f32[8,768]{1,0:T(8,128)}, f32[8,768]{1,0:T(8,128)}, f32[8,768]{1,0:T(8,128)}, f32[8,128]{1,0:T(8,128)}, /*index=5*/f32[8,512]{1,0:T(8,128)}) custom-call(f32[1024,512]{1,0:T(8,128)} %get-tuple-element.217.uin, f32[1024,256]{1,0:T(8,128)} %get-tuple-element.218.dbc, ...), custom_call_target="tpu_custom_call" | custom-call | flops 23000000512 | bytes 1048576 | tf_op jit(solution)/shard_map/in_proj_conv_back/pallas_call | solution.py:351
  631.3 23.5 %collective-permute-done.60 = f32[256,1024]{1,0:T(8,128)S(1)} collective-permute-done((f32[256,1024]{1,0:T(8,128)S(1)}, f32[256,1024]{1,0:T(8,128)S(1)}, u32[]{:S(2)}, u32[]{:S(2)}) %collective-permute-start.60) | collective-permute-done | bytes 1048608 | tf_op jit(solution)/shard_map/ppermute | solution.py:409
  655.7 6.7 collective-permute-start.61
  684.3 11.9 %collective-permute-done.64.value_s = f32[256,1024]{1,0:T(8,128)} collective-permute-done((f32[256,1024]{1,0:T(8,128)S(1)}, f32[256,1024]{1,0:T(8,128)}, u32[]{:S(2)}, u32[]{:S(2)}) %collective-permute-start.64) | collective-permute-done | bytes 1048608 | tf_op jit(solution)/shard_map/ppermute | solution.py:494
  697.9 14.5 %collective-permute-start.66 = (f32[256,1024]{1,0:T(8,128)}, f32[256,1024]{1,0:T(8,128)}, u32[]{:S(2)}, u32[]{:S(2)}) collective-permute-start(f32[256,1024]{1,0:T(8,128)} %collective-permute-done.63.near), channel_id=1, source_target_pairs={{0,1},{1,0},{6,7},{7,6},{8,9},{9,8},{14,15},{15,14},{16,17},{17,16... | collective-permute-start | bytes 3145736 | tf_op jit(solution)/shard_map/ppermute | solution.py:494
  740.1 13.5 %collective-permute-done.66.near_s = f32[256,1024]{1,0:T(8,128)} collective-permute-done((f32[256,1024]{1,0:T(8,128)}, f32[256,1024]{1,0:T(8,128)}, u32[]{:S(2)}, u32[]{:S(2)}) %collective-permute-start.66) | collective-permute-done | bytes 1048608 | tf_op jit(solution)/shard_map/ppermute | solution.py:494
  753.6 6.8 collective-permute-start.71
  770.8 7.1 collective-permute-start.72
  812.7 17.5 %collective-permute-done.74 = f32[256,1536]{0,1:T(8,128)} collective-permute-done((f32[256,1536]{0,1:T(8,128)}, f32[256,1536]{0,1:T(8,128)}, u32[]{:S(2)}, u32[]{:S(2)}) %collective-permute-start.74) | collective-permute-done | bytes 1572896 | tf_op jit(solution)/shard_map/ppermute | solution.py:1085
  (578 shorter events, 401.2 us)
Async XLA Ops:
  7.2 595.5 %reduce-scatter.3.cloned.1.call-start = ((), (), s32[]{:S(2)}) async-start(), calls=%async_computation.2 | async-start | bytes 9175040 | tf_op jit(solution)/shard_map/reduce_scatter | solution.py:1021
  10.8 33.5 %collective-permute-start.1 = (f32[256,512]{1,0:T(8,128)}, f32[256,512]{1,0:T(8,128)}, u32[]{:S(2)}, u32[]{:S(2)}) collective-permute-start(f32[256,512]{1,0:T(8,128)} %dynamic-slice_convert_fusion), channel_id=1, source_target_pairs={{0,2},{6,4},{1,3},{7,5},{8,10},{14,12},{9,11},{15,13},{16,18},{22,... | collective-permute-start | bytes 1572872 | tf_op jit(solution)/shard_map/ppermute | solution.py:598
  20.4 35.5 %collective-permute-start.6 = (f32[2,64,128]{2,1,0:T(8,128)S(1)}, f32[2,64,128]{2,1,0:T(8,128)S(1)}, u32[]{:S(2)}, u32[]{:S(2)}) collective-permute-start(f32[2,64,128]{2,1,0:T(8,128)S(1)} %reshape.406), channel_id=1, source_target_pairs={{0,2},{6,4},{1,3},{7,5},{8,10},{14,12},{9,11},{15,13},{16,18},{22,... | collective-permute-start | bytes 196616 | tf_op jit(solution)/shard_map/ppermute | solution.py:672
  24.4 42.3 %collective-permute-start = (f32[1024,1024]{1,0:T(8,128)}, f32[1024,1024]{1,0:T(8,128)}, u32[]{:S(2)}, u32[]{:S(2)}) collective-permute-start(f32[1024,1024]{1,0:T(8,128)} %convert_element_type.74), channel_id=1, source_target_pairs={{0,4},{6,2},{1,5},{7,3},{8,12},{14,10},{9,13},{15,11},{16,20},{22,... | collective-permute-start | bytes 12582920 | tf_op jit(solution)/shard_map/ppermute | solution.py:538
  103.6 53.0 %collective-permute-start.18 = (f32[1024,1024]{1,0:T(8,128)}, f32[1024,1024]{1,0:T(8,128)}, u32[]{:S(2)}, u32[]{:S(2)}) collective-permute-start(f32[1024,1024]{1,0:T(8,128)} %convert_element_type.80), channel_id=1, source_target_pairs={{0,4},{6,2},{1,5},{7,3},{8,12},{14,10},{9,13},{15,11},{16,20},{22,... | collective-permute-start | bytes 12582920 | tf_op jit(solution)/shard_map/ppermute | solution.py:786
  109.4 25.6 %collective-permute-start.11 = (f32[256,1024]{1,0:T(8,128)}, f32[256,1024]{1,0:T(8,128)S(1)}, u32[]{:S(2)}, u32[]{:S(2)}) collective-permute-start(f32[256,1024]{1,0:T(8,128)} %collective-permute-done.5.refs_2_), channel_id=1, source_target_pairs={{2,10},{4,12},{10,2},{12,4},{18,26},{20,28},{26,18},{28,20},{3,11}... | collective-permute-start | bytes 3145736 | tf_op jit(solution)/shard_map/ppermute | solution.py:613
  110.2 31.5 %collective-permute-start.12 = (f32[256,1024]{1,0:T(8,128)}, f32[256,1024]{1,0:T(8,128)S(1)}, u32[]{:S(2)}, u32[]{:S(2)}) collective-permute-start(f32[256,1024]{1,0:T(8,128)} %collective-permute-done.5.refs_2_), channel_id=1, source_target_pairs={{2,18},{4,20},{10,26},{12,28},{18,2},{20,4},{26,10},{28,12},{3,19}... | collective-permute-start | bytes 3145736 | tf_op jit(solution)/shard_map/ppermute | solution.py:613
  110.9 30.8 %collective-permute-start.13 = (f32[256,1024]{1,0:T(8,128)}, f32[256,1024]{1,0:T(8,128)S(1)}, u32[]{:S(2)}, u32[]{:S(2)}) collective-permute-start(f32[256,1024]{1,0:T(8,128)} %collective-permute-done.5.refs_2_), channel_id=1, source_target_pairs={{2,26},{4,28},{10,18},{12,20},{18,10},{20,12},{26,2},{28,4},{3,27}... | collective-permute-start | bytes 3145736 | tf_op jit(solution)/shard_map/ppermute | solution.py:613
  120.4 36.3 %collective-permute-start.17 = (f32[256,1536]{1,0:T(8,128)}, f32[256,1536]{1,0:T(8,128)}, u32[]{:S(2)}, u32[]{:S(2)}) collective-permute-start(f32[256,1536]{1,0:T(8,128)} %maximum_convert_fusion), channel_id=1, source_target_pairs={{0,2},{6,4},{1,3},{7,5},{8,10},{14,12},{9,11},{15,13},{16,18},{22,... | collective-permute-start | bytes 4718600 | tf_op jit(solution)/shard_map/ppermute | solution.py:598
  185.0 29.3 %collective-permute-start.22 = (f32[256,1024]{1,0:T(8,128)}, f32[256,1024]{1,0:T(8,128)}, u32[]{:S(2)}, u32[]{:S(2)}) collective-permute-start(f32[256,1024]{1,0:T(8,128)} %constant_dynamic-slice_fusion.10), channel_id=1, source_target_pairs={{0,1},{1,0},{2,3},{3,2},{4,5},{5,4},{6,7},{7,6},{8,9},{9,8},{10,11... | collective-permute-start | bytes 3145736 | tf_op jit(solution)/shard_map/ppermute | solution.py:409
  191.1 52.2 %collective-permute-start.23 = (f32[256,1536]{1,0:T(8,128)}, f32[256,1536]{1,0:T(8,128)}, u32[]{:S(2)}, u32[]{:S(2)}) collective-permute-start(f32[256,1536]{1,0:T(8,128)} %collective-permute-done.17.refs_3_), channel_id=1, source_target_pairs={{2,10},{4,12},{10,2},{12,4},{18,26},{20,28},{26,18},{28,20},{3,11}... | collective-permute-start | bytes 4718600 | tf_op jit(solution)/shard_map/ppermute | solution.py:613
  192.9 50.4 %collective-permute-start.24 = (f32[256,1536]{1,0:T(8,128)}, f32[256,1536]{1,0:T(8,128)}, u32[]{:S(2)}, u32[]{:S(2)}) collective-permute-start(f32[256,1536]{1,0:T(8,128)} %collective-permute-done.17.refs_3_), channel_id=1, source_target_pairs={{2,18},{4,20},{10,26},{12,28},{18,2},{20,4},{26,10},{28,12},{3,19}... | collective-permute-start | bytes 4718600 | tf_op jit(solution)/shard_map/ppermute | solution.py:613
  194.8 48.6 %collective-permute-start.25 = (f32[256,1536]{1,0:T(8,128)}, f32[256,1536]{1,0:T(8,128)}, u32[]{:S(2)}, u32[]{:S(2)}) collective-permute-start(f32[256,1536]{1,0:T(8,128)} %collective-permute-done.17.refs_3_), channel_id=1, source_target_pairs={{2,26},{4,28},{10,18},{12,20},{18,10},{20,12},{26,2},{28,4},{3,27}... | collective-permute-start | bytes 4718600 | tf_op jit(solution)/shard_map/ppermute | solution.py:613
  219.3 32.9 %collective-permute-start.27 = (f32[256,1024]{1,0:T(8,128)}, f32[256,1024]{1,0:T(8,128)}, u32[]{:S(2)}, u32[]{:S(2)}) collective-permute-start(f32[256,1024]{1,0:T(8,128)} %get-tuple-element.344.refs_0_), channel_id=1, source_target_pairs={{0,4},{4,0},{1,5},{5,1},{2,6},{6,2},{3,7},{7,3},{8,12},{12,8},{9,1... | collective-permute-start | bytes 3145736 | tf_op jit(solution)/shard_map/ppermute | solution.py:409
  335.3 29.9 %collective-permute-start.35 = (f32[512,1024]{1,0:T(8,128)}, f32[512,1024]{1,0:T(8,128)}, u32[]{:S(2)}, u32[]{:S(2)}) collective-permute-start(f32[512,1024]{1,0:T(8,128)} %constant_dynamic-slice_fusion.8), channel_id=1, source_target_pairs={{0,4},{4,0},{1,5},{5,1},{2,6},{6,2},{3,7},{7,3},{8,12},{12,8},{9,1... | collective-permute-start | bytes 6291464 | tf_op jit(solution)/shard_map/ppermute | solution.py:409
  396.3 42.0 %collective-permute-start.37 = (f32[256,1024]{1,0:T(8,128)S(1)}, f32[256,1024]{1,0:T(8,128)}, u32[]{:S(2)}, u32[]{:S(2)}) collective-permute-start(f32[256,1024]{1,0:T(8,128)S(1)} %multiply_add_fusion.2.value), channel_id=1, source_target_pairs={{0,2},{6,4},{1,3},{7,5},{8,10},{14,12},{9,11},{15,13},{16,18},{22,... | collective-permute-start | bytes 3145736 | tf_op jit(solution)/shard_map/ppermute | solution.py:487
  399.4 38.8 %collective-permute-start.39 = (f32[256,1024]{1,0:T(8,128)S(1)}, f32[256,1024]{1,0:T(8,128)}, u32[]{:S(2)}, u32[]{:S(2)}) collective-permute-start(f32[256,1024]{1,0:T(8,128)S(1)} %multiply_add_fusion.2.value), channel_id=1, source_target_pairs={{4,2},{2,4},{5,3},{3,5},{12,10},{10,12},{13,11},{11,13},{20,18},{1... | collective-permute-start | bytes 3145736 | tf_op jit(solution)/shard_map/ppermute | solution.py:487
  401.1 37.1 %collective-permute-start.40 = (f32[256,1024]{1,0:T(8,128)S(1)}, f32[256,1024]{1,0:T(8,128)S(1)}, u32[]{:S(2)}, u32[]{:S(2)}) collective-permute-start(f32[256,1024]{1,0:T(8,128)S(1)} %multiply_add_fusion.2.value), channel_id=1, source_target_pairs={{0,1},{1,0},{6,7},{7,6},{8,9},{9,8},{14,15},{15,14},{16,17},{17,16... | collective-permute-start | bytes 3145736 | tf_op jit(solution)/shard_map/ppermute | solution.py:494
  414.1 39.6 %collective-permute-start.44 = (f32[256,1024]{1,0:T(8,128)S(1)}, f32[256,1024]{1,0:T(8,128)S(1)}, u32[]{:S(2)}, u32[]{:S(2)}) collective-permute-start(f32[256,1024]{1,0:T(8,128)S(1)} %collective-permute-done.38.near), channel_id=1, source_target_pairs={{0,1},{1,0},{6,7},{7,6},{8,9},{9,8},{14,15},{15,14},{16,17},{17,16... | collective-permute-start | bytes 3145736 | tf_op jit(solution)/shard_map/ppermute | solution.py:494
  468.5 313.3 %reduce-scatter.5.cloned.1.call-start = ((), (), s32[]{:S(2)}) async-start(), calls=%async_computation.3 | async-start | bytes 9175040 | tf_op jit(solution)/shard_map/reduce_scatter | solution.py:1021
  505.3 30.0 %collective-permute-start.51 = (f32[256,1024]{1,0:T(8,128)S(1)}, f32[256,1024]{1,0:T(8,128)}, u32[]{:S(2)}, u32[]{:S(2)}) collective-permute-start(f32[256,1024]{1,0:T(8,128)S(1)} %get-tuple-element.341.refs_0_), channel_id=1, source_target_pairs={{0,4},{4,0},{1,5},{5,1},{2,6},{6,2},{3,7},{7,3},{8,12},{12,8},{9,1... | collective-permute-start | bytes 3145736 | tf_op jit(solution)/shard_map/ppermute | solution.py:409
  575.2 25.5 %collective-permute-start.54 = (f32[256,1024]{1,0:T(8,128)}, f32[256,1024]{1,0:T(8,128)S(1)}, u32[]{:S(2)}, u32[]{:S(2)}) collective-permute-start(f32[256,1024]{1,0:T(8,128)} %collective-permute-done.37.mine), channel_id=1, source_target_pairs={{2,3},{3,2},{4,5},{5,4},{10,11},{11,10},{12,13},{13,12},{18,19},{1... | collective-permute-start | bytes 3145736 | tf_op jit(solution)/shard_map/ppermute | solution.py:504
  575.9 25.8 %collective-permute-start.55 = (f32[256,1024]{1,0:T(8,128)}, f32[256,1024]{1,0:T(8,128)S(1)}, u32[]{:S(2)}, u32[]{:S(2)}) collective-permute-start(f32[256,1024]{1,0:T(8,128)} %collective-permute-done.39.theirs), channel_id=1, source_target_pairs={{2,3},{3,2},{4,5},{5,4},{10,11},{11,10},{12,13},{13,12},{18,19},{1... | collective-permute-start | bytes 3145736 | tf_op jit(solution)/shard_map/ppermute | solution.py:505
  629.3 25.5 %collective-permute-start.60 = (f32[256,1024]{1,0:T(8,128)S(1)}, f32[256,1024]{1,0:T(8,128)S(1)}, u32[]{:S(2)}, u32[]{:S(2)}) collective-permute-start(f32[256,1024]{1,0:T(8,128)S(1)} %constant_dynamic-slice_fusion.3), channel_id=1, source_target_pairs={{0,1},{1,0},{2,3},{3,2},{4,5},{5,4},{6,7},{7,6},{8,9},{9,8},{10,11... | collective-permute-start | bytes 3145736 | tf_op jit(solution)/shard_map/ppermute | solution.py:409
  655.7 28.6 %collective-permute-start.61 = (f32[256,1024]{1,0:T(8,128)S(1)}, f32[256,1024]{1,0:T(8,128)}, u32[]{:S(2)}, u32[]{:S(2)}) collective-permute-start(f32[256,1024]{1,0:T(8,128)S(1)} %multiply_add_fusion.value), channel_id=1, source_target_pairs={{0,2},{6,4},{1,3},{7,5},{8,10},{14,12},{9,11},{15,13},{16,18},{22,... | collective-permute-start | bytes 3145736 | tf_op jit(solution)/shard_map/ppermute | solution.py:487
  665.4 30.9 %collective-permute-start.64 = (f32[256,1024]{1,0:T(8,128)S(1)}, f32[256,1024]{1,0:T(8,128)}, u32[]{:S(2)}, u32[]{:S(2)}) collective-permute-start(f32[256,1024]{1,0:T(8,128)S(1)} %multiply_add_fusion.value), channel_id=1, source_target_pairs={{0,1},{1,0},{6,7},{7,6},{8,9},{9,8},{14,15},{15,14},{16,17},{17,16... | collective-permute-start | bytes 3145736 | tf_op jit(solution)/shard_map/ppermute | solution.py:494
  696.2 43.9 %collective-permute-start.65 = (f32[256,1024]{1,0:T(8,128)}, f32[256,1024]{1,0:T(8,128)}, u32[]{:S(2)}, u32[]{:S(2)}) collective-permute-start(f32[256,1024]{1,0:T(8,128)} %collective-permute-done.61.mine), channel_id=1, source_target_pairs={{2,3},{3,2},{4,5},{5,4},{10,11},{11,10},{12,13},{13,12},{18,19},{1... | collective-permute-start | bytes 3145736 | tf_op jit(solution)/shard_map/ppermute | solution.py:504
  697.9 55.7 %collective-permute-start.66 = (f32[256,1024]{1,0:T(8,128)}, f32[256,1024]{1,0:T(8,128)}, u32[]{:S(2)}, u32[]{:S(2)}) collective-permute-start(f32[256,1024]{1,0:T(8,128)} %collective-permute-done.63.near), channel_id=1, source_target_pairs={{0,1},{1,0},{6,7},{7,6},{8,9},{9,8},{14,15},{15,14},{16,17},{17,16... | collective-permute-start | bytes 3145736 | tf_op jit(solution)/shard_map/ppermute | solution.py:494
  712.4 41.2 %collective-permute-start.67 = (f32[256,1024]{1,0:T(8,128)}, f32[256,1024]{1,0:T(8,128)}, u32[]{:S(2)}, u32[]{:S(2)}) collective-permute-start(f32[256,1024]{1,0:T(8,128)} %collective-permute-done.62.theirs), channel_id=1, source_target_pairs={{2,3},{3,2},{4,5},{5,4},{10,11},{11,10},{12,13},{13,12},{18,19},{1... | collective-permute-start | bytes 3145736 | tf_op jit(solution)/shard_map/ppermute | solution.py:505
  778.8 56.1 %collective-permute-start.76 = (f32[128,1536]{0,1:T(8,128)}, f32[128,1536]{0,1:T(8,128)}, u32[]{:S(2)}, u32[]{:S(2)}) collective-permute-start(f32[128,1536]{0,1:T(8,128)} %constant_dynamic-slice_fusion.1), channel_id=1, source_target_pairs={{0,4},{6,2},{1,5},{7,3},{8,12},{14,10},{9,13},{15,11},{16,20},{22,... | collective-permute-start | bytes 2359304 | tf_op jit(solution)/shard_map/ppermute | solution.py:1098
  784.7 45.6 %collective-permute-start.74 = (f32[256,1536]{0,1:T(8,128)}, f32[256,1536]{0,1:T(8,128)}, u32[]{:S(2)}, u32[]{:S(2)}) collective-permute-start(f32[256,1536]{0,1:T(8,128)} %slice.491), channel_id=1, source_target_pairs={{2,0},{4,6},{3,1},{5,7},{10,8},{12,14},{11,9},{13,15},{18,16},{20,... | collective-permute-start | bytes 4718600 | tf_op jit(solution)/shard_map/ppermute | solution.py:1085
  807.0 28.1 %collective-permute-start.79 = (f32[128,2,256]{0,2,1:T(8,128)S(1)}, f32[128,2,256]{0,2,1:T(8,128)S(1)}, u32[]{:S(2)}, u32[]{:S(2)}) collective-permute-start(f32[128,2,256]{0,2,1:T(8,128)S(1)} %fusion.103), channel_id=1, source_target_pairs={{0,2},{2,0},{1,3},{3,1},{4,6},{6,4},{5,7},{7,5},{8,10},{10,8},{9,1... | collective-permute-start | bytes 786440 | tf_op jit(solution)/shard_map/ppermute | solution.py:417
  (137 other events, 1913.6 us)
Sparse Core Ops, SparseCore 0:
  468.6 77.3 reduce-scatter.2
  622.6 80.9 reduce-scatter.4

commit v9 on v8

--- a/solution.py
+++ b/solution.py
@@ -908,6 +908,7 @@
             last_sum = scatter_sum(kept["proj"], (gate_scale,))
             hidden_own = hidden_own + own_rows(gate_scale)[:, None] * last_sum
             dy = behind(dy, hidden_own)
+            gsend = behind(gsend, hidden_own)
             out_parts = cross_over(hidden_own)
             out_held = (near_swap(hidden_own), near_swap(out_parts[2]))
         u, dbc, partial_z = call(
@@ -1036,19 +1037,21 @@
                 grad_ngain,
             ]
         )
-    vector = total(behind(jnp.stack(vectors), mark), ("chip",))
+    vector = total(behind(jnp.stack(vectors), mark), ("zh",))
+    first_sums = join_halves(behind(matrices[1][:, : 3 * inner], vector))
+    vector = total(vector, ("chip",))
+    other = swap(vector, "core")
+    common = (CONV + 1) * BC + width
+    shared = total((vector + other)[:, -common:], ("zl",))
+    grad_swaps, first_sums, g_last, vector, other, shared = behind(
+        (grad_swaps, first_sums, matrices[0], vector, other, shared)
+    )
     input_grad = deliver(grad_own, *grad_parts, f32, grad_swaps)
-    final_out = deliver(hidden_own, *out_parts, bf16, out_swaps, (mark,))
-    g_last = behind(matrices[0], *(grad_swaps or (mark,)))
+    final_out = deliver(hidden_own, *out_parts, bf16, out_swaps, (first_sums,))
     last_sums = join_halves(g_last[:, : 3 * inner])
     grad_wbc = jnp.stack([g_last[:, 3 * inner :], matrices[1][:, 3 * inner :]], axis=1)
     grad_wbc = total(half_rows(grad_wbc), ("zh",))
-    first_sums = join_halves(behind(matrices[1][:, : 3 * inner], mark))
     g_cols = [place_rows(last_sums), place_rows(first_sums)]
-    vector = total(behind(vector, first_sums, *(grad_swaps or (mark,))), ("zh",))
-    other = swap(vector, "core")
-    common = (CONV + 1) * BC + width
-    shared = total((vector + other)[:, -common:], ("zl",))
     by_head = jnp.where(held, vector, other)[:, :-common]
     g_bc = shared[:, :-width].reshape(LAYERS, CONV + 1, BC)
     g_ngain = shared[:, -width:]

time: 858 us -> 861 us (level)
    ppermute x10, waiting for transfers between devices: 32.7 us -> 71.2 us  [total(): lax.ppermute(value, axis, [(i, i ^ step) for i in range(count)])]
    ppermute x2, waiting for transfers between devices: 22.4 us -> 0.01 us  [join_halves(): return part + lax.ppermute(part, BOTH, CROSS_BACK)]
    ppermute x4, waiting for transfers between devices: 40.8 us -> 27.3 us  [near_swap(): return lax.ppermute(value, ('core', 'zh', 'zl'), here)]
    ppermute x10, starting transfers between devices: 18 us -> 30.9 us  [total(): lax.ppermute(value, axis, [(i, i ^ step) for i in range(count)])]
  transfers between devices with their start and end apart: 82 -> 82, of which waited for: 39 -> 40; matrix products, arithmetic and copies ran while one was open for 14% -> 13% of each run, Pallas kernels for 13% -> 13%
where the time goes in v9:
time: 861 us; the launch traced here: 848 us
  waiting for transfers between devices  288 us (33%)
  starting transfers between devices  193 us (22%)
  Pallas kernels  167 us (19%)
  local copies, waits for them, and re-layouts  76.2 us (9%)
  other arithmetic  73.3 us (9%)
  matrix products  34.5 us (4%)
  between operations  16.1 us (2%)
    pallas_call x12, Pallas kernels, call(): pl.pallas_call(kernel, grid=(count,), in_specs=[spec for spec, _ in ins],...  149 us
    ppermute x18, waiting for transfers between devices, swap(): return lax.ppermute(value, axis, SWAP)  129 us
    ppermute x10, waiting for transfers between devices, total(): lax.ppermute(value, axis, [(i, i ^ step) for i in range(count)])  71.2 us
    ppermute x12, waiting for transfers between devices, chain(): got = lax.ppermute(part, BLOCKS, [(i, i ^ step) for i in range(count)])  45.8 us
    ppermute x10, starting transfers between devices, total(): lax.ppermute(value, axis, [(i, i ^ step) for i in range(count)])  30.9 us
    dot_general x14, matrix products, mm(): lax.dot_general(left, right, (dims, ((), ())), preferred_element_type=f32...  29.8 us
    ppermute x18, starting transfers between devices, swap(): return lax.ppermute(value, axis, SWAP)  27.8 us
    ppermute x4, waiting for transfers between devices, near_swap(): return lax.ppermute(value, ('core', 'zh', 'zl'), here)  27.3 us
  transfers between devices with their start and end apart: 82, of which 40 were waited for; matrix products, arithmetic and copies ran while one was open for 13% of the time, Pallas kernels for 13%

profile of v9, /device:TPU:0, one launch (start us, length us, event | category | flops | bytes accessed | tf_op | source)
XLA Modules:
  0.0 848.1 jit_solution(13940089457013783299)
XLA Ops:
  10.8 6.7 collective-permute-start.1
  45.5 7.4 collective-permute-start.5
  68.6 12.0 %collective-permute-start.10 = (f32[8,768]{1,0:T(8,128)S(1)}, f32[8,768]{1,0:T(8,128)S(1)}, u32[]{:S(2)}, u32[]{:S(2)}) collective-permute-start(f32[8,768]{1,0:T(8,128)S(1)} %fusion), channel_id=1, source_target_pairs={{0,2},{2,8},{8,10},{10,16},{16,18},{18,24},{24,26},{1,3},{3,9},{9,... | collective-permute-start | bytes 73736 | tf_op jit(solution)/shard_map/ppermute | solution.py:385
  83.9 15.5 %in_proj_conv.2 = (bf16[1024,1024]{1,0:T(8,128)(2,1)}, f32[1024,768]{1,0:T(8,128)}, f32[1024,768]{1,0:T(8,128)}, f32[1024,128]{1,0:T(8,128)}, f32[1024,128]{1,0:...) custom-call(s32[2]{0:T(128)} %pad_add_fusion.place, ...), custom_call_target="tpu_custom_call" | custom-call | flops 18400000000 | bytes 1048576 | tf_op jit(solution)/shard_map/in_proj_conv/pallas_call | solution.py:351
  111.6 6.2 collective-permute-done.14
  120.4 12.1 %collective-permute-start.17 = (f32[256,1536]{1,0:T(8,128)}, f32[256,1536]{1,0:T(8,128)}, u32[]{:S(2)}, u32[]{:S(2)}) collective-permute-start(f32[256,1536]{1,0:T(8,128)} %maximum_convert_fusion), channel_id=1, source_target_pairs={{0,2},{6,4},{1,3},{7,5},{8,10},{14,12},{9,11},{15,13},{16,18},{22,... | collective-permute-start | bytes 4718600 | tf_op jit(solution)/shard_map/ppermute | solution.py:598
  157.9 11.2 %gate_out_proj.2 = (f32[1024,512]{1,0:T(8,128)}, bf16[1024,512]{1,0:T(8,128)(2,1)}, f32[1024,1024]{1,0:T(8,128)}, f32[8,1024]{1,0:T(8,128)}) custom-call(f32[1024,512]{1,0:T(8,128)} %ssd_within.2.yin, f32[1024,768]{1,0:T(8,128)} %get-tuple-element.158.cpre, f32[1024,128]{1,0:T(8,128)} %get-tuple-element.155.cum, bf16[1024,256]{1,0:T(8,128)(2,1)} %get-tuple-element.157.bc, ...), custom_call_target="tpu_custom_call" | custom-call | flops 13799999488 | bytes 1048576 | tf_op jit(solution)/shard_map/gate_out_proj/pallas_call | solution.py:351
  170.8 6.5 collective-permute-start.21
  196.7 17.6 %collective-permute-done.20 = f32[8,1024]{1,0:T(8,128)S(1)} collective-permute-done((f32[8,1024]{1,0:T(8,128)S(1)}, f32[8,1024]{1,0:T(8,128)S(1)}, u32[]{:S(2)}, u32[]{:S(2)}) %collective-permute-start.20) | collective-permute-done | bytes 32800 | tf_op jit(solution)/shard_map/ppermute | solution.py:417
  219.4 23.4 %collective-permute-done.26.refs_1_ = f32[256,1024]{1,0:T(8,128)} collective-permute-done((f32[256,1024]{1,0:T(8,128)}, f32[256,1024]{1,0:T(8,128)}, u32[]{:S(2)}, u32[]{:S(2)}) %collective-permute-start.26) | collective-permute-done | bytes 1048608 | tf_op jit(solution)/shard_map/ppermute | solution.py:409
  263.3 17.2 %in_proj_conv.3 = (bf16[1024,1024]{1,0:T(8,128)(2,1)}, f32[1024,768]{1,0:T(8,128)}, f32[1024,768]{1,0:T(8,128)}, f32[1024,128]{1,0:T(8,128)}, f32[1024,128]{1,0:...) custom-call(s32[2]{0:T(128)} %pad_add_fusion.place, ...), custom_call_target="tpu_custom_call" | custom-call | flops 18400000000 | bytes 1048576 | tf_op jit(solution)/shard_map/in_proj_conv/pallas_call | solution.py:351
  287.0 9.2 %collective-permute-done.30 = f32[136,512]{1,0:T(8,128)S(1)} collective-permute-done((f32[136,512]{1,0:T(8,128)}, f32[136,512]{1,0:T(8,128)S(1)}, u32[]{:S(2)}, u32[]{:S(2)}) %collective-permute-start.30) | collective-permute-done | bytes 278560 | tf_op jit(solution)/shard_map/ppermute | solution.py:395
  314.2 14.1 %gate_out_proj.3 = (f32[1024,512]{1,0:T(8,128)}, bf16[1024,512]{1,0:T(8,128)(2,1)}, f32[1024,1024]{1,0:T(8,128)}, f32[8,1024]{1,0:T(8,128)}) custom-call(f32[1024,512]{1,0:T(8,128)} %ssd_within.3.yin, f32[1024,768]{1,0:T(8,128)} %get-tuple-element.186.cpre, f32[1024,128]{1,0:T(8,128)} %get-tuple-element.183.cum, bf16[1024,256]{1,0:T(8,128)(2,1)} %get-tuple-element.185.bc, ...), custom_call_target="tpu_custom_call" | custom-call | flops 13799999488 | bytes 1048576 | tf_op jit(solution)/shard_map/gate_out_proj/pallas_call | solution.py:351
  347.4 10.1 %gate_back.2 = (bf16[1024,1024]{1,0:T(8,128)(2,1)}, bf16[1024,512]{1,0:T(8,128)(2,1)}, bf16[1024,512]{1,0:T(8,128)(2,1)}, f32[4,128,512]{2,1,0:T(8,128)}, f32[4,...) custom-call(s32[2]{0:T(128)} %pad_add_fusion.place, f32[1024,1]{1,0:T(8,128)} %copy-done.51, ...), custom_call_target="tpu_custom_call" | custom-call | flops 11500000256 | bytes 1048576 | tf_op jit(solution)/shard_map/gate_back/pallas_call | solution.py:351
  357.5 12.5 %collective-permute-done.36 = f32[256,1024]{1,0:T(8,128)S(1)} collective-permute-done((f32[256,1024]{1,0:T(8,128)S(1)}, f32[256,1024]{1,0:T(8,128)S(1)}, u32[]{:S(2)}, u32[]{:S(2)}) %collective-permute-start.36) | collective-permute-done | bytes 1048608 | tf_op jit(solution)/shard_map/ppermute | solution.py:409
  377.8 9.0 %collective-permute-done.41 = f32[136,512]{1,0:T(8,128)S(1)} collective-permute-done((f32[136,512]{1,0:T(8,128)S(1)}, f32[136,512]{1,0:T(8,128)S(1)}, u32[]{:S(2)}, u32[]{:S(2)}) %collective-permute-start.41) | collective-permute-done | bytes 278560 | tf_op jit(solution)/shard_map/ppermute | solution.py:395
  403.4 9.3 %ssd_within_back.2 = (f32[1024,512]{1,0:T(8,128)}, f32[1024,256]{1,0:T(8,128)}, f32[1024,1024]{1,0:T(8,128)}) custom-call(f32[1024,128]{1,0:T(8,128)} %get-tuple-element.183.cum, bf16[1024,512]{1,0:T(8,128)(2,1)} %get-tuple-element.184.xdt, bf16[1024,256]{1,0:T(8,128)(2,1)} %get-tuple-element.185.bc, f32[1024,1]{1,0:T(8,128)} %copy.111.seg, ...), custom_call_target="tpu_custom_call" | custom-call | flops 9200000000 | bytes 1048576 | tf_op jit(solution)/shard_map/ssd_within_back/pallas_call | solution.py:351
  415.4 20.4 %in_proj_conv_back.2 = (bf16[1024,896]{1,0:T(8,128)(2,1)}, f32[8,768]{1,0:T(8,128)}, f32[8,768]{1,0:T(8,128)}, f32[8,768]{1,0:T(8,128)}, f32[8,128]{1,0:T(8,128)}, /*index=5*/f32[8,512]{1,0:T(8,128)}) custom-call(f32[1024,512]{1,0:T(8,128)} %get-tuple-element.203.uin, f32[1024,256]{1,0:T(8,128)} %get-tuple-element.204.dbc, ...), custom_call_target="tpu_custom_call" | custom-call | flops 23000000512 | bytes 1048576 | tf_op jit(solution)/shard_map/in_proj_conv_back/pallas_call | solution.py:351
  437.3 15.4 %collective-permute-done.44.near_s = f32[256,1024]{1,0:T(8,128)S(1)} collective-permute-done((f32[256,1024]{1,0:T(8,128)S(1)}, f32[256,1024]{1,0:T(8,128)S(1)}, u32[]{:S(2)}, u32[]{:S(2)}) %collective-permute-start.44) | collective-permute-done | bytes 1048608 | tf_op jit(solution)/shard_map/ppermute | solution.py:494
  474.5 25.2 %collective-permute-done.47 = f32[256,1024]{1,0:T(8,128)S(1)} collective-permute-done((f32[256,1024]{1,0:T(8,128)S(1)}, f32[256,1024]{1,0:T(8,128)S(1)}, u32[]{:S(2)}, u32[]{:S(2)}) %collective-permute-start.47) | collective-permute-done | bytes 1048608 | tf_op jit(solution)/shard_map/ppermute | solution.py:409
  504.2 24.4 %collective-permute-done.50.refs_1_ = f32[256,1024]{1,0:T(8,128)} collective-permute-done((f32[256,1024]{1,0:T(8,128)S(1)}, f32[256,1024]{1,0:T(8,128)}, u32[]{:S(2)}, u32[]{:S(2)}) %collective-permute-start.50) | collective-permute-done | bytes 1048608 | tf_op jit(solution)/shard_map/ppermute | solution.py:409
  534.5 10.8 %gate_back.3 = (bf16[1024,1024]{1,0:T(8,128)(2,1)}, bf16[1024,512]{1,0:T(8,128)(2,1)}, bf16[1024,512]{1,0:T(8,128)(2,1)}, f32[4,128,512]{2,1,0:T(8,128)}, f32[4,...) custom-call(s32[2]{0:T(128)} %pad_add_fusion.place, f32[1024,1]{1,0:T(8,128)} %copy-done.49, ...), custom_call_target="tpu_custom_call" | custom-call | flops 11500000256 | bytes 1048576 | tf_op jit(solution)/shard_map/gate_back/pallas_call | solution.py:351
  545.4 9.4 %ssd_within_back.3 = (f32[1024,512]{1,0:T(8,128)}, f32[1024,256]{1,0:T(8,128)}, f32[1024,1024]{1,0:T(8,128)}) custom-call(f32[1024,128]{1,0:T(8,128)} %get-tuple-element.155.cum, bf16[1024,512]{1,0:T(8,128)(2,1)} %get-tuple-element.156.xdt, bf16[1024,256]{1,0:T(8,128)(2,1)} %get-tuple-element.157.bc, f32[1024,1]{1,0:T(8,128)} %copy.111.seg, ...), custom_call_target="tpu_custom_call" | custom-call | flops 9200000000 | bytes 1048576 | tf_op jit(solution)/shard_map/ssd_within_back/pallas_call | solution.py:351
  554.8 6.3 collective-permute-done.53
  578.7 20.3 %in_proj_conv_back.3 = (bf16[1024,896]{1,0:T(8,128)(2,1)}, f32[8,768]{1,0:T(8,128)}, f32[8,768]{1,0:T(8,128)}, f32[8,768]{1,0:T(8,128)}, f32[8,128]{1,0:T(8,128)}, /*index=5*/f32[8,512]{1,0:T(8,128)}) custom-call(f32[1024,512]{1,0:T(8,128)} %get-tuple-element.226.uin, f32[1024,256]{1,0:T(8,128)} %get-tuple-element.227.dbc, ...), custom_call_target="tpu_custom_call" | custom-call | flops 23000000512 | bytes 1048576 | tf_op jit(solution)/shard_map/in_proj_conv_back/pallas_call | solution.py:351
  627.7 25.2 %collective-permute-done.60 = f32[256,1024]{1,0:T(8,128)S(1)} collective-permute-done((f32[256,1024]{1,0:T(8,128)S(1)}, f32[256,1024]{1,0:T(8,128)S(1)}, u32[]{:S(2)}, u32[]{:S(2)}) %collective-permute-start.60) | collective-permute-done | bytes 1048608 | tf_op jit(solution)/shard_map/ppermute | solution.py:409
  657.3 6.1 collective-permute-start.61
  685.3 11.9 %collective-permute-done.64.value_s = f32[256,1024]{1,0:T(8,128)} collective-permute-done((f32[256,1024]{1,0:T(8,128)S(1)}, f32[256,1024]{1,0:T(8,128)}, u32[]{:S(2)}, u32[]{:S(2)}) %collective-permute-start.64) | collective-permute-done | bytes 1048608 | tf_op jit(solution)/shard_map/ppermute | solution.py:494
  697.4 12.0 %collective-permute-start.68 = (f32[2,14096]{1,0:T(2,128)S(1)}, f32[2,14096]{1,0:T(2,128)S(1)}, u32[]{:S(2)}, u32[]{:S(2)}) collective-permute-start(f32[2,14096]{1,0:T(2,128)S(1)} %pad_maximum_fusion.14), channel_id=1, source_target_pairs={{0,2},{2,0},{1,3},{3,1},{4,6},{6,4},{5,7},{7,5},{8,10},{10,8},{9,1... | collective-permute-start | bytes 338312 | tf_op jit(solution)/shard_map/ppermute | solution.py:417
  733.7 33.7 %collective-permute-done.73 = f32[2,2304]{1,0:T(2,128)S(1)} collective-permute-done((f32[2,2304]{1,0:T(2,128)S(1)}, f32[2,2304]{1,0:T(2,128)S(1)}, u32[]{:S(2)}, u32[]{:S(2)}) %collective-permute-start.73) | collective-permute-done | bytes 18464 | tf_op jit(solution)/shard_map/ppermute | solution.py:417
  775.8 10.3 %collective-permute-start.77 = (f32[128,2,256]{0,2,1:T(8,128)S(1)}, f32[128,2,256]{0,2,1:T(8,128)S(1)}, u32[]{:S(2)}, u32[]{:S(2)}) collective-permute-start(f32[128,2,256]{0,2,1:T(8,128)S(1)} %fusion.16), channel_id=1, source_target_pairs={{0,4},{4,0},{1,5},{5,1},{2,6},{6,2},{3,7},{7,3},{8,12},{12,8},{9,1... | collective-permute-start | bytes 786440 | tf_op jit(solution)/shard_map/ppermute | solution.py:409
  799.7 12.2 %collective-permute-start.79 = (f32[128,2,256]{0,2,1:T(8,128)S(1)}, f32[128,2,256]{0,2,1:T(8,128)S(1)}, u32[]{:S(2)}, u32[]{:S(2)}) collective-permute-start(f32[128,2,256]{0,2,1:T(8,128)S(1)} %fusion.103), channel_id=1, source_target_pairs={{0,2},{2,0},{1,3},{3,1},{4,6},{6,4},{5,7},{7,5},{8,10},{10,8},{9,1... | collective-permute-start | bytes 786440 | tf_op jit(solution)/shard_map/ppermute | solution.py:417
  (576 shorter events, 388.2 us)
Async XLA Ops:
  7.2 595.1 %reduce-scatter.3.cloned.1.call-start = ((), (), s32[]{:S(2)}) async-start(), calls=%async_computation.2 | async-start | bytes 9175040 | tf_op jit(solution)/shard_map/reduce_scatter | solution.py:1022
  10.8 33.6 %collective-permute-start.1 = (f32[256,512]{1,0:T(8,128)}, f32[256,512]{1,0:T(8,128)}, u32[]{:S(2)}, u32[]{:S(2)}) collective-permute-start(f32[256,512]{1,0:T(8,128)} %dynamic-slice_convert_fusion), channel_id=1, source_target_pairs={{0,2},{6,4},{1,3},{7,5},{8,10},{14,12},{9,11},{15,13},{16,18},{22,... | collective-permute-start | bytes 1572872 | tf_op jit(solution)/shard_map/ppermute | solution.py:598
  20.4 35.6 %collective-permute-start.6 = (f32[2,64,128]{2,1,0:T(8,128)S(1)}, f32[2,64,128]{2,1,0:T(8,128)S(1)}, u32[]{:S(2)}, u32[]{:S(2)}) collective-permute-start(f32[2,64,128]{2,1,0:T(8,128)S(1)} %reshape.406), channel_id=1, source_target_pairs={{0,2},{6,4},{1,3},{7,5},{8,10},{14,12},{9,11},{15,13},{16,18},{22,... | collective-permute-start | bytes 196616 | tf_op jit(solution)/shard_map/ppermute | solution.py:672
  24.3 42.3 %collective-permute-start = (f32[1024,1024]{1,0:T(8,128)}, f32[1024,1024]{1,0:T(8,128)}, u32[]{:S(2)}, u32[]{:S(2)}) collective-permute-start(f32[1024,1024]{1,0:T(8,128)} %convert_element_type.74), channel_id=1, source_target_pairs={{0,4},{6,2},{1,5},{7,3},{8,12},{14,10},{9,13},{15,11},{16,20},{22,... | collective-permute-start | bytes 12582920 | tf_op jit(solution)/shard_map/ppermute | solution.py:538
  103.7 53.0 %collective-permute-start.18 = (f32[1024,1024]{1,0:T(8,128)}, f32[1024,1024]{1,0:T(8,128)}, u32[]{:S(2)}, u32[]{:S(2)}) collective-permute-start(f32[1024,1024]{1,0:T(8,128)} %convert_element_type.80), channel_id=1, source_target_pairs={{0,4},{6,2},{1,5},{7,3},{8,12},{14,10},{9,13},{15,11},{16,20},{22,... | collective-permute-start | bytes 12582920 | tf_op jit(solution)/shard_map/ppermute | solution.py:786
  109.5 25.6 %collective-permute-start.11 = (f32[256,1024]{1,0:T(8,128)}, f32[256,1024]{1,0:T(8,128)S(1)}, u32[]{:S(2)}, u32[]{:S(2)}) collective-permute-start(f32[256,1024]{1,0:T(8,128)} %collective-permute-done.5.refs_2_), channel_id=1, source_target_pairs={{2,10},{4,12},{10,2},{12,4},{18,26},{20,28},{26,18},{28,20},{3,11}... | collective-permute-start | bytes 3145736 | tf_op jit(solution)/shard_map/ppermute | solution.py:613
  110.2 31.5 %collective-permute-start.12 = (f32[256,1024]{1,0:T(8,128)}, f32[256,1024]{1,0:T(8,128)S(1)}, u32[]{:S(2)}, u32[]{:S(2)}) collective-permute-start(f32[256,1024]{1,0:T(8,128)} %collective-permute-done.5.refs_2_), channel_id=1, source_target_pairs={{2,18},{4,20},{10,26},{12,28},{18,2},{20,4},{26,10},{28,12},{3,19}... | collective-permute-start | bytes 3145736 | tf_op jit(solution)/shard_map/ppermute | solution.py:613
  110.9 30.8 %collective-permute-start.13 = (f32[256,1024]{1,0:T(8,128)}, f32[256,1024]{1,0:T(8,128)S(1)}, u32[]{:S(2)}, u32[]{:S(2)}) collective-permute-start(f32[256,1024]{1,0:T(8,128)} %collective-permute-done.5.refs_2_), channel_id=1, source_target_pairs={{2,26},{4,28},{10,18},{12,20},{18,10},{20,12},{26,2},{28,4},{3,27}... | collective-permute-start | bytes 3145736 | tf_op jit(solution)/shard_map/ppermute | solution.py:613
  120.4 36.3 %collective-permute-start.17 = (f32[256,1536]{1,0:T(8,128)}, f32[256,1536]{1,0:T(8,128)}, u32[]{:S(2)}, u32[]{:S(2)}) collective-permute-start(f32[256,1536]{1,0:T(8,128)} %maximum_convert_fusion), channel_id=1, source_target_pairs={{0,2},{6,4},{1,3},{7,5},{8,10},{14,12},{9,11},{15,13},{16,18},{22,... | collective-permute-start | bytes 4718600 | tf_op jit(solution)/shard_map/ppermute | solution.py:598
  185.0 29.3 %collective-permute-start.22 = (f32[256,1024]{1,0:T(8,128)}, f32[256,1024]{1,0:T(8,128)}, u32[]{:S(2)}, u32[]{:S(2)}) collective-permute-start(f32[256,1024]{1,0:T(8,128)} %constant_dynamic-slice_fusion.10), channel_id=1, source_target_pairs={{0,1},{1,0},{2,3},{3,2},{4,5},{5,4},{6,7},{7,6},{8,9},{9,8},{10,11... | collective-permute-start | bytes 3145736 | tf_op jit(solution)/shard_map/ppermute | solution.py:409
  191.1 52.2 %collective-permute-start.23 = (f32[256,1536]{1,0:T(8,128)}, f32[256,1536]{1,0:T(8,128)}, u32[]{:S(2)}, u32[]{:S(2)}) collective-permute-start(f32[256,1536]{1,0:T(8,128)} %collective-permute-done.17.refs_3_), channel_id=1, source_target_pairs={{2,10},{4,12},{10,2},{12,4},{18,26},{20,28},{26,18},{28,20},{3,11}... | collective-permute-start | bytes 4718600 | tf_op jit(solution)/shard_map/ppermute | solution.py:613
  193.0 50.4 %collective-permute-start.24 = (f32[256,1536]{1,0:T(8,128)}, f32[256,1536]{1,0:T(8,128)}, u32[]{:S(2)}, u32[]{:S(2)}) collective-permute-start(f32[256,1536]{1,0:T(8,128)} %collective-permute-done.17.refs_3_), channel_id=1, source_target_pairs={{2,18},{4,20},{10,26},{12,28},{18,2},{20,4},{26,10},{28,12},{3,19}... | collective-permute-start | bytes 4718600 | tf_op jit(solution)/shard_map/ppermute | solution.py:613
  194.8 48.6 %collective-permute-start.25 = (f32[256,1536]{1,0:T(8,128)}, f32[256,1536]{1,0:T(8,128)}, u32[]{:S(2)}, u32[]{:S(2)}) collective-permute-start(f32[256,1536]{1,0:T(8,128)} %collective-permute-done.17.refs_3_), channel_id=1, source_target_pairs={{2,26},{4,28},{10,18},{12,20},{18,10},{20,12},{26,2},{28,4},{3,27}... | collective-permute-start | bytes 4718600 | tf_op jit(solution)/shard_map/ppermute | solution.py:613
  219.4 32.9 %collective-permute-start.27 = (f32[256,1024]{1,0:T(8,128)}, f32[256,1024]{1,0:T(8,128)}, u32[]{:S(2)}, u32[]{:S(2)}) collective-permute-start(f32[256,1024]{1,0:T(8,128)} %get-tuple-element.360.refs_0_), channel_id=1, source_target_pairs={{0,4},{4,0},{1,5},{5,1},{2,6},{6,2},{3,7},{7,3},{8,12},{12,8},{9,1... | collective-permute-start | bytes 3145736 | tf_op jit(solution)/shard_map/ppermute | solution.py:409
  391.5 45.8 %collective-permute-start.37 = (f32[256,1024]{1,0:T(8,128)S(1)}, f32[256,1024]{1,0:T(8,128)}, u32[]{:S(2)}, u32[]{:S(2)}) collective-permute-start(f32[256,1024]{1,0:T(8,128)S(1)} %multiply_add_fusion.2.value), channel_id=1, source_target_pairs={{0,2},{6,4},{1,3},{7,5},{8,10},{14,12},{9,11},{15,13},{16,18},{22,... | collective-permute-start | bytes 3145736 | tf_op jit(solution)/shard_map/ppermute | solution.py:487
  394.1 43.2 %collective-permute-start.39 = (f32[256,1024]{1,0:T(8,128)S(1)}, f32[256,1024]{1,0:T(8,128)}, u32[]{:S(2)}, u32[]{:S(2)}) collective-permute-start(f32[256,1024]{1,0:T(8,128)S(1)} %multiply_add_fusion.2.value), channel_id=1, source_target_pairs={{4,2},{2,4},{5,3},{3,5},{12,10},{10,12},{13,11},{11,13},{20,18},{1... | collective-permute-start | bytes 3145736 | tf_op jit(solution)/shard_map/ppermute | solution.py:487
  395.8 41.5 %collective-permute-start.40 = (f32[256,1024]{1,0:T(8,128)S(1)}, f32[256,1024]{1,0:T(8,128)S(1)}, u32[]{:S(2)}, u32[]{:S(2)}) collective-permute-start(f32[256,1024]{1,0:T(8,128)S(1)} %multiply_add_fusion.2.value), channel_id=1, source_target_pairs={{0,1},{1,0},{6,7},{7,6},{8,9},{9,8},{14,15},{15,14},{16,17},{17,16... | collective-permute-start | bytes 3145736 | tf_op jit(solution)/shard_map/ppermute | solution.py:494
  413.4 39.3 %collective-permute-start.44 = (f32[256,1024]{1,0:T(8,128)S(1)}, f32[256,1024]{1,0:T(8,128)S(1)}, u32[]{:S(2)}, u32[]{:S(2)}) collective-permute-start(f32[256,1024]{1,0:T(8,128)S(1)} %collective-permute-done.38.near), channel_id=1, source_target_pairs={{0,1},{1,0},{6,7},{7,6},{8,9},{9,8},{14,15},{15,14},{16,17},{17,16... | collective-permute-start | bytes 3145736 | tf_op jit(solution)/shard_map/ppermute | solution.py:494
  467.6 303.1 %reduce-scatter.5.cloned.1.call-start = ((), (), s32[]{:S(2)}) async-start(), calls=%async_computation.3 | async-start | bytes 9175040 | tf_op jit(solution)/shard_map/reduce_scatter | solution.py:1022
  504.2 30.2 %collective-permute-start.51 = (f32[256,1024]{1,0:T(8,128)S(1)}, f32[256,1024]{1,0:T(8,128)}, u32[]{:S(2)}, u32[]{:S(2)}) collective-permute-start(f32[256,1024]{1,0:T(8,128)S(1)} %get-tuple-element.357.refs_0_), channel_id=1, source_target_pairs={{0,4},{4,0},{1,5},{5,1},{2,6},{6,2},{3,7},{7,3},{8,12},{12,8},{9,1... | collective-permute-start | bytes 3145736 | tf_op jit(solution)/shard_map/ppermute | solution.py:409
  573.2 27.2 %collective-permute-start.54 = (f32[256,1024]{1,0:T(8,128)}, f32[256,1024]{1,0:T(8,128)S(1)}, u32[]{:S(2)}, u32[]{:S(2)}) collective-permute-start(f32[256,1024]{1,0:T(8,128)} %collective-permute-done.37.mine), channel_id=1, source_target_pairs={{2,3},{3,2},{4,5},{5,4},{10,11},{11,10},{12,13},{13,12},{18,19},{1... | collective-permute-start | bytes 3145736 | tf_op jit(solution)/shard_map/ppermute | solution.py:504
  573.9 27.4 %collective-permute-start.55 = (f32[256,1024]{1,0:T(8,128)}, f32[256,1024]{1,0:T(8,128)S(1)}, u32[]{:S(2)}, u32[]{:S(2)}) collective-permute-start(f32[256,1024]{1,0:T(8,128)} %collective-permute-done.39.theirs), channel_id=1, source_target_pairs={{2,3},{3,2},{4,5},{5,4},{10,11},{11,10},{12,13},{13,12},{18,19},{1... | collective-permute-start | bytes 3145736 | tf_op jit(solution)/shard_map/ppermute | solution.py:505
  657.3 28.0 %collective-permute-start.61 = (f32[256,1024]{1,0:T(8,128)S(1)}, f32[256,1024]{1,0:T(8,128)}, u32[]{:S(2)}, u32[]{:S(2)}) collective-permute-start(f32[256,1024]{1,0:T(8,128)S(1)} %multiply_add_fusion.value), channel_id=1, source_target_pairs={{0,2},{6,4},{1,3},{7,5},{8,10},{14,12},{9,11},{15,13},{16,18},{22,... | collective-permute-start | bytes 3145736 | tf_op jit(solution)/shard_map/ppermute | solution.py:487
  665.1 32.2 %collective-permute-start.64 = (f32[256,1024]{1,0:T(8,128)S(1)}, f32[256,1024]{1,0:T(8,128)}, u32[]{:S(2)}, u32[]{:S(2)}) collective-permute-start(f32[256,1024]{1,0:T(8,128)S(1)} %multiply_add_fusion.value), channel_id=1, source_target_pairs={{0,1},{1,0},{6,7},{7,6},{8,9},{9,8},{14,15},{15,14},{16,17},{17,16... | collective-permute-start | bytes 3145736 | tf_op jit(solution)/shard_map/ppermute | solution.py:494
  712.6 54.8 %collective-permute-start.69 = (f32[256,1536]{0,1:T(8,128)}, f32[256,1536]{0,1:T(8,128)}, u32[]{:S(2)}, u32[]{:S(2)}) collective-permute-start(f32[256,1536]{0,1:T(8,128)} %slice.568), channel_id=1, source_target_pairs={{2,0},{4,6},{3,1},{5,7},{10,8},{12,14},{11,9},{13,15},{18,16},{20,... | collective-permute-start | bytes 4718600 | tf_op jit(solution)/shard_map/ppermute | solution.py:1088
  721.4 49.2 %collective-permute-start.65 = (f32[256,1024]{1,0:T(8,128)}, f32[256,1024]{1,0:T(8,128)}, u32[]{:S(2)}, u32[]{:S(2)}) collective-permute-start(f32[256,1024]{1,0:T(8,128)} %collective-permute-done.61.mine), channel_id=1, source_target_pairs={{2,3},{3,2},{4,5},{5,4},{10,11},{11,10},{12,13},{13,12},{18,19},{1... | collective-permute-start | bytes 3145736 | tf_op jit(solution)/shard_map/ppermute | solution.py:504
  723.1 47.6 %collective-permute-start.66 = (f32[256,1024]{1,0:T(8,128)}, f32[256,1024]{1,0:T(8,128)}, u32[]{:S(2)}, u32[]{:S(2)}) collective-permute-start(f32[256,1024]{1,0:T(8,128)} %collective-permute-done.62.theirs), channel_id=1, source_target_pairs={{2,3},{3,2},{4,5},{5,4},{10,11},{11,10},{12,13},{13,12},{18,19},{1... | collective-permute-start | bytes 3145736 | tf_op jit(solution)/shard_map/ppermute | solution.py:505
  724.7 45.9 %collective-permute-start.67 = (f32[256,1024]{1,0:T(8,128)}, f32[256,1024]{1,0:T(8,128)}, u32[]{:S(2)}, u32[]{:S(2)}) collective-permute-start(f32[256,1024]{1,0:T(8,128)} %collective-permute-done.63.near), channel_id=1, source_target_pairs={{0,1},{1,0},{6,7},{7,6},{8,9},{9,8},{14,15},{15,14},{16,17},{17,16... | collective-permute-start | bytes 3145736 | tf_op jit(solution)/shard_map/ppermute | solution.py:494
  732.2 35.1 %collective-permute-start.73 = (f32[2,2304]{1,0:T(2,128)S(1)}, f32[2,2304]{1,0:T(2,128)S(1)}, u32[]{:S(2)}, u32[]{:S(2)}) collective-permute-start(f32[2,2304]{1,0:T(2,128)S(1)} %slice_add_fusion), channel_id=1, source_target_pairs={{0,1},{1,0},{2,3},{3,2},{4,5},{5,4},{6,7},{7,6},{8,9},{9,8},{10,11... | collective-permute-start | bytes 55304 | tf_op jit(solution)/shard_map/ppermute | solution.py:417
  774.5 57.3 %collective-permute-start.74 = (f32[256,1536]{0,1:T(8,128)}, f32[256,1536]{0,1:T(8,128)}, u32[]{:S(2)}, u32[]{:S(2)}) collective-permute-start(f32[256,1536]{0,1:T(8,128)} %slice.491), channel_id=1, source_target_pairs={{2,0},{4,6},{3,1},{5,7},{10,8},{12,14},{11,9},{13,15},{18,16},{20,... | collective-permute-start | bytes 4718600 | tf_op jit(solution)/shard_map/ppermute | solution.py:1088
  790.4 47.0 %collective-permute-start.76 = (f32[128,1536]{0,1:T(8,128)}, f32[128,1536]{0,1:T(8,128)}, u32[]{:S(2)}, u32[]{:S(2)}) collective-permute-start(f32[128,1536]{0,1:T(8,128)} %constant_dynamic-slice_fusion.1), channel_id=1, source_target_pairs={{0,4},{6,2},{1,5},{7,3},{8,12},{14,10},{9,13},{15,11},{16,20},{22,... | collective-permute-start | bytes 2359304 | tf_op jit(solution)/shard_map/ppermute | solution.py:1101
  799.7 32.0 %collective-permute-start.79 = (f32[128,2,256]{0,2,1:T(8,128)S(1)}, f32[128,2,256]{0,2,1:T(8,128)S(1)}, u32[]{:S(2)}, u32[]{:S(2)}) collective-permute-start(f32[128,2,256]{0,2,1:T(8,128)S(1)} %fusion.103), channel_id=1, source_target_pairs={{0,2},{2,0},{1,3},{3,1},{4,6},{6,4},{5,7},{7,5},{8,10},{10,8},{9,1... | collective-permute-start | bytes 786440 | tf_op jit(solution)/shard_map/ppermute | solution.py:417
  (136 other events, 1701.4 us)
Sparse Core Ops, SparseCore 0:
  467.7 76.1 reduce-scatter.2
  620.9 78.8 reduce-scatter.4

commit v10 on v9

--- a/solution.py
+++ b/solution.py
@@ -782,8 +782,6 @@
             wz, wout = gather_weights(
                 behind(first_rest, wall), [w_z[0], w_out[0]], third=(send,)
             )
-            cotangent = behind(cotangent, send).astype(f32)
-            cot_sent = lax.ppermute(cotangent, BOTH, CORE_OUT)
         else:
             wz, wout = next_wz, next_wout
         zval = mm(normed, wz)
@@ -806,6 +804,8 @@
         entry = chain(send, False, stages)
         if layer == 0:
             second_all = weights_over([w_x[1], w_z[1], w_out[1]], stages[0])
+            cotangent = behind(cotangent, stages[0]).astype(f32)
+            cot_sent = lax.ppermute(cotangent, BOTH, CORE_OUT)
             entry = behind(entry, second_all, cot_sent)
             cotangent = jnp.where(held, cotangent, cot_sent)
         y, gate_in, proj, sums = call(
@@ -992,10 +992,10 @@
             gall, (last8 + rim_back).astype(bf16), (tok - ROWS, 0)
         )
         partial = partial_z + mm(gall, kept["wall"], ((1,), (1,)))
-        grad_normed = scatter_sum(partial)
         late = behind(gall, partial)
         grad_wbc = mm(kept["normed"], late[:, inner : inner + BC], ((0,), (0,)))
         grad_win = mm(kept["normed"], behind(late, grad_wbc)[:, :inner], ((0,), (0,)))
+        grad_normed = scatter_sum(partial, (grad_win,) if layer == 0 else ())
         if layer == 0:
             grad_own = input_gradient(grad_own, grad_normed, kept["hidden"], norm_gain[layer])
             grad_parts = cross_over(grad_own)
@@ -1038,11 +1038,14 @@
             ]
         )
     vector = total(behind(jnp.stack(vectors), mark), ("zh",))
+    common = (CONV + 1) * BC + width
+    vector = jnp.concatenate(
+        [vector[:, :-common], total(vector[:, -common:], ("zl",))], axis=1
+    )
     first_sums = join_halves(behind(matrices[1][:, : 3 * inner], vector))
     vector = total(vector, ("chip",))
     other = swap(vector, "core")
-    common = (CONV + 1) * BC + width
-    shared = total((vector + other)[:, -common:], ("zl",))
+    shared = (vector + other)[:, -common:]
     grad_swaps, first_sums, g_last, vector, other, shared = behind(
         (grad_swaps, first_sums, matrices[0], vector, other, shared)
     )

time: 861 us -> 864 us (level)
    ppermute x10, waiting for transfers between devices: 71.2 us -> 39.8 us  [total(): lax.ppermute(value, axis, [(i, i ^ step) for i in range(count)])]
    ppermute x2, waiting for transfers between devices: 0.01 us -> 15.8 us  [join_halves(): return part + lax.ppermute(part, BOTH, CROSS_BACK)]
    ppermute x4, waiting for transfers between devices: 27.3 us -> 42 us  [near_swap(): return lax.ppermute(value, ('core', 'zh', 'zl'), here)]
  transfers between devices with their start and end apart: 82 -> 82, of which waited for: 40 -> 42; matrix products, arithmetic and copies ran while one was open for 13% -> 13% of each run, Pallas kernels for 13% -> 13%
where the time goes in v10:
time: 864 us; the launch traced here: 853 us
  waiting for transfers between devices  286 us (33%)
  starting transfers between devices  201 us (23%)
  Pallas kernels  167 us (19%)
  local copies, waits for them, and re-layouts  76.3 us (9%)
  other arithmetic  72.1 us (8%)
  matrix products  34.5 us (4%)
  between operations  16.1 us (2%)
    pallas_call x12, Pallas kernels, call(): pl.pallas_call(kernel, grid=(count,), in_specs=[spec for spec, _ in ins],...  150 us
    ppermute x18, waiting for transfers between devices, swap(): return lax.ppermute(value, axis, SWAP)  128 us
    ppermute x12, waiting for transfers between devices, chain(): got = lax.ppermute(part, BLOCKS, [(i, i ^ step) for i in range(count)])  46.4 us
    ppermute x4, waiting for transfers between devices, near_swap(): return lax.ppermute(value, ('core', 'zh', 'zl'), here)  42 us
    ppermute x10, waiting for transfers between devices, total(): lax.ppermute(value, axis, [(i, i ^ step) for i in range(count)])  39.8 us
    ppermute x10, starting transfers between devices, total(): lax.ppermute(value, axis, [(i, i ^ step) for i in range(count)])  36.3 us
    ppermute x18, starting transfers between devices, swap(): return lax.ppermute(value, axis, SWAP)  31.6 us
    dot_general x14, matrix products, mm(): lax.dot_general(left, right, (dims, ((), ())), preferred_element_type=f32...  29.9 us
  transfers between devices with their start and end apart: 82, of which 42 were waited for; matrix products, arithmetic and copies ran while one was open for 13% of the time, Pallas kernels for 13%

profile of v10, /device:TPU:0, one launch (start us, length us, event | category | flops | bytes accessed | tf_op | source)
XLA Modules:
  0.0 853.0 jit_solution(14067754640434064829)
XLA Ops:
  10.8 6.8 collective-permute-start.1
  45.6 7.3 collective-permute-start.5
  68.6 12.0 %collective-permute-start.10 = (f32[8,768]{1,0:T(8,128)S(1)}, f32[8,768]{1,0:T(8,128)S(1)}, u32[]{:S(2)}, u32[]{:S(2)}) collective-permute-start(f32[8,768]{1,0:T(8,128)S(1)} %fusion), channel_id=1, source_target_pairs={{0,2},{2,8},{8,10},{10,16},{16,18},{18,24},{24,26},{1,3},{3,9},{9,... | collective-permute-start | bytes 73736 | tf_op jit(solution)/shard_map/ppermute | solution.py:385
  84.0 15.5 %in_proj_conv.2 = (bf16[1024,1024]{1,0:T(8,128)(2,1)}, f32[1024,768]{1,0:T(8,128)}, f32[1024,768]{1,0:T(8,128)}, f32[1024,128]{1,0:T(8,128)}, f32[1024,128]{1,0:...) custom-call(s32[2]{0:T(128)} %pad_add_fusion.place, ...), custom_call_target="tpu_custom_call" | custom-call | flops 18400000000 | bytes 1048576 | tf_op jit(solution)/shard_map/in_proj_conv/pallas_call | solution.py:351
  102.8 7.4 collective-permute-done.14
  124.5 10.8 %collective-permute-start.17 = (f32[256,1536]{1,0:T(8,128)}, f32[256,1536]{1,0:T(8,128)}, u32[]{:S(2)}, u32[]{:S(2)}) collective-permute-start(f32[256,1536]{1,0:T(8,128)} %maximum_convert_fusion), channel_id=1, source_target_pairs={{0,2},{6,4},{1,3},{7,5},{8,10},{14,12},{9,11},{15,13},{16,18},{22,... | collective-permute-start | bytes 4718600 | tf_op jit(solution)/shard_map/ppermute | solution.py:598
  156.3 11.2 %gate_out_proj.2 = (f32[1024,512]{1,0:T(8,128)}, bf16[1024,512]{1,0:T(8,128)(2,1)}, f32[1024,1024]{1,0:T(8,128)}, f32[8,1024]{1,0:T(8,128)}) custom-call(f32[1024,512]{1,0:T(8,128)} %ssd_within.2.yin, f32[1024,768]{1,0:T(8,128)} %get-tuple-element.159.cpre, f32[1024,128]{1,0:T(8,128)} %get-tuple-element.156.cum, bf16[1024,256]{1,0:T(8,128)(2,1)} %get-tuple-element.158.bc, ...), custom_call_target="tpu_custom_call" | custom-call | flops 13799999488 | bytes 1048576 | tf_op jit(solution)/shard_map/gate_out_proj/pallas_call | solution.py:351
  169.3 13.9 %collective-permute-start.21 = (f32[512,1024]{1,0:T(8,128)S(1)}, f32[512,1024]{1,0:T(8,128)}, u32[]{:S(2)}, u32[]{:S(2)}) collective-permute-start(f32[512,1024]{1,0:T(8,128)S(1)} %constant_dynamic-slice_fusion.11), channel_id=1, source_target_pairs={{0,4},{4,0},{1,5},{5,1},{2,6},{6,2},{3,7},{7,3},{8,12},{12,8},{9,1... | collective-permute-start | bytes 6291464 | tf_op jit(solution)/shard_map/ppermute | solution.py:409
  199.6 17.6 %collective-permute-done.20 = f32[8,1024]{1,0:T(8,128)S(1)} collective-permute-done((f32[8,1024]{1,0:T(8,128)S(1)}, f32[8,1024]{1,0:T(8,128)S(1)}, u32[]{:S(2)}, u32[]{:S(2)}) %collective-permute-start.20) | collective-permute-done | bytes 32800 | tf_op jit(solution)/shard_map/ppermute | solution.py:417
  222.1 23.5 %collective-permute-done.26.refs_1_ = f32[256,1024]{1,0:T(8,128)} collective-permute-done((f32[256,1024]{1,0:T(8,128)}, f32[256,1024]{1,0:T(8,128)}, u32[]{:S(2)}, u32[]{:S(2)}) %collective-permute-start.26) | collective-permute-done | bytes 1048608 | tf_op jit(solution)/shard_map/ppermute | solution.py:409
  266.1 17.2 %in_proj_conv.3 = (bf16[1024,1024]{1,0:T(8,128)(2,1)}, f32[1024,768]{1,0:T(8,128)}, f32[1024,768]{1,0:T(8,128)}, f32[1024,128]{1,0:T(8,128)}, f32[1024,128]{1,0:...) custom-call(s32[2]{0:T(128)} %pad_add_fusion.place, ...), custom_call_target="tpu_custom_call" | custom-call | flops 18400000000 | bytes 1048576 | tf_op jit(solution)/shard_map/in_proj_conv/pallas_call | solution.py:351
  289.7 9.2 %collective-permute-done.30 = f32[136,512]{1,0:T(8,128)S(1)} collective-permute-done((f32[136,512]{1,0:T(8,128)}, f32[136,512]{1,0:T(8,128)S(1)}, u32[]{:S(2)}, u32[]{:S(2)}) %collective-permute-start.30) | collective-permute-done | bytes 278560 | tf_op jit(solution)/shard_map/ppermute | solution.py:395
  318.6 14.1 %gate_out_proj.3 = (f32[1024,512]{1,0:T(8,128)}, bf16[1024,512]{1,0:T(8,128)(2,1)}, f32[1024,1024]{1,0:T(8,128)}, f32[8,1024]{1,0:T(8,128)}) custom-call(f32[1024,512]{1,0:T(8,128)} %ssd_within.3.yin, f32[1024,768]{1,0:T(8,128)} %get-tuple-element.187.cpre, f32[1024,128]{1,0:T(8,128)} %get-tuple-element.184.cum, bf16[1024,256]{1,0:T(8,128)(2,1)} %get-tuple-element.186.bc, ...), custom_call_target="tpu_custom_call" | custom-call | flops 13799999488 | bytes 1048576 | tf_op jit(solution)/shard_map/gate_out_proj/pallas_call | solution.py:351
  350.2 10.2 %gate_back.2 = (bf16[1024,1024]{1,0:T(8,128)(2,1)}, bf16[1024,512]{1,0:T(8,128)(2,1)}, bf16[1024,512]{1,0:T(8,128)(2,1)}, f32[4,128,512]{2,1,0:T(8,128)}, f32[4,...) custom-call(s32[2]{0:T(128)} %pad_add_fusion.place, f32[1024,1]{1,0:T(8,128)} %copy-done.51, ...), custom_call_target="tpu_custom_call" | custom-call | flops 11500000256 | bytes 1048576 | tf_op jit(solution)/shard_map/gate_back/pallas_call | solution.py:351
  360.3 14.1 %collective-permute-done.36 = f32[256,1024]{1,0:T(8,128)S(1)} collective-permute-done((f32[256,1024]{1,0:T(8,128)S(1)}, f32[256,1024]{1,0:T(8,128)S(1)}, u32[]{:S(2)}, u32[]{:S(2)}) %collective-permute-start.36) | collective-permute-done | bytes 1048608 | tf_op jit(solution)/shard_map/ppermute | solution.py:409
  380.3 9.4 %collective-permute-done.41 = f32[136,512]{1,0:T(8,128)S(1)} collective-permute-done((f32[136,512]{1,0:T(8,128)S(1)}, f32[136,512]{1,0:T(8,128)S(1)}, u32[]{:S(2)}, u32[]{:S(2)}) %collective-permute-start.41) | collective-permute-done | bytes 278560 | tf_op jit(solution)/shard_map/ppermute | solution.py:395
  404.6 9.3 %ssd_within_back.2 = (f32[1024,512]{1,0:T(8,128)}, f32[1024,256]{1,0:T(8,128)}, f32[1024,1024]{1,0:T(8,128)}) custom-call(f32[1024,128]{1,0:T(8,128)} %get-tuple-element.184.cum, bf16[1024,512]{1,0:T(8,128)(2,1)} %get-tuple-element.185.xdt, bf16[1024,256]{1,0:T(8,128)(2,1)} %get-tuple-element.186.bc, f32[1024,1]{1,0:T(8,128)} %copy.111.seg, ...), custom_call_target="tpu_custom_call" | custom-call | flops 9200000000 | bytes 1048576 | tf_op jit(solution)/shard_map/ssd_within_back/pallas_call | solution.py:351
  416.6 20.4 %in_proj_conv_back.2 = (bf16[1024,896]{1,0:T(8,128)(2,1)}, f32[8,768]{1,0:T(8,128)}, f32[8,768]{1,0:T(8,128)}, f32[8,768]{1,0:T(8,128)}, f32[8,128]{1,0:T(8,128)}, /*index=5*/f32[8,512]{1,0:T(8,128)}) custom-call(f32[1024,512]{1,0:T(8,128)} %get-tuple-element.204.uin, f32[1024,256]{1,0:T(8,128)} %get-tuple-element.205.dbc, ...), custom_call_target="tpu_custom_call" | custom-call | flops 23000000512 | bytes 1048576 | tf_op jit(solution)/shard_map/in_proj_conv_back/pallas_call | solution.py:351
  438.5 15.7 %collective-permute-done.44.near_s = f32[256,1024]{1,0:T(8,128)S(1)} collective-permute-done((f32[256,1024]{1,0:T(8,128)S(1)}, f32[256,1024]{1,0:T(8,128)S(1)}, u32[]{:S(2)}, u32[]{:S(2)}) %collective-permute-start.44) | collective-permute-done | bytes 1048608 | tf_op jit(solution)/shard_map/ppermute | solution.py:494
  476.0 25.2 %collective-permute-done.47 = f32[256,1024]{1,0:T(8,128)S(1)} collective-permute-done((f32[256,1024]{1,0:T(8,128)S(1)}, f32[256,1024]{1,0:T(8,128)S(1)}, u32[]{:S(2)}, u32[]{:S(2)}) %collective-permute-start.47) | collective-permute-done | bytes 1048608 | tf_op jit(solution)/shard_map/ppermute | solution.py:409
  505.8 24.2 %collective-permute-done.50.refs_1_ = f32[256,1024]{1,0:T(8,128)} collective-permute-done((f32[256,1024]{1,0:T(8,128)S(1)}, f32[256,1024]{1,0:T(8,128)}, u32[]{:S(2)}, u32[]{:S(2)}) %collective-permute-start.50) | collective-permute-done | bytes 1048608 | tf_op jit(solution)/shard_map/ppermute | solution.py:409
  535.9 10.9 %gate_back.3 = (bf16[1024,1024]{1,0:T(8,128)(2,1)}, bf16[1024,512]{1,0:T(8,128)(2,1)}, bf16[1024,512]{1,0:T(8,128)(2,1)}, f32[4,128,512]{2,1,0:T(8,128)}, f32[4,...) custom-call(s32[2]{0:T(128)} %pad_add_fusion.place, f32[1024,1]{1,0:T(8,128)} %copy-done.49, ...), custom_call_target="tpu_custom_call" | custom-call | flops 11500000256 | bytes 1048576 | tf_op jit(solution)/shard_map/gate_back/pallas_call | solution.py:351
  547.3 9.4 %ssd_within_back.3 = (f32[1024,512]{1,0:T(8,128)}, f32[1024,256]{1,0:T(8,128)}, f32[1024,1024]{1,0:T(8,128)}) custom-call(f32[1024,128]{1,0:T(8,128)} %get-tuple-element.156.cum, bf16[1024,512]{1,0:T(8,128)(2,1)} %get-tuple-element.157.xdt, bf16[1024,256]{1,0:T(8,128)(2,1)} %get-tuple-element.158.bc, f32[1024,1]{1,0:T(8,128)} %copy.111.seg, ...), custom_call_target="tpu_custom_call" | custom-call | flops 9200000000 | bytes 1048576 | tf_op jit(solution)/shard_map/ssd_within_back/pallas_call | solution.py:351
  579.7 20.3 %in_proj_conv_back.3 = (bf16[1024,896]{1,0:T(8,128)(2,1)}, f32[8,768]{1,0:T(8,128)}, f32[8,768]{1,0:T(8,128)}, f32[8,768]{1,0:T(8,128)}, f32[8,128]{1,0:T(8,128)}, /*index=5*/f32[8,512]{1,0:T(8,128)}) custom-call(f32[1024,512]{1,0:T(8,128)} %get-tuple-element.227.uin, f32[1024,256]{1,0:T(8,128)} %get-tuple-element.228.dbc, ...), custom_call_target="tpu_custom_call" | custom-call | flops 23000000512 | bytes 1048576 | tf_op jit(solution)/shard_map/in_proj_conv_back/pallas_call | solution.py:351
  630.3 23.6 %collective-permute-done.60 = f32[256,1024]{1,0:T(8,128)S(1)} collective-permute-done((f32[256,1024]{1,0:T(8,128)S(1)}, f32[256,1024]{1,0:T(8,128)S(1)}, u32[]{:S(2)}, u32[]{:S(2)}) %collective-permute-start.60) | collective-permute-done | bytes 1048608 | tf_op jit(solution)/shard_map/ppermute | solution.py:409
  658.4 8.0 collective-permute-start.61
  688.3 11.9 %collective-permute-done.64.value_s = f32[256,1024]{1,0:T(8,128)} collective-permute-done((f32[256,1024]{1,0:T(8,128)S(1)}, f32[256,1024]{1,0:T(8,128)}, u32[]{:S(2)}, u32[]{:S(2)}) %collective-permute-start.64) | collective-permute-done | bytes 1048608 | tf_op jit(solution)/shard_map/ppermute | solution.py:494
  700.3 10.3 %collective-permute-start.68 = (f32[2,14096]{1,0:T(2,128)S(1)}, f32[2,14096]{1,0:T(2,128)S(1)}, u32[]{:S(2)}, u32[]{:S(2)}) collective-permute-start(f32[2,14096]{1,0:T(2,128)S(1)} %pad_maximum_fusion.14), channel_id=1, source_target_pairs={{0,2},{2,0},{1,3},{3,1},{4,6},{6,4},{5,7},{7,5},{8,10},{10,8},{9,1... | collective-permute-start | bytes 338312 | tf_op jit(solution)/shard_map/ppermute | solution.py:417
  744.2 15.8 %collective-permute-done.70 = f32[256,1536]{0,1:T(8,128)} collective-permute-done((f32[256,1536]{0,1:T(8,128)}, f32[256,1536]{0,1:T(8,128)}, u32[]{:S(2)}, u32[]{:S(2)}) %collective-permute-start.70) | collective-permute-done | bytes 1572896 | tf_op jit(solution)/shard_map/ppermute | solution.py:1091
  763.3 14.4 %collective-permute-done.67.near_s = f32[256,1024]{1,0:T(8,128)} collective-permute-done((f32[256,1024]{1,0:T(8,128)}, f32[256,1024]{1,0:T(8,128)}, u32[]{:S(2)}, u32[]{:S(2)}) %collective-permute-start.67) | collective-permute-done | bytes 1048608 | tf_op jit(solution)/shard_map/ppermute | solution.py:494
  782.8 11.3 %collective-permute-start.77 = (f32[128,2,256]{0,2,1:T(8,128)S(1)}, f32[128,2,256]{0,2,1:T(8,128)S(1)}, u32[]{:S(2)}, u32[]{:S(2)}) collective-permute-start(f32[128,2,256]{0,2,1:T(8,128)S(1)} %fusion.16), channel_id=1, source_target_pairs={{0,4},{4,0},{1,5},{5,1},{2,6},{6,2},{3,7},{7,3},{8,12},{12,8},{9,1... | collective-permute-start | bytes 786440 | tf_op jit(solution)/shard_map/ppermute | solution.py:409
  807.6 14.2 %collective-permute-start.79 = (f32[128,2,256]{0,2,1:T(8,128)S(1)}, f32[128,2,256]{0,2,1:T(8,128)S(1)}, u32[]{:S(2)}, u32[]{:S(2)}) collective-permute-start(f32[128,2,256]{0,2,1:T(8,128)S(1)} %fusion.104), channel_id=1, source_target_pairs={{0,2},{2,0},{1,3},{3,1},{4,6},{6,4},{5,7},{7,5},{8,10},{10,8},{9,1... | collective-permute-start | bytes 786440 | tf_op jit(solution)/shard_map/ppermute | solution.py:417
  (581 shorter events, 391.8 us)
Async XLA Ops:
  7.2 596.2 %reduce-scatter.3.cloned.1.call-start = ((), (), s32[]{:S(2)}) async-start(), calls=%async_computation.2 | async-start | bytes 9175040 | tf_op jit(solution)/shard_map/reduce_scatter | solution.py:1022
  10.8 33.6 %collective-permute-start.1 = (f32[256,512]{1,0:T(8,128)}, f32[256,512]{1,0:T(8,128)}, u32[]{:S(2)}, u32[]{:S(2)}) collective-permute-start(f32[256,512]{1,0:T(8,128)} %dynamic-slice_convert_fusion), channel_id=1, source_target_pairs={{0,2},{6,4},{1,3},{7,5},{8,10},{14,12},{9,11},{15,13},{16,18},{22,... | collective-permute-start | bytes 1572872 | tf_op jit(solution)/shard_map/ppermute | solution.py:598
  20.4 35.6 %collective-permute-start.6 = (f32[2,64,128]{2,1,0:T(8,128)S(1)}, f32[2,64,128]{2,1,0:T(8,128)S(1)}, u32[]{:S(2)}, u32[]{:S(2)}) collective-permute-start(f32[2,64,128]{2,1,0:T(8,128)S(1)} %reshape.406), channel_id=1, source_target_pairs={{0,2},{6,4},{1,3},{7,5},{8,10},{14,12},{9,11},{15,13},{16,18},{22,... | collective-permute-start | bytes 196616 | tf_op jit(solution)/shard_map/ppermute | solution.py:672
  24.4 42.3 %collective-permute-start = (f32[1024,1024]{1,0:T(8,128)}, f32[1024,1024]{1,0:T(8,128)}, u32[]{:S(2)}, u32[]{:S(2)}) collective-permute-start(f32[1024,1024]{1,0:T(8,128)} %convert_element_type.74), channel_id=1, source_target_pairs={{0,4},{6,2},{1,5},{7,3},{8,12},{14,10},{9,13},{15,11},{16,20},{22,... | collective-permute-start | bytes 12582920 | tf_op jit(solution)/shard_map/ppermute | solution.py:538
  114.3 40.8 %collective-permute-start.18 = (f32[1024,1024]{1,0:T(8,128)}, f32[1024,1024]{1,0:T(8,128)}, u32[]{:S(2)}, u32[]{:S(2)}) collective-permute-start(f32[1024,1024]{1,0:T(8,128)} %convert_element_type.80), channel_id=1, source_target_pairs={{0,4},{6,2},{1,5},{7,3},{8,12},{14,10},{9,13},{15,11},{16,20},{22,... | collective-permute-start | bytes 12582920 | tf_op jit(solution)/shard_map/ppermute | solution.py:808
  124.5 30.6 %collective-permute-start.17 = (f32[256,1536]{1,0:T(8,128)}, f32[256,1536]{1,0:T(8,128)}, u32[]{:S(2)}, u32[]{:S(2)}) collective-permute-start(f32[256,1536]{1,0:T(8,128)} %maximum_convert_fusion), channel_id=1, source_target_pairs={{0,2},{6,4},{1,3},{7,5},{8,10},{14,12},{9,11},{15,13},{16,18},{22,... | collective-permute-start | bytes 4718600 | tf_op jit(solution)/shard_map/ppermute | solution.py:598
  190.8 26.5 %collective-permute-start.22 = (f32[256,1024]{1,0:T(8,128)}, f32[256,1024]{1,0:T(8,128)}, u32[]{:S(2)}, u32[]{:S(2)}) collective-permute-start(f32[256,1024]{1,0:T(8,128)} %constant_dynamic-slice_fusion.10), channel_id=1, source_target_pairs={{0,1},{1,0},{2,3},{3,2},{4,5},{5,4},{6,7},{7,6},{8,9},{9,8},{10,11... | collective-permute-start | bytes 3145736 | tf_op jit(solution)/shard_map/ppermute | solution.py:409
  194.1 52.1 %collective-permute-start.23 = (f32[256,1536]{1,0:T(8,128)}, f32[256,1536]{1,0:T(8,128)}, u32[]{:S(2)}, u32[]{:S(2)}) collective-permute-start(f32[256,1536]{1,0:T(8,128)} %collective-permute-done.17.refs_3_), channel_id=1, source_target_pairs={{2,10},{4,12},{10,2},{12,4},{18,26},{20,28},{26,18},{28,20},{3,11}... | collective-permute-start | bytes 4718600 | tf_op jit(solution)/shard_map/ppermute | solution.py:613
  195.9 50.3 %collective-permute-start.24 = (f32[256,1536]{1,0:T(8,128)}, f32[256,1536]{1,0:T(8,128)}, u32[]{:S(2)}, u32[]{:S(2)}) collective-permute-start(f32[256,1536]{1,0:T(8,128)} %collective-permute-done.17.refs_3_), channel_id=1, source_target_pairs={{2,18},{4,20},{10,26},{12,28},{18,2},{20,4},{26,10},{28,12},{3,19}... | collective-permute-start | bytes 4718600 | tf_op jit(solution)/shard_map/ppermute | solution.py:613
  197.8 48.5 %collective-permute-start.25 = (f32[256,1536]{1,0:T(8,128)}, f32[256,1536]{1,0:T(8,128)}, u32[]{:S(2)}, u32[]{:S(2)}) collective-permute-start(f32[256,1536]{1,0:T(8,128)} %collective-permute-done.17.refs_3_), channel_id=1, source_target_pairs={{2,26},{4,28},{10,18},{12,20},{18,10},{20,12},{26,2},{28,4},{3,27}... | collective-permute-start | bytes 4718600 | tf_op jit(solution)/shard_map/ppermute | solution.py:613
  220.6 25.0 %collective-permute-start.26 = (f32[256,1024]{1,0:T(8,128)}, f32[256,1024]{1,0:T(8,128)}, u32[]{:S(2)}, u32[]{:S(2)}) collective-permute-start(f32[256,1024]{1,0:T(8,128)} %get-tuple-element.362.refs_0_), channel_id=1, source_target_pairs={{0,1},{1,0},{2,3},{3,2},{4,5},{5,4},{6,7},{7,6},{8,9},{9,8},{10,11... | collective-permute-start | bytes 3145736 | tf_op jit(solution)/shard_map/ppermute | solution.py:409
  222.1 33.1 %collective-permute-start.27 = (f32[256,1024]{1,0:T(8,128)}, f32[256,1024]{1,0:T(8,128)}, u32[]{:S(2)}, u32[]{:S(2)}) collective-permute-start(f32[256,1024]{1,0:T(8,128)} %get-tuple-element.362.refs_0_), channel_id=1, source_target_pairs={{0,4},{4,0},{1,5},{5,1},{2,6},{6,2},{3,7},{7,3},{8,12},{12,8},{9,1... | collective-permute-start | bytes 3145736 | tf_op jit(solution)/shard_map/ppermute | solution.py:409
  350.1 24.3 %collective-permute-start.36 = (f32[256,1024]{1,0:T(8,128)S(1)}, f32[256,1024]{1,0:T(8,128)S(1)}, u32[]{:S(2)}, u32[]{:S(2)}) collective-permute-start(f32[256,1024]{1,0:T(8,128)S(1)} %constant_dynamic-slice_fusion.7), channel_id=1, source_target_pairs={{0,1},{1,0},{2,3},{3,2},{4,5},{5,4},{6,7},{7,6},{8,9},{9,8},{10,11... | collective-permute-start | bytes 3145736 | tf_op jit(solution)/shard_map/ppermute | solution.py:409
  394.4 44.1 %collective-permute-start.37 = (f32[256,1024]{1,0:T(8,128)S(1)}, f32[256,1024]{1,0:T(8,128)}, u32[]{:S(2)}, u32[]{:S(2)}) collective-permute-start(f32[256,1024]{1,0:T(8,128)S(1)} %multiply_add_fusion.2.value), channel_id=1, source_target_pairs={{0,2},{6,4},{1,3},{7,5},{8,10},{14,12},{9,11},{15,13},{16,18},{22,... | collective-permute-start | bytes 3145736 | tf_op jit(solution)/shard_map/ppermute | solution.py:487
  396.9 41.5 %collective-permute-start.39 = (f32[256,1024]{1,0:T(8,128)S(1)}, f32[256,1024]{1,0:T(8,128)}, u32[]{:S(2)}, u32[]{:S(2)}) collective-permute-start(f32[256,1024]{1,0:T(8,128)S(1)} %multiply_add_fusion.2.value), channel_id=1, source_target_pairs={{4,2},{2,4},{5,3},{3,5},{12,10},{10,12},{13,11},{11,13},{20,18},{1... | collective-permute-start | bytes 3145736 | tf_op jit(solution)/shard_map/ppermute | solution.py:487
  398.6 39.9 %collective-permute-start.40 = (f32[256,1024]{1,0:T(8,128)S(1)}, f32[256,1024]{1,0:T(8,128)S(1)}, u32[]{:S(2)}, u32[]{:S(2)}) collective-permute-start(f32[256,1024]{1,0:T(8,128)S(1)} %multiply_add_fusion.2.value), channel_id=1, source_target_pairs={{0,1},{1,0},{6,7},{7,6},{8,9},{9,8},{14,15},{15,14},{16,17},{17,16... | collective-permute-start | bytes 3145736 | tf_op jit(solution)/shard_map/ppermute | solution.py:494
  414.6 39.6 %collective-permute-start.44 = (f32[256,1024]{1,0:T(8,128)S(1)}, f32[256,1024]{1,0:T(8,128)S(1)}, u32[]{:S(2)}, u32[]{:S(2)}) collective-permute-start(f32[256,1024]{1,0:T(8,128)S(1)} %collective-permute-done.38.near), channel_id=1, source_target_pairs={{0,1},{1,0},{6,7},{7,6},{8,9},{9,8},{14,15},{15,14},{16,17},{17,16... | collective-permute-start | bytes 3145736 | tf_op jit(solution)/shard_map/ppermute | solution.py:494
  469.1 308.6 %reduce-scatter.5.cloned.1.call-start = ((), (), s32[]{:S(2)}) async-start(), calls=%async_computation.3 | async-start | bytes 9175040 | tf_op jit(solution)/shard_map/reduce_scatter | solution.py:1022
  475.9 25.3 %collective-permute-start.47 = (f32[256,1024]{1,0:T(8,128)S(1)}, f32[256,1024]{1,0:T(8,128)S(1)}, u32[]{:S(2)}, u32[]{:S(2)}) collective-permute-start(f32[256,1024]{1,0:T(8,128)S(1)} %constant_dynamic-slice_fusion.5), channel_id=1, source_target_pairs={{0,1},{1,0},{2,3},{3,2},{4,5},{5,4},{6,7},{7,6},{8,9},{9,8},{10,11... | collective-permute-start | bytes 3145736 | tf_op jit(solution)/shard_map/ppermute | solution.py:409
  505.4 24.6 %collective-permute-start.50 = (f32[256,1024]{1,0:T(8,128)S(1)}, f32[256,1024]{1,0:T(8,128)}, u32[]{:S(2)}, u32[]{:S(2)}) collective-permute-start(f32[256,1024]{1,0:T(8,128)S(1)} %get-tuple-element.359.refs_0_), channel_id=1, source_target_pairs={{0,1},{1,0},{2,3},{3,2},{4,5},{5,4},{6,7},{7,6},{8,9},{9,8},{10,11... | collective-permute-start | bytes 3145736 | tf_op jit(solution)/shard_map/ppermute | solution.py:409
  505.8 30.0 %collective-permute-start.51 = (f32[256,1024]{1,0:T(8,128)S(1)}, f32[256,1024]{1,0:T(8,128)}, u32[]{:S(2)}, u32[]{:S(2)}) collective-permute-start(f32[256,1024]{1,0:T(8,128)S(1)} %get-tuple-element.359.refs_0_), channel_id=1, source_target_pairs={{0,4},{4,0},{1,5},{5,1},{2,6},{6,2},{3,7},{7,3},{8,12},{12,8},{9,1... | collective-permute-start | bytes 3145736 | tf_op jit(solution)/shard_map/ppermute | solution.py:409
  575.3 26.0 %collective-permute-start.54 = (f32[256,1024]{1,0:T(8,128)}, f32[256,1024]{1,0:T(8,128)S(1)}, u32[]{:S(2)}, u32[]{:S(2)}) collective-permute-start(f32[256,1024]{1,0:T(8,128)} %collective-permute-done.37.mine), channel_id=1, source_target_pairs={{2,3},{3,2},{4,5},{5,4},{10,11},{11,10},{12,13},{13,12},{18,19},{1... | collective-permute-start | bytes 3145736 | tf_op jit(solution)/shard_map/ppermute | solution.py:504
  576.1 26.3 %collective-permute-start.55 = (f32[256,1024]{1,0:T(8,128)}, f32[256,1024]{1,0:T(8,128)S(1)}, u32[]{:S(2)}, u32[]{:S(2)}) collective-permute-start(f32[256,1024]{1,0:T(8,128)} %collective-permute-done.39.theirs), channel_id=1, source_target_pairs={{2,3},{3,2},{4,5},{5,4},{10,11},{11,10},{12,13},{13,12},{18,19},{1... | collective-permute-start | bytes 3145736 | tf_op jit(solution)/shard_map/ppermute | solution.py:505
  628.6 25.3 %collective-permute-start.60 = (f32[256,1024]{1,0:T(8,128)S(1)}, f32[256,1024]{1,0:T(8,128)S(1)}, u32[]{:S(2)}, u32[]{:S(2)}) collective-permute-start(f32[256,1024]{1,0:T(8,128)S(1)} %constant_dynamic-slice_fusion.3), channel_id=1, source_target_pairs={{0,1},{1,0},{2,3},{3,2},{4,5},{5,4},{6,7},{7,6},{8,9},{9,8},{10,11... | collective-permute-start | bytes 3145736 | tf_op jit(solution)/shard_map/ppermute | solution.py:409
  658.4 29.9 %collective-permute-start.61 = (f32[256,1024]{1,0:T(8,128)S(1)}, f32[256,1024]{1,0:T(8,128)}, u32[]{:S(2)}, u32[]{:S(2)}) collective-permute-start(f32[256,1024]{1,0:T(8,128)S(1)} %multiply_add_fusion.value), channel_id=1, source_target_pairs={{0,2},{6,4},{1,3},{7,5},{8,10},{14,12},{9,11},{15,13},{16,18},{22,... | collective-permute-start | bytes 3145736 | tf_op jit(solution)/shard_map/ppermute | solution.py:487
  668.0 32.2 %collective-permute-start.64 = (f32[256,1024]{1,0:T(8,128)S(1)}, f32[256,1024]{1,0:T(8,128)}, u32[]{:S(2)}, u32[]{:S(2)}) collective-permute-start(f32[256,1024]{1,0:T(8,128)S(1)} %multiply_add_fusion.value), channel_id=1, source_target_pairs={{0,1},{1,0},{6,7},{7,6},{8,9},{9,8},{14,15},{15,14},{16,17},{17,16... | collective-permute-start | bytes 3145736 | tf_op jit(solution)/shard_map/ppermute | solution.py:494
  729.2 34.1 %collective-permute-start.65 = (f32[256,1024]{1,0:T(8,128)}, f32[256,1024]{1,0:T(8,128)}, u32[]{:S(2)}, u32[]{:S(2)}) collective-permute-start(f32[256,1024]{1,0:T(8,128)} %collective-permute-done.61.mine), channel_id=1, source_target_pairs={{2,3},{3,2},{4,5},{5,4},{10,11},{11,10},{12,13},{13,12},{18,19},{1... | collective-permute-start | bytes 3145736 | tf_op jit(solution)/shard_map/ppermute | solution.py:504
  730.9 32.4 %collective-permute-start.66 = (f32[256,1024]{1,0:T(8,128)}, f32[256,1024]{1,0:T(8,128)}, u32[]{:S(2)}, u32[]{:S(2)}) collective-permute-start(f32[256,1024]{1,0:T(8,128)} %collective-permute-done.62.theirs), channel_id=1, source_target_pairs={{2,3},{3,2},{4,5},{5,4},{10,11},{11,10},{12,13},{13,12},{18,19},{1... | collective-permute-start | bytes 3145736 | tf_op jit(solution)/shard_map/ppermute | solution.py:505
  732.5 45.2 %collective-permute-start.67 = (f32[256,1024]{1,0:T(8,128)}, f32[256,1024]{1,0:T(8,128)}, u32[]{:S(2)}, u32[]{:S(2)}) collective-permute-start(f32[256,1024]{1,0:T(8,128)} %collective-permute-done.63.near), channel_id=1, source_target_pairs={{0,1},{1,0},{6,7},{7,6},{8,9},{9,8},{14,15},{15,14},{16,17},{17,16... | collective-permute-start | bytes 3145736 | tf_op jit(solution)/shard_map/ppermute | solution.py:494
  781.4 55.2 %collective-permute-start.74 = (f32[256,1536]{0,1:T(8,128)}, f32[256,1536]{0,1:T(8,128)}, u32[]{:S(2)}, u32[]{:S(2)}) collective-permute-start(f32[256,1536]{0,1:T(8,128)} %slice.499), channel_id=1, source_target_pairs={{2,0},{4,6},{3,1},{5,7},{10,8},{12,14},{11,9},{13,15},{18,16},{20,... | collective-permute-start | bytes 4718600 | tf_op jit(solution)/shard_map/ppermute | solution.py:1091
  798.6 43.7 %collective-permute-start.76 = (f32[128,1536]{0,1:T(8,128)}, f32[128,1536]{0,1:T(8,128)}, u32[]{:S(2)}, u32[]{:S(2)}) collective-permute-start(f32[128,1536]{0,1:T(8,128)} %constant_dynamic-slice_fusion.1), channel_id=1, source_target_pairs={{0,4},{6,2},{1,5},{7,3},{8,12},{14,10},{9,13},{15,11},{16,20},{22,... | collective-permute-start | bytes 2359304 | tf_op jit(solution)/shard_map/ppermute | solution.py:1104
  807.6 29.0 %collective-permute-start.79 = (f32[128,2,256]{0,2,1:T(8,128)S(1)}, f32[128,2,256]{0,2,1:T(8,128)S(1)}, u32[]{:S(2)}, u32[]{:S(2)}) collective-permute-start(f32[128,2,256]{0,2,1:T(8,128)S(1)} %fusion.104), channel_id=1, source_target_pairs={{0,2},{2,0},{1,3},{3,1},{4,6},{6,4},{5,7},{7,5},{8,10},{10,8},{9,1... | collective-permute-start | bytes 786440 | tf_op jit(solution)/shard_map/ppermute | solution.py:417
  (137 other events, 1685.6 us)
Sparse Core Ops, SparseCore 0:
  469.2 76.8 reduce-scatter.2
  622.0 81.4 reduce-scatter.4

commit v11 on v10

--- a/solution.py
+++ b/solution.py
@@ -782,6 +782,8 @@
             wz, wout = gather_weights(
                 behind(first_rest, wall), [w_z[0], w_out[0]], third=(send,)
             )
+            cotangent = behind(cotangent, send).astype(f32)
+            cot_sent = lax.ppermute(cotangent, BOTH, CORE_OUT)
         else:
             wz, wout = next_wz, next_wout
         zval = mm(normed, wz)
@@ -804,8 +806,6 @@
         entry = chain(send, False, stages)
         if layer == 0:
             second_all = weights_over([w_x[1], w_z[1], w_out[1]], stages[0])
-            cotangent = behind(cotangent, stages[0]).astype(f32)
-            cot_sent = lax.ppermute(cotangent, BOTH, CORE_OUT)
             entry = behind(entry, second_all, cot_sent)
             cotangent = jnp.where(held, cotangent, cot_sent)
         y, gate_in, proj, sums = call(
@@ -997,6 +997,9 @@
         grad_win = mm(kept["normed"], behind(late, grad_wbc)[:, :inner], ((0,), (0,)))
         grad_normed = scatter_sum(partial, (grad_win,) if layer == 0 else ())
         if layer == 0:
+            first_part = behind(matrices[1][:, : 3 * inner], partial)
+            first_got = lax.ppermute(first_part, BOTH, CROSS_BACK)
+            grad_normed = behind(grad_normed, first_got)
             grad_own = input_gradient(grad_own, grad_normed, kept["hidden"], norm_gain[layer])
             grad_parts = cross_over(grad_own)
             own_s = near_swap(grad_own)
@@ -1042,7 +1045,7 @@
     vector = jnp.concatenate(
         [vector[:, :-common], total(vector[:, -common:], ("zl",))], axis=1
     )
-    first_sums = join_halves(behind(matrices[1][:, : 3 * inner], vector))
+    first_sums = first_part + first_got
     vector = total(vector, ("chip",))
     other = swap(vector, "core")
     shared = (vector + other)[:, -common:]

time: 864 us -> 859 us (level)
  starting transfers between devices: 201 us -> 188 us
    ppermute x2 -> x1, waiting for transfers between devices: 15.8 us -> 0.01 us  [join_halves(): return part + lax.ppermute(part, BOTH, CROSS_BACK)]
    ppermute x18, waiting for transfers between devices: 128 us -> 140 us  [swap(): return lax.ppermute(value, axis, SWAP)]
    ppermute x10, waiting for transfers between devices: 39.8 us -> 49.1 us  [total(): lax.ppermute(value, axis, [(i, i ^ step) for i in range(count)])]
  transfers between devices with their start and end apart: 82 -> 82, of which waited for: 42 -> 39; matrix products, arithmetic and copies ran while one was open for 13% -> 13% of each run, Pallas kernels for 13% -> 13%
where the time goes in v11:
time: 859 us; the launch traced here: 848 us
  waiting for transfers between devices  292 us (34%)
  starting transfers between devices  188 us (22%)
  Pallas kernels  167 us (19%)
  local copies, waits for them, and re-layouts  78 us (9%)
  other arithmetic  72.8 us (8%)
  matrix products  34.5 us (4%)
  between operations  16.2 us (2%)
    pallas_call x12, Pallas kernels, call(): pl.pallas_call(kernel, grid=(count,), in_specs=[spec for spec, _ in ins],...  150 us
    ppermute x18, waiting for transfers between devices, swap(): return lax.ppermute(value, axis, SWAP)  140 us
    ppermute x10, waiting for transfers between devices, total(): lax.ppermute(value, axis, [(i, i ^ step) for i in range(count)])  49.1 us
    ppermute x12, waiting for transfers between devices, chain(): got = lax.ppermute(part, BLOCKS, [(i, i ^ step) for i in range(count)])  45.7 us
    ppermute x4, waiting for transfers between devices, near_swap(): return lax.ppermute(value, ('core', 'zh', 'zl'), here)  43.4 us
    ppermute x10, starting transfers between devices, total(): lax.ppermute(value, axis, [(i, i ^ step) for i in range(count)])  32.3 us
    dot_general x14, matrix products, mm(): lax.dot_general(left, right, (dims, ((), ())), preferred_element_type=f32...  29.9 us
    ppermute x3, starting transfers between devices, weights_over(): return lax.ppermute(piece, BOTH, CROSS)  26.2 us
  transfers between devices with their start and end apart: 82, of which 39 were waited for; matrix products, arithmetic and copies ran while one was open for 13% of the time, Pallas kernels for 13%

profile of v11, /device:TPU:0, one launch (start us, length us, event | category | flops | bytes accessed | tf_op | source)
XLA Modules:
  0.0 847.7 jit_solution(15955861619724352033)
XLA Ops:
  10.8 6.8 collective-permute-start.1
  45.6 7.3 collective-permute-start.5
  68.6 12.0 %collective-permute-start.10 = (f32[8,768]{1,0:T(8,128)S(1)}, f32[8,768]{1,0:T(8,128)S(1)}, u32[]{:S(2)}, u32[]{:S(2)}) collective-permute-start(f32[8,768]{1,0:T(8,128)S(1)} %fusion), channel_id=1, source_target_pairs={{0,2},{2,8},{8,10},{10,16},{16,18},{18,24},{24,26},{1,3},{3,9},{9,... | collective-permute-start | bytes 73736 | tf_op jit(solution)/shard_map/ppermute | solution.py:385
  83.9 15.6 %in_proj_conv.2 = (bf16[1024,1024]{1,0:T(8,128)(2,1)}, f32[1024,768]{1,0:T(8,128)}, f32[1024,768]{1,0:T(8,128)}, f32[1024,128]{1,0:T(8,128)}, f32[1024,128]{1,0:...) custom-call(s32[2]{0:T(128)} %pad_add_fusion.place, ...), custom_call_target="tpu_custom_call" | custom-call | flops 18400000000 | bytes 1048576 | tf_op jit(solution)/shard_map/in_proj_conv/pallas_call | solution.py:351
  111.7 6.3 collective-permute-done.14
  120.5 12.1 %collective-permute-start.17 = (f32[256,1536]{1,0:T(8,128)}, f32[256,1536]{1,0:T(8,128)}, u32[]{:S(2)}, u32[]{:S(2)}) collective-permute-start(f32[256,1536]{1,0:T(8,128)} %maximum_convert_fusion), channel_id=1, source_target_pairs={{0,2},{6,4},{1,3},{7,5},{8,10},{14,12},{9,11},{15,13},{16,18},{22,... | collective-permute-start | bytes 4718600 | tf_op jit(solution)/shard_map/ppermute | solution.py:598
  158.0 11.2 %gate_out_proj.2 = (f32[1024,512]{1,0:T(8,128)}, bf16[1024,512]{1,0:T(8,128)(2,1)}, f32[1024,1024]{1,0:T(8,128)}, f32[8,1024]{1,0:T(8,128)}) custom-call(f32[1024,512]{1,0:T(8,128)} %ssd_within.2.yin, f32[1024,768]{1,0:T(8,128)} %get-tuple-element.160.cpre, f32[1024,128]{1,0:T(8,128)} %get-tuple-element.157.cum, bf16[1024,256]{1,0:T(8,128)(2,1)} %get-tuple-element.159.bc, ...), custom_call_target="tpu_custom_call" | custom-call | flops 13799999488 | bytes 1048576 | tf_op jit(solution)/shard_map/gate_out_proj/pallas_call | solution.py:351
  170.9 6.5 collective-permute-start.21
  196.8 17.6 %collective-permute-done.20 = f32[8,1024]{1,0:T(8,128)S(1)} collective-permute-done((f32[8,1024]{1,0:T(8,128)S(1)}, f32[8,1024]{1,0:T(8,128)S(1)}, u32[]{:S(2)}, u32[]{:S(2)}) %collective-permute-start.20) | collective-permute-done | bytes 32800 | tf_op jit(solution)/shard_map/ppermute | solution.py:417
  219.5 23.4 %collective-permute-done.26.refs_1_ = f32[256,1024]{1,0:T(8,128)} collective-permute-done((f32[256,1024]{1,0:T(8,128)}, f32[256,1024]{1,0:T(8,128)}, u32[]{:S(2)}, u32[]{:S(2)}) %collective-permute-start.26) | collective-permute-done | bytes 1048608 | tf_op jit(solution)/shard_map/ppermute | solution.py:409
  263.4 17.2 %in_proj_conv.3 = (bf16[1024,1024]{1,0:T(8,128)(2,1)}, f32[1024,768]{1,0:T(8,128)}, f32[1024,768]{1,0:T(8,128)}, f32[1024,128]{1,0:T(8,128)}, f32[1024,128]{1,0:...) custom-call(s32[2]{0:T(128)} %pad_add_fusion.place, ...), custom_call_target="tpu_custom_call" | custom-call | flops 18400000000 | bytes 1048576 | tf_op jit(solution)/shard_map/in_proj_conv/pallas_call | solution.py:351
  287.0 9.2 %collective-permute-done.30 = f32[136,512]{1,0:T(8,128)S(1)} collective-permute-done((f32[136,512]{1,0:T(8,128)}, f32[136,512]{1,0:T(8,128)S(1)}, u32[]{:S(2)}, u32[]{:S(2)}) %collective-permute-start.30) | collective-permute-done | bytes 278560 | tf_op jit(solution)/shard_map/ppermute | solution.py:395
  314.3 14.1 %gate_out_proj.3 = (f32[1024,512]{1,0:T(8,128)}, bf16[1024,512]{1,0:T(8,128)(2,1)}, f32[1024,1024]{1,0:T(8,128)}, f32[8,1024]{1,0:T(8,128)}) custom-call(f32[1024,512]{1,0:T(8,128)} %ssd_within.3.yin, f32[1024,768]{1,0:T(8,128)} %get-tuple-element.188.cpre, f32[1024,128]{1,0:T(8,128)} %get-tuple-element.185.cum, bf16[1024,256]{1,0:T(8,128)(2,1)} %get-tuple-element.187.bc, ...), custom_call_target="tpu_custom_call" | custom-call | flops 13799999488 | bytes 1048576 | tf_op jit(solution)/shard_map/gate_out_proj/pallas_call | solution.py:351
  347.5 10.1 %gate_back.2 = (bf16[1024,1024]{1,0:T(8,128)(2,1)}, bf16[1024,512]{1,0:T(8,128)(2,1)}, bf16[1024,512]{1,0:T(8,128)(2,1)}, f32[4,128,512]{2,1,0:T(8,128)}, f32[4,...) custom-call(s32[2]{0:T(128)} %pad_add_fusion.place, f32[1024,1]{1,0:T(8,128)} %copy-done.52, ...), custom_call_target="tpu_custom_call" | custom-call | flops 11500000256 | bytes 1048576 | tf_op jit(solution)/shard_map/gate_back/pallas_call | solution.py:351
  357.6 12.5 %collective-permute-done.36 = f32[256,1024]{1,0:T(8,128)S(1)} collective-permute-done((f32[256,1024]{1,0:T(8,128)S(1)}, f32[256,1024]{1,0:T(8,128)S(1)}, u32[]{:S(2)}, u32[]{:S(2)}) %collective-permute-start.36) | collective-permute-done | bytes 1048608 | tf_op jit(solution)/shard_map/ppermute | solution.py:409
  377.9 9.0 %collective-permute-done.41 = f32[136,512]{1,0:T(8,128)S(1)} collective-permute-done((f32[136,512]{1,0:T(8,128)S(1)}, f32[136,512]{1,0:T(8,128)S(1)}, u32[]{:S(2)}, u32[]{:S(2)}) %collective-permute-start.41) | collective-permute-done | bytes 278560 | tf_op jit(solution)/shard_map/ppermute | solution.py:395
  403.5 9.3 %ssd_within_back.2 = (f32[1024,512]{1,0:T(8,128)}, f32[1024,256]{1,0:T(8,128)}, f32[1024,1024]{1,0:T(8,128)}) custom-call(f32[1024,128]{1,0:T(8,128)} %get-tuple-element.185.cum, bf16[1024,512]{1,0:T(8,128)(2,1)} %get-tuple-element.186.xdt, bf16[1024,256]{1,0:T(8,128)(2,1)} %get-tuple-element.187.bc, f32[1024,1]{1,0:T(8,128)} %copy.108.seg, ...), custom_call_target="tpu_custom_call" | custom-call | flops 9200000000 | bytes 1048576 | tf_op jit(solution)/shard_map/ssd_within_back/pallas_call | solution.py:351
  415.5 20.4 %in_proj_conv_back.2 = (bf16[1024,896]{1,0:T(8,128)(2,1)}, f32[8,768]{1,0:T(8,128)}, f32[8,768]{1,0:T(8,128)}, f32[8,768]{1,0:T(8,128)}, f32[8,128]{1,0:T(8,128)}, /*index=5*/f32[8,512]{1,0:T(8,128)}) custom-call(f32[1024,512]{1,0:T(8,128)} %get-tuple-element.205.uin, f32[1024,256]{1,0:T(8,128)} %get-tuple-element.206.dbc, ...), custom_call_target="tpu_custom_call" | custom-call | flops 23000000512 | bytes 1048576 | tf_op jit(solution)/shard_map/in_proj_conv_back/pallas_call | solution.py:351
  437.5 15.4 %collective-permute-done.44.near_s = f32[256,1024]{1,0:T(8,128)S(1)} collective-permute-done((f32[256,1024]{1,0:T(8,128)S(1)}, f32[256,1024]{1,0:T(8,128)S(1)}, u32[]{:S(2)}, u32[]{:S(2)}) %collective-permute-start.44) | collective-permute-done | bytes 1048608 | tf_op jit(solution)/shard_map/ppermute | solution.py:494
  474.7 25.2 %collective-permute-done.47 = f32[256,1024]{1,0:T(8,128)S(1)} collective-permute-done((f32[256,1024]{1,0:T(8,128)S(1)}, f32[256,1024]{1,0:T(8,128)S(1)}, u32[]{:S(2)}, u32[]{:S(2)}) %collective-permute-start.47) | collective-permute-done | bytes 1048608 | tf_op jit(solution)/shard_map/ppermute | solution.py:409
  504.4 24.4 %collective-permute-done.50.refs_1_ = f32[256,1024]{1,0:T(8,128)} collective-permute-done((f32[256,1024]{1,0:T(8,128)S(1)}, f32[256,1024]{1,0:T(8,128)}, u32[]{:S(2)}, u32[]{:S(2)}) %collective-permute-start.50) | collective-permute-done | bytes 1048608 | tf_op jit(solution)/shard_map/ppermute | solution.py:409
  534.6 10.9 %gate_back.3 = (bf16[1024,1024]{1,0:T(8,128)(2,1)}, bf16[1024,512]{1,0:T(8,128)(2,1)}, bf16[1024,512]{1,0:T(8,128)(2,1)}, f32[4,128,512]{2,1,0:T(8,128)}, f32[4,...) custom-call(s32[2]{0:T(128)} %pad_add_fusion.place, f32[1024,1]{1,0:T(8,128)} %copy-done.50, ...), custom_call_target="tpu_custom_call" | custom-call | flops 11500000256 | bytes 1048576 | tf_op jit(solution)/shard_map/gate_back/pallas_call | solution.py:351
  545.6 9.4 %ssd_within_back.3 = (f32[1024,512]{1,0:T(8,128)}, f32[1024,256]{1,0:T(8,128)}, f32[1024,1024]{1,0:T(8,128)}) custom-call(f32[1024,128]{1,0:T(8,128)} %get-tuple-element.157.cum, bf16[1024,512]{1,0:T(8,128)(2,1)} %get-tuple-element.158.xdt, bf16[1024,256]{1,0:T(8,128)(2,1)} %get-tuple-element.159.bc, f32[1024,1]{1,0:T(8,128)} %copy.108.seg, ...), custom_call_target="tpu_custom_call" | custom-call | flops 9200000000 | bytes 1048576 | tf_op jit(solution)/shard_map/ssd_within_back/pallas_call | solution.py:351
  555.0 6.3 collective-permute-done.53
  578.9 20.3 %in_proj_conv_back.3 = (bf16[1024,896]{1,0:T(8,128)(2,1)}, f32[8,768]{1,0:T(8,128)}, f32[8,768]{1,0:T(8,128)}, f32[8,768]{1,0:T(8,128)}, f32[8,128]{1,0:T(8,128)}, /*index=5*/f32[8,512]{1,0:T(8,128)}) custom-call(f32[1024,512]{1,0:T(8,128)} %get-tuple-element.228.uin, f32[1024,256]{1,0:T(8,128)} %get-tuple-element.229.dbc, ...), custom_call_target="tpu_custom_call" | custom-call | flops 23000000512 | bytes 1048576 | tf_op jit(solution)/shard_map/in_proj_conv_back/pallas_call | solution.py:351
  628.7 41.9 %collective-permute-done.60 = f32[256,1024]{1,0:T(8,128)S(1)} collective-permute-done((f32[256,1024]{1,0:T(8,128)S(1)}, f32[256,1024]{1,0:T(8,128)S(1)}, u32[]{:S(2)}, u32[]{:S(2)}) %collective-permute-start.60) | collective-permute-done | bytes 1048608 | tf_op jit(solution)/shard_map/ppermute | solution.py:409
  700.5 13.0 %collective-permute-done.65.value_s = f32[256,1024]{1,0:T(8,128)} collective-permute-done((f32[256,1024]{1,0:T(8,128)S(1)}, f32[256,1024]{1,0:T(8,128)}, u32[]{:S(2)}, u32[]{:S(2)}) %collective-permute-start.65) | collective-permute-done | bytes 1048608 | tf_op jit(solution)/shard_map/ppermute | solution.py:494
  713.6 13.3 %collective-permute-start.69 = (f32[2,14096]{1,0:T(2,128)S(1)}, f32[2,14096]{1,0:T(2,128)S(1)}, u32[]{:S(2)}, u32[]{:S(2)}) collective-permute-start(f32[2,14096]{1,0:T(2,128)S(1)} %pad_maximum_fusion.14), channel_id=1, source_target_pairs={{0,2},{2,0},{1,3},{3,1},{4,6},{6,4},{5,7},{7,5},{8,10},{10,8},{9,1... | collective-permute-start | bytes 338312 | tf_op jit(solution)/shard_map/ppermute | solution.py:417
  755.0 15.0 %collective-permute-done.68.near_s = f32[256,1024]{1,0:T(8,128)} collective-permute-done((f32[256,1024]{1,0:T(8,128)}, f32[256,1024]{1,0:T(8,128)}, u32[]{:S(2)}, u32[]{:S(2)}) %collective-permute-start.68) | collective-permute-done | bytes 1048608 | tf_op jit(solution)/shard_map/ppermute | solution.py:494
  775.1 7.9 collective-permute-start.77
  796.4 13.1 %collective-permute-start.79 = (f32[128,2,256]{0,2,1:T(8,128)S(1)}, f32[128,2,256]{0,2,1:T(8,128)S(1)}, u32[]{:S(2)}, u32[]{:S(2)}) collective-permute-start(f32[128,2,256]{0,2,1:T(8,128)S(1)} %fusion.104), channel_id=1, source_target_pairs={{0,2},{2,0},{1,3},{3,1},{4,6},{6,4},{5,7},{7,5},{8,10},{10,8},{9,1... | collective-permute-start | bytes 786440 | tf_op jit(solution)/shard_map/ppermute | solution.py:417
  823.3 8.0 collective-permute-done.79
  (584 shorter events, 387.0 us)
Async XLA Ops:
  7.2 595.3 %reduce-scatter.3.cloned.1.call-start = ((), (), s32[]{:S(2)}) async-start(), calls=%async_computation.2 | async-start | bytes 9175040 | tf_op jit(solution)/shard_map/reduce_scatter | solution.py:1025
  10.8 33.6 %collective-permute-start.1 = (f32[256,512]{1,0:T(8,128)}, f32[256,512]{1,0:T(8,128)}, u32[]{:S(2)}, u32[]{:S(2)}) collective-permute-start(f32[256,512]{1,0:T(8,128)} %dynamic-slice_convert_fusion), channel_id=1, source_target_pairs={{0,2},{6,4},{1,3},{7,5},{8,10},{14,12},{9,11},{15,13},{16,18},{22,... | collective-permute-start | bytes 1572872 | tf_op jit(solution)/shard_map/ppermute | solution.py:598
  20.4 35.6 %collective-permute-start.6 = (f32[2,64,128]{2,1,0:T(8,128)S(1)}, f32[2,64,128]{2,1,0:T(8,128)S(1)}, u32[]{:S(2)}, u32[]{:S(2)}) collective-permute-start(f32[2,64,128]{2,1,0:T(8,128)S(1)} %reshape.406), channel_id=1, source_target_pairs={{0,2},{6,4},{1,3},{7,5},{8,10},{14,12},{9,11},{15,13},{16,18},{22,... | collective-permute-start | bytes 196616 | tf_op jit(solution)/shard_map/ppermute | solution.py:672
  24.4 42.3 %collective-permute-start = (f32[1024,1024]{1,0:T(8,128)}, f32[1024,1024]{1,0:T(8,128)}, u32[]{:S(2)}, u32[]{:S(2)}) collective-permute-start(f32[1024,1024]{1,0:T(8,128)} %convert_element_type.74), channel_id=1, source_target_pairs={{0,4},{6,2},{1,5},{7,3},{8,12},{14,10},{9,13},{15,11},{16,20},{22,... | collective-permute-start | bytes 12582920 | tf_op jit(solution)/shard_map/ppermute | solution.py:538
  103.7 53.0 %collective-permute-start.18 = (f32[1024,1024]{1,0:T(8,128)}, f32[1024,1024]{1,0:T(8,128)}, u32[]{:S(2)}, u32[]{:S(2)}) collective-permute-start(f32[1024,1024]{1,0:T(8,128)} %convert_element_type.80), channel_id=1, source_target_pairs={{0,4},{6,2},{1,5},{7,3},{8,12},{14,10},{9,13},{15,11},{16,20},{22,... | collective-permute-start | bytes 12582920 | tf_op jit(solution)/shard_map/ppermute | solution.py:786
  109.5 25.6 %collective-permute-start.11 = (f32[256,1024]{1,0:T(8,128)}, f32[256,1024]{1,0:T(8,128)S(1)}, u32[]{:S(2)}, u32[]{:S(2)}) collective-permute-start(f32[256,1024]{1,0:T(8,128)} %collective-permute-done.5.refs_2_), channel_id=1, source_target_pairs={{2,10},{4,12},{10,2},{12,4},{18,26},{20,28},{26,18},{28,20},{3,11}... | collective-permute-start | bytes 3145736 | tf_op jit(solution)/shard_map/ppermute | solution.py:613
  110.2 31.5 %collective-permute-start.12 = (f32[256,1024]{1,0:T(8,128)}, f32[256,1024]{1,0:T(8,128)S(1)}, u32[]{:S(2)}, u32[]{:S(2)}) collective-permute-start(f32[256,1024]{1,0:T(8,128)} %collective-permute-done.5.refs_2_), channel_id=1, source_target_pairs={{2,18},{4,20},{10,26},{12,28},{18,2},{20,4},{26,10},{28,12},{3,19}... | collective-permute-start | bytes 3145736 | tf_op jit(solution)/shard_map/ppermute | solution.py:613
  111.0 30.8 %collective-permute-start.13 = (f32[256,1024]{1,0:T(8,128)}, f32[256,1024]{1,0:T(8,128)S(1)}, u32[]{:S(2)}, u32[]{:S(2)}) collective-permute-start(f32[256,1024]{1,0:T(8,128)} %collective-permute-done.5.refs_2_), channel_id=1, source_target_pairs={{2,26},{4,28},{10,18},{12,20},{18,10},{20,12},{26,2},{28,4},{3,27}... | collective-permute-start | bytes 3145736 | tf_op jit(solution)/shard_map/ppermute | solution.py:613
  120.5 36.3 %collective-permute-start.17 = (f32[256,1536]{1,0:T(8,128)}, f32[256,1536]{1,0:T(8,128)}, u32[]{:S(2)}, u32[]{:S(2)}) collective-permute-start(f32[256,1536]{1,0:T(8,128)} %maximum_convert_fusion), channel_id=1, source_target_pairs={{0,2},{6,4},{1,3},{7,5},{8,10},{14,12},{9,11},{15,13},{16,18},{22,... | collective-permute-start | bytes 4718600 | tf_op jit(solution)/shard_map/ppermute | solution.py:598
  185.1 29.3 %collective-permute-start.22 = (f32[256,1024]{1,0:T(8,128)}, f32[256,1024]{1,0:T(8,128)}, u32[]{:S(2)}, u32[]{:S(2)}) collective-permute-start(f32[256,1024]{1,0:T(8,128)} %constant_dynamic-slice_fusion.10), channel_id=1, source_target_pairs={{0,1},{1,0},{2,3},{3,2},{4,5},{5,4},{6,7},{7,6},{8,9},{9,8},{10,11... | collective-permute-start | bytes 3145736 | tf_op jit(solution)/shard_map/ppermute | solution.py:409
  191.2 52.2 %collective-permute-start.23 = (f32[256,1536]{1,0:T(8,128)}, f32[256,1536]{1,0:T(8,128)}, u32[]{:S(2)}, u32[]{:S(2)}) collective-permute-start(f32[256,1536]{1,0:T(8,128)} %collective-permute-done.17.refs_3_), channel_id=1, source_target_pairs={{2,10},{4,12},{10,2},{12,4},{18,26},{20,28},{26,18},{28,20},{3,11}... | collective-permute-start | bytes 4718600 | tf_op jit(solution)/shard_map/ppermute | solution.py:613
  193.0 50.4 %collective-permute-start.24 = (f32[256,1536]{1,0:T(8,128)}, f32[256,1536]{1,0:T(8,128)}, u32[]{:S(2)}, u32[]{:S(2)}) collective-permute-start(f32[256,1536]{1,0:T(8,128)} %collective-permute-done.17.refs_3_), channel_id=1, source_target_pairs={{2,18},{4,20},{10,26},{12,28},{18,2},{20,4},{26,10},{28,12},{3,19}... | collective-permute-start | bytes 4718600 | tf_op jit(solution)/shard_map/ppermute | solution.py:613
  194.9 48.6 %collective-permute-start.25 = (f32[256,1536]{1,0:T(8,128)}, f32[256,1536]{1,0:T(8,128)}, u32[]{:S(2)}, u32[]{:S(2)}) collective-permute-start(f32[256,1536]{1,0:T(8,128)} %collective-permute-done.17.refs_3_), channel_id=1, source_target_pairs={{2,26},{4,28},{10,18},{12,20},{18,10},{20,12},{26,2},{28,4},{3,27}... | collective-permute-start | bytes 4718600 | tf_op jit(solution)/shard_map/ppermute | solution.py:613
  217.7 25.1 %collective-permute-start.26 = (f32[256,1024]{1,0:T(8,128)}, f32[256,1024]{1,0:T(8,128)}, u32[]{:S(2)}, u32[]{:S(2)}) collective-permute-start(f32[256,1024]{1,0:T(8,128)} %get-tuple-element.364.refs_0_), channel_id=1, source_target_pairs={{0,1},{1,0},{2,3},{3,2},{4,5},{5,4},{6,7},{7,6},{8,9},{9,8},{10,11... | collective-permute-start | bytes 3145736 | tf_op jit(solution)/shard_map/ppermute | solution.py:409
  219.5 32.9 %collective-permute-start.27 = (f32[256,1024]{1,0:T(8,128)}, f32[256,1024]{1,0:T(8,128)}, u32[]{:S(2)}, u32[]{:S(2)}) collective-permute-start(f32[256,1024]{1,0:T(8,128)} %get-tuple-element.364.refs_0_), channel_id=1, source_target_pairs={{0,4},{4,0},{1,5},{5,1},{2,6},{6,2},{3,7},{7,3},{8,12},{12,8},{9,1... | collective-permute-start | bytes 3145736 | tf_op jit(solution)/shard_map/ppermute | solution.py:409
  391.6 45.8 %collective-permute-start.37 = (f32[256,1024]{1,0:T(8,128)S(1)}, f32[256,1024]{1,0:T(8,128)}, u32[]{:S(2)}, u32[]{:S(2)}) collective-permute-start(f32[256,1024]{1,0:T(8,128)S(1)} %multiply_add_fusion.2.value), channel_id=1, source_target_pairs={{0,2},{6,4},{1,3},{7,5},{8,10},{14,12},{9,11},{15,13},{16,18},{22,... | collective-permute-start | bytes 3145736 | tf_op jit(solution)/shard_map/ppermute | solution.py:487
  394.3 43.2 %collective-permute-start.39 = (f32[256,1024]{1,0:T(8,128)S(1)}, f32[256,1024]{1,0:T(8,128)}, u32[]{:S(2)}, u32[]{:S(2)}) collective-permute-start(f32[256,1024]{1,0:T(8,128)S(1)} %multiply_add_fusion.2.value), channel_id=1, source_target_pairs={{4,2},{2,4},{5,3},{3,5},{12,10},{10,12},{13,11},{11,13},{20,18},{1... | collective-permute-start | bytes 3145736 | tf_op jit(solution)/shard_map/ppermute | solution.py:487
  395.9 41.5 %collective-permute-start.40 = (f32[256,1024]{1,0:T(8,128)S(1)}, f32[256,1024]{1,0:T(8,128)S(1)}, u32[]{:S(2)}, u32[]{:S(2)}) collective-permute-start(f32[256,1024]{1,0:T(8,128)S(1)} %multiply_add_fusion.2.value), channel_id=1, source_target_pairs={{0,1},{1,0},{6,7},{7,6},{8,9},{9,8},{14,15},{15,14},{16,17},{17,16... | collective-permute-start | bytes 3145736 | tf_op jit(solution)/shard_map/ppermute | solution.py:494
  413.6 39.3 %collective-permute-start.44 = (f32[256,1024]{1,0:T(8,128)S(1)}, f32[256,1024]{1,0:T(8,128)S(1)}, u32[]{:S(2)}, u32[]{:S(2)}) collective-permute-start(f32[256,1024]{1,0:T(8,128)S(1)} %collective-permute-done.38.near), channel_id=1, source_target_pairs={{0,1},{1,0},{6,7},{7,6},{8,9},{9,8},{14,15},{15,14},{16,17},{17,16... | collective-permute-start | bytes 3145736 | tf_op jit(solution)/shard_map/ppermute | solution.py:494
  467.7 302.2 %reduce-scatter.5.cloned.1.call-start = ((), (), s32[]{:S(2)}) async-start(), calls=%async_computation.3 | async-start | bytes 9175040 | tf_op jit(solution)/shard_map/reduce_scatter | solution.py:1025
  474.6 25.3 %collective-permute-start.47 = (f32[256,1024]{1,0:T(8,128)S(1)}, f32[256,1024]{1,0:T(8,128)S(1)}, u32[]{:S(2)}, u32[]{:S(2)}) collective-permute-start(f32[256,1024]{1,0:T(8,128)S(1)} %constant_dynamic-slice_fusion.5), channel_id=1, source_target_pairs={{0,1},{1,0},{2,3},{3,2},{4,5},{5,4},{6,7},{7,6},{8,9},{9,8},{10,11... | collective-permute-start | bytes 3145736 | tf_op jit(solution)/shard_map/ppermute | solution.py:409
  504.4 30.2 %collective-permute-start.51 = (f32[256,1024]{1,0:T(8,128)S(1)}, f32[256,1024]{1,0:T(8,128)}, u32[]{:S(2)}, u32[]{:S(2)}) collective-permute-start(f32[256,1024]{1,0:T(8,128)S(1)} %get-tuple-element.361.refs_0_), channel_id=1, source_target_pairs={{0,4},{4,0},{1,5},{5,1},{2,6},{6,2},{3,7},{7,3},{8,12},{12,8},{9,1... | collective-permute-start | bytes 3145736 | tf_op jit(solution)/shard_map/ppermute | solution.py:409
  573.3 27.2 %collective-permute-start.54 = (f32[256,1024]{1,0:T(8,128)}, f32[256,1024]{1,0:T(8,128)S(1)}, u32[]{:S(2)}, u32[]{:S(2)}) collective-permute-start(f32[256,1024]{1,0:T(8,128)} %collective-permute-done.37.mine), channel_id=1, source_target_pairs={{2,3},{3,2},{4,5},{5,4},{10,11},{11,10},{12,13},{13,12},{18,19},{1... | collective-permute-start | bytes 3145736 | tf_op jit(solution)/shard_map/ppermute | solution.py:504
  574.1 27.5 %collective-permute-start.55 = (f32[256,1024]{1,0:T(8,128)}, f32[256,1024]{1,0:T(8,128)S(1)}, u32[]{:S(2)}, u32[]{:S(2)}) collective-permute-start(f32[256,1024]{1,0:T(8,128)} %collective-permute-done.39.theirs), channel_id=1, source_target_pairs={{2,3},{3,2},{4,5},{5,4},{10,11},{11,10},{12,13},{13,12},{18,19},{1... | collective-permute-start | bytes 3145736 | tf_op jit(solution)/shard_map/ppermute | solution.py:505
  625.2 45.6 %collective-permute-start.61 = (f32[256,1536]{0,1:T(8,128)S(1)}, f32[256,1536]{0,1:T(8,128)S(1)}, u32[]{:S(2)}, u32[]{:S(2)}) collective-permute-start(f32[256,1536]{0,1:T(8,128)S(1)} %slice.576), channel_id=1, source_target_pairs={{2,0},{4,6},{3,1},{5,7},{10,8},{12,14},{11,9},{13,15},{18,16},{20,... | collective-permute-start | bytes 4718600 | tf_op jit(solution)/shard_map/ppermute | solution.py:1001
  628.6 42.0 %collective-permute-start.60 = (f32[256,1024]{1,0:T(8,128)S(1)}, f32[256,1024]{1,0:T(8,128)S(1)}, u32[]{:S(2)}, u32[]{:S(2)}) collective-permute-start(f32[256,1024]{1,0:T(8,128)S(1)} %constant_dynamic-slice_fusion.3), channel_id=1, source_target_pairs={{0,1},{1,0},{2,3},{3,2},{4,5},{5,4},{6,7},{7,6},{8,9},{9,8},{10,11... | collective-permute-start | bytes 3145736 | tf_op jit(solution)/shard_map/ppermute | solution.py:409
  675.6 24.8 %collective-permute-start.62 = (f32[256,1024]{1,0:T(8,128)S(1)}, f32[256,1024]{1,0:T(8,128)}, u32[]{:S(2)}, u32[]{:S(2)}) collective-permute-start(f32[256,1024]{1,0:T(8,128)S(1)} %multiply_add_fusion.value), channel_id=1, source_target_pairs={{0,2},{6,4},{1,3},{7,5},{8,10},{14,12},{9,11},{15,13},{16,18},{22,... | collective-permute-start | bytes 3145736 | tf_op jit(solution)/shard_map/ppermute | solution.py:487
  681.3 32.2 %collective-permute-start.65 = (f32[256,1024]{1,0:T(8,128)S(1)}, f32[256,1024]{1,0:T(8,128)}, u32[]{:S(2)}, u32[]{:S(2)}) collective-permute-start(f32[256,1024]{1,0:T(8,128)S(1)} %multiply_add_fusion.value), channel_id=1, source_target_pairs={{0,1},{1,0},{6,7},{7,6},{8,9},{9,8},{14,15},{15,14},{16,17},{17,16... | collective-permute-start | bytes 3145736 | tf_op jit(solution)/shard_map/ppermute | solution.py:494
  741.7 28.3 %collective-permute-start.68 = (f32[256,1024]{1,0:T(8,128)}, f32[256,1024]{1,0:T(8,128)}, u32[]{:S(2)}, u32[]{:S(2)}) collective-permute-start(f32[256,1024]{1,0:T(8,128)} %collective-permute-done.64.near), channel_id=1, source_target_pairs={{0,1},{1,0},{6,7},{7,6},{8,9},{9,8},{14,15},{15,14},{16,17},{17,16... | collective-permute-start | bytes 3145736 | tf_op jit(solution)/shard_map/ppermute | solution.py:494
  773.7 57.5 %collective-permute-start.74 = (f32[256,1536]{0,1:T(8,128)}, f32[256,1536]{0,1:T(8,128)}, u32[]{:S(2)}, u32[]{:S(2)}) collective-permute-start(f32[256,1536]{0,1:T(8,128)} %slice.499), channel_id=1, source_target_pairs={{2,0},{4,6},{3,1},{5,7},{10,8},{12,14},{11,9},{13,15},{18,16},{20,... | collective-permute-start | bytes 4718600 | tf_op jit(solution)/shard_map/ppermute | solution.py:1094
  787.5 49.4 %collective-permute-start.76 = (f32[128,1536]{0,1:T(8,128)}, f32[128,1536]{0,1:T(8,128)}, u32[]{:S(2)}, u32[]{:S(2)}) collective-permute-start(f32[128,1536]{0,1:T(8,128)} %constant_dynamic-slice_fusion.1), channel_id=1, source_target_pairs={{0,4},{6,2},{1,5},{7,3},{8,12},{14,10},{9,13},{15,11},{16,20},{22,... | collective-permute-start | bytes 2359304 | tf_op jit(solution)/shard_map/ppermute | solution.py:1107
  796.4 34.9 %collective-permute-start.79 = (f32[128,2,256]{0,2,1:T(8,128)S(1)}, f32[128,2,256]{0,2,1:T(8,128)S(1)}, u32[]{:S(2)}, u32[]{:S(2)}) collective-permute-start(f32[128,2,256]{0,2,1:T(8,128)S(1)} %fusion.104), channel_id=1, source_target_pairs={{0,2},{2,0},{1,3},{3,1},{4,6},{6,4},{5,7},{7,5},{8,10},{10,8},{9,1... | collective-permute-start | bytes 786440 | tf_op jit(solution)/shard_map/ppermute | solution.py:417
  (138 other events, 1716.4 us)
Sparse Core Ops, SparseCore 0:
  467.8 76.1 reduce-scatter.2
  623.8 78.8 reduce-scatter.4
